TPU v7x, 32 devices: a whole 2x2x4 slice. The times are simulated.
32 devices in a mesh: tok: 4 (over y, x), hid: 8 (over z, core).
Axes of the slice: x: 2, y: 2, z: 4, core: 2. Of those that a mesh axis runs over, the one named last changes fastest.
Arguments:
- tokens: bfloat16 [512, 8192], P('tok', 'hid'), may hold values from -6 to 6
- gate_weight: bfloat16 [8192, 16384], P('tok', 'hid'), may hold values from -0.09375 to 0.09375
- up_weight: bfloat16 [8192, 16384], P('tok', 'hid'), may hold values from -0.09375 to 0.09375
- down_weight: bfloat16 [16384, 8192], P('hid', 'tok'), may hold values from -0.0625 to 0.0625
- gate_keep: int32 [64, 128], P('tok', 'hid'), may hold values from 0 to 1, as said below
- up_keep: int32 [64, 128], P('tok', 'hid'), may hold values from 0 to 1, as said below
- down_keep: int32 [128, 64], P('hid', 'tok'), may hold values from 0 to 1, as said below
Outputs:
- mixed: bfloat16 [512, 8192], P('hid', 'tok')
Inputs may be any that keep to these rules, and one draw needn't show every extreme that they name: `gate_keep`: in every device's shard of 16 x 16 blocks of a mask, between 64 and 128 blocks are kept; in every mask some shard keeps exactly 128. Shards of down_keep are 16 x 16. `up_keep`: as for gate_keep, drawn independently. `down_keep`: as for gate_keep, drawn independently.
All inputs are finite; a program needn't handle non-finite values.
Results may differ from a plain program's by a relative error of at most 0.0049.
Values may be sent and summed in bfloat16 or wider, within the bound.
No kernel may reach another device: no remote copies, remote signals or barrier semaphores. Data moves between devices by JAX's collectives and lax.ppermute only.
A program may use at most 256 MiB of HBM per device.

v0:
```python
import functools

import jax
import jax.numpy as jnp
from jax import lax
from jax.experimental import pallas as pl
from jax.experimental.pallas import tpu as pltpu
from jax.sharding import PartitionSpec as P

AXES = ("tok", "hid")
BATCHES = 2
VMEM_BYTES = 48 * 1024 * 1024


def masked_tile(weight_ref, keep_ref, out_ref, first_col):
    block_rows = keep_ref.shape[0]
    side = weight_ref.shape[0] // block_rows
    for i in range(block_rows):
        for j in range(weight_ref.shape[1] // side):
            rows, cols = pl.ds(i * side, side), pl.ds(j * side, side)
            block = weight_ref[rows, cols]
            kept = keep_ref[i, first_col + j] != 0
            out_ref[rows, cols] = jnp.where(kept, block, jnp.zeros_like(block))


def gate_up_kernel(place_ref, gate_keep, up_keep, own_ref, other_ref, gate_ref, up_ref, keep_ref, send_ref, x, gate_w, up_w):
    n, rows, half = own_ref.shape
    step = pl.program_id(0)

    @pl.when(step == 0)
    def _():
        core = place_ref[0]
        mine = pl.ds(pl.multiple_of(core * half, half), half)
        others = pl.ds(pl.multiple_of((1 - core) * half, half), half)
        for p in range(n):
            at = pl.ds(p * rows, rows)
            x[at, mine] = own_ref[p]
            x[at, others] = other_ref[mirror(p, n)]

    side = gate_ref.shape[0] // gate_keep.shape[0]
    first_col = step * (gate_ref.shape[1] // side)
    for which, (weight, keep, dense) in enumerate(((gate_ref, gate_keep, gate_w), (up_ref, up_keep, up_w))):
        masked_tile(weight, keep, dense, first_col)
        product = jnp.dot(x[...], dense[...], preferred_element_type=jnp.float32)
        for p in range(n // 2):
            q = p + n // 2
            keep_ref[p, which] = product[p * rows : (p + 1) * rows]
            send_ref[p, which] = product[q * rows : (q + 1) * rows].astype(jnp.bfloat16)


def gate_up(place, own, other, gate_weight, up_weight, gate_keep, up_keep):
    n, rows, half = own.shape
    depth, width = gate_weight.shape
    tile = min(width, 256)
    whole = pl.BlockSpec((n, rows, half), lambda i, *_: (0, 0, 0))
    strip = pl.BlockSpec((depth, tile), lambda i, *_: (0, i))
    out = pl.BlockSpec((n // 2, 2, rows, tile), lambda i, *_: (0, 0, 0, i))
    return pl.pallas_call(
        gate_up_kernel,
        grid_spec=pltpu.PrefetchScalarGridSpec(
            num_scalar_prefetch=3,
            grid=(width // tile,),
            in_specs=[whole, whole, strip, strip],
            out_specs=[out, out],
            scratch_shapes=[
                pltpu.VMEM((n * rows, depth), jnp.bfloat16),
                pltpu.VMEM((depth, tile), jnp.bfloat16),
                pltpu.VMEM((depth, tile), jnp.bfloat16),
            ],
        ),
        out_shape=[
            jax.ShapeDtypeStruct((n // 2, 2, rows, width), jnp.float32),
            jax.ShapeDtypeStruct((n // 2, 2, rows, width), jnp.bfloat16),
        ],
        compiler_params=pltpu.CompilerParams(vmem_limit_bytes=VMEM_BYTES),
        cost_estimate=pl.CostEstimate(
            flops=4 * n * rows * depth * width, bytes_accessed=4 * depth * width, transcendentals=0
        ),
        name="gate_up",
    )(place, gate_keep, up_keep, own, other, gate_weight, up_weight)


def activate(gate, up):
    return (gate / (1.0 + jnp.exp(-gate)) * up).astype(jnp.bfloat16)


def down_kernel(n, place_ref, keep_ref, *refs):
    parts = refs[:n]
    weight_ref, mine_ref, other_ref, h, dense = refs[n:]
    rows = parts[0].shape[0]
    step = pl.program_id(0)

    @pl.when(step == 0)
    def _():
        for p in range(n):
            h[p * rows : (p + 1) * rows] = parts[p][...]

    side = weight_ref.shape[0] // keep_ref.shape[0]
    masked_tile(weight_ref, keep_ref, dense, step * (weight_ref.shape[1] // side))
    product = jnp.dot(h[...], dense[...], preferred_element_type=jnp.float32)
    core = place_ref[0]
    half = rows // 2
    for p in range(n):
        slot = place_ref[1 + p]
        low = product[p * rows : p * rows + half]
        high = product[p * rows + half : (p + 1) * rows]
        mine_ref[slot] = jnp.where(core == 0, low, high)
        other_ref[slot] = jnp.where(core == 0, high, low).astype(jnp.bfloat16)


def down(place, parts, weight, keep):
    n = len(parts)
    rows = parts[0].shape[0]
    depth, width = weight.shape
    tile = min(width, 256)
    out = pl.BlockSpec((n, rows // 2, tile), lambda i, *_: (0, 0, i))
    return pl.pallas_call(
        functools.partial(down_kernel, n),
        grid_spec=pltpu.PrefetchScalarGridSpec(
            num_scalar_prefetch=2,
            grid=(width // tile,),
            in_specs=[pl.BlockSpec((rows, depth), lambda i, *_: (0, 0))] * n
            + [pl.BlockSpec((depth, tile), lambda i, *_: (0, i))],
            out_specs=[out, out],
            scratch_shapes=[
                pltpu.VMEM((n * rows, depth), jnp.bfloat16),
                pltpu.VMEM((depth, tile), jnp.bfloat16),
            ],
        ),
        out_shape=[
            jax.ShapeDtypeStruct((n, rows // 2, width), jnp.float32),
            jax.ShapeDtypeStruct((n, rows // 2, width), jnp.bfloat16),
        ],
        compiler_params=pltpu.CompilerParams(vmem_limit_bytes=VMEM_BYTES),
        cost_estimate=pl.CostEstimate(
            flops=2 * n * rows * depth * width, bytes_accessed=2 * depth * width, transcendentals=0
        ),
        name="down",
    )(place, keep, *parts, weight)


def pick(parts, index):
    chosen = parts[0]
    for i in range(1, len(parts)):
        chosen = jnp.where(index == i, parts[i], chosen)
    return chosen


def mirror(p, n):
    out = 0
    while n > 1:
        out, p, n = out * 2 + p % 2, p // 2, n // 2
    return out


def local(n_tok, n_hid, tokens, gate_weight, up_weight, down_weight, gate_keep, up_keep, down_keep):
    n_z = n_hid // 2
    tok, hid = lax.axis_index("tok"), lax.axis_index("hid")
    z, core = hid // 2, hid % 2
    offsets = [jnp.where(core == 0, p, mirror(p, n_tok)) for p in range(n_tok)]
    place = jnp.stack([core] + [tok ^ z ^ off for off in offsets]).astype(jnp.int32)

    def send(value, to):
        perm = []
        for t in range(n_tok):
            for zz in range(n_z):
                for c in range(2):
                    a, b, d = to(t, zz, c)
                    perm.append((t * n_hid + zz * 2 + c, a * n_hid + b * 2 + d))
        return lax.ppermute(value, AXES, perm)

    def across_tok(value, p):
        return send(value, lambda t, zz, c: (t ^ (p if c == 0 else mirror(p, n_tok)), zz, c))

    def across_z(value, j):
        return send(value, lambda t, zz, c: (t, zz ^ j, c))

    def across_core(value):
        return send(value, lambda t, zz, c: (t, zz, 1 - c))

    def spread(block):
        along_z = [block] + [across_z(block, j) for j in range(1, n_z)]
        picked = [pick(along_z, z ^ tok ^ off) for off in offsets]
        own = jnp.stack([picked[0]] + [across_tok(picked[p], p) for p in range(1, n_tok)])
        return own, across_core(own)

    def middle(own, other):
        kept, sent = gate_up(place, own, other, gate_weight, up_weight, gate_keep, up_keep)
        left = n_tok // 2
        kept = [kept]
        while True:
            kept.append(across_tok(sent, left))
            if left == 1:
                break
            left //= 2
            sent = sum(part[left : 2 * left].astype(jnp.float32) for part in kept).astype(jnp.bfloat16)
        total = sum(part[0].astype(jnp.float32) for part in kept)
        parts = [activate(total[0], total[1])]
        while left < n_tok:
            parts += [across_tok(part, left) for part in parts]
            left *= 2
        return parts

    def finish(parts):
        mine, theirs = down(place, parts, down_weight, down_keep)
        paired = across_core(theirs)
        out = mine[0] + paired[0].astype(jnp.float32)
        for j in range(1, n_z):
            both = (mine[j] + paired[j].astype(jnp.float32)).astype(jnp.bfloat16)
            out += across_z(both, j).astype(jnp.float32)
        return out.astype(jnp.bfloat16)

    rows, features = tokens.shape
    piece = rows // (2 * BATCHES)
    split = tokens.reshape(2, BATCHES, piece, features)
    batches = [split[:, s].reshape(2 * piece, features) for s in range(BATCHES)]
    ready = [spread(block) for block in batches]
    hidden = [middle(*pair) for pair in ready]
    return jnp.concatenate([finish(parts) for parts in hidden], axis=0)


def solution(mesh):
    n_tok, n_hid = mesh.shape["tok"], mesh.shape["hid"]
    return jax.shard_map(
        functools.partial(local, n_tok, n_hid),
        mesh=mesh,
        in_specs=(
            P("tok", "hid"),
            P("tok", "hid"),
            P("tok", "hid"),
            P("hid", "tok"),
            P("tok", "hid"),
            P("tok", "hid"),
            P("hid", "tok"),
        ),
        out_specs=P("hid", "tok"),
        check_vma=False,
    )
```

profile of v0, /device:TPU:0, one launch (start us, length us, event | category | flops | bytes accessed | tf_op | source)
XLA Modules:
  0.0 163.6 jit_solution(12487185965948879714)
XLA Ops:
  0.0 1.0 fusion.16
  1.0 5.1 %collective-permute-start = (bf16[64,1024]{1,0:T(8,128)(2,1)S(1)}, bf16[64,1024]{1,0:T(8,128)(2,1)S(1)}, u32[]{:S(2)}, u32[]{:S(2)}) collective-permute-start(bf16[64,1024]{1,0:T(8,128)(2,1)S(1)} %bitcast.81), channel_id=1, source_target_pairs={{0,6},{1,7},{2,4},{3,5},{4,2},{5,3},{6,0},{7,1},{8,14},{9,15},{10,... | collective-permute-start | bytes 393224 | tf_op jit(solution)/shard_map/ppermute | solution.py:170
  6.1 0.6 collective-permute-start.2
  6.8 3.8 %collective-permute-done = bf16[64,1024]{1,0:T(8,128)(2,1)S(1)} collective-permute-done((bf16[64,1024]{1,0:T(8,128)(2,1)S(1)}, bf16[64,1024]{1,0:T(8,128)(2,1)S(1)}, u32[]{:S(2)}, u32[]{:S(2)}) %collective-permute-start) | collective-permute-done | bytes 131104 | tf_op jit(solution)/shard_map/ppermute | solution.py:170
  10.5 6.6 %collective-permute-done.1 = bf16[64,1024]{1,0:T(8,128)(2,1)S(1)} collective-permute-done((bf16[64,1024]{1,0:T(8,128)(2,1)S(1)}, bf16[64,1024]{1,0:T(8,128)(2,1)S(1)}, u32[]{:S(2)}, u32[]{:S(2)}) %collective-permute-start.1) | collective-permute-done | bytes 131104 | tf_op jit(solution)/shard_map/ppermute | solution.py:170
  17.3 2.5 %collective-permute-start.5 = (bf16[64,1024]{1,0:T(8,128)(2,1)S(1)}, bf16[64,1024]{1,0:T(8,128)(2,1)S(1)}, u32[]{:S(2)}, u32[]{:S(2)}) collective-permute-start(bf16[64,1024]{1,0:T(8,128)(2,1)S(1)} %get-tuple-element.28), channel_id=1, source_target_pairs={{0,24},{1,25},{2,26},{3,27},{4,28},{5,29},{6,30},{7,31},{8,16},{9,... | collective-permute-start | bytes 393224 | tf_op jit(solution)/shard_map/ppermute | solution.py:170
  19.8 0.5 collective-permute-start.3
  20.3 0.5 collective-permute-start.4
  20.8 2.5 %collective-permute-start.16 = (bf16[64,1024]{1,0:T(8,128)(2,1)S(1)}, bf16[64,1024]{1,0:T(8,128)(2,1)S(1)}, u32[]{:S(2)}, u32[]{:S(2)}) collective-permute-start(bf16[64,1024]{1,0:T(8,128)(2,1)S(1)} %bitcast.78), channel_id=1, source_target_pairs={{0,6},{1,7},{2,4},{3,5},{4,2},{5,3},{6,0},{7,1},{8,14},{9,15},{10,... | collective-permute-start | bytes 393224 | tf_op jit(solution)/shard_map/ppermute | solution.py:170
  23.3 0.7 collective-permute-done.5
  24.0 1.2 collective-permute-start.18
  25.8 3.2 %collective-permute-done.16 = bf16[64,1024]{1,0:T(8,128)(2,1)S(1)} collective-permute-done((bf16[64,1024]{1,0:T(8,128)(2,1)S(1)}, bf16[64,1024]{1,0:T(8,128)(2,1)S(1)}, u32[]{:S(2)}, u32[]{:S(2)}) %collective-permute-start.16) | collective-permute-done | bytes 131104 | tf_op jit(solution)/shard_map/ppermute | solution.py:170
  29.1 4.3 %collective-permute-done.17 = bf16[64,1024]{1,0:T(8,128)(2,1)S(1)} collective-permute-done((bf16[64,1024]{1,0:T(8,128)(2,1)S(1)}, bf16[64,1024]{1,0:T(8,128)(2,1)S(1)}, u32[]{:S(2)}, u32[]{:S(2)}) %collective-permute-start.17) | collective-permute-done | bytes 131104 | tf_op jit(solution)/shard_map/ppermute | solution.py:170
  33.4 1.6 collective-permute-start.19
  35.0 1.5 collective-permute-start.20
  36.5 0.5 collective-permute-start.21
  37.1 2.8 %collective-permute-done.19 = bf16[64,1024]{1,0:T(8,128)(2,1)S(1)} collective-permute-done((bf16[64,1024]{1,0:T(8,128)(2,1)S(1)}, bf16[64,1024]{1,0:T(8,128)(2,1)S(1)}, u32[]{:S(2)}, u32[]{:S(2)}) %collective-permute-start.19) | collective-permute-done | bytes 131104 | tf_op jit(solution)/shard_map/ppermute | solution.py:170
  39.9 2.8 %collective-permute-done.20 = bf16[64,1024]{1,0:T(8,128)(2,1)S(1)} collective-permute-done((bf16[64,1024]{1,0:T(8,128)(2,1)S(1)}, bf16[64,1024]{1,0:T(8,128)(2,1)S(1)}, u32[]{:S(2)}, u32[]{:S(2)}) %collective-permute-start.20) | collective-permute-done | bytes 131104 | tf_op jit(solution)/shard_map/ppermute | solution.py:170
  42.8 12.1 %gate_up.2 = (f32[2,2,64,2048]{3,2,1,0:T(8,128)S(1)}, bf16[2,2,64,2048]{3,2,1,0:T(8,128)(2,1)S(1)}) custom-call(s32[5]{0:T(128)S(1)} %stack.53.place_ref, s32[16,16]{1,0:T(8,128)S(1)} %copy-done, s32[16,16]{1,0:T(8,128)S(1)} %copy-done.1, bf16[4,64,1024]{2,1,0:T(8,128)(2,1)S(1)} %pad_maximum_fusion.own_ref, ...), custom_call_target="tpu_custom_call" | custom-call | flops 4294967296 | bytes 16777216 | tf_op jit(solution)/shard_map/gate_up/pallas_call | solution.py:58
  54.9 1.4 collective-permute-start.7
  56.3 12.1 %gate_up.3 = (f32[2,2,64,2048]{3,2,1,0:T(8,128)S(1)}, bf16[2,2,64,2048]{3,2,1,0:T(8,128)(2,1)S(1)}) custom-call(s32[5]{0:T(128)S(1)} %stack.53.place_ref, s32[16,16]{1,0:T(8,128)S(1)} %copy-done, s32[16,16]{1,0:T(8,128)S(1)} %copy-done.1, bf16[4,64,1024]{2,1,0:T(8,128)(2,1)S(1)} %pad_maximum_fusion.1.own_ref, ...), custom_call_target="tpu_custom_call" | custom-call | flops 4294967296 | bytes 16777216 | tf_op jit(solution)/shard_map/gate_up/pallas_call | solution.py:58
  68.4 0.7 collective-permute-start.23
  69.1 0.6 collective-permute-done.7
  69.9 0.6 collective-permute-start.8
  70.5 18.4 %collective-permute-done.23 = bf16[2,2,64,2048]{3,2,1,0:T(8,128)(2,1)S(1)} collective-permute-done((bf16[2,2,64,2048]{3,2,1,0:T(8,128)(2,1)S(1)}, bf16[2,2,64,2048]{3,2,1,0:T(8,128)(2,1)S(1)}, u32[]{:S(2)}, u32[]{:S(2)}) %collective-permute-start.23) | collective-permute-done | bytes 1048608 | tf_op jit(solution)/shard_map/ppermute | solution.py:170
  89.0 0.7 collective-permute-start.24
  90.1 1.4 collective-permute-start.9
  91.5 0.7 collective-permute-start.10
  92.2 8.4 %collective-permute-done.24 = bf16[1,2,64,2048]{3,2,1,0:T(8,128)(2,1)S(1)} collective-permute-done((bf16[1,2,64,2048]{3,2,1,0:T(8,128)(2,1)S(1)}, bf16[1,2,64,2048]{3,2,1,0:T(8,128)(2,1)S(1)}, u32[]{:S(2)}, u32[]{:S(2)}) %collective-permute-start.24) | collective-permute-done | bytes 524320 | tf_op jit(solution)/shard_map/ppermute | solution.py:170
  100.7 2.6 %collective-permute-done.9.refs_1_ = bf16[64,2048]{1,0:T(8,128)(2,1)S(1)} collective-permute-done((bf16[64,2048]{1,0:T(8,128)(2,1)S(1)}, bf16[64,2048]{1,0:T(8,128)(2,1)S(1)}, u32[]{:S(2)}, u32[]{:S(2)}) %collective-permute-start.9) | collective-permute-done | bytes 262176 | tf_op jit(solution)/shard_map/ppermute | solution.py:170
  103.3 1.2 collective-permute-start.11
  104.7 0.6 collective-permute-start.25
  105.3 5.8 %collective-permute-done.11.refs_3_ = bf16[64,2048]{1,0:T(8,128)(2,1)S(1)} collective-permute-done((bf16[64,2048]{1,0:T(8,128)(2,1)S(1)}, bf16[64,2048]{1,0:T(8,128)(2,1)S(1)}, u32[]{:S(2)}, u32[]{:S(2)}) %collective-permute-start.11) | collective-permute-done | bytes 262176 | tf_op jit(solution)/shard_map/ppermute | solution.py:170
  111.2 8.9 %down.2 = (f32[4,32,2048]{2,1,0:T(8,128)S(1)}, bf16[4,32,2048]{2,1,0:T(8,128)(2,1)S(1)}) custom-call(s32[5]{0:T(128)S(1)} %stack.53.place_ref, s32[16,16]{1,0:T(8,128)S(1)} %copy-done.2, bf16[64,2048]{1,0:T(8,128)(2,1)S(1)} %fusion.3.refs_0_, bf16[64,2048]{1,0:T(8,128)(2,1)S(1)} %collective-permute-done.9.refs_1_, ...), custom_call_target="tpu_custom_call" | custom-call | flops 2147483648 | bytes 8388608 | tf_op jit(solution)/shard_map/down/pallas_call | solution.py:117
  120.2 1.4 collective-permute-start.26
  121.6 0.7 collective-permute-start.27
  122.3 4.3 %collective-permute-done.26.refs_2_ = bf16[64,2048]{1,0:T(8,128)(2,1)S(1)} collective-permute-done((bf16[64,2048]{1,0:T(8,128)(2,1)S(1)}, bf16[64,2048]{1,0:T(8,128)(2,1)S(1)}, u32[]{:S(2)}, u32[]{:S(2)}) %collective-permute-start.26) | collective-permute-done | bytes 262176 | tf_op jit(solution)/shard_map/ppermute | solution.py:170
  126.6 2.8 %collective-permute-done.27.refs_3_ = bf16[64,2048]{1,0:T(8,128)(2,1)S(1)} collective-permute-done((bf16[64,2048]{1,0:T(8,128)(2,1)S(1)}, bf16[64,2048]{1,0:T(8,128)(2,1)S(1)}, u32[]{:S(2)}, u32[]{:S(2)}) %collective-permute-start.27) | collective-permute-done | bytes 262176 | tf_op jit(solution)/shard_map/ppermute | solution.py:170
  129.4 8.9 %down.3 = (f32[4,32,2048]{2,1,0:T(8,128)S(1)}, bf16[4,32,2048]{2,1,0:T(8,128)(2,1)S(1)}) custom-call(s32[5]{0:T(128)S(1)} %stack.53.place_ref, s32[16,16]{1,0:T(8,128)S(1)} %copy-done.2, bf16[64,2048]{1,0:T(8,128)(2,1)S(1)} %fusion.1.refs_0_, bf16[64,2048]{1,0:T(8,128)(2,1)S(1)} %collective-permute-done.25.refs_1_, ...), custom_call_target="tpu_custom_call" | custom-call | flops 2147483648 | bytes 8388608 | tf_op jit(solution)/shard_map/down/pallas_call | solution.py:117
  138.6 2.4 %collective-permute-start.14 = (bf16[32,2048]{1,0:T(8,128)(2,1)S(1)}, bf16[32,2048]{1,0:T(8,128)(2,1)S(1)}, u32[]{:S(2)}, u32[]{:S(2)}) collective-permute-start(bf16[32,2048]{1,0:T(8,128)(2,1)S(1)} %get-tuple-element.23), channel_id=1, source_target_pairs={{0,4},{1,5},{2,6},{3,7},{4,0},{5,1},{6,2},{7,3},{8,12},{9,13},{10,... | collective-permute-start | bytes 393224 | tf_op jit(solution)/shard_map/ppermute | solution.py:170
  141.0 2.0 %collective-permute-start.15 = (bf16[32,2048]{1,0:T(8,128)(2,1)S(1)}, bf16[32,2048]{1,0:T(8,128)(2,1)S(1)}, u32[]{:S(2)}, u32[]{:S(2)}) collective-permute-start(bf16[32,2048]{1,0:T(8,128)(2,1)S(1)} %get-tuple-element.22), channel_id=1, source_target_pairs={{0,6},{1,7},{2,4},{3,5},{4,2},{5,3},{6,0},{7,1},{8,14},{9,15},{10,... | collective-permute-start | bytes 393224 | tf_op jit(solution)/shard_map/ppermute | solution.py:170
  143.1 2.4 %collective-permute-start.30 = (bf16[32,2048]{1,0:T(8,128)(2,1)S(1)}, bf16[32,2048]{1,0:T(8,128)(2,1)S(1)}, u32[]{:S(2)}, u32[]{:S(2)}) collective-permute-start(bf16[32,2048]{1,0:T(8,128)(2,1)S(1)} %get-tuple-element.26), channel_id=1, source_target_pairs={{0,4},{1,5},{2,6},{3,7},{4,0},{5,1},{6,2},{7,3},{8,12},{9,13},{10,... | collective-permute-start | bytes 393224 | tf_op jit(solution)/shard_map/ppermute | solution.py:170
  145.5 1.3 collective-permute-done.13
  146.8 2.0 %collective-permute-start.31 = (bf16[32,2048]{1,0:T(8,128)(2,1)S(1)}, bf16[32,2048]{1,0:T(8,128)(2,1)S(1)}, u32[]{:S(2)}, u32[]{:S(2)}) collective-permute-start(bf16[32,2048]{1,0:T(8,128)(2,1)S(1)} %get-tuple-element.25), channel_id=1, source_target_pairs={{0,6},{1,7},{2,4},{3,5},{4,2},{5,3},{6,0},{7,1},{8,14},{9,15},{10,... | collective-permute-start | bytes 393224 | tf_op jit(solution)/shard_map/ppermute | solution.py:170
  148.8 2.7 %collective-permute-done.14 = bf16[32,2048]{1,0:T(8,128)(2,1)S(1)} collective-permute-done((bf16[32,2048]{1,0:T(8,128)(2,1)S(1)}, bf16[32,2048]{1,0:T(8,128)(2,1)S(1)}, u32[]{:S(2)}, u32[]{:S(2)}) %collective-permute-start.14) | collective-permute-done | bytes 131104 | tf_op jit(solution)/shard_map/ppermute | solution.py:170
  151.7 1.2 collective-permute-done.29
  152.9 9.9 %collective-permute-done.30 = bf16[32,2048]{1,0:T(8,128)(2,1)S(1)} collective-permute-done((bf16[32,2048]{1,0:T(8,128)(2,1)S(1)}, bf16[32,2048]{1,0:T(8,128)(2,1)S(1)}, u32[]{:S(2)}, u32[]{:S(2)}) %collective-permute-start.30) | collective-permute-done | bytes 131104 | tf_op jit(solution)/shard_map/ppermute | solution.py:170
  162.9 0.7 pad_maximum_fusion.2
  (43 shorter events, 2.5 us)
Async XLA Ops:
  1.0 9.5 %collective-permute-start = (bf16[64,1024]{1,0:T(8,128)(2,1)S(1)}, bf16[64,1024]{1,0:T(8,128)(2,1)S(1)}, u32[]{:S(2)}, u32[]{:S(2)}) collective-permute-start(bf16[64,1024]{1,0:T(8,128)(2,1)S(1)} %bitcast.81), channel_id=1, source_target_pairs={{0,6},{1,7},{2,4},{3,5},{4,2},{5,3},{6,0},{7,1},{8,14},{9,15},{10,... | collective-permute-start | bytes 393224 | tf_op jit(solution)/shard_map/ppermute | solution.py:170
  6.1 11.1 %collective-permute-start.1 = (bf16[64,1024]{1,0:T(8,128)(2,1)S(1)}, bf16[64,1024]{1,0:T(8,128)(2,1)S(1)}, u32[]{:S(2)}, u32[]{:S(2)}) collective-permute-start(bf16[64,1024]{1,0:T(8,128)(2,1)S(1)} %bitcast.82), channel_id=1, source_target_pairs={{0,4},{1,5},{2,6},{3,7},{4,0},{5,1},{6,2},{7,3},{8,12},{9,13},{10,... | collective-permute-start | bytes 393224 | tf_op jit(solution)/shard_map/ppermute | solution.py:170
  6.1 11.1 %collective-permute-start.2 = (bf16[64,1024]{1,0:T(8,128)(2,1)S(1)}, bf16[64,1024]{1,0:T(8,128)(2,1)S(1)}, u32[]{:S(2)}, u32[]{:S(2)}) collective-permute-start(bf16[64,1024]{1,0:T(8,128)(2,1)S(1)} %bitcast.83), channel_id=1, source_target_pairs={{0,2},{1,3},{2,0},{3,1},{4,6},{5,7},{6,4},{7,5},{8,10},{9,11},{10,... | collective-permute-start | bytes 393224 | tf_op jit(solution)/shard_map/ppermute | solution.py:170
  6.7 36.0 %copy-start = (s32[16,16]{1,0:T(8,128)S(1)}, s32[16,16]{1,0:T(8,128)}, u32[]{:S(2)}) copy-start(s32[16,16]{1,0:T(8,128)} %gate_keep.3) | copy-start | bytes 3076
  6.8 36.0 %copy-start.1 = (s32[16,16]{1,0:T(8,128)S(1)}, s32[16,16]{1,0:T(8,128)}, u32[]{:S(2)}) copy-start(s32[16,16]{1,0:T(8,128)} %up_keep.3) | copy-start | bytes 3076
  17.3 6.8 %collective-permute-start.5 = (bf16[64,1024]{1,0:T(8,128)(2,1)S(1)}, bf16[64,1024]{1,0:T(8,128)(2,1)S(1)}, u32[]{:S(2)}, u32[]{:S(2)}) collective-permute-start(bf16[64,1024]{1,0:T(8,128)(2,1)S(1)} %get-tuple-element.28), channel_id=1, source_target_pairs={{0,24},{1,25},{2,26},{3,27},{4,28},{5,29},{6,30},{7,31},{8,16},{9,... | collective-permute-start | bytes 393224 | tf_op jit(solution)/shard_map/ppermute | solution.py:170
  19.8 5.9 %collective-permute-start.3 = (bf16[64,1024]{1,0:T(8,128)(2,1)S(1)}, bf16[64,1024]{1,0:T(8,128)(2,1)S(1)}, u32[]{:S(2)}, u32[]{:S(2)}) collective-permute-start(bf16[64,1024]{1,0:T(8,128)(2,1)S(1)} %get-tuple-element.30), channel_id=1, source_target_pairs={{0,8},{1,17},{2,10},{3,19},{4,12},{5,21},{6,14},{7,23},{8,0},{9,25... | collective-permute-start | bytes 393224 | tf_op jit(solution)/shard_map/ppermute | solution.py:170
  20.3 5.4 %collective-permute-start.4 = (bf16[64,1024]{1,0:T(8,128)(2,1)S(1)}, bf16[64,1024]{1,0:T(8,128)(2,1)S(1)}, u32[]{:S(2)}, u32[]{:S(2)}) collective-permute-start(bf16[64,1024]{1,0:T(8,128)(2,1)S(1)} %get-tuple-element.29), channel_id=1, source_target_pairs={{0,16},{1,9},{2,18},{3,11},{4,20},{5,13},{6,22},{7,15},{8,24},{9,1... | collective-permute-start | bytes 393224 | tf_op jit(solution)/shard_map/ppermute | solution.py:170
  20.8 8.2 %collective-permute-start.16 = (bf16[64,1024]{1,0:T(8,128)(2,1)S(1)}, bf16[64,1024]{1,0:T(8,128)(2,1)S(1)}, u32[]{:S(2)}, u32[]{:S(2)}) collective-permute-start(bf16[64,1024]{1,0:T(8,128)(2,1)S(1)} %bitcast.78), channel_id=1, source_target_pairs={{0,6},{1,7},{2,4},{3,5},{4,2},{5,3},{6,0},{7,1},{8,14},{9,15},{10,... | collective-permute-start | bytes 393224 | tf_op jit(solution)/shard_map/ppermute | solution.py:170
  23.3 10.1 %collective-permute-start.17 = (bf16[64,1024]{1,0:T(8,128)(2,1)S(1)}, bf16[64,1024]{1,0:T(8,128)(2,1)S(1)}, u32[]{:S(2)}, u32[]{:S(2)}) collective-permute-start(bf16[64,1024]{1,0:T(8,128)(2,1)S(1)} %bitcast.79), channel_id=1, source_target_pairs={{0,4},{1,5},{2,6},{3,7},{4,0},{5,1},{6,2},{7,3},{8,12},{9,13},{10,... | collective-permute-start | bytes 393224 | tf_op jit(solution)/shard_map/ppermute | solution.py:170
  24.0 9.3 %collective-permute-start.18 = (bf16[64,1024]{1,0:T(8,128)(2,1)S(1)}, bf16[64,1024]{1,0:T(8,128)(2,1)S(1)}, u32[]{:S(2)}, u32[]{:S(2)}) collective-permute-start(bf16[64,1024]{1,0:T(8,128)(2,1)S(1)} %bitcast.80), channel_id=1, source_target_pairs={{0,2},{1,3},{2,0},{3,1},{4,6},{5,7},{6,4},{7,5},{8,10},{9,11},{10,... | collective-permute-start | bytes 393224 | tf_op jit(solution)/shard_map/ppermute | solution.py:170
  25.8 17.0 %collective-permute-start.6 = (bf16[4,64,1024]{2,1,0:T(8,128)(2,1)S(1)}, bf16[4,64,1024]{2,1,0:T(8,128)(2,1)S(1)}, u32[]{:S(2)}, u32[]{:S(2)}) collective-permute-start(bf16[4,64,1024]{2,1,0:T(8,128)(2,1)S(1)} %pad_maximum_fusion.own_ref), channel_id=1, source_target_pairs={{0,1},{1,0},{2,3},{3,2},{4,5},{5,4},{6,7},{7,6},{8,9},{9,8},{10,11... | collective-permute-start | bytes 1572872 | tf_op jit(solution)/shard_map/ppermute | solution.py:170
  33.4 6.4 %collective-permute-start.19 = (bf16[64,1024]{1,0:T(8,128)(2,1)S(1)}, bf16[64,1024]{1,0:T(8,128)(2,1)S(1)}, u32[]{:S(2)}, u32[]{:S(2)}) collective-permute-start(bf16[64,1024]{1,0:T(8,128)(2,1)S(1)} %get-tuple-element.34), channel_id=1, source_target_pairs={{0,8},{1,17},{2,10},{3,19},{4,12},{5,21},{6,14},{7,23},{8,0},{9,25... | collective-permute-start | bytes 393224 | tf_op jit(solution)/shard_map/ppermute | solution.py:170
  35.0 7.6 %collective-permute-start.20 = (bf16[64,1024]{1,0:T(8,128)(2,1)S(1)}, bf16[64,1024]{1,0:T(8,128)(2,1)S(1)}, u32[]{:S(2)}, u32[]{:S(2)}) collective-permute-start(bf16[64,1024]{1,0:T(8,128)(2,1)S(1)} %get-tuple-element.33), channel_id=1, source_target_pairs={{0,16},{1,9},{2,18},{3,11},{4,20},{5,13},{6,22},{7,15},{8,24},{9,1... | collective-permute-start | bytes 393224 | tf_op jit(solution)/shard_map/ppermute | solution.py:170
  36.5 6.1 %collective-permute-start.21 = (bf16[64,1024]{1,0:T(8,128)(2,1)S(1)}, bf16[64,1024]{1,0:T(8,128)(2,1)S(1)}, u32[]{:S(2)}, u32[]{:S(2)}) collective-permute-start(bf16[64,1024]{1,0:T(8,128)(2,1)S(1)} %get-tuple-element.32), channel_id=1, source_target_pairs={{0,24},{1,25},{2,26},{3,27},{4,28},{5,29},{6,30},{7,31},{8,16},{9,... | collective-permute-start | bytes 393224 | tf_op jit(solution)/shard_map/ppermute | solution.py:170
  42.7 13.6 %collective-permute-start.22 = (bf16[4,64,1024]{2,1,0:T(8,128)(2,1)S(1)}, bf16[4,64,1024]{2,1,0:T(8,128)(2,1)S(1)}, u32[]{:S(2)}, u32[]{:S(2)}) collective-permute-start(bf16[4,64,1024]{2,1,0:T(8,128)(2,1)S(1)} %pad_maximum_fusion.1.own_ref), channel_id=1, source_target_pairs={{0,1},{1,0},{2,3},{3,2},{4,5},{5,4},{6,7},{7,6},{8,9},{9,8},{10,11... | collective-permute-start | bytes 1572872 | tf_op jit(solution)/shard_map/ppermute | solution.py:170
  54.9 14.9 %collective-permute-start.7 = (bf16[2,2,64,2048]{3,2,1,0:T(8,128)(2,1)S(1)}, bf16[2,2,64,2048]{3,2,1,0:T(8,128)(2,1)S(1)}, u32[]{:S(2)}, u32[]{:S(2)}) collective-permute-start(bf16[2,2,64,2048]{3,2,1,0:T(8,128)(2,1)S(1)} %get-tuple-element.14), channel_id=1, source_target_pairs={{0,16},{1,9},{2,18},{3,11},{4,20},{5,13},{6,22},{7,15},{8,24},{9,1... | collective-permute-start | bytes 3145736 | tf_op jit(solution)/shard_map/ppermute | solution.py:170
  68.4 20.5 %collective-permute-start.23 = (bf16[2,2,64,2048]{3,2,1,0:T(8,128)(2,1)S(1)}, bf16[2,2,64,2048]{3,2,1,0:T(8,128)(2,1)S(1)}, u32[]{:S(2)}, u32[]{:S(2)}) collective-permute-start(bf16[2,2,64,2048]{3,2,1,0:T(8,128)(2,1)S(1)} %get-tuple-element.18), channel_id=1, source_target_pairs={{0,16},{1,9},{2,18},{3,11},{4,20},{5,13},{6,22},{7,15},{8,24},{9,1... | collective-permute-start | bytes 3145736 | tf_op jit(solution)/shard_map/ppermute | solution.py:170
  69.9 19.9 %collective-permute-start.8 = (bf16[1,2,64,2048]{3,2,1,0:T(8,128)(2,1)S(1)}, bf16[1,2,64,2048]{3,2,1,0:T(8,128)(2,1)S(1)}, u32[]{:S(2)}, u32[]{:S(2)}) collective-permute-start(bf16[1,2,64,2048]{3,2,1,0:T(8,128)(2,1)S(1)} %add_convert_fusion.1), channel_id=1, source_target_pairs={{0,8},{1,17},{2,10},{3,19},{4,12},{5,21},{6,14},{7,23},{8,0},{9,25... | collective-permute-start | bytes 1572872 | tf_op jit(solution)/shard_map/ppermute | solution.py:170
  89.0 11.5 %collective-permute-start.24 = (bf16[1,2,64,2048]{3,2,1,0:T(8,128)(2,1)S(1)}, bf16[1,2,64,2048]{3,2,1,0:T(8,128)(2,1)S(1)}, u32[]{:S(2)}, u32[]{:S(2)}) collective-permute-start(bf16[1,2,64,2048]{3,2,1,0:T(8,128)(2,1)S(1)} %add_convert_fusion), channel_id=1, source_target_pairs={{0,8},{1,17},{2,10},{3,19},{4,12},{5,21},{6,14},{7,23},{8,0},{9,25... | collective-permute-start | bytes 1572872 | tf_op jit(solution)/shard_map/ppermute | solution.py:170
  90.1 21.1 %copy-start.2 = (s32[16,16]{1,0:T(8,128)S(1)}, s32[16,16]{1,0:T(8,128)}, u32[]{:S(2)}) copy-start(s32[16,16]{1,0:T(8,128)} %keep_ref.3) | copy-start | bytes 3076
  90.1 13.2 %collective-permute-start.9 = (bf16[64,2048]{1,0:T(8,128)(2,1)S(1)}, bf16[64,2048]{1,0:T(8,128)(2,1)S(1)}, u32[]{:S(2)}, u32[]{:S(2)}) collective-permute-start(bf16[64,2048]{1,0:T(8,128)(2,1)S(1)} %fusion.3.refs_0_), channel_id=1, source_target_pairs={{0,8},{1,17},{2,10},{3,19},{4,12},{5,21},{6,14},{7,23},{8,0},{9,25... | collective-permute-start | bytes 786440 | tf_op jit(solution)/shard_map/ppermute | solution.py:170
  91.5 13.8 %collective-permute-start.10 = (bf16[64,2048]{1,0:T(8,128)(2,1)S(1)}, bf16[64,2048]{1,0:T(8,128)(2,1)S(1)}, u32[]{:S(2)}, u32[]{:S(2)}) collective-permute-start(bf16[64,2048]{1,0:T(8,128)(2,1)S(1)} %fusion.3.refs_0_), channel_id=1, source_target_pairs={{0,16},{1,9},{2,18},{3,11},{4,20},{5,13},{6,22},{7,15},{8,24},{9,1... | collective-permute-start | bytes 786440 | tf_op jit(solution)/shard_map/ppermute | solution.py:170
  103.3 7.8 %collective-permute-start.11 = (bf16[64,2048]{1,0:T(8,128)(2,1)S(1)}, bf16[64,2048]{1,0:T(8,128)(2,1)S(1)}, u32[]{:S(2)}, u32[]{:S(2)}) collective-permute-start(bf16[64,2048]{1,0:T(8,128)(2,1)S(1)} %collective-permute-done.9.refs_1_), channel_id=1, source_target_pairs={{0,16},{1,9},{2,18},{3,11},{4,20},{5,13},{6,22},{7,15},{8,24},{9,1... | collective-permute-start | bytes 786440 | tf_op jit(solution)/shard_map/ppermute | solution.py:170
  104.7 16.9 %collective-permute-start.25 = (bf16[64,2048]{1,0:T(8,128)(2,1)S(1)}, bf16[64,2048]{1,0:T(8,128)(2,1)S(1)}, u32[]{:S(2)}, u32[]{:S(2)}) collective-permute-start(bf16[64,2048]{1,0:T(8,128)(2,1)S(1)} %fusion.1.refs_0_), channel_id=1, source_target_pairs={{0,8},{1,17},{2,10},{3,19},{4,12},{5,21},{6,14},{7,23},{8,0},{9,25... | collective-permute-start | bytes 786440 | tf_op jit(solution)/shard_map/ppermute | solution.py:170
  120.1 18.3 %collective-permute-start.12 = (bf16[4,32,2048]{2,1,0:T(8,128)(2,1)S(1)}, bf16[4,32,2048]{2,1,0:T(8,128)(2,1)S(1)}, u32[]{:S(2)}, u32[]{:S(2)}) collective-permute-start(bf16[4,32,2048]{2,1,0:T(8,128)(2,1)S(1)} %get-tuple-element.16), channel_id=1, source_target_pairs={{0,1},{1,0},{2,3},{3,2},{4,5},{5,4},{6,7},{7,6},{8,9},{9,8},{10,11... | collective-permute-start | bytes 1572872 | tf_op jit(solution)/shard_map/ppermute | solution.py:170
  120.2 6.4 %collective-permute-start.26 = (bf16[64,2048]{1,0:T(8,128)(2,1)S(1)}, bf16[64,2048]{1,0:T(8,128)(2,1)S(1)}, u32[]{:S(2)}, u32[]{:S(2)}) collective-permute-start(bf16[64,2048]{1,0:T(8,128)(2,1)S(1)} %fusion.1.refs_0_), channel_id=1, source_target_pairs={{0,16},{1,9},{2,18},{3,11},{4,20},{5,13},{6,22},{7,15},{8,24},{9,1... | collective-permute-start | bytes 786440 | tf_op jit(solution)/shard_map/ppermute | solution.py:170
  121.6 7.8 %collective-permute-start.27 = (bf16[64,2048]{1,0:T(8,128)(2,1)S(1)}, bf16[64,2048]{1,0:T(8,128)(2,1)S(1)}, u32[]{:S(2)}, u32[]{:S(2)}) collective-permute-start(bf16[64,2048]{1,0:T(8,128)(2,1)S(1)} %collective-permute-done.25.refs_1_), channel_id=1, source_target_pairs={{0,16},{1,9},{2,18},{3,11},{4,20},{5,13},{6,22},{7,15},{8,24},{9,1... | collective-permute-start | bytes 786440 | tf_op jit(solution)/shard_map/ppermute | solution.py:170
  138.3 4.6 %collective-permute-start.28 = (bf16[4,32,2048]{2,1,0:T(8,128)(2,1)S(1)}, bf16[4,32,2048]{2,1,0:T(8,128)(2,1)S(1)}, u32[]{:S(2)}, u32[]{:S(2)}) collective-permute-start(bf16[4,32,2048]{2,1,0:T(8,128)(2,1)S(1)} %get-tuple-element.20), channel_id=1, source_target_pairs={{0,1},{1,0},{2,3},{3,2},{4,5},{5,4},{6,7},{7,6},{8,9},{9,8},{10,11... | collective-permute-start | bytes 1572872 | tf_op jit(solution)/shard_map/ppermute | solution.py:170
  138.5 8.3 %collective-permute-start.13 = (bf16[32,2048]{1,0:T(8,128)(2,1)S(1)}, bf16[32,2048]{1,0:T(8,128)(2,1)S(1)}, u32[]{:S(2)}, u32[]{:S(2)}) collective-permute-start(bf16[32,2048]{1,0:T(8,128)(2,1)S(1)} %get-tuple-element.21), channel_id=1, source_target_pairs={{0,2},{1,3},{2,0},{3,1},{4,6},{5,7},{6,4},{7,5},{8,10},{9,11},{10,... | collective-permute-start | bytes 393224 | tf_op jit(solution)/shard_map/ppermute | solution.py:170
  138.6 13.0 %collective-permute-start.14 = (bf16[32,2048]{1,0:T(8,128)(2,1)S(1)}, bf16[32,2048]{1,0:T(8,128)(2,1)S(1)}, u32[]{:S(2)}, u32[]{:S(2)}) collective-permute-start(bf16[32,2048]{1,0:T(8,128)(2,1)S(1)} %get-tuple-element.23), channel_id=1, source_target_pairs={{0,4},{1,5},{2,6},{3,7},{4,0},{5,1},{6,2},{7,3},{8,12},{9,13},{10,... | collective-permute-start | bytes 393224 | tf_op jit(solution)/shard_map/ppermute | solution.py:170
  141.0 10.6 %collective-permute-start.15 = (bf16[32,2048]{1,0:T(8,128)(2,1)S(1)}, bf16[32,2048]{1,0:T(8,128)(2,1)S(1)}, u32[]{:S(2)}, u32[]{:S(2)}) collective-permute-start(bf16[32,2048]{1,0:T(8,128)(2,1)S(1)} %get-tuple-element.22), channel_id=1, source_target_pairs={{0,6},{1,7},{2,4},{3,5},{4,2},{5,3},{6,0},{7,1},{8,14},{9,15},{10,... | collective-permute-start | bytes 393224 | tf_op jit(solution)/shard_map/ppermute | solution.py:170
  143.1 9.8 %collective-permute-start.29 = (bf16[32,2048]{1,0:T(8,128)(2,1)S(1)}, bf16[32,2048]{1,0:T(8,128)(2,1)S(1)}, u32[]{:S(2)}, u32[]{:S(2)}) collective-permute-start(bf16[32,2048]{1,0:T(8,128)(2,1)S(1)} %get-tuple-element.24), channel_id=1, source_target_pairs={{0,2},{1,3},{2,0},{3,1},{4,6},{5,7},{6,4},{7,5},{8,10},{9,11},{10,... | collective-permute-start | bytes 393224 | tf_op jit(solution)/shard_map/ppermute | solution.py:170
  143.1 19.6 %collective-permute-start.30 = (bf16[32,2048]{1,0:T(8,128)(2,1)S(1)}, bf16[32,2048]{1,0:T(8,128)(2,1)S(1)}, u32[]{:S(2)}, u32[]{:S(2)}) collective-permute-start(bf16[32,2048]{1,0:T(8,128)(2,1)S(1)} %get-tuple-element.26), channel_id=1, source_target_pairs={{0,4},{1,5},{2,6},{3,7},{4,0},{5,1},{6,2},{7,3},{8,12},{9,13},{10,... | collective-permute-start | bytes 393224 | tf_op jit(solution)/shard_map/ppermute | solution.py:170
  146.8 15.9 %collective-permute-start.31 = (bf16[32,2048]{1,0:T(8,128)(2,1)S(1)}, bf16[32,2048]{1,0:T(8,128)(2,1)S(1)}, u32[]{:S(2)}, u32[]{:S(2)}) collective-permute-start(bf16[32,2048]{1,0:T(8,128)(2,1)S(1)} %get-tuple-element.25), channel_id=1, source_target_pairs={{0,6},{1,7},{2,4},{3,5},{4,2},{5,3},{6,0},{7,1},{8,14},{9,15},{10,... | collective-permute-start | bytes 393224 | tf_op jit(solution)/shard_map/ppermute | solution.py:170
where the time goes:
time: 164 us
  waiting for transfers between devices  82.9 us (51%)
  Pallas kernels  42 us (26%)
  starting transfers between devices  35.2 us (21%)
  other arithmetic  2.22 us (1%)
    ppermute x32, waiting for transfers between devices, send(): return lax.ppermute(value, AXES, perm)  82.9 us
    ppermute x32, starting transfers between devices, send(): return lax.ppermute(value, AXES, perm)  35.2 us
    pallas_call x2, Pallas kernels, gate_up(): pl.pallas_call(gate_up_kernel, grid_spec=pltpu.PrefetchScalarGridSpec(num...  24.2 us
    pallas_call x2, Pallas kernels, down(): pl.pallas_call(functools.partial(down_kernel, n), grid_spec=pltpu.Prefetc...  17.8 us
  transfers between devices with their start and end apart: 32, of which 19 were waited for; matrix products, arithmetic and copies ran while one was open for 1% of the time, Pallas kernels for 26%

commit v1 on v0

v1 whole, which is shorter than its diff:
```python
import functools

import jax
import jax.numpy as jnp
from jax import lax
from jax.experimental import pallas as pl
from jax.experimental.pallas import tpu as pltpu
from jax.sharding import PartitionSpec as P

AXES = ("tok", "hid")
BATCHES = 2
VMEM_BYTES = 48 * 1024 * 1024


def masked_product(x_ref, weight_ref, keep_ref):
    block_rows, width = keep_ref.shape
    side = weight_ref.shape[0] // block_rows
    group = min(4, block_rows)
    total = None
    for first in range(0, block_rows, group):
        strips = []
        for i in range(first, first + group):
            keep = jnp.broadcast_to(keep_ref[i : i + 1, :], (16, width)).astype(jnp.bfloat16)
            block = weight_ref[i * side : (i + 1) * side, :].reshape(side // 16, 16, width)
            strips.append((block * keep[None]).reshape(side, width))
        term = jnp.dot(
            x_ref[:, first * side : (first + group) * side],
            jnp.concatenate(strips, axis=0),
            preferred_element_type=jnp.float32,
        )
        total = term if total is None else total + term
    return total


def widen(keep_mask, width):
    return jnp.repeat(keep_mask.astype(jnp.float32), width // keep_mask.shape[1], axis=1)


def gate_up_kernel(place_ref, own_ref, other_ref, gate_ref, up_ref, gate_keep, up_keep, *refs):
    keep_ref, send_ref, x = refs[-3:]
    n, rows, half = own_ref.shape
    step = pl.program_id(0)

    @pl.when(step == 0)
    def _():
        core = place_ref[0]
        mine = pl.ds(pl.multiple_of(core * half, half), half)
        others = pl.ds(pl.multiple_of((1 - core) * half, half), half)
        for p in range(n):
            at = pl.ds(p * rows, rows)
            x[at, mine] = own_ref[p]
            x[at, others] = other_ref[mirror(p, n)]

    for which, (weight, keep) in enumerate(((gate_ref, gate_keep), (up_ref, up_keep))):
        product = masked_product(x, weight, keep)
        for p in range(n // 2):
            q = p + n // 2
            keep_ref[p, which] = product[p * rows : (p + 1) * rows]
            send_ref[p, which] = product[q * rows : (q + 1) * rows].astype(jnp.bfloat16)


def gate_up(place, own, other, gate_weight, up_weight, gate_keep, up_keep, after):
    n, rows, half = own.shape
    depth, width = gate_weight.shape
    tile = min(width, 256)
    whole = pl.BlockSpec((n, rows, half), lambda i, *_: (0, 0, 0))
    strip = pl.BlockSpec((depth, tile), lambda i, *_: (0, i))
    mask = pl.BlockSpec((gate_keep.shape[0], tile), lambda i, *_: (0, i))
    out = pl.BlockSpec((n // 2, 2, rows, tile), lambda i, *_: (0, 0, 0, i))
    return pl.pallas_call(
        gate_up_kernel,
        grid_spec=pltpu.PrefetchScalarGridSpec(
            num_scalar_prefetch=1,
            grid=(width // tile,),
            in_specs=[whole, whole, strip, strip, mask, mask] + [pl.BlockSpec(memory_space=pl.ANY)] * len(after),
            out_specs=[out, out],
            scratch_shapes=[pltpu.VMEM((n * rows, depth), jnp.bfloat16)],
        ),
        out_shape=[
            jax.ShapeDtypeStruct((n // 2, 2, rows, width), jnp.float32),
            jax.ShapeDtypeStruct((n // 2, 2, rows, width), jnp.bfloat16),
        ],
        compiler_params=pltpu.CompilerParams(vmem_limit_bytes=VMEM_BYTES),
        cost_estimate=pl.CostEstimate(
            flops=4 * n * rows * depth * width, bytes_accessed=4 * depth * width, transcendentals=0
        ),
        name="gate_up",
    )(place, own, other, gate_weight, up_weight, gate_keep, up_keep, *after)


def activate(gate, up):
    return (gate / (1.0 + jnp.exp(-gate)) * up).astype(jnp.bfloat16)


def down_kernel(n, place_ref, *refs):
    parts = refs[:n]
    weight_ref, keep_ref = refs[n : n + 2]
    mine_ref, other_ref, h = refs[-3:]
    rows = parts[0].shape[0]
    step = pl.program_id(0)

    @pl.when(step == 0)
    def _():
        for p in range(n):
            h[p * rows : (p + 1) * rows] = parts[p][...]

    product = masked_product(h, weight_ref, keep_ref)
    core = place_ref[0]
    half = rows // 2
    for p in range(n):
        slot = place_ref[1 + p]
        low = product[p * rows : p * rows + half]
        high = product[p * rows + half : (p + 1) * rows]
        mine_ref[slot] = jnp.where(core == 0, low, high)
        other_ref[slot] = jnp.where(core == 0, high, low).astype(jnp.bfloat16)


def down(place, parts, weight, keep, after):
    n = len(parts)
    rows = parts[0].shape[0]
    depth, width = weight.shape
    tile = min(width, 256)
    out = pl.BlockSpec((n, rows // 2, tile), lambda i, *_: (0, 0, i))
    return pl.pallas_call(
        functools.partial(down_kernel, n),
        grid_spec=pltpu.PrefetchScalarGridSpec(
            num_scalar_prefetch=1,
            grid=(width // tile,),
            in_specs=[pl.BlockSpec((rows, depth), lambda i, *_: (0, 0))] * n
            + [pl.BlockSpec((depth, tile), lambda i, *_: (0, i))]
            + [pl.BlockSpec((keep.shape[0], tile), lambda i, *_: (0, i))]
            + [pl.BlockSpec(memory_space=pl.ANY)] * len(after),
            out_specs=[out, out],
            scratch_shapes=[pltpu.VMEM((n * rows, depth), jnp.bfloat16)],
        ),
        out_shape=[
            jax.ShapeDtypeStruct((n, rows // 2, width), jnp.float32),
            jax.ShapeDtypeStruct((n, rows // 2, width), jnp.bfloat16),
        ],
        compiler_params=pltpu.CompilerParams(vmem_limit_bytes=VMEM_BYTES),
        cost_estimate=pl.CostEstimate(
            flops=2 * n * rows * depth * width, bytes_accessed=2 * depth * width, transcendentals=0
        ),
        name="down",
    )(place, *parts, weight, keep, *after)


def pick_kernel(n, order_ref, *refs):
    outs = refs[-n:]
    for p in range(n):
        for i in range(n):

            @pl.when(order_ref[p] == i)
            def _():
                outs[p][...] = refs[i][...]


def pick(order, parts, after):
    n = len(parts)
    spec = pl.BlockSpec(memory_space=pltpu.VMEM)
    return pl.pallas_call(
        functools.partial(pick_kernel, n),
        grid_spec=pltpu.PrefetchScalarGridSpec(
            num_scalar_prefetch=1,
            grid=(),
            in_specs=[spec] * n + [pl.BlockSpec(memory_space=pl.ANY)] * len(after),
            out_specs=[spec] * n,
        ),
        out_shape=[jax.ShapeDtypeStruct(parts[0].shape, parts[0].dtype)] * n,
        compiler_params=pltpu.CompilerParams(vmem_limit_bytes=VMEM_BYTES),
        name="pick",
    )(order, *parts, *after)


def join_kernel(n, *refs):
    for p in range(n):
        refs[-1][p] = refs[p][...]


def join(parts, after):
    n = len(parts)
    spec = pl.BlockSpec(memory_space=pltpu.VMEM)
    return pl.pallas_call(
        functools.partial(join_kernel, n),
        in_specs=[spec] * n + [pl.BlockSpec(memory_space=pl.ANY)] * len(after),
        out_specs=spec,
        out_shape=jax.ShapeDtypeStruct((n,) + parts[0].shape, parts[0].dtype),
        compiler_params=pltpu.CompilerParams(vmem_limit_bytes=VMEM_BYTES),
        name="join",
    )(*parts, *after)


def mirror(p, n):
    out = 0
    while n > 1:
        out, p, n = out * 2 + p % 2, p // 2, n // 2
    return out


def local(n_tok, n_hid, tokens, gate_weight, up_weight, down_weight, gate_keep, up_keep, down_keep):
    n_z = n_hid // 2
    tok, hid = lax.axis_index("tok"), lax.axis_index("hid")
    z, core = hid // 2, hid % 2
    offsets = [jnp.where(core == 0, p, mirror(p, n_tok)) for p in range(n_tok)]
    place = jnp.stack([core] + [tok ^ z ^ off for off in offsets]).astype(jnp.int32)

    def send(value, to):
        perm = []
        for t in range(n_tok):
            for zz in range(n_z):
                for c in range(2):
                    a, b, d = to(t, zz, c)
                    perm.append((t * n_hid + zz * 2 + c, a * n_hid + b * 2 + d))
        return lax.ppermute(value, AXES, perm)

    def across_tok(value, p):
        return send(value, lambda t, zz, c: (t ^ (p if c == 0 else mirror(p, n_tok)), zz, c))

    def across_z(value, j):
        return send(value, lambda t, zz, c: (t, zz ^ j, c))

    def across_core(value):
        return send(value, lambda t, zz, c: (t, zz, 1 - c))

    def along(block):
        return pick(place[1:], [block] + [across_z(block, j) for j in range(1, n_z)], ())

    def spread(picked, after):
        own = join([picked[0]] + [across_tok(picked[p], p) for p in range(1, n_tok)], after)
        return own, across_core(own)

    def halve(kept, sent):
        left = n_tok // 2
        kept = [kept]
        while True:
            kept.append(across_tok(sent, left))
            if left == 1:
                break
            left //= 2
            sent = sum(part[left : 2 * left].astype(jnp.float32) for part in kept).astype(jnp.bfloat16)
        total = sum(part[0].astype(jnp.float32) for part in kept)
        parts = [activate(total[0], total[1])]
        while left < n_tok:
            parts += [across_tok(part, left) for part in parts]
            left *= 2
        return parts

    def combine(mine, theirs):
        paired = across_core(theirs)
        sums = [mine[j] + paired[j].astype(jnp.float32) for j in range(n_z)]
        return sums[0], [part.astype(jnp.bfloat16) for part in sums[1:]]

    rows, features = tokens.shape
    piece = rows // (2 * BATCHES)
    split = tokens.reshape(2, BATCHES, piece, features)
    gate_wide = widen(gate_keep, gate_weight.shape[1])
    up_wide = widen(up_keep, up_weight.shape[1])
    down_wide = widen(down_keep, down_weight.shape[1])
    blocks = [split[:, s].reshape(2 * piece, features) for s in range(BATCHES)]
    picked = [along(block) for block in blocks]
    hidden, before = [], ()
    for s in range(BATCHES):
        own, other = spread(picked[s], before)
        after = picked[s + 1] if s + 1 < BATCHES else ()
        kept, sent = gate_up(place, own, other, gate_weight, up_weight, gate_wide, up_wide, after)
        before = (sent,)
        hidden.append(halve(kept, sent))
    out, after = [], []
    for s, parts in enumerate(hidden):
        after += [later[0] for later in hidden[s + 1 : s + 2]]
        mine, theirs = down(place, parts, down_weight, down_wide, after)
        total, sent = combine(mine, theirs)
        after = [across_z(sent[j - 1], j) for j in range(1, n_z)]
        for part in after:
            total += part.astype(jnp.float32)
        out.append(total.astype(jnp.bfloat16))
    return jnp.concatenate(out, axis=0)


def solution(mesh):
    n_tok, n_hid = mesh.shape["tok"], mesh.shape["hid"]
    return jax.shard_map(
        functools.partial(local, n_tok, n_hid),
        mesh=mesh,
        in_specs=(
            P("tok", "hid"),
            P("tok", "hid"),
            P("tok", "hid"),
            P("hid", "tok"),
            P("tok", "hid"),
            P("tok", "hid"),
            P("hid", "tok"),
        ),
        out_specs=P("hid", "tok"),
        check_vma=False,
    )
```

time: 164 us -> 168 us (1.024)
  starting transfers between devices: 35.2 us -> 39.2 us
  Pallas kernels: 42 us -> 39.8 us
  waiting for transfers between devices: 82.9 us -> 84.7 us
    ppermute x32, starting transfers between devices: 35.2 us -> 39.2 us  [send(): return lax.ppermute(value, AXES, perm)]
    pallas_call x2, Pallas kernels: 24.2 us -> 22.1 us  [gate_up(): pl.pallas_call(gate_up_kernel, grid_spec=pltpu.PrefetchScalarGridSpec(num...]
    ppermute x32, waiting for transfers between devices: 82.9 us -> 84.7 us  [send(): return lax.ppermute(value, AXES, perm)]
  transfers between devices with their start and end apart: 32 -> 32, of which waited for: 19 -> 18; matrix products, arithmetic and copies ran while one was open for 1% -> 1% of each run, Pallas kernels for 26% -> 14%
where the time goes in v1:
time: 168 us; the launch traced here: 167 us
  waiting for transfers between devices  84.7 us (50%)
  Pallas kernels  39.8 us (24%)
  starting transfers between devices  39.2 us (23%)
  other arithmetic  1.98 us (1%)
    ppermute x32, waiting for transfers between devices, send(): return lax.ppermute(value, AXES, perm)  84.7 us
    ppermute x32, starting transfers between devices, send(): return lax.ppermute(value, AXES, perm)  39.2 us
    pallas_call x2, Pallas kernels, gate_up(): pl.pallas_call(gate_up_kernel, grid_spec=pltpu.PrefetchScalarGridSpec(num...  22.1 us
    pallas_call x2, Pallas kernels, down(): pl.pallas_call(functools.partial(down_kernel, n), grid_spec=pltpu.Prefetc...  16.3 us
  transfers between devices with their start and end apart: 32, of which 18 were waited for; matrix products, arithmetic and copies ran while one was open for 1% of the time, Pallas kernels for 14%

profile of v1, /device:TPU:0, one launch (start us, length us, event | category | flops | bytes accessed | tf_op | source)
XLA Modules:
  0.0 167.5 jit_solution(9200292626682171628)
XLA Ops:
  0.0 1.0 fusion.16
  1.0 5.1 %collective-permute-start.2 = (bf16[64,1024]{1,0:T(8,128)(2,1)S(1)}, bf16[64,1024]{1,0:T(8,128)(2,1)S(1)}, u32[]{:S(2)}, u32[]{:S(2)}) collective-permute-start(bf16[64,1024]{1,0:T(8,128)(2,1)S(1)} %bitcast.76), channel_id=1, source_target_pairs={{0,6},{1,7},{2,4},{3,5},{4,2},{5,3},{6,0},{7,1},{8,14},{9,15},{10,... | collective-permute-start | bytes 393224 | tf_op jit(solution)/shard_map/ppermute | solution.py:214
  6.1 0.6 collective-permute-start
  6.9 3.7 %collective-permute-done.2.refs_3_ = bf16[64,1024]{1,0:T(8,128)(2,1)S(1)} collective-permute-done((bf16[64,1024]{1,0:T(8,128)(2,1)S(1)}, bf16[64,1024]{1,0:T(8,128)(2,1)S(1)}, u32[]{:S(2)}, u32[]{:S(2)}) %collective-permute-start.2) | collective-permute-done | bytes 131104 | tf_op jit(solution)/shard_map/ppermute | solution.py:214
  10.6 6.6 %collective-permute-done.1.refs_2_ = bf16[64,1024]{1,0:T(8,128)(2,1)S(1)} collective-permute-done((bf16[64,1024]{1,0:T(8,128)(2,1)S(1)}, bf16[64,1024]{1,0:T(8,128)(2,1)S(1)}, u32[]{:S(2)}, u32[]{:S(2)}) %collective-permute-start.1) | collective-permute-done | bytes 131104 | tf_op jit(solution)/shard_map/ppermute | solution.py:214
  17.2 0.7 pick.2
  17.9 1.6 collective-permute-start.3
  19.5 1.5 collective-permute-start.4
  21.0 0.5 collective-permute-start.5
  21.5 2.8 %collective-permute-done.3.refs_1_ = bf16[64,1024]{1,0:T(8,128)(2,1)S(1)} collective-permute-done((bf16[64,1024]{1,0:T(8,128)(2,1)S(1)}, bf16[64,1024]{1,0:T(8,128)(2,1)S(1)}, u32[]{:S(2)}, u32[]{:S(2)}) %collective-permute-start.3) | collective-permute-done | bytes 131104 | tf_op jit(solution)/shard_map/ppermute | solution.py:214
  24.3 3.0 %collective-permute-done.4.refs_2_ = bf16[64,1024]{1,0:T(8,128)(2,1)S(1)} collective-permute-done((bf16[64,1024]{1,0:T(8,128)(2,1)S(1)}, bf16[64,1024]{1,0:T(8,128)(2,1)S(1)}, u32[]{:S(2)}, u32[]{:S(2)}) %collective-permute-start.4) | collective-permute-done | bytes 131104 | tf_op jit(solution)/shard_map/ppermute | solution.py:214
  27.4 2.4 %collective-permute-start.9 = (bf16[64,1024]{1,0:T(8,128)(2,1)S(1)}, bf16[64,1024]{1,0:T(8,128)(2,1)S(1)}, u32[]{:S(2)}, u32[]{:S(2)}) collective-permute-start(bf16[64,1024]{1,0:T(8,128)(2,1)S(1)} %bitcast.72), channel_id=1, source_target_pairs={{0,6},{1,7},{2,4},{3,5},{4,2},{5,3},{6,0},{7,1},{8,14},{9,15},{10,... | collective-permute-start | bytes 393224 | tf_op jit(solution)/shard_map/ppermute | solution.py:214
  29.8 2.1 %collective-permute-start.7 = (bf16[64,1024]{1,0:T(8,128)(2,1)S(1)}, bf16[64,1024]{1,0:T(8,128)(2,1)S(1)}, u32[]{:S(2)}, u32[]{:S(2)}) collective-permute-start(bf16[64,1024]{1,0:T(8,128)(2,1)S(1)} %bitcast.74), channel_id=1, source_target_pairs={{0,2},{1,3},{2,0},{3,1},{4,6},{5,7},{6,4},{7,5},{8,10},{9,11},{10,... | collective-permute-start | bytes 393224 | tf_op jit(solution)/shard_map/ppermute | solution.py:214
  32.2 3.5 %collective-permute-done.9.refs_3_ = bf16[64,1024]{1,0:T(8,128)(2,1)S(1)} collective-permute-done((bf16[64,1024]{1,0:T(8,128)(2,1)S(1)}, bf16[64,1024]{1,0:T(8,128)(2,1)S(1)}, u32[]{:S(2)}, u32[]{:S(2)}) %collective-permute-start.9) | collective-permute-done | bytes 131104 | tf_op jit(solution)/shard_map/ppermute | solution.py:214
  35.7 5.2 %collective-permute-done.8.refs_2_ = bf16[64,1024]{1,0:T(8,128)(2,1)S(1)} collective-permute-done((bf16[64,1024]{1,0:T(8,128)(2,1)S(1)}, bf16[64,1024]{1,0:T(8,128)(2,1)S(1)}, u32[]{:S(2)}, u32[]{:S(2)}) %collective-permute-start.8) | collective-permute-done | bytes 131104 | tf_op jit(solution)/shard_map/ppermute | solution.py:214
  40.9 0.7 pick.3
  41.6 0.8 collective-permute-start.15
  42.3 1.5 collective-permute-start.16
  43.8 1.3 collective-permute-start.17
  45.1 11.0 %gate_up.2 = (f32[2,2,64,2048]{3,2,1,0:T(8,128)S(1)}, bf16[2,2,64,2048]{3,2,1,0:T(8,128)(2,1)S(1)}) custom-call(s32[5]{0:T(128)S(1)} %stack.25.place_ref, bf16[4,64,1024]{2,1,0:T(8,128)(2,1)S(1)} %join.2.own_ref, bf16[4,64,1024]{2,1,0:T(8,128)(2,1)S(1)} %collective-permute-done.6.other_ref, bf16[2048,2048]{1,0:T(8,128)(2,1)} %gate_ref.3, ...), custom_call_target="tpu_custom_call" | custom-call | flops 4294967296 | bytes 16777216 | tf_op jit(solution)/shard_map/gate_up/pallas_call | solution.py:70
  56.3 1.6 collective-permute-start.10
  58.2 11.0 %gate_up.3 = (f32[2,2,64,2048]{3,2,1,0:T(8,128)S(1)}, bf16[2,2,64,2048]{3,2,1,0:T(8,128)(2,1)S(1)}) custom-call(s32[5]{0:T(128)S(1)} %stack.25.place_ref, bf16[4,64,1024]{2,1,0:T(8,128)(2,1)S(1)} %join.3.own_ref, bf16[4,64,1024]{2,1,0:T(8,128)(2,1)S(1)} %collective-permute-done.18.other_ref, bf16[2048,2048]{1,0:T(8,128)(2,1)} %gate_ref.3, ...), custom_call_target="tpu_custom_call" | custom-call | flops 4294967296 | bytes 16777216 | tf_op jit(solution)/shard_map/gate_up/pallas_call | solution.py:70
  69.3 1.6 collective-permute-start.19
  71.3 0.8 collective-permute-start.11
  72.1 17.7 %collective-permute-done.19 = bf16[2,2,64,2048]{3,2,1,0:T(8,128)(2,1)S(1)} collective-permute-done((bf16[2,2,64,2048]{3,2,1,0:T(8,128)(2,1)S(1)}, bf16[2,2,64,2048]{3,2,1,0:T(8,128)(2,1)S(1)}, u32[]{:S(2)}, u32[]{:S(2)}) %collective-permute-start.19) | collective-permute-done | bytes 1048608 | tf_op jit(solution)/shard_map/ppermute | solution.py:214
  89.9 0.8 collective-permute-start.20
  91.0 1.4 collective-permute-start.12
  92.5 1.6 collective-permute-start.13
  94.2 10.6 %collective-permute-done.12.refs_1_ = bf16[64,2048]{1,0:T(8,128)(2,1)S(1)} collective-permute-done((bf16[64,2048]{1,0:T(8,128)(2,1)S(1)}, bf16[64,2048]{1,0:T(8,128)(2,1)S(1)}, u32[]{:S(2)}, u32[]{:S(2)}) %collective-permute-start.12) | collective-permute-done | bytes 262176 | tf_op jit(solution)/shard_map/ppermute | solution.py:214
  104.7 1.6 collective-permute-start.14
  106.7 4.5 %collective-permute-done.14.refs_3_ = bf16[64,2048]{1,0:T(8,128)(2,1)S(1)} collective-permute-done((bf16[64,2048]{1,0:T(8,128)(2,1)S(1)}, bf16[64,2048]{1,0:T(8,128)(2,1)S(1)}, u32[]{:S(2)}, u32[]{:S(2)}) %collective-permute-start.14) | collective-permute-done | bytes 262176 | tf_op jit(solution)/shard_map/ppermute | solution.py:214
  111.1 8.1 %down.2 = (f32[4,32,2048]{2,1,0:T(8,128)S(1)}, bf16[4,32,2048]{2,1,0:T(8,128)(2,1)S(1)}) custom-call(s32[5]{0:T(128)S(1)} %stack.25.place_ref, bf16[64,2048]{1,0:T(8,128)(2,1)S(1)} %fusion.3.refs_0_, bf16[64,2048]{1,0:T(8,128)(2,1)S(1)} %collective-permute-done.12.refs_1_, bf16[64,2048]{1,0:T(8,128)(2,1)S(1)} %collective-permute-done.13.refs_2_, ...), custom_call_target="tpu_custom_call" | custom-call | flops 2147483648 | bytes 8388608 | tf_op jit(solution)/shard_map/down/pallas_call | solution.py:124
  119.3 0.8 collective-permute-start.25
  120.1 1.5 collective-permute-start.26
  121.6 6.2 %collective-permute-done.25.refs_1_ = bf16[64,2048]{1,0:T(8,128)(2,1)S(1)} collective-permute-done((bf16[64,2048]{1,0:T(8,128)(2,1)S(1)}, bf16[64,2048]{1,0:T(8,128)(2,1)S(1)}, u32[]{:S(2)}, u32[]{:S(2)}) %collective-permute-start.25) | collective-permute-done | bytes 262176 | tf_op jit(solution)/shard_map/ppermute | solution.py:214
  127.9 1.9 %collective-permute-start.27 = (bf16[64,2048]{1,0:T(8,128)(2,1)S(1)}, bf16[64,2048]{1,0:T(8,128)(2,1)S(1)}, u32[]{:S(2)}, u32[]{:S(2)}) collective-permute-start(bf16[64,2048]{1,0:T(8,128)(2,1)S(1)} %collective-permute-done.25.refs_1_), channel_id=1, source_target_pairs={{0,16},{1,9},{2,18},{3,11},{4,20},{5,13},{6,22},{7,15},{8,24},{9,1... | collective-permute-start | bytes 786440 | tf_op jit(solution)/shard_map/ppermute | solution.py:214
  129.9 2.3 %collective-permute-start.24 = (bf16[32,2048]{1,0:T(8,128)(2,1)S(1)}, bf16[32,2048]{1,0:T(8,128)(2,1)S(1)}, u32[]{:S(2)}, u32[]{:S(2)}) collective-permute-start(bf16[32,2048]{1,0:T(8,128)(2,1)S(1)} %get-tuple-element.40), channel_id=1, source_target_pairs={{0,6},{1,7},{2,4},{3,5},{4,2},{5,3},{6,0},{7,1},{8,14},{9,15},{10,... | collective-permute-start | bytes 393224 | tf_op jit(solution)/shard_map/ppermute | solution.py:214
  132.2 2.1 %collective-permute-start.22 = (bf16[32,2048]{1,0:T(8,128)(2,1)S(1)}, bf16[32,2048]{1,0:T(8,128)(2,1)S(1)}, u32[]{:S(2)}, u32[]{:S(2)}) collective-permute-start(bf16[32,2048]{1,0:T(8,128)(2,1)S(1)} %get-tuple-element.42), channel_id=1, source_target_pairs={{0,2},{1,3},{2,0},{3,1},{4,6},{5,7},{6,4},{7,5},{8,10},{9,11},{10,... | collective-permute-start | bytes 393224 | tf_op jit(solution)/shard_map/ppermute | solution.py:214
  134.3 2.9 %collective-permute-done.24.refs_8_ = bf16[32,2048]{1,0:T(8,128)(2,1)S(1)} collective-permute-done((bf16[32,2048]{1,0:T(8,128)(2,1)S(1)}, bf16[32,2048]{1,0:T(8,128)(2,1)S(1)}, u32[]{:S(2)}, u32[]{:S(2)}) %collective-permute-start.24) | collective-permute-done | bytes 131104 | tf_op jit(solution)/shard_map/ppermute | solution.py:214
  137.2 4.0 %collective-permute-done.23.refs_7_ = bf16[32,2048]{1,0:T(8,128)(2,1)S(1)} collective-permute-done((bf16[32,2048]{1,0:T(8,128)(2,1)S(1)}, bf16[32,2048]{1,0:T(8,128)(2,1)S(1)}, u32[]{:S(2)}, u32[]{:S(2)}) %collective-permute-start.23) | collective-permute-done | bytes 131104 | tf_op jit(solution)/shard_map/ppermute | solution.py:214
  141.3 8.1 %down.3 = (f32[4,32,2048]{2,1,0:T(8,128)S(1)}, bf16[4,32,2048]{2,1,0:T(8,128)(2,1)S(1)}) custom-call(s32[5]{0:T(128)S(1)} %stack.25.place_ref, bf16[64,2048]{1,0:T(8,128)(2,1)S(1)} %fusion.1.refs_6_.refs_0_, bf16[64,2048]{1,0:T(8,128)(2,1)S(1)} %collective-permute-done.25.refs_1_, bf16[64,2048]{1,0:T(8,128)(2,1)S(1)} %collective-permute-done.26.refs_2_, ...), custom_call_target="tpu_custom_call" | custom-call | flops 2147483648 | bytes 8388608 | tf_op jit(solution)/shard_map/down/pallas_call | solution.py:124
  149.5 1.9 %collective-permute-done.28 = bf16[4,32,2048]{2,1,0:T(8,128)(2,1)S(1)} collective-permute-done((bf16[4,32,2048]{2,1,0:T(8,128)(2,1)S(1)}, bf16[4,32,2048]{2,1,0:T(8,128)(2,1)S(1)}, u32[]{:S(2)}, u32[]{:S(2)}) %collective-permute-start.28) | collective-permute-done | bytes 524320 | tf_op jit(solution)/shard_map/ppermute | solution.py:214
  151.5 2.3 %collective-permute-start.31 = (bf16[32,2048]{1,0:T(8,128)(2,1)S(1)}, bf16[32,2048]{1,0:T(8,128)(2,1)S(1)}, u32[]{:S(2)}, u32[]{:S(2)}) collective-permute-start(bf16[32,2048]{1,0:T(8,128)(2,1)S(1)} %get-tuple-element.38), channel_id=1, source_target_pairs={{0,6},{1,7},{2,4},{3,5},{4,2},{5,3},{6,0},{7,1},{8,14},{9,15},{10,... | collective-permute-start | bytes 393224 | tf_op jit(solution)/shard_map/ppermute | solution.py:214
  153.9 1.1 collective-permute-start.30
  155.1 2.0 %collective-permute-done.29 = bf16[32,2048]{1,0:T(8,128)(2,1)S(1)} collective-permute-done((bf16[32,2048]{1,0:T(8,128)(2,1)S(1)}, bf16[32,2048]{1,0:T(8,128)(2,1)S(1)}, u32[]{:S(2)}, u32[]{:S(2)}) %collective-permute-start.29) | collective-permute-done | bytes 131104 | tf_op jit(solution)/shard_map/ppermute | solution.py:214
  157.1 3.9 %collective-permute-done.31 = bf16[32,2048]{1,0:T(8,128)(2,1)S(1)} collective-permute-done((bf16[32,2048]{1,0:T(8,128)(2,1)S(1)}, bf16[32,2048]{1,0:T(8,128)(2,1)S(1)}, u32[]{:S(2)}, u32[]{:S(2)}) %collective-permute-start.31) | collective-permute-done | bytes 131104 | tf_op jit(solution)/shard_map/ppermute | solution.py:214
  161.0 5.7 %collective-permute-done.30 = bf16[32,2048]{1,0:T(8,128)(2,1)S(1)} collective-permute-done((bf16[32,2048]{1,0:T(8,128)(2,1)S(1)}, bf16[32,2048]{1,0:T(8,128)(2,1)S(1)}, u32[]{:S(2)}, u32[]{:S(2)}) %collective-permute-start.30) | collective-permute-done | bytes 131104 | tf_op jit(solution)/shard_map/ppermute | solution.py:214
  166.8 0.7 pad_maximum_fusion
  (52 shorter events, 2.8 us)
Async XLA Ops:
  0.0 31.8 %copy-start = (s32[16,16]{1,0:T(8,128)S(1)}, s32[16,16]{1,0:T(8,128)}, u32[]{:S(2)}) copy-start(s32[16,16]{1,0:T(8,128)} %param.11) | copy-start | bytes 3076
  0.0 31.9 %copy-start.1 = (s32[16,16]{1,0:T(8,128)S(1)}, s32[16,16]{1,0:T(8,128)}, u32[]{:S(2)}) copy-start(s32[16,16]{1,0:T(8,128)} %param.12) | copy-start | bytes 3076
  1.0 9.5 %collective-permute-start.2 = (bf16[64,1024]{1,0:T(8,128)(2,1)S(1)}, bf16[64,1024]{1,0:T(8,128)(2,1)S(1)}, u32[]{:S(2)}, u32[]{:S(2)}) collective-permute-start(bf16[64,1024]{1,0:T(8,128)(2,1)S(1)} %bitcast.76), channel_id=1, source_target_pairs={{0,6},{1,7},{2,4},{3,5},{4,2},{5,3},{6,0},{7,1},{8,14},{9,15},{10,... | collective-permute-start | bytes 393224 | tf_op jit(solution)/shard_map/ppermute | solution.py:214
  6.1 11.1 %collective-permute-start.1 = (bf16[64,1024]{1,0:T(8,128)(2,1)S(1)}, bf16[64,1024]{1,0:T(8,128)(2,1)S(1)}, u32[]{:S(2)}, u32[]{:S(2)}) collective-permute-start(bf16[64,1024]{1,0:T(8,128)(2,1)S(1)} %bitcast.77), channel_id=1, source_target_pairs={{0,4},{1,5},{2,6},{3,7},{4,0},{5,1},{6,2},{7,3},{8,12},{9,13},{10,... | collective-permute-start | bytes 393224 | tf_op jit(solution)/shard_map/ppermute | solution.py:214
  6.1 11.1 %collective-permute-start = (bf16[64,1024]{1,0:T(8,128)(2,1)S(1)}, bf16[64,1024]{1,0:T(8,128)(2,1)S(1)}, u32[]{:S(2)}, u32[]{:S(2)}) collective-permute-start(bf16[64,1024]{1,0:T(8,128)(2,1)S(1)} %bitcast.78), channel_id=1, source_target_pairs={{0,2},{1,3},{2,0},{3,1},{4,6},{5,7},{6,4},{7,5},{8,10},{9,11},{10,... | collective-permute-start | bytes 393224 | tf_op jit(solution)/shard_map/ppermute | solution.py:214
  17.9 6.4 %collective-permute-start.3 = (bf16[64,1024]{1,0:T(8,128)(2,1)S(1)}, bf16[64,1024]{1,0:T(8,128)(2,1)S(1)}, u32[]{:S(2)}, u32[]{:S(2)}) collective-permute-start(bf16[64,1024]{1,0:T(8,128)(2,1)S(1)} %get-tuple-element.22), channel_id=1, source_target_pairs={{0,8},{1,17},{2,10},{3,19},{4,12},{5,21},{6,14},{7,23},{8,0},{9,25... | collective-permute-start | bytes 393224 | tf_op jit(solution)/shard_map/ppermute | solution.py:214
  19.5 7.8 %collective-permute-start.4 = (bf16[64,1024]{1,0:T(8,128)(2,1)S(1)}, bf16[64,1024]{1,0:T(8,128)(2,1)S(1)}, u32[]{:S(2)}, u32[]{:S(2)}) collective-permute-start(bf16[64,1024]{1,0:T(8,128)(2,1)S(1)} %get-tuple-element.23), channel_id=1, source_target_pairs={{0,16},{1,9},{2,18},{3,11},{4,20},{5,13},{6,22},{7,15},{8,24},{9,1... | collective-permute-start | bytes 393224 | tf_op jit(solution)/shard_map/ppermute | solution.py:214
  21.0 6.3 %collective-permute-start.5 = (bf16[64,1024]{1,0:T(8,128)(2,1)S(1)}, bf16[64,1024]{1,0:T(8,128)(2,1)S(1)}, u32[]{:S(2)}, u32[]{:S(2)}) collective-permute-start(bf16[64,1024]{1,0:T(8,128)(2,1)S(1)} %get-tuple-element.24), channel_id=1, source_target_pairs={{0,24},{1,25},{2,26},{3,27},{4,28},{5,29},{6,30},{7,31},{8,16},{9,... | collective-permute-start | bytes 393224 | tf_op jit(solution)/shard_map/ppermute | solution.py:214
  27.3 17.8 %collective-permute-start.6 = (bf16[4,64,1024]{2,1,0:T(8,128)(2,1)S(1)}, bf16[4,64,1024]{2,1,0:T(8,128)(2,1)S(1)}, u32[]{:S(2)}, u32[]{:S(2)}) collective-permute-start(bf16[4,64,1024]{2,1,0:T(8,128)(2,1)S(1)} %join.2.own_ref), channel_id=1, source_target_pairs={{0,1},{1,0},{2,3},{3,2},{4,5},{5,4},{6,7},{7,6},{8,9},{9,8},{10,11... | collective-permute-start | bytes 1572872 | tf_op jit(solution)/shard_map/ppermute | solution.py:214
  27.4 8.3 %collective-permute-start.9 = (bf16[64,1024]{1,0:T(8,128)(2,1)S(1)}, bf16[64,1024]{1,0:T(8,128)(2,1)S(1)}, u32[]{:S(2)}, u32[]{:S(2)}) collective-permute-start(bf16[64,1024]{1,0:T(8,128)(2,1)S(1)} %bitcast.72), channel_id=1, source_target_pairs={{0,6},{1,7},{2,4},{3,5},{4,2},{5,3},{6,0},{7,1},{8,14},{9,15},{10,... | collective-permute-start | bytes 393224 | tf_op jit(solution)/shard_map/ppermute | solution.py:214
  29.8 11.1 %collective-permute-start.8 = (bf16[64,1024]{1,0:T(8,128)(2,1)S(1)}, bf16[64,1024]{1,0:T(8,128)(2,1)S(1)}, u32[]{:S(2)}, u32[]{:S(2)}) collective-permute-start(bf16[64,1024]{1,0:T(8,128)(2,1)S(1)} %bitcast.73), channel_id=1, source_target_pairs={{0,4},{1,5},{2,6},{3,7},{4,0},{5,1},{6,2},{7,3},{8,12},{9,13},{10,... | collective-permute-start | bytes 393224 | tf_op jit(solution)/shard_map/ppermute | solution.py:214
  29.8 11.1 %collective-permute-start.7 = (bf16[64,1024]{1,0:T(8,128)(2,1)S(1)}, bf16[64,1024]{1,0:T(8,128)(2,1)S(1)}, u32[]{:S(2)}, u32[]{:S(2)}) collective-permute-start(bf16[64,1024]{1,0:T(8,128)(2,1)S(1)} %bitcast.74), channel_id=1, source_target_pairs={{0,2},{1,3},{2,0},{3,1},{4,6},{5,7},{6,4},{7,5},{8,10},{9,11},{10,... | collective-permute-start | bytes 393224 | tf_op jit(solution)/shard_map/ppermute | solution.py:214
  41.6 14.6 %collective-permute-start.15 = (bf16[64,1024]{1,0:T(8,128)(2,1)S(1)}, bf16[64,1024]{1,0:T(8,128)(2,1)S(1)}, u32[]{:S(2)}, u32[]{:S(2)}) collective-permute-start(bf16[64,1024]{1,0:T(8,128)(2,1)S(1)} %get-tuple-element.26.refs_1_), channel_id=1, source_target_pairs={{0,8},{1,17},{2,10},{3,19},{4,12},{5,21},{6,14},{7,23},{8,0},{9,25... | collective-permute-start | bytes 393224 | tf_op jit(solution)/shard_map/ppermute | solution.py:214
  42.3 13.9 %collective-permute-start.16 = (bf16[64,1024]{1,0:T(8,128)(2,1)S(1)}, bf16[64,1024]{1,0:T(8,128)(2,1)S(1)}, u32[]{:S(2)}, u32[]{:S(2)}) collective-permute-start(bf16[64,1024]{1,0:T(8,128)(2,1)S(1)} %get-tuple-element.27.refs_2_), channel_id=1, source_target_pairs={{0,16},{1,9},{2,18},{3,11},{4,20},{5,13},{6,22},{7,15},{8,24},{9,1... | collective-permute-start | bytes 393224 | tf_op jit(solution)/shard_map/ppermute | solution.py:214
  43.8 12.3 %collective-permute-start.17 = (bf16[64,1024]{1,0:T(8,128)(2,1)S(1)}, bf16[64,1024]{1,0:T(8,128)(2,1)S(1)}, u32[]{:S(2)}, u32[]{:S(2)}) collective-permute-start(bf16[64,1024]{1,0:T(8,128)(2,1)S(1)} %get-tuple-element.28.refs_3_), channel_id=1, source_target_pairs={{0,24},{1,25},{2,26},{3,27},{4,28},{5,29},{6,30},{7,31},{8,16},{9,... | collective-permute-start | bytes 393224 | tf_op jit(solution)/shard_map/ppermute | solution.py:214
  56.2 2.0 %collective-permute-start.18 = (bf16[4,64,1024]{2,1,0:T(8,128)(2,1)S(1)}, bf16[4,64,1024]{2,1,0:T(8,128)(2,1)S(1)}, u32[]{:S(2)}, u32[]{:S(2)}) collective-permute-start(bf16[4,64,1024]{2,1,0:T(8,128)(2,1)S(1)} %join.3.own_ref), channel_id=1, source_target_pairs={{0,1},{1,0},{2,3},{3,2},{4,5},{5,4},{6,7},{7,6},{8,9},{9,8},{10,11... | collective-permute-start | bytes 1572872 | tf_op jit(solution)/shard_map/ppermute | solution.py:214
  56.3 14.9 %collective-permute-start.10 = (bf16[2,2,64,2048]{3,2,1,0:T(8,128)(2,1)S(1)}, bf16[2,2,64,2048]{3,2,1,0:T(8,128)(2,1)S(1)}, u32[]{:S(2)}, u32[]{:S(2)}) collective-permute-start(bf16[2,2,64,2048]{3,2,1,0:T(8,128)(2,1)S(1)} %get-tuple-element.30.refs_4_), channel_id=1, source_target_pairs={{0,16},{1,9},{2,18},{3,11},{4,20},{5,13},{6,22},{7,15},{8,24},{9,1... | collective-permute-start | bytes 3145736 | tf_op jit(solution)/shard_map/ppermute | solution.py:214
  69.3 20.5 %collective-permute-start.19 = (bf16[2,2,64,2048]{3,2,1,0:T(8,128)(2,1)S(1)}, bf16[2,2,64,2048]{3,2,1,0:T(8,128)(2,1)S(1)}, u32[]{:S(2)}, u32[]{:S(2)}) collective-permute-start(bf16[2,2,64,2048]{3,2,1,0:T(8,128)(2,1)S(1)} %get-tuple-element.32), channel_id=1, source_target_pairs={{0,16},{1,9},{2,18},{3,11},{4,20},{5,13},{6,22},{7,15},{8,24},{9,1... | collective-permute-start | bytes 3145736 | tf_op jit(solution)/shard_map/ppermute | solution.py:214
  71.3 19.3 %collective-permute-start.11 = (bf16[1,2,64,2048]{3,2,1,0:T(8,128)(2,1)S(1)}, bf16[1,2,64,2048]{3,2,1,0:T(8,128)(2,1)S(1)}, u32[]{:S(2)}, u32[]{:S(2)}) collective-permute-start(bf16[1,2,64,2048]{3,2,1,0:T(8,128)(2,1)S(1)} %add_convert_fusion.1), channel_id=1, source_target_pairs={{0,8},{1,17},{2,10},{3,19},{4,12},{5,21},{6,14},{7,23},{8,0},{9,25... | collective-permute-start | bytes 1572872 | tf_op jit(solution)/shard_map/ppermute | solution.py:214
  89.9 2.5 %copy-start.2 = (s32[16,16]{1,0:T(8,128)S(1)}, s32[16,16]{1,0:T(8,128)}, u32[]{:S(2)}) copy-start(s32[16,16]{1,0:T(8,128)} %param.13) | copy-start | bytes 3076
  89.9 16.4 %collective-permute-start.20 = (bf16[1,2,64,2048]{3,2,1,0:T(8,128)(2,1)S(1)}, bf16[1,2,64,2048]{3,2,1,0:T(8,128)(2,1)S(1)}, u32[]{:S(2)}, u32[]{:S(2)}) collective-permute-start(bf16[1,2,64,2048]{3,2,1,0:T(8,128)(2,1)S(1)} %add_convert_fusion), channel_id=1, source_target_pairs={{0,8},{1,17},{2,10},{3,19},{4,12},{5,21},{6,14},{7,23},{8,0},{9,25... | collective-permute-start | bytes 1572872 | tf_op jit(solution)/shard_map/ppermute | solution.py:214
  91.0 13.7 %collective-permute-start.12 = (bf16[64,2048]{1,0:T(8,128)(2,1)S(1)}, bf16[64,2048]{1,0:T(8,128)(2,1)S(1)}, u32[]{:S(2)}, u32[]{:S(2)}) collective-permute-start(bf16[64,2048]{1,0:T(8,128)(2,1)S(1)} %fusion.3.refs_0_), channel_id=1, source_target_pairs={{0,8},{1,17},{2,10},{3,19},{4,12},{5,21},{6,14},{7,23},{8,0},{9,25... | collective-permute-start | bytes 786440 | tf_op jit(solution)/shard_map/ppermute | solution.py:214
  92.5 14.1 %collective-permute-start.13 = (bf16[64,2048]{1,0:T(8,128)(2,1)S(1)}, bf16[64,2048]{1,0:T(8,128)(2,1)S(1)}, u32[]{:S(2)}, u32[]{:S(2)}) collective-permute-start(bf16[64,2048]{1,0:T(8,128)(2,1)S(1)} %fusion.3.refs_0_), channel_id=1, source_target_pairs={{0,16},{1,9},{2,18},{3,11},{4,20},{5,13},{6,22},{7,15},{8,24},{9,1... | collective-permute-start | bytes 786440 | tf_op jit(solution)/shard_map/ppermute | solution.py:214
  104.7 6.4 %collective-permute-start.14 = (bf16[64,2048]{1,0:T(8,128)(2,1)S(1)}, bf16[64,2048]{1,0:T(8,128)(2,1)S(1)}, u32[]{:S(2)}, u32[]{:S(2)}) collective-permute-start(bf16[64,2048]{1,0:T(8,128)(2,1)S(1)} %collective-permute-done.12.refs_1_), channel_id=1, source_target_pairs={{0,16},{1,9},{2,18},{3,11},{4,20},{5,13},{6,22},{7,15},{8,24},{9,1... | collective-permute-start | bytes 786440 | tf_op jit(solution)/shard_map/ppermute | solution.py:214
  119.3 10.5 %collective-permute-start.21 = (bf16[4,32,2048]{2,1,0:T(8,128)(2,1)S(1)}, bf16[4,32,2048]{2,1,0:T(8,128)(2,1)S(1)}, u32[]{:S(2)}, u32[]{:S(2)}) collective-permute-start(bf16[4,32,2048]{2,1,0:T(8,128)(2,1)S(1)} %get-tuple-element.34), channel_id=1, source_target_pairs={{0,1},{1,0},{2,3},{3,2},{4,5},{5,4},{6,7},{7,6},{8,9},{9,8},{10,11... | collective-permute-start | bytes 1572872 | tf_op jit(solution)/shard_map/ppermute | solution.py:214
  119.3 8.5 %collective-permute-start.25 = (bf16[64,2048]{1,0:T(8,128)(2,1)S(1)}, bf16[64,2048]{1,0:T(8,128)(2,1)S(1)}, u32[]{:S(2)}, u32[]{:S(2)}) collective-permute-start(bf16[64,2048]{1,0:T(8,128)(2,1)S(1)} %fusion.1.refs_6_.refs_0_), channel_id=1, source_target_pairs={{0,8},{1,17},{2,10},{3,19},{4,12},{5,21},{6,14},{7,23},{8,0},{9,25... | collective-permute-start | bytes 786440 | tf_op jit(solution)/shard_map/ppermute | solution.py:214
  120.1 14.2 %collective-permute-start.26 = (bf16[64,2048]{1,0:T(8,128)(2,1)S(1)}, bf16[64,2048]{1,0:T(8,128)(2,1)S(1)}, u32[]{:S(2)}, u32[]{:S(2)}) collective-permute-start(bf16[64,2048]{1,0:T(8,128)(2,1)S(1)} %fusion.1.refs_6_.refs_0_), channel_id=1, source_target_pairs={{0,16},{1,9},{2,18},{3,11},{4,20},{5,13},{6,22},{7,15},{8,24},{9,1... | collective-permute-start | bytes 786440 | tf_op jit(solution)/shard_map/ppermute | solution.py:214
  127.9 6.5 %collective-permute-start.27 = (bf16[64,2048]{1,0:T(8,128)(2,1)S(1)}, bf16[64,2048]{1,0:T(8,128)(2,1)S(1)}, u32[]{:S(2)}, u32[]{:S(2)}) collective-permute-start(bf16[64,2048]{1,0:T(8,128)(2,1)S(1)} %collective-permute-done.25.refs_1_), channel_id=1, source_target_pairs={{0,16},{1,9},{2,18},{3,11},{4,20},{5,13},{6,22},{7,15},{8,24},{9,1... | collective-permute-start | bytes 786440 | tf_op jit(solution)/shard_map/ppermute | solution.py:214
  129.9 7.4 %collective-permute-start.24 = (bf16[32,2048]{1,0:T(8,128)(2,1)S(1)}, bf16[32,2048]{1,0:T(8,128)(2,1)S(1)}, u32[]{:S(2)}, u32[]{:S(2)}) collective-permute-start(bf16[32,2048]{1,0:T(8,128)(2,1)S(1)} %get-tuple-element.40), channel_id=1, source_target_pairs={{0,6},{1,7},{2,4},{3,5},{4,2},{5,3},{6,0},{7,1},{8,14},{9,15},{10,... | collective-permute-start | bytes 393224 | tf_op jit(solution)/shard_map/ppermute | solution.py:214
  132.2 9.1 %collective-permute-start.23 = (bf16[32,2048]{1,0:T(8,128)(2,1)S(1)}, bf16[32,2048]{1,0:T(8,128)(2,1)S(1)}, u32[]{:S(2)}, u32[]{:S(2)}) collective-permute-start(bf16[32,2048]{1,0:T(8,128)(2,1)S(1)} %get-tuple-element.41), channel_id=1, source_target_pairs={{0,4},{1,5},{2,6},{3,7},{4,0},{5,1},{6,2},{7,3},{8,12},{9,13},{10,... | collective-permute-start | bytes 393224 | tf_op jit(solution)/shard_map/ppermute | solution.py:214
  132.2 9.1 %collective-permute-start.22 = (bf16[32,2048]{1,0:T(8,128)(2,1)S(1)}, bf16[32,2048]{1,0:T(8,128)(2,1)S(1)}, u32[]{:S(2)}, u32[]{:S(2)}) collective-permute-start(bf16[32,2048]{1,0:T(8,128)(2,1)S(1)} %get-tuple-element.42), channel_id=1, source_target_pairs={{0,2},{1,3},{2,0},{3,1},{4,6},{5,7},{6,4},{7,5},{8,10},{9,11},{10,... | collective-permute-start | bytes 393224 | tf_op jit(solution)/shard_map/ppermute | solution.py:214
  149.4 2.0 %collective-permute-start.28 = (bf16[4,32,2048]{2,1,0:T(8,128)(2,1)S(1)}, bf16[4,32,2048]{2,1,0:T(8,128)(2,1)S(1)}, u32[]{:S(2)}, u32[]{:S(2)}) collective-permute-start(bf16[4,32,2048]{2,1,0:T(8,128)(2,1)S(1)} %get-tuple-element.36), channel_id=1, source_target_pairs={{0,1},{1,0},{2,3},{3,2},{4,5},{5,4},{6,7},{7,6},{8,9},{9,8},{10,11... | collective-permute-start | bytes 1572872 | tf_op jit(solution)/shard_map/ppermute | solution.py:214
  151.5 5.6 %collective-permute-start.29 = (bf16[32,2048]{1,0:T(8,128)(2,1)S(1)}, bf16[32,2048]{1,0:T(8,128)(2,1)S(1)}, u32[]{:S(2)}, u32[]{:S(2)}) collective-permute-start(bf16[32,2048]{1,0:T(8,128)(2,1)S(1)} %get-tuple-element.37), channel_id=1, source_target_pairs={{0,2},{1,3},{2,0},{3,1},{4,6},{5,7},{6,4},{7,5},{8,10},{9,11},{10,... | collective-permute-start | bytes 393224 | tf_op jit(solution)/shard_map/ppermute | solution.py:214
  151.5 9.4 %collective-permute-start.31 = (bf16[32,2048]{1,0:T(8,128)(2,1)S(1)}, bf16[32,2048]{1,0:T(8,128)(2,1)S(1)}, u32[]{:S(2)}, u32[]{:S(2)}) collective-permute-start(bf16[32,2048]{1,0:T(8,128)(2,1)S(1)} %get-tuple-element.38), channel_id=1, source_target_pairs={{0,6},{1,7},{2,4},{3,5},{4,2},{5,3},{6,0},{7,1},{8,14},{9,15},{10,... | collective-permute-start | bytes 393224 | tf_op jit(solution)/shard_map/ppermute | solution.py:214
  153.9 12.8 %collective-permute-start.30 = (bf16[32,2048]{1,0:T(8,128)(2,1)S(1)}, bf16[32,2048]{1,0:T(8,128)(2,1)S(1)}, u32[]{:S(2)}, u32[]{:S(2)}) collective-permute-start(bf16[32,2048]{1,0:T(8,128)(2,1)S(1)} %get-tuple-element.39), channel_id=1, source_target_pairs={{0,4},{1,5},{2,6},{3,7},{4,0},{5,1},{6,2},{7,3},{8,12},{9,13},{10,... | collective-permute-start | bytes 393224 | tf_op jit(solution)/shard_map/ppermute | solution.py:214

commit v2 on v1

--- a/solution.py
+++ b/solution.py
@@ -9,6 +9,7 @@
 
 AXES = ("tok", "hid")
 BATCHES = 2
+TILE = 512
 VMEM_BYTES = 48 * 1024 * 1024
 
 
@@ -36,20 +37,21 @@
     return jnp.repeat(keep_mask.astype(jnp.float32), width // keep_mask.shape[1], axis=1)
 
 
-def gate_up_kernel(place_ref, own_ref, other_ref, gate_ref, up_ref, gate_keep, up_keep, *refs):
-    keep_ref, send_ref, x = refs[-3:]
-    n, rows, half = own_ref.shape
-    step = pl.program_id(0)
-
-    @pl.when(step == 0)
+def gate_up_kernel(n, place_ref, *refs):
+    own, other = refs[:n], refs[n : 2 * n]
+    gate_ref, up_ref, gate_keep, up_keep, keep_ref, send_ref, x = refs[2 * n :]
+    _, piece, half = own[0].shape
+    rows = 2 * piece
+
+    @pl.when(pl.program_id(0) == 0)
     def _():
         core = place_ref[0]
         mine = pl.ds(pl.multiple_of(core * half, half), half)
         others = pl.ds(pl.multiple_of((1 - core) * half, half), half)
-        for p in range(n):
-            at = pl.ds(p * rows, rows)
-            x[at, mine] = own_ref[p]
-            x[at, others] = other_ref[mirror(p, n)]
+        for k in range(n):
+            at = pl.ds(pl.multiple_of(place_ref[1 + n + k] * rows, rows), rows)
+            x[at, mine] = own[k][...].reshape(rows, half)
+            x[at, others] = other[k][...].reshape(rows, half)
 
     for which, (weight, keep) in enumerate(((gate_ref, gate_keep), (up_ref, up_keep))):
         product = masked_product(x, weight, keep)
@@ -59,20 +61,23 @@
             send_ref[p, which] = product[q * rows : (q + 1) * rows].astype(jnp.bfloat16)
 
 
-def gate_up(place, own, other, gate_weight, up_weight, gate_keep, up_keep, after):
-    n, rows, half = own.shape
+def gate_up(place, batch, own, other, gate_weight, up_weight, gate_keep, up_keep):
+    n = len(own)
+    _, whole, half = own[0].shape
+    piece = whole // BATCHES
+    rows = 2 * piece
     depth, width = gate_weight.shape
-    tile = min(width, 256)
-    whole = pl.BlockSpec((n, rows, half), lambda i, *_: (0, 0, 0))
+    tile = min(width, TILE)
+    part = pl.BlockSpec((2, piece, half), lambda i, *_: (0, batch, 0))
     strip = pl.BlockSpec((depth, tile), lambda i, *_: (0, i))
     mask = pl.BlockSpec((gate_keep.shape[0], tile), lambda i, *_: (0, i))
     out = pl.BlockSpec((n // 2, 2, rows, tile), lambda i, *_: (0, 0, 0, i))
     return pl.pallas_call(
-        gate_up_kernel,
+        functools.partial(gate_up_kernel, n),
         grid_spec=pltpu.PrefetchScalarGridSpec(
             num_scalar_prefetch=1,
             grid=(width // tile,),
-            in_specs=[whole, whole, strip, strip, mask, mask] + [pl.BlockSpec(memory_space=pl.ANY)] * len(after),
+            in_specs=[part] * (2 * n) + [strip, strip, mask, mask],
             out_specs=[out, out],
             scratch_shapes=[pltpu.VMEM((n * rows, depth), jnp.bfloat16)],
         ),
@@ -85,7 +90,7 @@
             flops=4 * n * rows * depth * width, bytes_accessed=4 * depth * width, transcendentals=0
         ),
         name="gate_up",
-    )(place, own, other, gate_weight, up_weight, gate_keep, up_keep, *after)
+    )(place, *own, *other, gate_weight, up_weight, gate_keep, up_keep)
 
 
 def activate(gate, up):
@@ -119,7 +124,7 @@
     n = len(parts)
     rows = parts[0].shape[0]
     depth, width = weight.shape
-    tile = min(width, 256)
+    tile = min(width, TILE)
     out = pl.BlockSpec((n, rows // 2, tile), lambda i, *_: (0, 0, i))
     return pl.pallas_call(
         functools.partial(down_kernel, n),
@@ -145,51 +150,6 @@
     )(place, *parts, weight, keep, *after)
 
 
-def pick_kernel(n, order_ref, *refs):
-    outs = refs[-n:]
-    for p in range(n):
-        for i in range(n):
-
-            @pl.when(order_ref[p] == i)
-            def _():
-                outs[p][...] = refs[i][...]
-
-
-def pick(order, parts, after):
-    n = len(parts)
-    spec = pl.BlockSpec(memory_space=pltpu.VMEM)
-    return pl.pallas_call(
-        functools.partial(pick_kernel, n),
-        grid_spec=pltpu.PrefetchScalarGridSpec(
-            num_scalar_prefetch=1,
-            grid=(),
-            in_specs=[spec] * n + [pl.BlockSpec(memory_space=pl.ANY)] * len(after),
-            out_specs=[spec] * n,
-        ),
-        out_shape=[jax.ShapeDtypeStruct(parts[0].shape, parts[0].dtype)] * n,
-        compiler_params=pltpu.CompilerParams(vmem_limit_bytes=VMEM_BYTES),
-        name="pick",
-    )(order, *parts, *after)
-
-
-def join_kernel(n, *refs):
-    for p in range(n):
-        refs[-1][p] = refs[p][...]
-
-
-def join(parts, after):
-    n = len(parts)
-    spec = pl.BlockSpec(memory_space=pltpu.VMEM)
-    return pl.pallas_call(
-        functools.partial(join_kernel, n),
-        in_specs=[spec] * n + [pl.BlockSpec(memory_space=pl.ANY)] * len(after),
-        out_specs=spec,
-        out_shape=jax.ShapeDtypeStruct((n,) + parts[0].shape, parts[0].dtype),
-        compiler_params=pltpu.CompilerParams(vmem_limit_bytes=VMEM_BYTES),
-        name="join",
-    )(*parts, *after)
-
-
 def mirror(p, n):
     out = 0
     while n > 1:
@@ -202,7 +162,8 @@
     tok, hid = lax.axis_index("tok"), lax.axis_index("hid")
     z, core = hid // 2, hid % 2
     offsets = [jnp.where(core == 0, p, mirror(p, n_tok)) for p in range(n_tok)]
-    place = jnp.stack([core] + [tok ^ z ^ off for off in offsets]).astype(jnp.int32)
+    positions = [sum(jnp.where(off == tok ^ z ^ k, p, 0) for p, off in enumerate(offsets)) for k in range(n_tok)]
+    place = jnp.stack([core] + [tok ^ z ^ off for off in offsets] + positions).astype(jnp.int32)
 
     def send(value, to):
         perm = []
@@ -221,13 +182,6 @@
 
     def across_core(value):
         return send(value, lambda t, zz, c: (t, zz, 1 - c))
-
-    def along(block):
-        return pick(place[1:], [block] + [across_z(block, j) for j in range(1, n_z)], ())
-
-    def spread(picked, after):
-        own = join([picked[0]] + [across_tok(picked[p], p) for p in range(1, n_tok)], after)
-        return own, across_core(own)
 
     def halve(kept, sent):
         left = n_tok // 2
@@ -251,23 +205,20 @@
         return sums[0], [part.astype(jnp.bfloat16) for part in sums[1:]]
 
     rows, features = tokens.shape
-    piece = rows // (2 * BATCHES)
-    split = tokens.reshape(2, BATCHES, piece, features)
     gate_wide = widen(gate_keep, gate_weight.shape[1])
     up_wide = widen(up_keep, up_weight.shape[1])
     down_wide = widen(down_keep, down_weight.shape[1])
-    blocks = [split[:, s].reshape(2 * piece, features) for s in range(BATCHES)]
-    picked = [along(block) for block in blocks]
-    hidden, before = [], ()
+    moved = [send(tokens, lambda t, zz, c: (zz, t ^ k, c)) for k in range(n_z)]
+    swapped = [across_core(block) for block in moved]
+    own = [block.reshape(2, rows // 2, features) for block in moved]
+    other = [block.reshape(2, rows // 2, features) for block in swapped]
+    hidden = []
     for s in range(BATCHES):
-        own, other = spread(picked[s], before)
-        after = picked[s + 1] if s + 1 < BATCHES else ()
-        kept, sent = gate_up(place, own, other, gate_weight, up_weight, gate_wide, up_wide, after)
-        before = (sent,)
+        kept, sent = gate_up(place, s, own, other, gate_weight, up_weight, gate_wide, up_wide)
         hidden.append(halve(kept, sent))
     out, after = [], []
     for s, parts in enumerate(hidden):
-        after += [later[0] for later in hidden[s + 1 : s + 2]]
+        after += [later[1] for later in hidden[s + 1 : s + 2]]
         mine, theirs = down(place, parts, down_weight, down_wide, after)
         total, sent = combine(mine, theirs)
         after = [across_z(sent[j - 1], j) for j in range(1, n_z)]

time: 168 us -> 145 us (0.86)
  waiting for transfers between devices: 84.7 us -> 67 us
  Pallas kernels: 39.8 us -> 31.1 us
  starting transfers between devices: 39.2 us -> 42.6 us
    ppermute x32 -> x26, waiting for transfers between devices: 84.7 us -> 67 us  [send(): return lax.ppermute(value, AXES, perm)]
    pallas_call x6 -> x2, Pallas kernels: 23.5 us -> 18.6 us  [gate_up(): pl.pallas_call(functools.partial(gate_up_kernel, n), grid_spec=pltpu.Pref...]
    pallas_call x2, Pallas kernels: 16.3 us -> 12.5 us  [down(): pl.pallas_call(functools.partial(down_kernel, n), grid_spec=pltpu.Prefetc...]
    ppermute x32 -> x26, starting transfers between devices: 39.2 us -> 42.6 us  [send(): return lax.ppermute(value, AXES, perm)]
  transfers between devices with their start and end apart: 32 -> 26, of which waited for: 18 -> 16; matrix products, arithmetic and copies ran while one was open for 1% -> 2% of each run, Pallas kernels for 14% -> 6%
where the time goes in v2:
time: 145 us
  waiting for transfers between devices  67 us (46%)
  starting transfers between devices  42.6 us (29%)
  Pallas kernels  31.1 us (21%)
  other arithmetic  3.27 us (2%)
    ppermute x26, waiting for transfers between devices, send(): return lax.ppermute(value, AXES, perm)  67 us
    ppermute x26, starting transfers between devices, send(): return lax.ppermute(value, AXES, perm)  42.6 us
    pallas_call x2, Pallas kernels, gate_up(): pl.pallas_call(functools.partial(gate_up_kernel, n), grid_spec=pltpu.Pref...  18.6 us
    pallas_call x2, Pallas kernels, down(): pl.pallas_call(functools.partial(down_kernel, n), grid_spec=pltpu.Prefetc...  12.5 us
  transfers between devices with their start and end apart: 26, of which 16 were waited for; matrix products, arithmetic and copies ran while one was open for 2% of the time, Pallas kernels for 6%

profile of v2, /device:TPU:0, one launch (start us, length us, event | category | flops | bytes accessed | tf_op | source)
XLA Modules:
  0.0 144.7 jit_solution(667979357780540108)
XLA Ops:
  0.0 1.6 %collective-permute-start = (bf16[128,1024]{1,0:T(8,128)(2,1)}, bf16[128,1024]{1,0:T(8,128)(2,1)S(1)}, u32[]{:S(2)}, u32[]{:S(2)}) collective-permute-start(bf16[128,1024]{1,0:T(8,128)(2,1)} %param.7), channel_id=1, source_target_pairs={{0,0},{1,1},{2,8},{3,9},{4,16},{5,17},{6,24},{7,25},{8,2},{9,3},{1... | collective-permute-start | bytes 786440 | tf_op jit(solution)/shard_map/ppermute | solution.py:175
  1.6 4.8 %collective-permute-start.1 = (bf16[128,1024]{1,0:T(8,128)(2,1)}, bf16[128,1024]{1,0:T(8,128)(2,1)S(1)}, u32[]{:S(2)}, u32[]{:S(2)}) collective-permute-start(bf16[128,1024]{1,0:T(8,128)(2,1)} %param.7), channel_id=1, source_target_pairs={{0,2},{1,3},{2,10},{3,11},{4,18},{5,19},{6,26},{7,27},{8,0},{9,1},... | collective-permute-start | bytes 786440 | tf_op jit(solution)/shard_map/ppermute | solution.py:175
  6.4 3.5 %collective-permute-start.2 = (bf16[128,1024]{1,0:T(8,128)(2,1)}, bf16[128,1024]{1,0:T(8,128)(2,1)S(1)}, u32[]{:S(2)}, u32[]{:S(2)}) collective-permute-start(bf16[128,1024]{1,0:T(8,128)(2,1)} %param.7), channel_id=1, source_target_pairs={{0,4},{1,5},{2,12},{3,13},{4,20},{5,21},{6,28},{7,29},{8,6},{9,7},... | collective-permute-start | bytes 786440 | tf_op jit(solution)/shard_map/ppermute | solution.py:175
  9.8 1.9 %collective-permute-start.3 = (bf16[128,1024]{1,0:T(8,128)(2,1)}, bf16[128,1024]{1,0:T(8,128)(2,1)S(1)}, u32[]{:S(2)}, u32[]{:S(2)}) collective-permute-start(bf16[128,1024]{1,0:T(8,128)(2,1)} %param.7), channel_id=1, source_target_pairs={{0,6},{1,7},{2,14},{3,15},{4,22},{5,23},{6,30},{7,31},{8,4},{9,5},... | collective-permute-start | bytes 786440 | tf_op jit(solution)/shard_map/ppermute | solution.py:175
  11.8 0.7 convert_element_type.135
  12.5 0.7 convert_element_type.136
  13.3 0.1 collective-permute-done.1
  13.4 0.4 collective-permute-start.5
  13.8 8.4 %collective-permute-done.2 = bf16[128,1024]{1,0:T(8,128)(2,1)S(1)} collective-permute-done((bf16[128,1024]{1,0:T(8,128)(2,1)}, bf16[128,1024]{1,0:T(8,128)(2,1)S(1)}, u32[]{:S(2)}, u32[]{:S(2)}) %collective-permute-start.2) | collective-permute-done | bytes 262176 | tf_op jit(solution)/shard_map/ppermute | solution.py:175
  22.2 1.1 collective-permute-done.3
  23.3 0.1 broadcast_in_dim.10
  23.6 0.2 collective-permute-done.6
  23.7 1.1 collective-permute-done.7
  24.8 9.3 %gate_up.2 = (f32[2,2,64,2048]{3,2,1,0:T(8,128)S(1)}, bf16[2,2,64,2048]{3,2,1,0:T(8,128)(2,1)S(1)}) custom-call(s32[9]{0:T(128)S(1)} %stack.39.place_ref, bf16[2,64,1024]{2,1,0:T(8,128)(2,1)S(1)} %bitcast.77, bf16[2,64,1024]{2,1,0:T(8,128)(2,1)S(1)} %bitcast.79, bf16[2,64,1024]{2,1,0:T(8,128)(2,1)S(1)} %bitcast.81, bf16[2,64,1024]{2,1,0:T(8,128)(2,1)S(1)} %bitcast.83, ...), custom_call_target="tpu_custom_call" | custom-call | flops 4294967296 | bytes 16777216 | tf_op jit(solution)/shard_map/gate_up/pallas_call | solution.py:75
  34.1 13.0 %collective-permute-start.8 = (bf16[2,2,64,2048]{3,2,1,0:T(8,128)(2,1)S(1)}, bf16[2,2,64,2048]{3,2,1,0:T(8,128)(2,1)S(1)}, u32[]{:S(2)}, u32[]{:S(2)}) collective-permute-start(bf16[2,2,64,2048]{3,2,1,0:T(8,128)(2,1)S(1)} %get-tuple-element.14), channel_id=1, source_target_pairs={{0,16},{1,9},{2,18},{3,11},{4,20},{5,13},{6,22},{7,15},{8,24},{9,1... | collective-permute-start | bytes 3145736 | tf_op jit(solution)/shard_map/ppermute | solution.py:175
  47.1 9.3 %gate_up.3 = (f32[2,2,64,2048]{3,2,1,0:T(8,128)S(1)}, bf16[2,2,64,2048]{3,2,1,0:T(8,128)(2,1)S(1)}) custom-call(s32[9]{0:T(128)S(1)} %stack.39.place_ref, bf16[2,64,1024]{2,1,0:T(8,128)(2,1)S(1)} %bitcast.78, bf16[2,64,1024]{2,1,0:T(8,128)(2,1)S(1)} %bitcast.80, bf16[2,64,1024]{2,1,0:T(8,128)(2,1)S(1)} %bitcast.82, bf16[2,64,1024]{2,1,0:T(8,128)(2,1)S(1)} %bitcast.84, ...), custom_call_target="tpu_custom_call" | custom-call | flops 4294967296 | bytes 16777216 | tf_op jit(solution)/shard_map/gate_up/pallas_call | solution.py:75
  56.5 3.4 %collective-permute-done.8 = bf16[2,2,64,2048]{3,2,1,0:T(8,128)(2,1)S(1)} collective-permute-done((bf16[2,2,64,2048]{3,2,1,0:T(8,128)(2,1)S(1)}, bf16[2,2,64,2048]{3,2,1,0:T(8,128)(2,1)S(1)}, u32[]{:S(2)}, u32[]{:S(2)}) %collective-permute-start.8) | collective-permute-done | bytes 1048608 | tf_op jit(solution)/shard_map/ppermute | solution.py:175
  59.8 0.1 add_convert_fusion.1
  60.0 16.8 %collective-permute-done.13 = bf16[2,2,64,2048]{3,2,1,0:T(8,128)(2,1)S(1)} collective-permute-done((bf16[2,2,64,2048]{3,2,1,0:T(8,128)(2,1)S(1)}, bf16[2,2,64,2048]{3,2,1,0:T(8,128)(2,1)S(1)}, u32[]{:S(2)}, u32[]{:S(2)}) %collective-permute-start.13) | collective-permute-done | bytes 1048608 | tf_op jit(solution)/shard_map/ppermute | solution.py:175
  76.9 0.1 add_convert_fusion
  77.1 0.2 convert_add_fusion.1
  77.2 0.1 fusion.3.refs_0_
  77.4 2.1 %collective-permute-start.10 = (bf16[64,2048]{1,0:T(8,128)(2,1)S(1)}, bf16[64,2048]{1,0:T(8,128)(2,1)S(1)}, u32[]{:S(2)}, u32[]{:S(2)}) collective-permute-start(bf16[64,2048]{1,0:T(8,128)(2,1)S(1)} %fusion.3.refs_0_), channel_id=1, source_target_pairs={{0,8},{1,17},{2,10},{3,19},{4,12},{5,21},{6,14},{7,23},{8,0},{9,25... | collective-permute-start | bytes 786440 | tf_op jit(solution)/shard_map/ppermute | solution.py:175
  79.5 1.9 %collective-permute-start.11 = (bf16[64,2048]{1,0:T(8,128)(2,1)S(1)}, bf16[64,2048]{1,0:T(8,128)(2,1)S(1)}, u32[]{:S(2)}, u32[]{:S(2)}) collective-permute-start(bf16[64,2048]{1,0:T(8,128)(2,1)S(1)} %fusion.3.refs_0_), channel_id=1, source_target_pairs={{0,16},{1,9},{2,18},{3,11},{4,20},{5,13},{6,22},{7,15},{8,24},{9,1... | collective-permute-start | bytes 786440 | tf_op jit(solution)/shard_map/ppermute | solution.py:175
  81.3 7.7 %collective-permute-done.14 = bf16[1,2,64,2048]{3,2,1,0:T(8,128)(2,1)S(1)} collective-permute-done((bf16[1,2,64,2048]{3,2,1,0:T(8,128)(2,1)S(1)}, bf16[1,2,64,2048]{3,2,1,0:T(8,128)(2,1)S(1)}, u32[]{:S(2)}, u32[]{:S(2)}) %collective-permute-start.14) | collective-permute-done | bytes 524320 | tf_op jit(solution)/shard_map/ppermute | solution.py:175
  89.0 0.2 convert_add_fusion
  89.2 0.1 fusion.1.refs_0_
  89.4 2.4 %collective-permute-done.10.refs_1_ = bf16[64,2048]{1,0:T(8,128)(2,1)S(1)} collective-permute-done((bf16[64,2048]{1,0:T(8,128)(2,1)S(1)}, bf16[64,2048]{1,0:T(8,128)(2,1)S(1)}, u32[]{:S(2)}, u32[]{:S(2)}) %collective-permute-start.10) | collective-permute-done | bytes 262176 | tf_op jit(solution)/shard_map/ppermute | solution.py:175
  91.8 1.9 %collective-permute-start.12 = (bf16[64,2048]{1,0:T(8,128)(2,1)S(1)}, bf16[64,2048]{1,0:T(8,128)(2,1)S(1)}, u32[]{:S(2)}, u32[]{:S(2)}) collective-permute-start(bf16[64,2048]{1,0:T(8,128)(2,1)S(1)} %collective-permute-done.10.refs_1_), channel_id=1, source_target_pairs={{0,16},{1,9},{2,18},{3,11},{4,20},{5,13},{6,22},{7,15},{8,24},{9,1... | collective-permute-start | bytes 786440 | tf_op jit(solution)/shard_map/ppermute | solution.py:175
  93.9 4.7 %collective-permute-done.15.refs_6_.refs_1_ = bf16[64,2048]{1,0:T(8,128)(2,1)S(1)} collective-permute-done((bf16[64,2048]{1,0:T(8,128)(2,1)S(1)}, bf16[64,2048]{1,0:T(8,128)(2,1)S(1)}, u32[]{:S(2)}, u32[]{:S(2)}) %collective-permute-start.15) | collective-permute-done | bytes 262176 | tf_op jit(solution)/shard_map/ppermute | solution.py:175
  98.6 6.2 %down.2 = (f32[4,32,2048]{2,1,0:T(8,128)S(1)}, bf16[4,32,2048]{2,1,0:T(8,128)(2,1)S(1)}) custom-call(s32[9]{0:T(128)S(1)} %stack.39.place_ref, bf16[64,2048]{1,0:T(8,128)(2,1)S(1)} %fusion.3.refs_0_, bf16[64,2048]{1,0:T(8,128)(2,1)S(1)} %collective-permute-done.10.refs_1_, bf16[64,2048]{1,0:T(8,128)(2,1)S(1)} %collective-permute-done.11.refs_2_, ...), custom_call_target="tpu_custom_call" | custom-call | flops 2147483648 | bytes 8388608 | tf_op jit(solution)/shard_map/down/pallas_call | solution.py:129
  104.8 0.2 collective-permute-start.16
  105.0 1.7 %collective-permute-start.20 = (bf16[64,2048]{1,0:T(8,128)(2,1)S(1)}, bf16[64,2048]{1,0:T(8,128)(2,1)S(1)}, u32[]{:S(2)}, u32[]{:S(2)}) collective-permute-start(bf16[64,2048]{1,0:T(8,128)(2,1)S(1)} %fusion.1.refs_0_), channel_id=1, source_target_pairs={{0,16},{1,9},{2,18},{3,11},{4,20},{5,13},{6,22},{7,15},{8,24},{9,1... | collective-permute-start | bytes 786440 | tf_op jit(solution)/shard_map/ppermute | solution.py:175
  106.7 0.3 collective-permute-start.21
  107.1 0.6 collective-permute-start.17
  107.7 2.1 %collective-permute-start.18 = (bf16[32,2048]{1,0:T(8,128)(2,1)S(1)}, bf16[32,2048]{1,0:T(8,128)(2,1)S(1)}, u32[]{:S(2)}, u32[]{:S(2)}) collective-permute-start(bf16[32,2048]{1,0:T(8,128)(2,1)S(1)} %get-tuple-element.25), channel_id=1, source_target_pairs={{0,4},{1,5},{2,6},{3,7},{4,0},{5,1},{6,2},{7,3},{8,12},{9,13},{10,... | collective-permute-start | bytes 393224 | tf_op jit(solution)/shard_map/ppermute | solution.py:175
  109.8 1.8 %collective-permute-start.19 = (bf16[32,2048]{1,0:T(8,128)(2,1)S(1)}, bf16[32,2048]{1,0:T(8,128)(2,1)S(1)}, u32[]{:S(2)}, u32[]{:S(2)}) collective-permute-start(bf16[32,2048]{1,0:T(8,128)(2,1)S(1)} %get-tuple-element.24), channel_id=1, source_target_pairs={{0,6},{1,7},{2,4},{3,5},{4,2},{5,3},{6,0},{7,1},{8,14},{9,15},{10,... | collective-permute-start | bytes 393224 | tf_op jit(solution)/shard_map/ppermute | solution.py:175
  111.6 2.6 %collective-permute-done.21.refs_3_ = bf16[64,2048]{1,0:T(8,128)(2,1)S(1)} collective-permute-done((bf16[64,2048]{1,0:T(8,128)(2,1)S(1)}, bf16[64,2048]{1,0:T(8,128)(2,1)S(1)}, u32[]{:S(2)}, u32[]{:S(2)}) %collective-permute-start.21) | collective-permute-done | bytes 262176 | tf_op jit(solution)/shard_map/ppermute | solution.py:175
  114.2 0.5 collective-permute-done.17.refs_6_
  114.6 5.9 %collective-permute-done.18.refs_7_ = bf16[32,2048]{1,0:T(8,128)(2,1)S(1)} collective-permute-done((bf16[32,2048]{1,0:T(8,128)(2,1)S(1)}, bf16[32,2048]{1,0:T(8,128)(2,1)S(1)}, u32[]{:S(2)}, u32[]{:S(2)}) %collective-permute-start.18) | collective-permute-done | bytes 131104 | tf_op jit(solution)/shard_map/ppermute | solution.py:175
  120.6 6.2 %down.3 = (f32[4,32,2048]{2,1,0:T(8,128)S(1)}, bf16[4,32,2048]{2,1,0:T(8,128)(2,1)S(1)}) custom-call(s32[9]{0:T(128)S(1)} %stack.39.place_ref, bf16[64,2048]{1,0:T(8,128)(2,1)S(1)} %fusion.1.refs_0_, bf16[64,2048]{1,0:T(8,128)(2,1)S(1)} %collective-permute-done.15.refs_6_.refs_1_, bf16[64,2048]{1,0:T(8,128)(2,1)S(1)} %collective-permute-done.20.refs_2_, ...), custom_call_target="tpu_custom_call" | custom-call | flops 2147483648 | bytes 8388608 | tf_op jit(solution)/shard_map/down/pallas_call | solution.py:129
  126.9 1.9 %collective-permute-done.22 = bf16[4,32,2048]{2,1,0:T(8,128)(2,1)S(1)} collective-permute-done((bf16[4,32,2048]{2,1,0:T(8,128)(2,1)S(1)}, bf16[4,32,2048]{2,1,0:T(8,128)(2,1)S(1)}, u32[]{:S(2)}, u32[]{:S(2)}) %collective-permute-start.22) | collective-permute-done | bytes 524320 | tf_op jit(solution)/shard_map/ppermute | solution.py:175
  128.9 2.1 %collective-permute-start.23 = (bf16[32,2048]{1,0:T(8,128)(2,1)S(1)}, bf16[32,2048]{1,0:T(8,128)(2,1)S(1)}, u32[]{:S(2)}, u32[]{:S(2)}) collective-permute-start(bf16[32,2048]{1,0:T(8,128)(2,1)S(1)} %get-tuple-element.21), channel_id=1, source_target_pairs={{0,2},{1,3},{2,0},{3,1},{4,6},{5,7},{6,4},{7,5},{8,10},{9,11},{10,... | collective-permute-start | bytes 393224 | tf_op jit(solution)/shard_map/ppermute | solution.py:175
  131.0 1.1 collective-permute-start.24
  132.2 1.4 collective-permute-start.25
  133.6 3.1 %collective-permute-done.23 = bf16[32,2048]{1,0:T(8,128)(2,1)S(1)} collective-permute-done((bf16[32,2048]{1,0:T(8,128)(2,1)S(1)}, bf16[32,2048]{1,0:T(8,128)(2,1)S(1)}, u32[]{:S(2)}, u32[]{:S(2)}) %collective-permute-start.23) | collective-permute-done | bytes 131104 | tf_op jit(solution)/shard_map/ppermute | solution.py:175
  136.7 7.2 %collective-permute-done.24 = bf16[32,2048]{1,0:T(8,128)(2,1)S(1)} collective-permute-done((bf16[32,2048]{1,0:T(8,128)(2,1)S(1)}, bf16[32,2048]{1,0:T(8,128)(2,1)S(1)}, u32[]{:S(2)}, u32[]{:S(2)}) %collective-permute-start.24) | collective-permute-done | bytes 131104 | tf_op jit(solution)/shard_map/ppermute | solution.py:175
  144.0 0.7 pad_maximum_fusion
  (30 shorter events, 1.2 us)
Async XLA Ops:
  0.0 13.2 %collective-permute-start = (bf16[128,1024]{1,0:T(8,128)(2,1)}, bf16[128,1024]{1,0:T(8,128)(2,1)S(1)}, u32[]{:S(2)}, u32[]{:S(2)}) collective-permute-start(bf16[128,1024]{1,0:T(8,128)(2,1)} %param.7), channel_id=1, source_target_pairs={{0,0},{1,1},{2,8},{3,9},{4,16},{5,17},{6,24},{7,25},{8,2},{9,3},{1... | collective-permute-start | bytes 786440 | tf_op jit(solution)/shard_map/ppermute | solution.py:175
  1.6 11.8 %collective-permute-start.1 = (bf16[128,1024]{1,0:T(8,128)(2,1)}, bf16[128,1024]{1,0:T(8,128)(2,1)S(1)}, u32[]{:S(2)}, u32[]{:S(2)}) collective-permute-start(bf16[128,1024]{1,0:T(8,128)(2,1)} %param.7), channel_id=1, source_target_pairs={{0,2},{1,3},{2,10},{3,11},{4,18},{5,19},{6,26},{7,27},{8,0},{9,1},... | collective-permute-start | bytes 786440 | tf_op jit(solution)/shard_map/ppermute | solution.py:175
  6.4 15.8 %collective-permute-start.2 = (bf16[128,1024]{1,0:T(8,128)(2,1)}, bf16[128,1024]{1,0:T(8,128)(2,1)S(1)}, u32[]{:S(2)}, u32[]{:S(2)}) collective-permute-start(bf16[128,1024]{1,0:T(8,128)(2,1)} %param.7), channel_id=1, source_target_pairs={{0,4},{1,5},{2,12},{3,13},{4,20},{5,21},{6,28},{7,29},{8,6},{9,7},... | collective-permute-start | bytes 786440 | tf_op jit(solution)/shard_map/ppermute | solution.py:175
  9.8 13.4 %collective-permute-start.3 = (bf16[128,1024]{1,0:T(8,128)(2,1)}, bf16[128,1024]{1,0:T(8,128)(2,1)S(1)}, u32[]{:S(2)}, u32[]{:S(2)}) collective-permute-start(bf16[128,1024]{1,0:T(8,128)(2,1)} %param.7), channel_id=1, source_target_pairs={{0,6},{1,7},{2,14},{3,15},{4,22},{5,23},{6,30},{7,31},{8,4},{9,5},... | collective-permute-start | bytes 786440 | tf_op jit(solution)/shard_map/ppermute | solution.py:175
  13.2 10.3 %collective-permute-start.4 = (bf16[128,1024]{1,0:T(8,128)(2,1)S(1)}, bf16[128,1024]{1,0:T(8,128)(2,1)S(1)}, u32[]{:S(2)}, u32[]{:S(2)}) collective-permute-start(bf16[128,1024]{1,0:T(8,128)(2,1)S(1)} %collective-permute-done), channel_id=1, source_target_pairs={{0,1},{1,0},{2,3},{3,2},{4,5},{5,4},{6,7},{7,6},{8,9},{9,8},{10,11... | collective-permute-start | bytes 786440 | tf_op jit(solution)/shard_map/ppermute | solution.py:175
  13.4 10.1 %collective-permute-start.5 = (bf16[128,1024]{1,0:T(8,128)(2,1)S(1)}, bf16[128,1024]{1,0:T(8,128)(2,1)S(1)}, u32[]{:S(2)}, u32[]{:S(2)}) collective-permute-start(bf16[128,1024]{1,0:T(8,128)(2,1)S(1)} %collective-permute-done.1), channel_id=1, source_target_pairs={{0,1},{1,0},{2,3},{3,2},{4,5},{5,4},{6,7},{7,6},{8,9},{9,8},{10,11... | collective-permute-start | bytes 786440 | tf_op jit(solution)/shard_map/ppermute | solution.py:175
  22.2 1.5 %collective-permute-start.6 = (bf16[128,1024]{1,0:T(8,128)(2,1)S(1)}, bf16[128,1024]{1,0:T(8,128)(2,1)S(1)}, u32[]{:S(2)}, u32[]{:S(2)}) collective-permute-start(bf16[128,1024]{1,0:T(8,128)(2,1)S(1)} %collective-permute-done.2), channel_id=1, source_target_pairs={{0,1},{1,0},{2,3},{3,2},{4,5},{5,4},{6,7},{7,6},{8,9},{9,8},{10,11... | collective-permute-start | bytes 786440 | tf_op jit(solution)/shard_map/ppermute | solution.py:175
  23.2 1.5 %collective-permute-start.7 = (bf16[128,1024]{1,0:T(8,128)(2,1)S(1)}, bf16[128,1024]{1,0:T(8,128)(2,1)S(1)}, u32[]{:S(2)}, u32[]{:S(2)}) collective-permute-start(bf16[128,1024]{1,0:T(8,128)(2,1)S(1)} %collective-permute-done.3), channel_id=1, source_target_pairs={{0,1},{1,0},{2,3},{3,2},{4,5},{5,4},{6,7},{7,6},{8,9},{9,8},{10,11... | collective-permute-start | bytes 786440 | tf_op jit(solution)/shard_map/ppermute | solution.py:175
  34.1 25.7 %collective-permute-start.8 = (bf16[2,2,64,2048]{3,2,1,0:T(8,128)(2,1)S(1)}, bf16[2,2,64,2048]{3,2,1,0:T(8,128)(2,1)S(1)}, u32[]{:S(2)}, u32[]{:S(2)}) collective-permute-start(bf16[2,2,64,2048]{3,2,1,0:T(8,128)(2,1)S(1)} %get-tuple-element.14), channel_id=1, source_target_pairs={{0,16},{1,9},{2,18},{3,11},{4,20},{5,13},{6,22},{7,15},{8,24},{9,1... | collective-permute-start | bytes 3145736 | tf_op jit(solution)/shard_map/ppermute | solution.py:175
  56.4 20.5 %collective-permute-start.13 = (bf16[2,2,64,2048]{3,2,1,0:T(8,128)(2,1)S(1)}, bf16[2,2,64,2048]{3,2,1,0:T(8,128)(2,1)S(1)}, u32[]{:S(2)}, u32[]{:S(2)}) collective-permute-start(bf16[2,2,64,2048]{3,2,1,0:T(8,128)(2,1)S(1)} %get-tuple-element.16), channel_id=1, source_target_pairs={{0,16},{1,9},{2,18},{3,11},{4,20},{5,13},{6,22},{7,15},{8,24},{9,1... | collective-permute-start | bytes 3145736 | tf_op jit(solution)/shard_map/ppermute | solution.py:175
  60.0 17.1 %collective-permute-start.9 = (bf16[1,2,64,2048]{3,2,1,0:T(8,128)(2,1)S(1)}, bf16[1,2,64,2048]{3,2,1,0:T(8,128)(2,1)S(1)}, u32[]{:S(2)}, u32[]{:S(2)}) collective-permute-start(bf16[1,2,64,2048]{3,2,1,0:T(8,128)(2,1)S(1)} %add_convert_fusion.1), channel_id=1, source_target_pairs={{0,8},{1,17},{2,10},{3,19},{4,12},{5,21},{6,14},{7,23},{8,0},{9,25... | collective-permute-start | bytes 1572872 | tf_op jit(solution)/shard_map/ppermute | solution.py:175
  77.0 12.1 %collective-permute-start.14 = (bf16[1,2,64,2048]{3,2,1,0:T(8,128)(2,1)S(1)}, bf16[1,2,64,2048]{3,2,1,0:T(8,128)(2,1)S(1)}, u32[]{:S(2)}, u32[]{:S(2)}) collective-permute-start(bf16[1,2,64,2048]{3,2,1,0:T(8,128)(2,1)S(1)} %add_convert_fusion), channel_id=1, source_target_pairs={{0,8},{1,17},{2,10},{3,19},{4,12},{5,21},{6,14},{7,23},{8,0},{9,25... | collective-permute-start | bytes 1572872 | tf_op jit(solution)/shard_map/ppermute | solution.py:175
  77.4 16.3 %copy-start = (s32[16,16]{1,0:T(8,128)S(1)}, s32[16,16]{1,0:T(8,128)}, u32[]{:S(2)}) copy-start(s32[16,16]{1,0:T(8,128)} %param.13) | copy-start | bytes 3076
  77.4 14.4 %collective-permute-start.10 = (bf16[64,2048]{1,0:T(8,128)(2,1)S(1)}, bf16[64,2048]{1,0:T(8,128)(2,1)S(1)}, u32[]{:S(2)}, u32[]{:S(2)}) collective-permute-start(bf16[64,2048]{1,0:T(8,128)(2,1)S(1)} %fusion.3.refs_0_), channel_id=1, source_target_pairs={{0,8},{1,17},{2,10},{3,19},{4,12},{5,21},{6,14},{7,23},{8,0},{9,25... | collective-permute-start | bytes 786440 | tf_op jit(solution)/shard_map/ppermute | solution.py:175
  79.5 14.4 %collective-permute-start.11 = (bf16[64,2048]{1,0:T(8,128)(2,1)S(1)}, bf16[64,2048]{1,0:T(8,128)(2,1)S(1)}, u32[]{:S(2)}, u32[]{:S(2)}) collective-permute-start(bf16[64,2048]{1,0:T(8,128)(2,1)S(1)} %fusion.3.refs_0_), channel_id=1, source_target_pairs={{0,16},{1,9},{2,18},{3,11},{4,20},{5,13},{6,22},{7,15},{8,24},{9,1... | collective-permute-start | bytes 786440 | tf_op jit(solution)/shard_map/ppermute | solution.py:175
  89.4 9.2 %collective-permute-start.15 = (bf16[64,2048]{1,0:T(8,128)(2,1)S(1)}, bf16[64,2048]{1,0:T(8,128)(2,1)S(1)}, u32[]{:S(2)}, u32[]{:S(2)}) collective-permute-start(bf16[64,2048]{1,0:T(8,128)(2,1)S(1)} %fusion.1.refs_0_), channel_id=1, source_target_pairs={{0,8},{1,17},{2,10},{3,19},{4,12},{5,21},{6,14},{7,23},{8,0},{9,25... | collective-permute-start | bytes 786440 | tf_op jit(solution)/shard_map/ppermute | solution.py:175
  91.8 6.8 %collective-permute-start.12 = (bf16[64,2048]{1,0:T(8,128)(2,1)S(1)}, bf16[64,2048]{1,0:T(8,128)(2,1)S(1)}, u32[]{:S(2)}, u32[]{:S(2)}) collective-permute-start(bf16[64,2048]{1,0:T(8,128)(2,1)S(1)} %collective-permute-done.10.refs_1_), channel_id=1, source_target_pairs={{0,16},{1,9},{2,18},{3,11},{4,20},{5,13},{6,22},{7,15},{8,24},{9,1... | collective-permute-start | bytes 786440 | tf_op jit(solution)/shard_map/ppermute | solution.py:175
  104.8 2.2 %collective-permute-start.16 = (bf16[4,32,2048]{2,1,0:T(8,128)(2,1)S(1)}, bf16[4,32,2048]{2,1,0:T(8,128)(2,1)S(1)}, u32[]{:S(2)}, u32[]{:S(2)}) collective-permute-start(bf16[4,32,2048]{2,1,0:T(8,128)(2,1)S(1)} %get-tuple-element.18), channel_id=1, source_target_pairs={{0,1},{1,0},{2,3},{3,2},{4,5},{5,4},{6,7},{7,6},{8,9},{9,8},{10,11... | collective-permute-start | bytes 1572872 | tf_op jit(solution)/shard_map/ppermute | solution.py:175
  105.0 6.6 %collective-permute-start.20 = (bf16[64,2048]{1,0:T(8,128)(2,1)S(1)}, bf16[64,2048]{1,0:T(8,128)(2,1)S(1)}, u32[]{:S(2)}, u32[]{:S(2)}) collective-permute-start(bf16[64,2048]{1,0:T(8,128)(2,1)S(1)} %fusion.1.refs_0_), channel_id=1, source_target_pairs={{0,16},{1,9},{2,18},{3,11},{4,20},{5,13},{6,22},{7,15},{8,24},{9,1... | collective-permute-start | bytes 786440 | tf_op jit(solution)/shard_map/ppermute | solution.py:175
  106.7 7.5 %collective-permute-start.21 = (bf16[64,2048]{1,0:T(8,128)(2,1)S(1)}, bf16[64,2048]{1,0:T(8,128)(2,1)S(1)}, u32[]{:S(2)}, u32[]{:S(2)}) collective-permute-start(bf16[64,2048]{1,0:T(8,128)(2,1)S(1)} %collective-permute-done.15.refs_6_.refs_1_), channel_id=1, source_target_pairs={{0,16},{1,9},{2,18},{3,11},{4,20},{5,13},{6,22},{7,15},{8,24},{9,1... | collective-permute-start | bytes 786440 | tf_op jit(solution)/shard_map/ppermute | solution.py:175
  107.1 7.5 %collective-permute-start.17 = (bf16[32,2048]{1,0:T(8,128)(2,1)S(1)}, bf16[32,2048]{1,0:T(8,128)(2,1)S(1)}, u32[]{:S(2)}, u32[]{:S(2)}) collective-permute-start(bf16[32,2048]{1,0:T(8,128)(2,1)S(1)} %get-tuple-element.26), channel_id=1, source_target_pairs={{0,2},{1,3},{2,0},{3,1},{4,6},{5,7},{6,4},{7,5},{8,10},{9,11},{10,... | collective-permute-start | bytes 393224 | tf_op jit(solution)/shard_map/ppermute | solution.py:175
  107.7 12.9 %collective-permute-start.18 = (bf16[32,2048]{1,0:T(8,128)(2,1)S(1)}, bf16[32,2048]{1,0:T(8,128)(2,1)S(1)}, u32[]{:S(2)}, u32[]{:S(2)}) collective-permute-start(bf16[32,2048]{1,0:T(8,128)(2,1)S(1)} %get-tuple-element.25), channel_id=1, source_target_pairs={{0,4},{1,5},{2,6},{3,7},{4,0},{5,1},{6,2},{7,3},{8,12},{9,13},{10,... | collective-permute-start | bytes 393224 | tf_op jit(solution)/shard_map/ppermute | solution.py:175
  109.8 10.8 %collective-permute-start.19 = (bf16[32,2048]{1,0:T(8,128)(2,1)S(1)}, bf16[32,2048]{1,0:T(8,128)(2,1)S(1)}, u32[]{:S(2)}, u32[]{:S(2)}) collective-permute-start(bf16[32,2048]{1,0:T(8,128)(2,1)S(1)} %get-tuple-element.24), channel_id=1, source_target_pairs={{0,6},{1,7},{2,4},{3,5},{4,2},{5,3},{6,0},{7,1},{8,14},{9,15},{10,... | collective-permute-start | bytes 393224 | tf_op jit(solution)/shard_map/ppermute | solution.py:175
  126.8 2.0 %collective-permute-start.22 = (bf16[4,32,2048]{2,1,0:T(8,128)(2,1)S(1)}, bf16[4,32,2048]{2,1,0:T(8,128)(2,1)S(1)}, u32[]{:S(2)}, u32[]{:S(2)}) collective-permute-start(bf16[4,32,2048]{2,1,0:T(8,128)(2,1)S(1)} %get-tuple-element.20), channel_id=1, source_target_pairs={{0,1},{1,0},{2,3},{3,2},{4,5},{5,4},{6,7},{7,6},{8,9},{9,8},{10,11... | collective-permute-start | bytes 1572872 | tf_op jit(solution)/shard_map/ppermute | solution.py:175
  128.9 7.8 %collective-permute-start.23 = (bf16[32,2048]{1,0:T(8,128)(2,1)S(1)}, bf16[32,2048]{1,0:T(8,128)(2,1)S(1)}, u32[]{:S(2)}, u32[]{:S(2)}) collective-permute-start(bf16[32,2048]{1,0:T(8,128)(2,1)S(1)} %get-tuple-element.21), channel_id=1, source_target_pairs={{0,2},{1,3},{2,0},{3,1},{4,6},{5,7},{6,4},{7,5},{8,10},{9,11},{10,... | collective-permute-start | bytes 393224 | tf_op jit(solution)/shard_map/ppermute | solution.py:175
  131.0 12.9 %collective-permute-start.24 = (bf16[32,2048]{1,0:T(8,128)(2,1)S(1)}, bf16[32,2048]{1,0:T(8,128)(2,1)S(1)}, u32[]{:S(2)}, u32[]{:S(2)}) collective-permute-start(bf16[32,2048]{1,0:T(8,128)(2,1)S(1)} %get-tuple-element.23), channel_id=1, source_target_pairs={{0,4},{1,5},{2,6},{3,7},{4,0},{5,1},{6,2},{7,3},{8,12},{9,13},{10,... | collective-permute-start | bytes 393224 | tf_op jit(solution)/shard_map/ppermute | solution.py:175
  132.2 11.8 %collective-permute-start.25 = (bf16[32,2048]{1,0:T(8,128)(2,1)S(1)}, bf16[32,2048]{1,0:T(8,128)(2,1)S(1)}, u32[]{:S(2)}, u32[]{:S(2)}) collective-permute-start(bf16[32,2048]{1,0:T(8,128)(2,1)S(1)} %get-tuple-element.22), channel_id=1, source_target_pairs={{0,6},{1,7},{2,4},{3,5},{4,2},{5,3},{6,0},{7,1},{8,14},{9,15},{10,... | collective-permute-start | bytes 393224 | tf_op jit(solution)/shard_map/ppermute | solution.py:175

commit v3 on v2

--- a/solution.py
+++ b/solution.py
@@ -93,8 +93,49 @@
     )(place, *own, *other, gate_weight, up_weight, gate_keep, up_keep)
 
 
-def activate(gate, up):
-    return (gate / (1.0 + jnp.exp(-gate)) * up).astype(jnp.bfloat16)
+def add_kernel(n, *refs):
+    total = refs[0][...].astype(jnp.float32)
+    for ref in refs[1:n]:
+        total += ref[...].astype(jnp.float32)
+    refs[-1][...] = total.astype(jnp.bfloat16)
+
+
+def add_slots(parts, first, count, after):
+    _, two, rows, width = parts[0].shape
+    return pl.pallas_call(
+        functools.partial(add_kernel, len(parts)),
+        grid=(count, two),
+        in_specs=[pl.BlockSpec((1, 1, rows, width), lambda i, j: (first + i, j, 0, 0))] * len(parts)
+        + [pl.BlockSpec(memory_space=pl.ANY)] * len(after),
+        out_specs=pl.BlockSpec((1, 1, rows, width), lambda i, j: (i, j, 0, 0)),
+        out_shape=jax.ShapeDtypeStruct((count, two, rows, width), jnp.bfloat16),
+        compiler_params=pltpu.CompilerParams(vmem_limit_bytes=VMEM_BYTES),
+        name="add_slots",
+    )(*parts, *after)
+
+
+def activate_kernel(n, *refs):
+    gate = refs[0][0, 0].astype(jnp.float32)
+    up = refs[0][0, 1].astype(jnp.float32)
+    for ref in refs[1:n]:
+        gate += ref[0, 0].astype(jnp.float32)
+        up += ref[0, 1].astype(jnp.float32)
+    refs[-1][...] = (gate / (1.0 + jnp.exp(-gate)) * up).astype(jnp.bfloat16)
+
+
+def activate(parts, after):
+    _, two, rows, width = parts[0].shape
+    tile = width // 2
+    return pl.pallas_call(
+        functools.partial(activate_kernel, len(parts)),
+        grid=(width // tile,),
+        in_specs=[pl.BlockSpec((1, two, rows, tile), lambda i: (0, 0, 0, i))] * len(parts)
+        + [pl.BlockSpec(memory_space=pl.ANY)] * len(after),
+        out_specs=pl.BlockSpec((rows, tile), lambda i: (0, i)),
+        out_shape=jax.ShapeDtypeStruct((rows, width), jnp.bfloat16),
+        compiler_params=pltpu.CompilerParams(vmem_limit_bytes=VMEM_BYTES),
+        name="hidden",
+    )(*parts, *after)
 
 
 def down_kernel(n, place_ref, *refs):
@@ -183,17 +224,18 @@
     def across_core(value):
         return send(value, lambda t, zz, c: (t, zz, 1 - c))
 
-    def halve(kept, sent):
+    def halve(kept, sent, after):
         left = n_tok // 2
         kept = [kept]
         while True:
             kept.append(across_tok(sent, left))
             if left == 1:
-                break
+                return kept
             left //= 2
-            sent = sum(part[left : 2 * left].astype(jnp.float32) for part in kept).astype(jnp.bfloat16)
-        total = sum(part[0].astype(jnp.float32) for part in kept)
-        parts = [activate(total[0], total[1])]
+            sent = add_slots(kept, left, left, after)
+
+    def gather(part):
+        parts, left = [part], 1
         while left < n_tok:
             parts += [across_tok(part, left) for part in parts]
             left *= 2
@@ -212,19 +254,18 @@
     swapped = [across_core(block) for block in moved]
     own = [block.reshape(2, rows // 2, features) for block in moved]
     other = [block.reshape(2, rows // 2, features) for block in swapped]
-    hidden = []
-    for s in range(BATCHES):
-        kept, sent = gate_up(place, s, own, other, gate_weight, up_weight, gate_wide, up_wide)
-        hidden.append(halve(kept, sent))
-    out, after = [], []
-    for s, parts in enumerate(hidden):
-        after += [later[1] for later in hidden[s + 1 : s + 2]]
-        mine, theirs = down(place, parts, down_weight, down_wide, after)
+    sums = [gate_up(place, s, own, other, gate_weight, up_weight, gate_wide, up_wide) for s in range(BATCHES)]
+    out, before_add, before_hidden, before_down = [], [], [], []
+    for kept, sent in sums:
+        kept = halve(kept, sent, before_add)
+        parts = gather(activate(kept, before_hidden))
+        mine, theirs = down(place, parts, down_weight, down_wide, before_down)
         total, sent = combine(mine, theirs)
-        after = [across_z(sent[j - 1], j) for j in range(1, n_z)]
-        for part in after:
+        arrived = [across_z(sent[j - 1], j) for j in range(1, n_z)]
+        for part in arrived:
             total += part.astype(jnp.float32)
         out.append(total.astype(jnp.bfloat16))
+        before_add, before_hidden, before_down = [parts[1]], [theirs], arrived
     return jnp.concatenate(out, axis=0)
 
 

time: 145 us -> 146 us (level)
  starting transfers between devices: 42.6 us -> 54.2 us
  waiting for transfers between devices: 67 us -> 55.5 us
    ppermute x26, starting transfers between devices: 42.6 us -> 54.2 us  [send(): return lax.ppermute(value, AXES, perm)]
    ppermute x26, waiting for transfers between devices: 67 us -> 55.5 us  [send(): return lax.ppermute(value, AXES, perm)]
  transfers between devices with their start and end apart: 26 -> 26, of which waited for: 16 -> 14; matrix products, arithmetic and copies ran while one was open for 2% -> 1% of each run, Pallas kernels for 6% -> 12%
where the time goes in v3:
time: 146 us; the launch traced here: 145 us
  waiting for transfers between devices  55.5 us (38%)
  starting transfers between devices  54.2 us (37%)
  Pallas kernels  32.3 us (22%)
  other arithmetic  2.43 us (2%)
    ppermute x26, waiting for transfers between devices, send(): return lax.ppermute(value, AXES, perm)  55.5 us
    ppermute x26, starting transfers between devices, send(): return lax.ppermute(value, AXES, perm)  54.2 us
    pallas_call x2, Pallas kernels, gate_up(): pl.pallas_call(functools.partial(gate_up_kernel, n), grid_spec=pltpu.Pref...  18.6 us
    pallas_call x2, Pallas kernels, down(): pl.pallas_call(functools.partial(down_kernel, n), grid_spec=pltpu.Prefetc...  12.5 us
  transfers between devices with their start and end apart: 26, of which 14 were waited for; matrix products, arithmetic and copies ran while one was open for 1% of the time, Pallas kernels for 12%

profile of v3, /device:TPU:0, one launch (start us, length us, event | category | flops | bytes accessed | tf_op | source)
XLA Modules:
  0.0 145.3 jit_solution(9772093672960298151)
XLA Ops:
  0.0 1.6 %collective-permute-start = (bf16[128,1024]{1,0:T(8,128)(2,1)}, bf16[128,1024]{1,0:T(8,128)(2,1)S(1)}, u32[]{:S(2)}, u32[]{:S(2)}) collective-permute-start(bf16[128,1024]{1,0:T(8,128)(2,1)} %param.7), channel_id=1, source_target_pairs={{0,0},{1,1},{2,8},{3,9},{4,16},{5,17},{6,24},{7,25},{8,2},{9,3},{1... | collective-permute-start | bytes 786440 | tf_op jit(solution)/shard_map/ppermute | solution.py:216
  1.6 4.8 %collective-permute-start.1 = (bf16[128,1024]{1,0:T(8,128)(2,1)}, bf16[128,1024]{1,0:T(8,128)(2,1)S(1)}, u32[]{:S(2)}, u32[]{:S(2)}) collective-permute-start(bf16[128,1024]{1,0:T(8,128)(2,1)} %param.7), channel_id=1, source_target_pairs={{0,2},{1,3},{2,10},{3,11},{4,18},{5,19},{6,26},{7,27},{8,0},{9,1},... | collective-permute-start | bytes 786440 | tf_op jit(solution)/shard_map/ppermute | solution.py:216
  6.4 3.5 %collective-permute-start.2 = (bf16[128,1024]{1,0:T(8,128)(2,1)}, bf16[128,1024]{1,0:T(8,128)(2,1)S(1)}, u32[]{:S(2)}, u32[]{:S(2)}) collective-permute-start(bf16[128,1024]{1,0:T(8,128)(2,1)} %param.7), channel_id=1, source_target_pairs={{0,4},{1,5},{2,12},{3,13},{4,20},{5,21},{6,28},{7,29},{8,6},{9,7},... | collective-permute-start | bytes 786440 | tf_op jit(solution)/shard_map/ppermute | solution.py:216
  9.8 1.9 %collective-permute-start.3 = (bf16[128,1024]{1,0:T(8,128)(2,1)}, bf16[128,1024]{1,0:T(8,128)(2,1)S(1)}, u32[]{:S(2)}, u32[]{:S(2)}) collective-permute-start(bf16[128,1024]{1,0:T(8,128)(2,1)} %param.7), channel_id=1, source_target_pairs={{0,6},{1,7},{2,14},{3,15},{4,22},{5,23},{6,30},{7,31},{8,4},{9,5},... | collective-permute-start | bytes 786440 | tf_op jit(solution)/shard_map/ppermute | solution.py:216
  11.8 0.7 convert_element_type.101
  12.5 0.7 convert_element_type.102
  13.3 0.1 collective-permute-done.1
  13.4 0.4 collective-permute-start.5
  13.8 8.4 %collective-permute-done.2 = bf16[128,1024]{1,0:T(8,128)(2,1)S(1)} collective-permute-done((bf16[128,1024]{1,0:T(8,128)(2,1)}, bf16[128,1024]{1,0:T(8,128)(2,1)S(1)}, u32[]{:S(2)}, u32[]{:S(2)}) %collective-permute-start.2) | collective-permute-done | bytes 262176 | tf_op jit(solution)/shard_map/ppermute | solution.py:216
  22.2 1.1 collective-permute-done.3
  23.2 0.1 broadcast_in_dim.9
  23.3 0.1 broadcast_in_dim.10
  23.4 0.1 copy_bitcast_fusion.1
  23.6 0.2 collective-permute-done.6
  23.7 1.1 collective-permute-done.7
  24.8 9.3 %gate_up.2 = (f32[2,2,64,2048]{3,2,1,0:T(8,128)S(1)}, bf16[2,2,64,2048]{3,2,1,0:T(8,128)(2,1)S(1)}) custom-call(s32[9]{0:T(128)S(1)} %stack.39.place_ref, bf16[2,64,1024]{2,1,0:T(8,128)(2,1)S(1)} %bitcast.57, bf16[2,64,1024]{2,1,0:T(8,128)(2,1)S(1)} %bitcast.59, bf16[2,64,1024]{2,1,0:T(8,128)(2,1)S(1)} %bitcast.61, bf16[2,64,1024]{2,1,0:T(8,128)(2,1)S(1)} %bitcast.63, ...), custom_call_target="tpu_custom_call" | custom-call | flops 4294967296 | bytes 16777216 | tf_op jit(solution)/shard_map/gate_up/pallas_call | solution.py:75
  34.1 13.0 %collective-permute-start.8 = (bf16[2,2,64,2048]{3,2,1,0:T(8,128)(2,1)S(1)}, bf16[2,2,64,2048]{3,2,1,0:T(8,128)(2,1)S(1)}, u32[]{:S(2)}, u32[]{:S(2)}) collective-permute-start(bf16[2,2,64,2048]{3,2,1,0:T(8,128)(2,1)S(1)} %get-tuple-element.14), channel_id=1, source_target_pairs={{0,16},{1,9},{2,18},{3,11},{4,20},{5,13},{6,22},{7,15},{8,24},{9,1... | collective-permute-start | bytes 3145736 | tf_op jit(solution)/shard_map/ppermute | solution.py:216
  47.1 9.3 %gate_up.3 = (f32[2,2,64,2048]{3,2,1,0:T(8,128)S(1)}, bf16[2,2,64,2048]{3,2,1,0:T(8,128)(2,1)S(1)}) custom-call(s32[9]{0:T(128)S(1)} %stack.39.place_ref, bf16[2,64,1024]{2,1,0:T(8,128)(2,1)S(1)} %bitcast.58, bf16[2,64,1024]{2,1,0:T(8,128)(2,1)S(1)} %bitcast.60, bf16[2,64,1024]{2,1,0:T(8,128)(2,1)S(1)} %bitcast.62, bf16[2,64,1024]{2,1,0:T(8,128)(2,1)S(1)} %bitcast.64, ...), custom_call_target="tpu_custom_call" | custom-call | flops 4294967296 | bytes 16777216 | tf_op jit(solution)/shard_map/gate_up/pallas_call | solution.py:75
  56.4 0.1 collective-permute-start.17
  56.5 3.4 %collective-permute-done.8.refs_1_ = bf16[2,2,64,2048]{3,2,1,0:T(8,128)(2,1)S(1)} collective-permute-done((bf16[2,2,64,2048]{3,2,1,0:T(8,128)(2,1)S(1)}, bf16[2,2,64,2048]{3,2,1,0:T(8,128)(2,1)S(1)}, u32[]{:S(2)}, u32[]{:S(2)}) %collective-permute-start.8) | collective-permute-done | bytes 1048608 | tf_op jit(solution)/shard_map/ppermute | solution.py:216
  59.8 0.1 add_slots.2
  60.0 9.2 %collective-permute-done.9.refs_2_ = bf16[1,2,64,2048]{3,2,1,0:T(8,128)(2,1)S(1)} collective-permute-done((bf16[1,2,64,2048]{3,2,1,0:T(8,128)(2,1)S(1)}, bf16[1,2,64,2048]{3,2,1,0:T(8,128)(2,1)S(1)}, u32[]{:S(2)}, u32[]{:S(2)}) %collective-permute-start.9) | collective-permute-done | bytes 524320 | tf_op jit(solution)/shard_map/ppermute | solution.py:216
  69.2 0.5 hidden.2.refs_0_
  69.8 7.8 %collective-permute-start.11 = (bf16[64,2048]{1,0:T(8,128)(2,1)S(1)}, bf16[64,2048]{1,0:T(8,128)(2,1)S(1)}, u32[]{:S(2)}, u32[]{:S(2)}) collective-permute-start(bf16[64,2048]{1,0:T(8,128)(2,1)S(1)} %hidden.2.refs_0_), channel_id=1, source_target_pairs={{0,16},{1,9},{2,18},{3,11},{4,20},{5,13},{6,22},{7,15},{8,24},{9,1... | collective-permute-start | bytes 786440 | tf_op jit(solution)/shard_map/ppermute | solution.py:216
  77.6 6.6 %collective-permute-start.12 = (bf16[64,2048]{1,0:T(8,128)(2,1)S(1)}, bf16[64,2048]{1,0:T(8,128)(2,1)S(1)}, u32[]{:S(2)}, u32[]{:S(2)}) collective-permute-start(bf16[64,2048]{1,0:T(8,128)(2,1)S(1)} %collective-permute-done.10.refs_1_.refs_2_), channel_id=1, source_target_pairs={{0,16},{1,9},{2,18},{3,11},{4,20},{5,13},{6,22},{7,15},{8,24},{9,1... | collective-permute-start | bytes 786440 | tf_op jit(solution)/shard_map/ppermute | solution.py:216
  84.2 0.1 add_slots.3
  84.3 0.4 collective-permute-start.18
  84.7 0.1 broadcast_in_dim.11
  84.9 6.6 %collective-permute-done.12.refs_3_ = bf16[64,2048]{1,0:T(8,128)(2,1)S(1)} collective-permute-done((bf16[64,2048]{1,0:T(8,128)(2,1)S(1)}, bf16[64,2048]{1,0:T(8,128)(2,1)S(1)}, u32[]{:S(2)}, u32[]{:S(2)}) %collective-permute-start.12) | collective-permute-done | bytes 262176 | tf_op jit(solution)/shard_map/ppermute | solution.py:216
  91.4 6.2 %down.2 = (f32[4,32,2048]{2,1,0:T(8,128)S(1)}, bf16[4,32,2048]{2,1,0:T(8,128)(2,1)S(1)}) custom-call(s32[9]{0:T(128)S(1)} %stack.39.place_ref, bf16[64,2048]{1,0:T(8,128)(2,1)S(1)} %hidden.2.refs_0_, bf16[64,2048]{1,0:T(8,128)(2,1)S(1)} %collective-permute-done.10.refs_1_.refs_2_, bf16[64,2048]{1,0:T(8,128)(2,1)S(1)} %collective-permute-done.11.refs_2_, ...), custom_call_target="tpu_custom_call" | custom-call | flops 2147483648 | bytes 8388608 | tf_op jit(solution)/shard_map/down/pallas_call | solution.py:170
  97.7 0.5 hidden.3.refs_0_
  98.3 0.3 collective-permute-start.19
  98.6 2.1 %collective-permute-start.20 = (bf16[64,2048]{1,0:T(8,128)(2,1)S(1)}, bf16[64,2048]{1,0:T(8,128)(2,1)S(1)}, u32[]{:S(2)}, u32[]{:S(2)}) collective-permute-start(bf16[64,2048]{1,0:T(8,128)(2,1)S(1)} %hidden.3.refs_0_), channel_id=1, source_target_pairs={{0,16},{1,9},{2,18},{3,11},{4,20},{5,13},{6,22},{7,15},{8,24},{9,1... | collective-permute-start | bytes 786440 | tf_op jit(solution)/shard_map/ppermute | solution.py:216
  100.6 5.8 %collective-permute-done.19.refs_1_ = bf16[64,2048]{1,0:T(8,128)(2,1)S(1)} collective-permute-done((bf16[64,2048]{1,0:T(8,128)(2,1)S(1)}, bf16[64,2048]{1,0:T(8,128)(2,1)S(1)}, u32[]{:S(2)}, u32[]{:S(2)}) %collective-permute-start.19) | collective-permute-done | bytes 262176 | tf_op jit(solution)/shard_map/ppermute | solution.py:216
  106.5 2.4 %collective-permute-start.21 = (bf16[64,2048]{1,0:T(8,128)(2,1)S(1)}, bf16[64,2048]{1,0:T(8,128)(2,1)S(1)}, u32[]{:S(2)}, u32[]{:S(2)}) collective-permute-start(bf16[64,2048]{1,0:T(8,128)(2,1)S(1)} %collective-permute-done.19.refs_1_), channel_id=1, source_target_pairs={{0,16},{1,9},{2,18},{3,11},{4,20},{5,13},{6,22},{7,15},{8,24},{9,1... | collective-permute-start | bytes 786440 | tf_op jit(solution)/shard_map/ppermute | solution.py:216
  109.0 1.0 collective-permute-start.14
  109.9 1.1 collective-permute-start.15
  111.0 2.4 %collective-permute-start.16 = (bf16[32,2048]{1,0:T(8,128)(2,1)S(1)}, bf16[32,2048]{1,0:T(8,128)(2,1)S(1)}, u32[]{:S(2)}, u32[]{:S(2)}) collective-permute-start(bf16[32,2048]{1,0:T(8,128)(2,1)S(1)} %get-tuple-element.24), channel_id=1, source_target_pairs={{0,6},{1,7},{2,4},{3,5},{4,2},{5,3},{6,0},{7,1},{8,14},{9,15},{10,... | collective-permute-start | bytes 393224 | tf_op jit(solution)/shard_map/ppermute | solution.py:216
  113.4 0.6 collective-permute-done.14.refs_6_
  114.0 7.2 %collective-permute-done.15.refs_7_ = bf16[32,2048]{1,0:T(8,128)(2,1)S(1)} collective-permute-done((bf16[32,2048]{1,0:T(8,128)(2,1)S(1)}, bf16[32,2048]{1,0:T(8,128)(2,1)S(1)}, u32[]{:S(2)}, u32[]{:S(2)}) %collective-permute-start.15) | collective-permute-done | bytes 131104 | tf_op jit(solution)/shard_map/ppermute | solution.py:216
  121.2 6.2 %down.3 = (f32[4,32,2048]{2,1,0:T(8,128)S(1)}, bf16[4,32,2048]{2,1,0:T(8,128)(2,1)S(1)}) custom-call(s32[9]{0:T(128)S(1)} %stack.39.place_ref, bf16[64,2048]{1,0:T(8,128)(2,1)S(1)} %hidden.3.refs_0_, bf16[64,2048]{1,0:T(8,128)(2,1)S(1)} %collective-permute-done.19.refs_1_, bf16[64,2048]{1,0:T(8,128)(2,1)S(1)} %collective-permute-done.20.refs_2_, ...), custom_call_target="tpu_custom_call" | custom-call | flops 2147483648 | bytes 8388608 | tf_op jit(solution)/shard_map/down/pallas_call | solution.py:170
  127.5 1.9 %collective-permute-done.22 = bf16[4,32,2048]{2,1,0:T(8,128)(2,1)S(1)} collective-permute-done((bf16[4,32,2048]{2,1,0:T(8,128)(2,1)S(1)}, bf16[4,32,2048]{2,1,0:T(8,128)(2,1)S(1)}, u32[]{:S(2)}, u32[]{:S(2)}) %collective-permute-start.22) | collective-permute-done | bytes 524320 | tf_op jit(solution)/shard_map/ppermute | solution.py:216
  129.5 2.0 %collective-permute-start.23 = (bf16[32,2048]{1,0:T(8,128)(2,1)S(1)}, bf16[32,2048]{1,0:T(8,128)(2,1)S(1)}, u32[]{:S(2)}, u32[]{:S(2)}) collective-permute-start(bf16[32,2048]{1,0:T(8,128)(2,1)S(1)} %get-tuple-element.21), channel_id=1, source_target_pairs={{0,2},{1,3},{2,0},{3,1},{4,6},{5,7},{6,4},{7,5},{8,10},{9,11},{10,... | collective-permute-start | bytes 393224 | tf_op jit(solution)/shard_map/ppermute | solution.py:216
  131.5 1.3 collective-permute-start.24
  132.8 1.4 collective-permute-start.25
  134.3 3.0 %collective-permute-done.23 = bf16[32,2048]{1,0:T(8,128)(2,1)S(1)} collective-permute-done((bf16[32,2048]{1,0:T(8,128)(2,1)S(1)}, bf16[32,2048]{1,0:T(8,128)(2,1)S(1)}, u32[]{:S(2)}, u32[]{:S(2)}) %collective-permute-start.23) | collective-permute-done | bytes 131104 | tf_op jit(solution)/shard_map/ppermute | solution.py:216
  137.3 7.2 %collective-permute-done.24 = bf16[32,2048]{1,0:T(8,128)(2,1)S(1)} collective-permute-done((bf16[32,2048]{1,0:T(8,128)(2,1)S(1)}, bf16[32,2048]{1,0:T(8,128)(2,1)S(1)}, u32[]{:S(2)}, u32[]{:S(2)}) %collective-permute-start.24) | collective-permute-done | bytes 131104 | tf_op jit(solution)/shard_map/ppermute | solution.py:216
  144.5 0.7 pad_maximum_fusion
  (28 shorter events, 0.8 us)
Async XLA Ops:
  0.0 13.2 %collective-permute-start = (bf16[128,1024]{1,0:T(8,128)(2,1)}, bf16[128,1024]{1,0:T(8,128)(2,1)S(1)}, u32[]{:S(2)}, u32[]{:S(2)}) collective-permute-start(bf16[128,1024]{1,0:T(8,128)(2,1)} %param.7), channel_id=1, source_target_pairs={{0,0},{1,1},{2,8},{3,9},{4,16},{5,17},{6,24},{7,25},{8,2},{9,3},{1... | collective-permute-start | bytes 786440 | tf_op jit(solution)/shard_map/ppermute | solution.py:216
  1.6 11.8 %collective-permute-start.1 = (bf16[128,1024]{1,0:T(8,128)(2,1)}, bf16[128,1024]{1,0:T(8,128)(2,1)S(1)}, u32[]{:S(2)}, u32[]{:S(2)}) collective-permute-start(bf16[128,1024]{1,0:T(8,128)(2,1)} %param.7), channel_id=1, source_target_pairs={{0,2},{1,3},{2,10},{3,11},{4,18},{5,19},{6,26},{7,27},{8,0},{9,1},... | collective-permute-start | bytes 786440 | tf_op jit(solution)/shard_map/ppermute | solution.py:216
  6.4 15.8 %collective-permute-start.2 = (bf16[128,1024]{1,0:T(8,128)(2,1)}, bf16[128,1024]{1,0:T(8,128)(2,1)S(1)}, u32[]{:S(2)}, u32[]{:S(2)}) collective-permute-start(bf16[128,1024]{1,0:T(8,128)(2,1)} %param.7), channel_id=1, source_target_pairs={{0,4},{1,5},{2,12},{3,13},{4,20},{5,21},{6,28},{7,29},{8,6},{9,7},... | collective-permute-start | bytes 786440 | tf_op jit(solution)/shard_map/ppermute | solution.py:216
  9.8 13.4 %collective-permute-start.3 = (bf16[128,1024]{1,0:T(8,128)(2,1)}, bf16[128,1024]{1,0:T(8,128)(2,1)S(1)}, u32[]{:S(2)}, u32[]{:S(2)}) collective-permute-start(bf16[128,1024]{1,0:T(8,128)(2,1)} %param.7), channel_id=1, source_target_pairs={{0,6},{1,7},{2,14},{3,15},{4,22},{5,23},{6,30},{7,31},{8,4},{9,5},... | collective-permute-start | bytes 786440 | tf_op jit(solution)/shard_map/ppermute | solution.py:216
  13.2 10.3 %collective-permute-start.4 = (bf16[128,1024]{1,0:T(8,128)(2,1)S(1)}, bf16[128,1024]{1,0:T(8,128)(2,1)S(1)}, u32[]{:S(2)}, u32[]{:S(2)}) collective-permute-start(bf16[128,1024]{1,0:T(8,128)(2,1)S(1)} %collective-permute-done), channel_id=1, source_target_pairs={{0,1},{1,0},{2,3},{3,2},{4,5},{5,4},{6,7},{7,6},{8,9},{9,8},{10,11... | collective-permute-start | bytes 786440 | tf_op jit(solution)/shard_map/ppermute | solution.py:216
  13.4 10.1 %collective-permute-start.5 = (bf16[128,1024]{1,0:T(8,128)(2,1)S(1)}, bf16[128,1024]{1,0:T(8,128)(2,1)S(1)}, u32[]{:S(2)}, u32[]{:S(2)}) collective-permute-start(bf16[128,1024]{1,0:T(8,128)(2,1)S(1)} %collective-permute-done.1), channel_id=1, source_target_pairs={{0,1},{1,0},{2,3},{3,2},{4,5},{5,4},{6,7},{7,6},{8,9},{9,8},{10,11... | collective-permute-start | bytes 786440 | tf_op jit(solution)/shard_map/ppermute | solution.py:216
  22.2 1.5 %collective-permute-start.6 = (bf16[128,1024]{1,0:T(8,128)(2,1)S(1)}, bf16[128,1024]{1,0:T(8,128)(2,1)S(1)}, u32[]{:S(2)}, u32[]{:S(2)}) collective-permute-start(bf16[128,1024]{1,0:T(8,128)(2,1)S(1)} %collective-permute-done.2), channel_id=1, source_target_pairs={{0,1},{1,0},{2,3},{3,2},{4,5},{5,4},{6,7},{7,6},{8,9},{9,8},{10,11... | collective-permute-start | bytes 786440 | tf_op jit(solution)/shard_map/ppermute | solution.py:216
  23.2 1.5 %collective-permute-start.7 = (bf16[128,1024]{1,0:T(8,128)(2,1)S(1)}, bf16[128,1024]{1,0:T(8,128)(2,1)S(1)}, u32[]{:S(2)}, u32[]{:S(2)}) collective-permute-start(bf16[128,1024]{1,0:T(8,128)(2,1)S(1)} %collective-permute-done.3), channel_id=1, source_target_pairs={{0,1},{1,0},{2,3},{3,2},{4,5},{5,4},{6,7},{7,6},{8,9},{9,8},{10,11... | collective-permute-start | bytes 786440 | tf_op jit(solution)/shard_map/ppermute | solution.py:216
  34.1 25.7 %collective-permute-start.8 = (bf16[2,2,64,2048]{3,2,1,0:T(8,128)(2,1)S(1)}, bf16[2,2,64,2048]{3,2,1,0:T(8,128)(2,1)S(1)}, u32[]{:S(2)}, u32[]{:S(2)}) collective-permute-start(bf16[2,2,64,2048]{3,2,1,0:T(8,128)(2,1)S(1)} %get-tuple-element.14), channel_id=1, source_target_pairs={{0,16},{1,9},{2,18},{3,11},{4,20},{5,13},{6,22},{7,15},{8,24},{9,1... | collective-permute-start | bytes 3145736 | tf_op jit(solution)/shard_map/ppermute | solution.py:216
  56.4 28.3 %copy-start = (s32[16,16]{1,0:T(8,128)S(1)}, s32[16,16]{1,0:T(8,128)}, u32[]{:S(2)}) copy-start(s32[16,16]{1,0:T(8,128)} %param.13) | copy-start | bytes 3076
  56.4 27.8 %collective-permute-start.17 = (bf16[2,2,64,2048]{3,2,1,0:T(8,128)(2,1)S(1)}, bf16[2,2,64,2048]{3,2,1,0:T(8,128)(2,1)S(1)}, u32[]{:S(2)}, u32[]{:S(2)}) collective-permute-start(bf16[2,2,64,2048]{3,2,1,0:T(8,128)(2,1)S(1)} %get-tuple-element.18), channel_id=1, source_target_pairs={{0,16},{1,9},{2,18},{3,11},{4,20},{5,13},{6,22},{7,15},{8,24},{9,1... | collective-permute-start | bytes 3145736 | tf_op jit(solution)/shard_map/ppermute | solution.py:216
  60.0 9.2 %collective-permute-start.9 = (bf16[1,2,64,2048]{3,2,1,0:T(8,128)(2,1)S(1)}, bf16[1,2,64,2048]{3,2,1,0:T(8,128)(2,1)S(1)}, u32[]{:S(2)}, u32[]{:S(2)}) collective-permute-start(bf16[1,2,64,2048]{3,2,1,0:T(8,128)(2,1)S(1)} %add_slots.2), channel_id=1, source_target_pairs={{0,8},{1,17},{2,10},{3,19},{4,12},{5,21},{6,14},{7,23},{8,0},{9,25... | collective-permute-start | bytes 1572872 | tf_op jit(solution)/shard_map/ppermute | solution.py:216
  69.7 7.8 %collective-permute-start.10 = (bf16[64,2048]{1,0:T(8,128)(2,1)S(1)}, bf16[64,2048]{1,0:T(8,128)(2,1)S(1)}, u32[]{:S(2)}, u32[]{:S(2)}) collective-permute-start(bf16[64,2048]{1,0:T(8,128)(2,1)S(1)} %hidden.2.refs_0_), channel_id=1, source_target_pairs={{0,8},{1,17},{2,10},{3,19},{4,12},{5,21},{6,14},{7,23},{8,0},{9,25... | collective-permute-start | bytes 786440 | tf_op jit(solution)/shard_map/ppermute | solution.py:216
  69.8 15.1 %collective-permute-start.11 = (bf16[64,2048]{1,0:T(8,128)(2,1)S(1)}, bf16[64,2048]{1,0:T(8,128)(2,1)S(1)}, u32[]{:S(2)}, u32[]{:S(2)}) collective-permute-start(bf16[64,2048]{1,0:T(8,128)(2,1)S(1)} %hidden.2.refs_0_), channel_id=1, source_target_pairs={{0,16},{1,9},{2,18},{3,11},{4,20},{5,13},{6,22},{7,15},{8,24},{9,1... | collective-permute-start | bytes 786440 | tf_op jit(solution)/shard_map/ppermute | solution.py:216
  77.6 13.9 %collective-permute-start.12 = (bf16[64,2048]{1,0:T(8,128)(2,1)S(1)}, bf16[64,2048]{1,0:T(8,128)(2,1)S(1)}, u32[]{:S(2)}, u32[]{:S(2)}) collective-permute-start(bf16[64,2048]{1,0:T(8,128)(2,1)S(1)} %collective-permute-done.10.refs_1_.refs_2_), channel_id=1, source_target_pairs={{0,16},{1,9},{2,18},{3,11},{4,20},{5,13},{6,22},{7,15},{8,24},{9,1... | collective-permute-start | bytes 786440 | tf_op jit(solution)/shard_map/ppermute | solution.py:216
  84.3 13.4 %collective-permute-start.18 = (bf16[1,2,64,2048]{3,2,1,0:T(8,128)(2,1)S(1)}, bf16[1,2,64,2048]{3,2,1,0:T(8,128)(2,1)S(1)}, u32[]{:S(2)}, u32[]{:S(2)}) collective-permute-start(bf16[1,2,64,2048]{3,2,1,0:T(8,128)(2,1)S(1)} %add_slots.3), channel_id=1, source_target_pairs={{0,8},{1,17},{2,10},{3,19},{4,12},{5,21},{6,14},{7,23},{8,0},{9,25... | collective-permute-start | bytes 1572872 | tf_op jit(solution)/shard_map/ppermute | solution.py:216
  97.7 11.2 %collective-permute-start.13 = (bf16[4,32,2048]{2,1,0:T(8,128)(2,1)S(1)}, bf16[4,32,2048]{2,1,0:T(8,128)(2,1)S(1)}, u32[]{:S(2)}, u32[]{:S(2)}) collective-permute-start(bf16[4,32,2048]{2,1,0:T(8,128)(2,1)S(1)} %get-tuple-element.16.refs_3_), channel_id=1, source_target_pairs={{0,1},{1,0},{2,3},{3,2},{4,5},{5,4},{6,7},{7,6},{8,9},{9,8},{10,11... | collective-permute-start | bytes 1572872 | tf_op jit(solution)/shard_map/ppermute | solution.py:216
  98.3 8.2 %collective-permute-start.19 = (bf16[64,2048]{1,0:T(8,128)(2,1)S(1)}, bf16[64,2048]{1,0:T(8,128)(2,1)S(1)}, u32[]{:S(2)}, u32[]{:S(2)}) collective-permute-start(bf16[64,2048]{1,0:T(8,128)(2,1)S(1)} %hidden.3.refs_0_), channel_id=1, source_target_pairs={{0,8},{1,17},{2,10},{3,19},{4,12},{5,21},{6,14},{7,23},{8,0},{9,25... | collective-permute-start | bytes 786440 | tf_op jit(solution)/shard_map/ppermute | solution.py:216
  98.6 14.9 %collective-permute-start.20 = (bf16[64,2048]{1,0:T(8,128)(2,1)S(1)}, bf16[64,2048]{1,0:T(8,128)(2,1)S(1)}, u32[]{:S(2)}, u32[]{:S(2)}) collective-permute-start(bf16[64,2048]{1,0:T(8,128)(2,1)S(1)} %hidden.3.refs_0_), channel_id=1, source_target_pairs={{0,16},{1,9},{2,18},{3,11},{4,20},{5,13},{6,22},{7,15},{8,24},{9,1... | collective-permute-start | bytes 786440 | tf_op jit(solution)/shard_map/ppermute | solution.py:216
  106.5 14.7 %collective-permute-start.21 = (bf16[64,2048]{1,0:T(8,128)(2,1)S(1)}, bf16[64,2048]{1,0:T(8,128)(2,1)S(1)}, u32[]{:S(2)}, u32[]{:S(2)}) collective-permute-start(bf16[64,2048]{1,0:T(8,128)(2,1)S(1)} %collective-permute-done.19.refs_1_), channel_id=1, source_target_pairs={{0,16},{1,9},{2,18},{3,11},{4,20},{5,13},{6,22},{7,15},{8,24},{9,1... | collective-permute-start | bytes 786440 | tf_op jit(solution)/shard_map/ppermute | solution.py:216
  109.0 5.1 %collective-permute-start.14 = (bf16[32,2048]{1,0:T(8,128)(2,1)S(1)}, bf16[32,2048]{1,0:T(8,128)(2,1)S(1)}, u32[]{:S(2)}, u32[]{:S(2)}) collective-permute-start(bf16[32,2048]{1,0:T(8,128)(2,1)S(1)} %get-tuple-element.26), channel_id=1, source_target_pairs={{0,2},{1,3},{2,0},{3,1},{4,6},{5,7},{6,4},{7,5},{8,10},{9,11},{10,... | collective-permute-start | bytes 393224 | tf_op jit(solution)/shard_map/ppermute | solution.py:216
  109.9 11.3 %collective-permute-start.15 = (bf16[32,2048]{1,0:T(8,128)(2,1)S(1)}, bf16[32,2048]{1,0:T(8,128)(2,1)S(1)}, u32[]{:S(2)}, u32[]{:S(2)}) collective-permute-start(bf16[32,2048]{1,0:T(8,128)(2,1)S(1)} %get-tuple-element.25), channel_id=1, source_target_pairs={{0,4},{1,5},{2,6},{3,7},{4,0},{5,1},{6,2},{7,3},{8,12},{9,13},{10,... | collective-permute-start | bytes 393224 | tf_op jit(solution)/shard_map/ppermute | solution.py:216
  111.0 10.2 %collective-permute-start.16 = (bf16[32,2048]{1,0:T(8,128)(2,1)S(1)}, bf16[32,2048]{1,0:T(8,128)(2,1)S(1)}, u32[]{:S(2)}, u32[]{:S(2)}) collective-permute-start(bf16[32,2048]{1,0:T(8,128)(2,1)S(1)} %get-tuple-element.24), channel_id=1, source_target_pairs={{0,6},{1,7},{2,4},{3,5},{4,2},{5,3},{6,0},{7,1},{8,14},{9,15},{10,... | collective-permute-start | bytes 393224 | tf_op jit(solution)/shard_map/ppermute | solution.py:216
  127.5 2.0 %collective-permute-start.22 = (bf16[4,32,2048]{2,1,0:T(8,128)(2,1)S(1)}, bf16[4,32,2048]{2,1,0:T(8,128)(2,1)S(1)}, u32[]{:S(2)}, u32[]{:S(2)}) collective-permute-start(bf16[4,32,2048]{2,1,0:T(8,128)(2,1)S(1)} %get-tuple-element.20), channel_id=1, source_target_pairs={{0,1},{1,0},{2,3},{3,2},{4,5},{5,4},{6,7},{7,6},{8,9},{9,8},{10,11... | collective-permute-start | bytes 1572872 | tf_op jit(solution)/shard_map/ppermute | solution.py:216
  129.5 7.8 %collective-permute-start.23 = (bf16[32,2048]{1,0:T(8,128)(2,1)S(1)}, bf16[32,2048]{1,0:T(8,128)(2,1)S(1)}, u32[]{:S(2)}, u32[]{:S(2)}) collective-permute-start(bf16[32,2048]{1,0:T(8,128)(2,1)S(1)} %get-tuple-element.21), channel_id=1, source_target_pairs={{0,2},{1,3},{2,0},{3,1},{4,6},{5,7},{6,4},{7,5},{8,10},{9,11},{10,... | collective-permute-start | bytes 393224 | tf_op jit(solution)/shard_map/ppermute | solution.py:216
  131.5 12.9 %collective-permute-start.24 = (bf16[32,2048]{1,0:T(8,128)(2,1)S(1)}, bf16[32,2048]{1,0:T(8,128)(2,1)S(1)}, u32[]{:S(2)}, u32[]{:S(2)}) collective-permute-start(bf16[32,2048]{1,0:T(8,128)(2,1)S(1)} %get-tuple-element.23), channel_id=1, source_target_pairs={{0,4},{1,5},{2,6},{3,7},{4,0},{5,1},{6,2},{7,3},{8,12},{9,13},{10,... | collective-permute-start | bytes 393224 | tf_op jit(solution)/shard_map/ppermute | solution.py:216
  132.8 11.6 %collective-permute-start.25 = (bf16[32,2048]{1,0:T(8,128)(2,1)S(1)}, bf16[32,2048]{1,0:T(8,128)(2,1)S(1)}, u32[]{:S(2)}, u32[]{:S(2)}) collective-permute-start(bf16[32,2048]{1,0:T(8,128)(2,1)S(1)} %get-tuple-element.22), channel_id=1, source_target_pairs={{0,6},{1,7},{2,4},{3,5},{4,2},{5,3},{6,0},{7,1},{8,14},{9,15},{10,... | collective-permute-start | bytes 393224 | tf_op jit(solution)/shard_map/ppermute | solution.py:216

commit v4 on v3

--- a/solution.py
+++ b/solution.py
@@ -37,11 +37,9 @@
     return jnp.repeat(keep_mask.astype(jnp.float32), width // keep_mask.shape[1], axis=1)
 
 
-def gate_up_kernel(n, place_ref, *refs):
-    own, other = refs[:n], refs[n : 2 * n]
-    gate_ref, up_ref, gate_keep, up_keep, keep_ref, send_ref, x = refs[2 * n :]
-    _, piece, half = own[0].shape
-    rows = 2 * piece
+def gate_up_kernel(n, place_ref, own_ref, other_ref, gate_ref, up_ref, gate_keep, up_keep, *refs):
+    outs, x = refs[:4], refs[4]
+    _, rows, half = own_ref.shape
 
     @pl.when(pl.program_id(0) == 0)
     def _():
@@ -50,92 +48,94 @@
         others = pl.ds(pl.multiple_of((1 - core) * half, half), half)
         for k in range(n):
             at = pl.ds(pl.multiple_of(place_ref[1 + n + k] * rows, rows), rows)
-            x[at, mine] = own[k][...].reshape(rows, half)
-            x[at, others] = other[k][...].reshape(rows, half)
+            x[at, mine] = own_ref[k]
+            x[at, others] = other_ref[k]
 
     for which, (weight, keep) in enumerate(((gate_ref, gate_keep), (up_ref, up_keep))):
         product = masked_product(x, weight, keep)
-        for p in range(n // 2):
-            q = p + n // 2
-            keep_ref[p, which] = product[p * rows : (p + 1) * rows]
-            send_ref[p, which] = product[q * rows : (q + 1) * rows].astype(jnp.bfloat16)
-
-
-def gate_up(place, batch, own, other, gate_weight, up_weight, gate_keep, up_keep):
-    n = len(own)
-    _, whole, half = own[0].shape
-    piece = whole // BATCHES
-    rows = 2 * piece
+        for p in range(n):
+            offset = p if which == 0 else mirror(p, n)
+            term = product[offset * rows : (offset + 1) * rows]
+            if p < n // 2:
+                outs[which][p] = term
+            else:
+                outs[2 + which][p - n // 2] = term.astype(jnp.bfloat16)
+
+
+def gate_up(place, own, other, gate_weight, up_weight, gate_keep, up_keep):
+    n, rows, half = own.shape
     depth, width = gate_weight.shape
     tile = min(width, TILE)
-    part = pl.BlockSpec((2, piece, half), lambda i, *_: (0, batch, 0))
+    whole = pl.BlockSpec((n, rows, half), lambda i, *_: (0, 0, 0))
     strip = pl.BlockSpec((depth, tile), lambda i, *_: (0, i))
     mask = pl.BlockSpec((gate_keep.shape[0], tile), lambda i, *_: (0, i))
-    out = pl.BlockSpec((n // 2, 2, rows, tile), lambda i, *_: (0, 0, 0, i))
+    out = pl.BlockSpec((n // 2, rows, tile), lambda i, *_: (0, 0, i))
     return pl.pallas_call(
         functools.partial(gate_up_kernel, n),
         grid_spec=pltpu.PrefetchScalarGridSpec(
             num_scalar_prefetch=1,
             grid=(width // tile,),
-            in_specs=[part] * (2 * n) + [strip, strip, mask, mask],
-            out_specs=[out, out],
+            in_specs=[whole, whole, strip, strip, mask, mask],
+            out_specs=[out] * 4,
             scratch_shapes=[pltpu.VMEM((n * rows, depth), jnp.bfloat16)],
         ),
-        out_shape=[
-            jax.ShapeDtypeStruct((n // 2, 2, rows, width), jnp.float32),
-            jax.ShapeDtypeStruct((n // 2, 2, rows, width), jnp.bfloat16),
-        ],
+        out_shape=[jax.ShapeDtypeStruct((n // 2, rows, width), jnp.float32)] * 2
+        + [jax.ShapeDtypeStruct((n // 2, rows, width), jnp.bfloat16)] * 2,
         compiler_params=pltpu.CompilerParams(vmem_limit_bytes=VMEM_BYTES),
         cost_estimate=pl.CostEstimate(
             flops=4 * n * rows * depth * width, bytes_accessed=4 * depth * width, transcendentals=0
         ),
         name="gate_up",
-    )(place, *own, *other, gate_weight, up_weight, gate_keep, up_keep)
+    )(place, own, other, gate_weight, up_weight, gate_keep, up_keep)
+
+
+def total_of(refs):
+    total = refs[0][...].astype(jnp.float32)
+    for ref in refs[1:]:
+        total += ref[...].astype(jnp.float32)
+    return total
 
 
 def add_kernel(n, *refs):
-    total = refs[0][...].astype(jnp.float32)
-    for ref in refs[1:n]:
-        total += ref[...].astype(jnp.float32)
-    refs[-1][...] = total.astype(jnp.bfloat16)
-
-
-def add_slots(parts, first, count, after):
-    _, two, rows, width = parts[0].shape
-    return pl.pallas_call(
-        functools.partial(add_kernel, len(parts)),
-        grid=(count, two),
-        in_specs=[pl.BlockSpec((1, 1, rows, width), lambda i, j: (first + i, j, 0, 0))] * len(parts)
+    refs[-2][...] = total_of(refs[:n]).astype(jnp.bfloat16)
+    refs[-1][...] = total_of(refs[n : 2 * n]).astype(jnp.bfloat16)
+
+
+def add_slots(gate_parts, up_parts, first, count, after):
+    _, rows, width = gate_parts[0].shape
+    n = len(gate_parts)
+    return pl.pallas_call(
+        functools.partial(add_kernel, n),
+        grid=(count,),
+        in_specs=[pl.BlockSpec((1, rows, width), lambda i: (first + i, 0, 0))] * (2 * n)
         + [pl.BlockSpec(memory_space=pl.ANY)] * len(after),
-        out_specs=pl.BlockSpec((1, 1, rows, width), lambda i, j: (i, j, 0, 0)),
-        out_shape=jax.ShapeDtypeStruct((count, two, rows, width), jnp.bfloat16),
+        out_specs=[pl.BlockSpec((1, rows, width), lambda i: (i, 0, 0))] * 2,
+        out_shape=[jax.ShapeDtypeStruct((count, rows, width), jnp.bfloat16)] * 2,
         compiler_params=pltpu.CompilerParams(vmem_limit_bytes=VMEM_BYTES),
         name="add_slots",
-    )(*parts, *after)
+    )(*gate_parts, *up_parts, *after)
 
 
 def activate_kernel(n, *refs):
-    gate = refs[0][0, 0].astype(jnp.float32)
-    up = refs[0][0, 1].astype(jnp.float32)
-    for ref in refs[1:n]:
-        gate += ref[0, 0].astype(jnp.float32)
-        up += ref[0, 1].astype(jnp.float32)
+    gate = total_of(refs[:n])[0]
+    up = total_of(refs[n : 2 * n])[0]
     refs[-1][...] = (gate / (1.0 + jnp.exp(-gate)) * up).astype(jnp.bfloat16)
 
 
-def activate(parts, after):
-    _, two, rows, width = parts[0].shape
+def activate(gate_parts, up_parts, after):
+    _, rows, width = gate_parts[0].shape
     tile = width // 2
-    return pl.pallas_call(
-        functools.partial(activate_kernel, len(parts)),
+    n = len(gate_parts)
+    return pl.pallas_call(
+        functools.partial(activate_kernel, n),
         grid=(width // tile,),
-        in_specs=[pl.BlockSpec((1, two, rows, tile), lambda i: (0, 0, 0, i))] * len(parts)
+        in_specs=[pl.BlockSpec((1, rows, tile), lambda i: (0, 0, i))] * (2 * n)
         + [pl.BlockSpec(memory_space=pl.ANY)] * len(after),
         out_specs=pl.BlockSpec((rows, tile), lambda i: (0, i)),
         out_shape=jax.ShapeDtypeStruct((rows, width), jnp.bfloat16),
         compiler_params=pltpu.CompilerParams(vmem_limit_bytes=VMEM_BYTES),
         name="hidden",
-    )(*parts, *after)
+    )(*gate_parts, *up_parts, *after)
 
 
 def down_kernel(n, place_ref, *refs):
@@ -191,6 +191,24 @@
     )(place, *parts, weight, keep, *after)
 
 
+def join_kernel(n, *refs):
+    for k in range(n):
+        refs[-1][k] = refs[k][...]
+
+
+def join(blocks, after):
+    n = len(blocks)
+    spec = pl.BlockSpec(memory_space=pltpu.VMEM)
+    return pl.pallas_call(
+        functools.partial(join_kernel, n),
+        in_specs=[spec] * n + [pl.BlockSpec(memory_space=pl.ANY)] * len(after),
+        out_specs=spec,
+        out_shape=jax.ShapeDtypeStruct((n,) + blocks[0].shape, blocks[0].dtype),
+        compiler_params=pltpu.CompilerParams(vmem_limit_bytes=VMEM_BYTES),
+        name="join",
+    )(*blocks, *after)
+
+
 def mirror(p, n):
     out = 0
     while n > 1:
@@ -203,8 +221,8 @@
     tok, hid = lax.axis_index("tok"), lax.axis_index("hid")
     z, core = hid // 2, hid % 2
     offsets = [jnp.where(core == 0, p, mirror(p, n_tok)) for p in range(n_tok)]
-    positions = [sum(jnp.where(off == tok ^ z ^ k, p, 0) for p, off in enumerate(offsets)) for k in range(n_tok)]
-    place = jnp.stack([core] + [tok ^ z ^ off for off in offsets] + positions).astype(jnp.int32)
+    place = jnp.stack([core] + [tok ^ z ^ off for off in offsets] + [tok ^ z ^ k for k in range(n_z)])
+    place = place.astype(jnp.int32)
 
     def send(value, to):
         perm = []
@@ -224,15 +242,17 @@
     def across_core(value):
         return send(value, lambda t, zz, c: (t, zz, 1 - c))
 
-    def halve(kept, sent, after):
+    def halve(gate_kept, up_kept, gate_sent, up_sent, after):
         left = n_tok // 2
-        kept = [kept]
+        gate_parts, up_parts = [gate_kept], [up_kept]
         while True:
-            kept.append(across_tok(sent, left))
+            turned = mirror(left, n_tok)
+            gate_parts.append(send(gate_sent, lambda t, zz, c: (t ^ left, zz, c)))
+            up_parts.append(send(up_sent, lambda t, zz, c: (t ^ turned, zz, c)))
             if left == 1:
-                return kept
+                return gate_parts, up_parts
             left //= 2
-            sent = add_slots(kept, left, left, after)
+            gate_sent, up_sent = add_slots(gate_parts, up_parts, left, left, after)
 
     def gather(part):
         parts, left = [part], 1
@@ -247,25 +267,30 @@
         return sums[0], [part.astype(jnp.bfloat16) for part in sums[1:]]
 
     rows, features = tokens.shape
+    piece = rows // (2 * BATCHES)
+    split = tokens.reshape(2, BATCHES, piece, features)
     gate_wide = widen(gate_keep, gate_weight.shape[1])
     up_wide = widen(up_keep, up_weight.shape[1])
     down_wide = widen(down_keep, down_weight.shape[1])
-    moved = [send(tokens, lambda t, zz, c: (zz, t ^ k, c)) for k in range(n_z)]
-    swapped = [across_core(block) for block in moved]
-    own = [block.reshape(2, rows // 2, features) for block in moved]
-    other = [block.reshape(2, rows // 2, features) for block in swapped]
-    sums = [gate_up(place, s, own, other, gate_weight, up_weight, gate_wide, up_wide) for s in range(BATCHES)]
+    moved = []
+    for s in range(BATCHES):
+        block = split[:, s].reshape(2 * piece, features)
+        moved.append([send(block, lambda t, zz, c: (zz, t ^ k, c)) for k in range(n_z)])
+    sums, before_swap = [], []
+    for blocks in moved:
+        own = join(blocks, before_swap)
+        sums.append(gate_up(place, own, across_core(own), gate_weight, up_weight, gate_wide, up_wide))
+        before_swap = [sums[-1][2]]
     out, before_add, before_hidden, before_down = [], [], [], []
-    for kept, sent in sums:
-        kept = halve(kept, sent, before_add)
-        parts = gather(activate(kept, before_hidden))
+    for terms in sums:
+        parts = gather(activate(*halve(*terms, before_add), before_hidden))
         mine, theirs = down(place, parts, down_weight, down_wide, before_down)
         total, sent = combine(mine, theirs)
         arrived = [across_z(sent[j - 1], j) for j in range(1, n_z)]
         for part in arrived:
             total += part.astype(jnp.float32)
         out.append(total.astype(jnp.bfloat16))
-        before_add, before_hidden, before_down = [parts[1]], [theirs], arrived
+        before_add, before_hidden, before_down = [parts[1]], sent, arrived
     return jnp.concatenate(out, axis=0)
 
 

time: 146 us -> 151 us (1.034)
  waiting for transfers between devices: 55.5 us -> 61.5 us
  starting transfers between devices: 54.2 us -> 52.3 us
    ppermute x26 -> x32, waiting for transfers between devices: 55.5 us -> 61.5 us  [send(): return lax.ppermute(value, AXES, perm)]
    ppermute x26 -> x32, starting transfers between devices: 54.2 us -> 52.3 us  [send(): return lax.ppermute(value, AXES, perm)]
  transfers between devices with their start and end apart: 26 -> 32, of which waited for: 14 -> 20; matrix products, arithmetic and copies ran while one was open for 1% -> 1% of each run, Pallas kernels for 12% -> 11%
where the time goes in v4:
time: 151 us; the launch traced here: 150 us
  waiting for transfers between devices  61.5 us (41%)
  starting transfers between devices  52.3 us (35%)
  Pallas kernels  32.3 us (21%)
  other arithmetic  2.43 us (2%)
    ppermute x32, waiting for transfers between devices, send(): return lax.ppermute(value, AXES, perm)  61.5 us
    ppermute x32, starting transfers between devices, send(): return lax.ppermute(value, AXES, perm)  52.3 us
    pallas_call x2, Pallas kernels, gate_up(): pl.pallas_call(functools.partial(gate_up_kernel, n), grid_spec=pltpu.Pref...  18.5 us
    pallas_call x2, Pallas kernels, down(): pl.pallas_call(functools.partial(down_kernel, n), grid_spec=pltpu.Prefetc...  12.5 us
  transfers between devices with their start and end apart: 32, of which 20 were waited for; matrix products, arithmetic and copies ran while one was open for 1% of the time, Pallas kernels for 11%

profile of v4, /device:TPU:0, one launch (start us, length us, event | category | flops | bytes accessed | tf_op | source)
XLA Modules:
  0.0 150.3 jit_solution(2879000773478096494)
XLA Ops:
  0.0 1.0 fusion.12
  1.0 5.1 %collective-permute-start.3 = (bf16[64,1024]{1,0:T(8,128)(2,1)S(1)}, bf16[64,1024]{1,0:T(8,128)(2,1)S(1)}, u32[]{:S(2)}, u32[]{:S(2)}) collective-permute-start(bf16[64,1024]{1,0:T(8,128)(2,1)S(1)} %bitcast.62), channel_id=1, source_target_pairs={{0,6},{1,7},{2,14},{3,15},{4,22},{5,23},{6,30},{7,31},{8,4},{9,5},... | collective-permute-start | bytes 393224 | tf_op jit(solution)/shard_map/ppermute | solution.py:234
  6.1 1.5 %collective-permute-start.2 = (bf16[64,1024]{1,0:T(8,128)(2,1)S(1)}, bf16[64,1024]{1,0:T(8,128)(2,1)S(1)}, u32[]{:S(2)}, u32[]{:S(2)}) collective-permute-start(bf16[64,1024]{1,0:T(8,128)(2,1)S(1)} %bitcast.63), channel_id=1, source_target_pairs={{0,4},{1,5},{2,12},{3,13},{4,20},{5,21},{6,28},{7,29},{8,6},{9,7},... | collective-permute-start | bytes 393224 | tf_op jit(solution)/shard_map/ppermute | solution.py:234
  8.1 0.7 collective-permute-start
  8.7 1.4 collective-permute-done.3.refs_3_
  10.1 2.8 %collective-permute-done.2.refs_2_ = bf16[64,1024]{1,0:T(8,128)(2,1)S(1)} collective-permute-done((bf16[64,1024]{1,0:T(8,128)(2,1)S(1)}, bf16[64,1024]{1,0:T(8,128)(2,1)S(1)}, u32[]{:S(2)}, u32[]{:S(2)}) %collective-permute-start.2) | collective-permute-done | bytes 131104 | tf_op jit(solution)/shard_map/ppermute | solution.py:234
  12.9 1.7 %collective-permute-done.1.refs_1_ = bf16[64,1024]{1,0:T(8,128)(2,1)S(1)} collective-permute-done((bf16[64,1024]{1,0:T(8,128)(2,1)S(1)}, bf16[64,1024]{1,0:T(8,128)(2,1)S(1)}, u32[]{:S(2)}, u32[]{:S(2)}) %collective-permute-start.1) | collective-permute-done | bytes 131104 | tf_op jit(solution)/shard_map/ppermute | solution.py:234
  14.7 0.7 convert_element_type.98
  15.4 0.7 convert_element_type.99
  16.6 9.3 %gate_up.2 = (f32[2,64,2048]{2,1,0:T(8,128)S(1)}, f32[2,64,2048]{2,1,0:T(8,128)S(1)}, bf16[2,64,2048]{2,1,0:T(8,128)(2,1)S(1)}, bf16[2,64,2048]{2,1,0:T(8,128)(2,1)S(1)}) custom-call(s32[9]{0:T(128)S(1)} %stack.33.place_ref, bf16[4,64,1024]{2,1,0:T(8,128)(2,1)S(1)} %join.2.own_ref, bf16[4,64,1024]{2,1,0:T(8,128)(2,1)S(1)} %collective-permute-done.4.other_ref, ...), custom_call_target="tpu_custom_call" | custom-call | flops 4294967296 | bytes 16777216 | tf_op jit(solution)/shard_map/gate_up/pallas_call | solution.py:73
  25.9 9.0 %collective-permute-start.6 = (bf16[2,64,2048]{2,1,0:T(8,128)(2,1)S(1)}, bf16[2,64,2048]{2,1,0:T(8,128)(2,1)S(1)}, u32[]{:S(2)}, u32[]{:S(2)}) collective-permute-start(bf16[2,64,2048]{2,1,0:T(8,128)(2,1)S(1)} %get-tuple-element.24), channel_id=1, source_target_pairs={{0,8},{1,9},{2,10},{3,11},{4,12},{5,13},{6,14},{7,15},{8,0},{9,1},... | collective-permute-start | bytes 1572872 | tf_op jit(solution)/shard_map/ppermute | solution.py:234
  35.2 2.0 %collective-permute-start.19 = (bf16[64,1024]{1,0:T(8,128)(2,1)S(1)}, bf16[64,1024]{1,0:T(8,128)(2,1)S(1)}, u32[]{:S(2)}, u32[]{:S(2)}) collective-permute-start(bf16[64,1024]{1,0:T(8,128)(2,1)S(1)} %bitcast.58), channel_id=1, source_target_pairs={{0,6},{1,7},{2,14},{3,15},{4,22},{5,23},{6,30},{7,31},{8,4},{9,5},... | collective-permute-start | bytes 393224 | tf_op jit(solution)/shard_map/ppermute | solution.py:234
  37.2 2.0 %collective-permute-start.18 = (bf16[64,1024]{1,0:T(8,128)(2,1)S(1)}, bf16[64,1024]{1,0:T(8,128)(2,1)S(1)}, u32[]{:S(2)}, u32[]{:S(2)}) collective-permute-start(bf16[64,1024]{1,0:T(8,128)(2,1)S(1)} %bitcast.59), channel_id=1, source_target_pairs={{0,4},{1,5},{2,12},{3,13},{4,20},{5,21},{6,28},{7,29},{8,6},{9,7},... | collective-permute-start | bytes 393224 | tf_op jit(solution)/shard_map/ppermute | solution.py:234
  39.3 11.1 %collective-permute-done.6.refs_3_.refs_4_ = bf16[2,64,2048]{2,1,0:T(8,128)(2,1)S(1)} collective-permute-done((bf16[2,64,2048]{2,1,0:T(8,128)(2,1)S(1)}, bf16[2,64,2048]{2,1,0:T(8,128)(2,1)S(1)}, u32[]{:S(2)}, u32[]{:S(2)}) %collective-permute-start.6) | collective-permute-done | bytes 524320 | tf_op jit(solution)/shard_map/ppermute | solution.py:234
  50.4 0.7 collective-permute-start.16
  51.2 3.9 %collective-permute-start.7 = (bf16[1,64,2048]{2,1,0:T(8,128)(2,1)S(1)}, bf16[1,64,2048]{2,1,0:T(8,128)(2,1)S(1)}, u32[]{:S(2)}, u32[]{:S(2)}) collective-permute-start(bf16[1,64,2048]{2,1,0:T(8,128)(2,1)S(1)} %get-tuple-element.25), channel_id=1, source_target_pairs={{0,8},{1,9},{2,10},{3,11},{4,12},{5,13},{6,14},{7,15},{8,0},{9,1},... | collective-permute-start | bytes 786440 | tf_op jit(solution)/shard_map/ppermute | solution.py:234
  55.1 5.2 %collective-permute-start.8 = (bf16[1,64,2048]{2,1,0:T(8,128)(2,1)S(1)}, bf16[1,64,2048]{2,1,0:T(8,128)(2,1)S(1)}, u32[]{:S(2)}, u32[]{:S(2)}) collective-permute-start(bf16[1,64,2048]{2,1,0:T(8,128)(2,1)S(1)} %get-tuple-element.26), channel_id=1, source_target_pairs={{0,16},{1,17},{2,18},{3,19},{4,20},{5,21},{6,22},{7,23},{8,24},{9,... | collective-permute-start | bytes 786440 | tf_op jit(solution)/shard_map/ppermute | solution.py:234
  60.4 3.3 %collective-permute-done.7.refs_2_ = bf16[1,64,2048]{2,1,0:T(8,128)(2,1)S(1)} collective-permute-done((bf16[1,64,2048]{2,1,0:T(8,128)(2,1)S(1)}, bf16[1,64,2048]{2,1,0:T(8,128)(2,1)S(1)}, u32[]{:S(2)}, u32[]{:S(2)}) %collective-permute-start.7) | collective-permute-done | bytes 262176 | tf_op jit(solution)/shard_map/ppermute | solution.py:234
  63.7 2.3 %collective-permute-done.8.refs_5_ = bf16[1,64,2048]{2,1,0:T(8,128)(2,1)S(1)} collective-permute-done((bf16[1,64,2048]{2,1,0:T(8,128)(2,1)S(1)}, bf16[1,64,2048]{2,1,0:T(8,128)(2,1)S(1)}, u32[]{:S(2)}, u32[]{:S(2)}) %collective-permute-start.8) | collective-permute-done | bytes 262176 | tf_op jit(solution)/shard_map/ppermute | solution.py:234
  66.0 0.5 hidden.2.refs_0_
  66.5 2.5 %collective-permute-start.9 = (bf16[64,2048]{1,0:T(8,128)(2,1)S(1)}, bf16[64,2048]{1,0:T(8,128)(2,1)S(1)}, u32[]{:S(2)}, u32[]{:S(2)}) collective-permute-start(bf16[64,2048]{1,0:T(8,128)(2,1)S(1)} %hidden.2.refs_0_), channel_id=1, source_target_pairs={{0,8},{1,17},{2,10},{3,19},{4,12},{5,21},{6,14},{7,23},{8,0},{9,25... | collective-permute-start | bytes 786440 | tf_op jit(solution)/shard_map/ppermute | solution.py:234
  69.1 2.5 %collective-permute-start.10 = (bf16[64,2048]{1,0:T(8,128)(2,1)S(1)}, bf16[64,2048]{1,0:T(8,128)(2,1)S(1)}, u32[]{:S(2)}, u32[]{:S(2)}) collective-permute-start(bf16[64,2048]{1,0:T(8,128)(2,1)S(1)} %hidden.2.refs_0_), channel_id=1, source_target_pairs={{0,16},{1,9},{2,18},{3,11},{4,20},{5,13},{6,22},{7,15},{8,24},{9,1... | collective-permute-start | bytes 786440 | tf_op jit(solution)/shard_map/ppermute | solution.py:234
  71.7 3.4 %collective-permute-done.9.refs_1_.refs_4_ = bf16[64,2048]{1,0:T(8,128)(2,1)S(1)} collective-permute-done((bf16[64,2048]{1,0:T(8,128)(2,1)S(1)}, bf16[64,2048]{1,0:T(8,128)(2,1)S(1)}, u32[]{:S(2)}, u32[]{:S(2)}) %collective-permute-start.9) | collective-permute-done | bytes 262176 | tf_op jit(solution)/shard_map/ppermute | solution.py:234
  75.1 2.4 %collective-permute-start.11 = (bf16[64,2048]{1,0:T(8,128)(2,1)S(1)}, bf16[64,2048]{1,0:T(8,128)(2,1)S(1)}, u32[]{:S(2)}, u32[]{:S(2)}) collective-permute-start(bf16[64,2048]{1,0:T(8,128)(2,1)S(1)} %collective-permute-done.9.refs_1_.refs_4_), channel_id=1, source_target_pairs={{0,16},{1,9},{2,18},{3,11},{4,20},{5,13},{6,22},{7,15},{8,24},{9,1... | collective-permute-start | bytes 786440 | tf_op jit(solution)/shard_map/ppermute | solution.py:234
  77.5 9.3 %gate_up.3 = (f32[2,64,2048]{2,1,0:T(8,128)S(1)}, f32[2,64,2048]{2,1,0:T(8,128)S(1)}, bf16[2,64,2048]{2,1,0:T(8,128)(2,1)S(1)}, bf16[2,64,2048]{2,1,0:T(8,128)(2,1)S(1)}) custom-call(s32[9]{0:T(128)S(1)} %stack.33.place_ref, bf16[4,64,1024]{2,1,0:T(8,128)(2,1)S(1)} %join.3.own_ref, bf16[4,64,1024]{2,1,0:T(8,128)(2,1)S(1)} %collective-permute-done.20.other_ref, ...), custom_call_target="tpu_custom_call" | custom-call | flops 4294967296 | bytes 16777216 | tf_op jit(solution)/shard_map/gate_up/pallas_call | solution.py:73
  86.8 2.0 %collective-permute-start.22 = (bf16[2,64,2048]{2,1,0:T(8,128)(2,1)S(1)}, bf16[2,64,2048]{2,1,0:T(8,128)(2,1)S(1)}, u32[]{:S(2)}, u32[]{:S(2)}) collective-permute-start(bf16[2,64,2048]{2,1,0:T(8,128)(2,1)S(1)} %get-tuple-element.32), channel_id=1, source_target_pairs={{0,8},{1,9},{2,10},{3,11},{4,12},{5,13},{6,14},{7,15},{8,0},{9,1},... | collective-permute-start | bytes 1572872 | tf_op jit(solution)/shard_map/ppermute | solution.py:234
  88.8 6.2 %down.2 = (f32[4,32,2048]{2,1,0:T(8,128)S(1)}, bf16[4,32,2048]{2,1,0:T(8,128)(2,1)S(1)}) custom-call(s32[9]{0:T(128)S(1)} %stack.33.place_ref, bf16[64,2048]{1,0:T(8,128)(2,1)S(1)} %hidden.2.refs_0_, bf16[64,2048]{1,0:T(8,128)(2,1)S(1)} %collective-permute-done.9.refs_1_.refs_4_, bf16[64,2048]{1,0:T(8,128)(2,1)S(1)} %collective-permute-done.10.refs_2_, ...), custom_call_target="tpu_custom_call" | custom-call | flops 2147483648 | bytes 8388608 | tf_op jit(solution)/shard_map/down/pallas_call | solution.py:170
  95.2 3.4 %collective-permute-done.21.refs_1_ = bf16[2,64,2048]{2,1,0:T(8,128)(2,1)S(1)} collective-permute-done((bf16[2,64,2048]{2,1,0:T(8,128)(2,1)S(1)}, bf16[2,64,2048]{2,1,0:T(8,128)(2,1)S(1)}, u32[]{:S(2)}, u32[]{:S(2)}) %collective-permute-start.21) | collective-permute-done | bytes 524320 | tf_op jit(solution)/shard_map/ppermute | solution.py:234
  98.5 1.2 collective-permute-done.22.refs_3_.refs_4_
  100.2 0.6 collective-permute-start.24
  100.8 5.4 %collective-permute-done.23.refs_2_ = bf16[1,64,2048]{2,1,0:T(8,128)(2,1)S(1)} collective-permute-done((bf16[1,64,2048]{2,1,0:T(8,128)(2,1)S(1)}, bf16[1,64,2048]{2,1,0:T(8,128)(2,1)S(1)}, u32[]{:S(2)}, u32[]{:S(2)}) %collective-permute-start.23) | collective-permute-done | bytes 262176 | tf_op jit(solution)/shard_map/ppermute | solution.py:234
  106.6 0.5 hidden.3.refs_0_
  107.1 1.7 %collective-permute-start.25 = (bf16[64,2048]{1,0:T(8,128)(2,1)S(1)}, bf16[64,2048]{1,0:T(8,128)(2,1)S(1)}, u32[]{:S(2)}, u32[]{:S(2)}) collective-permute-start(bf16[64,2048]{1,0:T(8,128)(2,1)S(1)} %hidden.3.refs_0_), channel_id=1, source_target_pairs={{0,8},{1,17},{2,10},{3,19},{4,12},{5,21},{6,14},{7,23},{8,0},{9,25... | collective-permute-start | bytes 786440 | tf_op jit(solution)/shard_map/ppermute | solution.py:234
  108.8 0.6 collective-permute-start.26
  109.4 5.8 %collective-permute-done.25.refs_1_ = bf16[64,2048]{1,0:T(8,128)(2,1)S(1)} collective-permute-done((bf16[64,2048]{1,0:T(8,128)(2,1)S(1)}, bf16[64,2048]{1,0:T(8,128)(2,1)S(1)}, u32[]{:S(2)}, u32[]{:S(2)}) %collective-permute-start.25) | collective-permute-done | bytes 262176 | tf_op jit(solution)/shard_map/ppermute | solution.py:234
  115.5 4.1 %collective-permute-start.15 = (bf16[32,2048]{1,0:T(8,128)(2,1)S(1)}, bf16[32,2048]{1,0:T(8,128)(2,1)S(1)}, u32[]{:S(2)}, u32[]{:S(2)}) collective-permute-start(bf16[32,2048]{1,0:T(8,128)(2,1)S(1)} %get-tuple-element.40.refs_8_), channel_id=1, source_target_pairs={{0,6},{1,7},{2,4},{3,5},{4,2},{5,3},{6,0},{7,1},{8,14},{9,15},{10,... | collective-permute-start | bytes 393224 | tf_op jit(solution)/shard_map/ppermute | solution.py:234
  119.6 0.6 collective-permute-start.13
  120.2 2.5 %collective-permute-done.15.refs_8_ = bf16[32,2048]{1,0:T(8,128)(2,1)S(1)} collective-permute-done((bf16[32,2048]{1,0:T(8,128)(2,1)S(1)}, bf16[32,2048]{1,0:T(8,128)(2,1)S(1)}, u32[]{:S(2)}, u32[]{:S(2)}) %collective-permute-start.15) | collective-permute-done | bytes 131104 | tf_op jit(solution)/shard_map/ppermute | solution.py:234
  122.6 3.1 %collective-permute-done.14.refs_7_ = bf16[32,2048]{1,0:T(8,128)(2,1)S(1)} collective-permute-done((bf16[32,2048]{1,0:T(8,128)(2,1)S(1)}, bf16[32,2048]{1,0:T(8,128)(2,1)S(1)}, u32[]{:S(2)}, u32[]{:S(2)}) %collective-permute-start.14) | collective-permute-done | bytes 131104 | tf_op jit(solution)/shard_map/ppermute | solution.py:234
  126.0 6.2 %down.3 = (f32[4,32,2048]{2,1,0:T(8,128)S(1)}, bf16[4,32,2048]{2,1,0:T(8,128)(2,1)S(1)}) custom-call(s32[9]{0:T(128)S(1)} %stack.33.place_ref, bf16[64,2048]{1,0:T(8,128)(2,1)S(1)} %hidden.3.refs_0_, bf16[64,2048]{1,0:T(8,128)(2,1)S(1)} %collective-permute-done.25.refs_1_, bf16[64,2048]{1,0:T(8,128)(2,1)S(1)} %collective-permute-done.26.refs_2_, ...), custom_call_target="tpu_custom_call" | custom-call | flops 2147483648 | bytes 8388608 | tf_op jit(solution)/shard_map/down/pallas_call | solution.py:170
  132.3 1.9 %collective-permute-done.28 = bf16[4,32,2048]{2,1,0:T(8,128)(2,1)S(1)} collective-permute-done((bf16[4,32,2048]{2,1,0:T(8,128)(2,1)S(1)}, bf16[4,32,2048]{2,1,0:T(8,128)(2,1)S(1)}, u32[]{:S(2)}, u32[]{:S(2)}) %collective-permute-start.28) | collective-permute-done | bytes 524320 | tf_op jit(solution)/shard_map/ppermute | solution.py:234
  134.3 1.5 %collective-permute-start.29 = (bf16[32,2048]{1,0:T(8,128)(2,1)S(1)}, bf16[32,2048]{1,0:T(8,128)(2,1)S(1)}, u32[]{:S(2)}, u32[]{:S(2)}) collective-permute-start(bf16[32,2048]{1,0:T(8,128)(2,1)S(1)} %get-tuple-element.37), channel_id=1, source_target_pairs={{0,2},{1,3},{2,0},{3,1},{4,6},{5,7},{6,4},{7,5},{8,10},{9,11},{10,... | collective-permute-start | bytes 393224 | tf_op jit(solution)/shard_map/ppermute | solution.py:234
  135.8 1.5 %collective-permute-start.31 = (bf16[32,2048]{1,0:T(8,128)(2,1)S(1)}, bf16[32,2048]{1,0:T(8,128)(2,1)S(1)}, u32[]{:S(2)}, u32[]{:S(2)}) collective-permute-start(bf16[32,2048]{1,0:T(8,128)(2,1)S(1)} %get-tuple-element.38), channel_id=1, source_target_pairs={{0,6},{1,7},{2,4},{3,5},{4,2},{5,3},{6,0},{7,1},{8,14},{9,15},{10,... | collective-permute-start | bytes 393224 | tf_op jit(solution)/shard_map/ppermute | solution.py:234
  137.3 0.5 collective-permute-start.30
  137.9 2.0 %collective-permute-done.29 = bf16[32,2048]{1,0:T(8,128)(2,1)S(1)} collective-permute-done((bf16[32,2048]{1,0:T(8,128)(2,1)S(1)}, bf16[32,2048]{1,0:T(8,128)(2,1)S(1)}, u32[]{:S(2)}, u32[]{:S(2)}) %collective-permute-start.29) | collective-permute-done | bytes 131104 | tf_op jit(solution)/shard_map/ppermute | solution.py:234
  139.9 4.6 %collective-permute-done.31 = bf16[32,2048]{1,0:T(8,128)(2,1)S(1)} collective-permute-done((bf16[32,2048]{1,0:T(8,128)(2,1)S(1)}, bf16[32,2048]{1,0:T(8,128)(2,1)S(1)}, u32[]{:S(2)}, u32[]{:S(2)}) %collective-permute-start.31) | collective-permute-done | bytes 131104 | tf_op jit(solution)/shard_map/ppermute | solution.py:234
  144.5 5.0 %collective-permute-done.30 = bf16[32,2048]{1,0:T(8,128)(2,1)S(1)} collective-permute-done((bf16[32,2048]{1,0:T(8,128)(2,1)S(1)}, bf16[32,2048]{1,0:T(8,128)(2,1)S(1)}, u32[]{:S(2)}, u32[]{:S(2)}) %collective-permute-start.30) | collective-permute-done | bytes 131104 | tf_op jit(solution)/shard_map/ppermute | solution.py:234
  149.6 0.7 pad_maximum_fusion
  (43 shorter events, 3.6 us)
Async XLA Ops:
  1.0 9.1 %collective-permute-start.3 = (bf16[64,1024]{1,0:T(8,128)(2,1)S(1)}, bf16[64,1024]{1,0:T(8,128)(2,1)S(1)}, u32[]{:S(2)}, u32[]{:S(2)}) collective-permute-start(bf16[64,1024]{1,0:T(8,128)(2,1)S(1)} %bitcast.62), channel_id=1, source_target_pairs={{0,6},{1,7},{2,14},{3,15},{4,22},{5,23},{6,30},{7,31},{8,4},{9,5},... | collective-permute-start | bytes 393224 | tf_op jit(solution)/shard_map/ppermute | solution.py:234
  6.1 6.8 %collective-permute-start.2 = (bf16[64,1024]{1,0:T(8,128)(2,1)S(1)}, bf16[64,1024]{1,0:T(8,128)(2,1)S(1)}, u32[]{:S(2)}, u32[]{:S(2)}) collective-permute-start(bf16[64,1024]{1,0:T(8,128)(2,1)S(1)} %bitcast.63), channel_id=1, source_target_pairs={{0,4},{1,5},{2,12},{3,13},{4,20},{5,21},{6,28},{7,29},{8,6},{9,7},... | collective-permute-start | bytes 393224 | tf_op jit(solution)/shard_map/ppermute | solution.py:234
  7.6 7.0 %collective-permute-start.1 = (bf16[64,1024]{1,0:T(8,128)(2,1)S(1)}, bf16[64,1024]{1,0:T(8,128)(2,1)S(1)}, u32[]{:S(2)}, u32[]{:S(2)}) collective-permute-start(bf16[64,1024]{1,0:T(8,128)(2,1)S(1)} %bitcast.64), channel_id=1, source_target_pairs={{0,2},{1,3},{2,10},{3,11},{4,18},{5,19},{6,26},{7,27},{8,0},{9,1},... | collective-permute-start | bytes 393224 | tf_op jit(solution)/shard_map/ppermute | solution.py:234
  8.1 6.5 %collective-permute-start = (bf16[64,1024]{1,0:T(8,128)(2,1)S(1)}, bf16[64,1024]{1,0:T(8,128)(2,1)S(1)}, u32[]{:S(2)}, u32[]{:S(2)}) collective-permute-start(bf16[64,1024]{1,0:T(8,128)(2,1)S(1)} %bitcast.65), channel_id=1, source_target_pairs={{0,0},{1,1},{2,8},{3,9},{4,16},{5,17},{6,24},{7,25},{8,2},{9,3},{1... | collective-permute-start | bytes 393224 | tf_op jit(solution)/shard_map/ppermute | solution.py:234
  14.6 2.0 %collective-permute-start.4 = (bf16[4,64,1024]{2,1,0:T(8,128)(2,1)S(1)}, bf16[4,64,1024]{2,1,0:T(8,128)(2,1)S(1)}, u32[]{:S(2)}, u32[]{:S(2)}) collective-permute-start(bf16[4,64,1024]{2,1,0:T(8,128)(2,1)S(1)} %join.2.own_ref), channel_id=1, source_target_pairs={{0,1},{1,0},{2,3},{3,2},{4,5},{5,4},{6,7},{7,6},{8,9},{9,8},{10,11... | collective-permute-start | bytes 1572872 | tf_op jit(solution)/shard_map/ppermute | solution.py:234
  25.9 43.1 %copy-start = (s32[16,16]{1,0:T(8,128)S(1)}, s32[16,16]{1,0:T(8,128)}, u32[]{:S(2)}) copy-start(s32[16,16]{1,0:T(8,128)} %param.13) | copy-start | bytes 3076
  25.9 24.5 %collective-permute-start.6 = (bf16[2,64,2048]{2,1,0:T(8,128)(2,1)S(1)}, bf16[2,64,2048]{2,1,0:T(8,128)(2,1)S(1)}, u32[]{:S(2)}, u32[]{:S(2)}) collective-permute-start(bf16[2,64,2048]{2,1,0:T(8,128)(2,1)S(1)} %get-tuple-element.24), channel_id=1, source_target_pairs={{0,8},{1,9},{2,10},{3,11},{4,12},{5,13},{6,14},{7,15},{8,0},{9,1},... | collective-permute-start | bytes 1572872 | tf_op jit(solution)/shard_map/ppermute | solution.py:234
  34.9 16.2 %collective-permute-start.5 = (bf16[2,64,2048]{2,1,0:T(8,128)(2,1)S(1)}, bf16[2,64,2048]{2,1,0:T(8,128)(2,1)S(1)}, u32[]{:S(2)}, u32[]{:S(2)}) collective-permute-start(bf16[2,64,2048]{2,1,0:T(8,128)(2,1)S(1)} %get-tuple-element.22.refs_4_), channel_id=1, source_target_pairs={{0,16},{1,17},{2,18},{3,19},{4,20},{5,21},{6,22},{7,23},{8,24},{9,... | collective-permute-start | bytes 1572872 | tf_op jit(solution)/shard_map/ppermute | solution.py:234
  35.2 19.9 %collective-permute-start.19 = (bf16[64,1024]{1,0:T(8,128)(2,1)S(1)}, bf16[64,1024]{1,0:T(8,128)(2,1)S(1)}, u32[]{:S(2)}, u32[]{:S(2)}) collective-permute-start(bf16[64,1024]{1,0:T(8,128)(2,1)S(1)} %bitcast.58), channel_id=1, source_target_pairs={{0,6},{1,7},{2,14},{3,15},{4,22},{5,23},{6,30},{7,31},{8,4},{9,5},... | collective-permute-start | bytes 393224 | tf_op jit(solution)/shard_map/ppermute | solution.py:234
  37.2 23.1 %collective-permute-start.18 = (bf16[64,1024]{1,0:T(8,128)(2,1)S(1)}, bf16[64,1024]{1,0:T(8,128)(2,1)S(1)}, u32[]{:S(2)}, u32[]{:S(2)}) collective-permute-start(bf16[64,1024]{1,0:T(8,128)(2,1)S(1)} %bitcast.59), channel_id=1, source_target_pairs={{0,4},{1,5},{2,12},{3,13},{4,20},{5,21},{6,28},{7,29},{8,6},{9,7},... | collective-permute-start | bytes 393224 | tf_op jit(solution)/shard_map/ppermute | solution.py:234
  39.2 21.1 %collective-permute-start.17 = (bf16[64,1024]{1,0:T(8,128)(2,1)S(1)}, bf16[64,1024]{1,0:T(8,128)(2,1)S(1)}, u32[]{:S(2)}, u32[]{:S(2)}) collective-permute-start(bf16[64,1024]{1,0:T(8,128)(2,1)S(1)} %bitcast.60), channel_id=1, source_target_pairs={{0,2},{1,3},{2,10},{3,11},{4,18},{5,19},{6,26},{7,27},{8,0},{9,1},... | collective-permute-start | bytes 393224 | tf_op jit(solution)/shard_map/ppermute | solution.py:234
  50.4 9.8 %collective-permute-start.16 = (bf16[64,1024]{1,0:T(8,128)(2,1)S(1)}, bf16[64,1024]{1,0:T(8,128)(2,1)S(1)}, u32[]{:S(2)}, u32[]{:S(2)}) collective-permute-start(bf16[64,1024]{1,0:T(8,128)(2,1)S(1)} %bitcast.61), channel_id=1, source_target_pairs={{0,0},{1,1},{2,8},{3,9},{4,16},{5,17},{6,24},{7,25},{8,2},{9,3},{1... | collective-permute-start | bytes 393224 | tf_op jit(solution)/shard_map/ppermute | solution.py:234
  51.2 12.4 %collective-permute-start.7 = (bf16[1,64,2048]{2,1,0:T(8,128)(2,1)S(1)}, bf16[1,64,2048]{2,1,0:T(8,128)(2,1)S(1)}, u32[]{:S(2)}, u32[]{:S(2)}) collective-permute-start(bf16[1,64,2048]{2,1,0:T(8,128)(2,1)S(1)} %get-tuple-element.25), channel_id=1, source_target_pairs={{0,8},{1,9},{2,10},{3,11},{4,12},{5,13},{6,14},{7,15},{8,0},{9,1},... | collective-permute-start | bytes 786440 | tf_op jit(solution)/shard_map/ppermute | solution.py:234
  55.1 10.9 %collective-permute-start.8 = (bf16[1,64,2048]{2,1,0:T(8,128)(2,1)S(1)}, bf16[1,64,2048]{2,1,0:T(8,128)(2,1)S(1)}, u32[]{:S(2)}, u32[]{:S(2)}) collective-permute-start(bf16[1,64,2048]{2,1,0:T(8,128)(2,1)S(1)} %get-tuple-element.26), channel_id=1, source_target_pairs={{0,16},{1,17},{2,18},{3,19},{4,20},{5,21},{6,22},{7,23},{8,24},{9,... | collective-permute-start | bytes 786440 | tf_op jit(solution)/shard_map/ppermute | solution.py:234
  60.3 17.2 %collective-permute-start.20 = (bf16[4,64,1024]{2,1,0:T(8,128)(2,1)S(1)}, bf16[4,64,1024]{2,1,0:T(8,128)(2,1)S(1)}, u32[]{:S(2)}, u32[]{:S(2)}) collective-permute-start(bf16[4,64,1024]{2,1,0:T(8,128)(2,1)S(1)} %join.3.own_ref), channel_id=1, source_target_pairs={{0,1},{1,0},{2,3},{3,2},{4,5},{5,4},{6,7},{7,6},{8,9},{9,8},{10,11... | collective-permute-start | bytes 1572872 | tf_op jit(solution)/shard_map/ppermute | solution.py:234
  66.5 8.6 %collective-permute-start.9 = (bf16[64,2048]{1,0:T(8,128)(2,1)S(1)}, bf16[64,2048]{1,0:T(8,128)(2,1)S(1)}, u32[]{:S(2)}, u32[]{:S(2)}) collective-permute-start(bf16[64,2048]{1,0:T(8,128)(2,1)S(1)} %hidden.2.refs_0_), channel_id=1, source_target_pairs={{0,8},{1,17},{2,10},{3,19},{4,12},{5,21},{6,14},{7,23},{8,0},{9,25... | collective-permute-start | bytes 786440 | tf_op jit(solution)/shard_map/ppermute | solution.py:234
  69.1 19.7 %collective-permute-start.10 = (bf16[64,2048]{1,0:T(8,128)(2,1)S(1)}, bf16[64,2048]{1,0:T(8,128)(2,1)S(1)}, u32[]{:S(2)}, u32[]{:S(2)}) collective-permute-start(bf16[64,2048]{1,0:T(8,128)(2,1)S(1)} %hidden.2.refs_0_), channel_id=1, source_target_pairs={{0,16},{1,9},{2,18},{3,11},{4,20},{5,13},{6,22},{7,15},{8,24},{9,1... | collective-permute-start | bytes 786440 | tf_op jit(solution)/shard_map/ppermute | solution.py:234
  75.1 13.7 %collective-permute-start.11 = (bf16[64,2048]{1,0:T(8,128)(2,1)S(1)}, bf16[64,2048]{1,0:T(8,128)(2,1)S(1)}, u32[]{:S(2)}, u32[]{:S(2)}) collective-permute-start(bf16[64,2048]{1,0:T(8,128)(2,1)S(1)} %collective-permute-done.9.refs_1_.refs_4_), channel_id=1, source_target_pairs={{0,16},{1,9},{2,18},{3,11},{4,20},{5,13},{6,22},{7,15},{8,24},{9,1... | collective-permute-start | bytes 786440 | tf_op jit(solution)/shard_map/ppermute | solution.py:234
  86.8 11.8 %collective-permute-start.21 = (bf16[2,64,2048]{2,1,0:T(8,128)(2,1)S(1)}, bf16[2,64,2048]{2,1,0:T(8,128)(2,1)S(1)}, u32[]{:S(2)}, u32[]{:S(2)}) collective-permute-start(bf16[2,64,2048]{2,1,0:T(8,128)(2,1)S(1)} %get-tuple-element.30), channel_id=1, source_target_pairs={{0,16},{1,17},{2,18},{3,19},{4,20},{5,21},{6,22},{7,23},{8,24},{9,... | collective-permute-start | bytes 1572872 | tf_op jit(solution)/shard_map/ppermute | solution.py:234
  86.8 12.9 %collective-permute-start.22 = (bf16[2,64,2048]{2,1,0:T(8,128)(2,1)S(1)}, bf16[2,64,2048]{2,1,0:T(8,128)(2,1)S(1)}, u32[]{:S(2)}, u32[]{:S(2)}) collective-permute-start(bf16[2,64,2048]{2,1,0:T(8,128)(2,1)S(1)} %get-tuple-element.32), channel_id=1, source_target_pairs={{0,8},{1,9},{2,10},{3,11},{4,12},{5,13},{6,14},{7,15},{8,0},{9,1},... | collective-permute-start | bytes 1572872 | tf_op jit(solution)/shard_map/ppermute | solution.py:234
  95.1 5.6 %collective-permute-start.12 = (bf16[4,32,2048]{2,1,0:T(8,128)(2,1)S(1)}, bf16[4,32,2048]{2,1,0:T(8,128)(2,1)S(1)}, u32[]{:S(2)}, u32[]{:S(2)}) collective-permute-start(bf16[4,32,2048]{2,1,0:T(8,128)(2,1)S(1)} %get-tuple-element.28), channel_id=1, source_target_pairs={{0,1},{1,0},{2,3},{3,2},{4,5},{5,4},{6,7},{7,6},{8,9},{9,8},{10,11... | collective-permute-start | bytes 1572872 | tf_op jit(solution)/shard_map/ppermute | solution.py:234
  99.8 6.4 %collective-permute-start.23 = (bf16[1,64,2048]{2,1,0:T(8,128)(2,1)S(1)}, bf16[1,64,2048]{2,1,0:T(8,128)(2,1)S(1)}, u32[]{:S(2)}, u32[]{:S(2)}) collective-permute-start(bf16[1,64,2048]{2,1,0:T(8,128)(2,1)S(1)} %get-tuple-element.33), channel_id=1, source_target_pairs={{0,8},{1,9},{2,10},{3,11},{4,12},{5,13},{6,14},{7,15},{8,0},{9,1},... | collective-permute-start | bytes 786440 | tf_op jit(solution)/shard_map/ppermute | solution.py:234
  100.2 6.4 %collective-permute-start.24 = (bf16[1,64,2048]{2,1,0:T(8,128)(2,1)S(1)}, bf16[1,64,2048]{2,1,0:T(8,128)(2,1)S(1)}, u32[]{:S(2)}, u32[]{:S(2)}) collective-permute-start(bf16[1,64,2048]{2,1,0:T(8,128)(2,1)S(1)} %get-tuple-element.34), channel_id=1, source_target_pairs={{0,16},{1,17},{2,18},{3,19},{4,20},{5,21},{6,22},{7,23},{8,24},{9,... | collective-permute-start | bytes 786440 | tf_op jit(solution)/shard_map/ppermute | solution.py:234
  107.1 8.1 %collective-permute-start.25 = (bf16[64,2048]{1,0:T(8,128)(2,1)S(1)}, bf16[64,2048]{1,0:T(8,128)(2,1)S(1)}, u32[]{:S(2)}, u32[]{:S(2)}) collective-permute-start(bf16[64,2048]{1,0:T(8,128)(2,1)S(1)} %hidden.3.refs_0_), channel_id=1, source_target_pairs={{0,8},{1,17},{2,10},{3,19},{4,12},{5,21},{6,14},{7,23},{8,0},{9,25... | collective-permute-start | bytes 786440 | tf_op jit(solution)/shard_map/ppermute | solution.py:234
  108.8 17.1 %collective-permute-start.26 = (bf16[64,2048]{1,0:T(8,128)(2,1)S(1)}, bf16[64,2048]{1,0:T(8,128)(2,1)S(1)}, u32[]{:S(2)}, u32[]{:S(2)}) collective-permute-start(bf16[64,2048]{1,0:T(8,128)(2,1)S(1)} %hidden.3.refs_0_), channel_id=1, source_target_pairs={{0,16},{1,9},{2,18},{3,11},{4,20},{5,13},{6,22},{7,15},{8,24},{9,1... | collective-permute-start | bytes 786440 | tf_op jit(solution)/shard_map/ppermute | solution.py:234
  115.2 10.8 %collective-permute-start.27 = (bf16[64,2048]{1,0:T(8,128)(2,1)S(1)}, bf16[64,2048]{1,0:T(8,128)(2,1)S(1)}, u32[]{:S(2)}, u32[]{:S(2)}) collective-permute-start(bf16[64,2048]{1,0:T(8,128)(2,1)S(1)} %collective-permute-done.25.refs_1_), channel_id=1, source_target_pairs={{0,16},{1,9},{2,18},{3,11},{4,20},{5,13},{6,22},{7,15},{8,24},{9,1... | collective-permute-start | bytes 786440 | tf_op jit(solution)/shard_map/ppermute | solution.py:234
  115.5 7.2 %collective-permute-start.15 = (bf16[32,2048]{1,0:T(8,128)(2,1)S(1)}, bf16[32,2048]{1,0:T(8,128)(2,1)S(1)}, u32[]{:S(2)}, u32[]{:S(2)}) collective-permute-start(bf16[32,2048]{1,0:T(8,128)(2,1)S(1)} %get-tuple-element.40.refs_8_), channel_id=1, source_target_pairs={{0,6},{1,7},{2,4},{3,5},{4,2},{5,3},{6,0},{7,1},{8,14},{9,15},{10,... | collective-permute-start | bytes 393224 | tf_op jit(solution)/shard_map/ppermute | solution.py:234
  119.6 6.2 %collective-permute-start.14 = (bf16[32,2048]{1,0:T(8,128)(2,1)S(1)}, bf16[32,2048]{1,0:T(8,128)(2,1)S(1)}, u32[]{:S(2)}, u32[]{:S(2)}) collective-permute-start(bf16[32,2048]{1,0:T(8,128)(2,1)S(1)} %get-tuple-element.41.refs_7_), channel_id=1, source_target_pairs={{0,4},{1,5},{2,6},{3,7},{4,0},{5,1},{6,2},{7,3},{8,12},{9,13},{10,... | collective-permute-start | bytes 393224 | tf_op jit(solution)/shard_map/ppermute | solution.py:234
  119.6 6.4 %collective-permute-start.13 = (bf16[32,2048]{1,0:T(8,128)(2,1)S(1)}, bf16[32,2048]{1,0:T(8,128)(2,1)S(1)}, u32[]{:S(2)}, u32[]{:S(2)}) collective-permute-start(bf16[32,2048]{1,0:T(8,128)(2,1)S(1)} %get-tuple-element.42.refs_6_), channel_id=1, source_target_pairs={{0,2},{1,3},{2,0},{3,1},{4,6},{5,7},{6,4},{7,5},{8,10},{9,11},{10,... | collective-permute-start | bytes 393224 | tf_op jit(solution)/shard_map/ppermute | solution.py:234
  132.2 2.0 %collective-permute-start.28 = (bf16[4,32,2048]{2,1,0:T(8,128)(2,1)S(1)}, bf16[4,32,2048]{2,1,0:T(8,128)(2,1)S(1)}, u32[]{:S(2)}, u32[]{:S(2)}) collective-permute-start(bf16[4,32,2048]{2,1,0:T(8,128)(2,1)S(1)} %get-tuple-element.36), channel_id=1, source_target_pairs={{0,1},{1,0},{2,3},{3,2},{4,5},{5,4},{6,7},{7,6},{8,9},{9,8},{10,11... | collective-permute-start | bytes 1572872 | tf_op jit(solution)/shard_map/ppermute | solution.py:234
  134.3 5.6 %collective-permute-start.29 = (bf16[32,2048]{1,0:T(8,128)(2,1)S(1)}, bf16[32,2048]{1,0:T(8,128)(2,1)S(1)}, u32[]{:S(2)}, u32[]{:S(2)}) collective-permute-start(bf16[32,2048]{1,0:T(8,128)(2,1)S(1)} %get-tuple-element.37), channel_id=1, source_target_pairs={{0,2},{1,3},{2,0},{3,1},{4,6},{5,7},{6,4},{7,5},{8,10},{9,11},{10,... | collective-permute-start | bytes 393224 | tf_op jit(solution)/shard_map/ppermute | solution.py:234
  135.8 8.7 %collective-permute-start.31 = (bf16[32,2048]{1,0:T(8,128)(2,1)S(1)}, bf16[32,2048]{1,0:T(8,128)(2,1)S(1)}, u32[]{:S(2)}, u32[]{:S(2)}) collective-permute-start(bf16[32,2048]{1,0:T(8,128)(2,1)S(1)} %get-tuple-element.38), channel_id=1, source_target_pairs={{0,6},{1,7},{2,4},{3,5},{4,2},{5,3},{6,0},{7,1},{8,14},{9,15},{10,... | collective-permute-start | bytes 393224 | tf_op jit(solution)/shard_map/ppermute | solution.py:234
  137.3 12.2 %collective-permute-start.30 = (bf16[32,2048]{1,0:T(8,128)(2,1)S(1)}, bf16[32,2048]{1,0:T(8,128)(2,1)S(1)}, u32[]{:S(2)}, u32[]{:S(2)}) collective-permute-start(bf16[32,2048]{1,0:T(8,128)(2,1)S(1)} %get-tuple-element.39), channel_id=1, source_target_pairs={{0,4},{1,5},{2,6},{3,7},{4,0},{5,1},{6,2},{7,3},{8,12},{9,13},{10,... | collective-permute-start | bytes 393224 | tf_op jit(solution)/shard_map/ppermute | solution.py:234

commit v5 on v4

--- a/solution.py
+++ b/solution.py
@@ -16,30 +16,24 @@
 def masked_product(x_ref, weight_ref, keep_ref):
     block_rows, width = keep_ref.shape
     side = weight_ref.shape[0] // block_rows
-    group = min(4, block_rows)
-    total = None
-    for first in range(0, block_rows, group):
-        strips = []
-        for i in range(first, first + group):
-            keep = jnp.broadcast_to(keep_ref[i : i + 1, :], (16, width)).astype(jnp.bfloat16)
-            block = weight_ref[i * side : (i + 1) * side, :].reshape(side // 16, 16, width)
-            strips.append((block * keep[None]).reshape(side, width))
-        term = jnp.dot(
-            x_ref[:, first * side : (first + group) * side],
-            jnp.concatenate(strips, axis=0),
-            preferred_element_type=jnp.float32,
-        )
-        total = term if total is None else total + term
-    return total
+    strips = []
+    for i in range(block_rows):
+        keep = jnp.broadcast_to(keep_ref[i : i + 1, :], (16, width)).astype(jnp.bfloat16)
+        block = weight_ref[i * side : (i + 1) * side, :].reshape(side // 16, 16, width)
+        strips.append((block * keep[None]).reshape(side, width))
+    return jnp.dot(x_ref[...], jnp.concatenate(strips, axis=0), preferred_element_type=jnp.float32)
 
 
 def widen(keep_mask, width):
     return jnp.repeat(keep_mask.astype(jnp.float32), width // keep_mask.shape[1], axis=1)
 
 
-def gate_up_kernel(n, place_ref, own_ref, other_ref, gate_ref, up_ref, gate_keep, up_keep, *refs):
-    outs, x = refs[:4], refs[4]
-    _, rows, half = own_ref.shape
+def gate_up_kernel(n, place_ref, *refs):
+    own, other = refs[:n], refs[n : 2 * n]
+    gate_ref, up_ref, gate_keep, up_keep = refs[2 * n : 2 * n + 4]
+    outs, x = refs[2 * n + 4 : 2 * n + 8], refs[2 * n + 8]
+    _, piece, half = own[0].shape
+    rows = 2 * piece
 
     @pl.when(pl.program_id(0) == 0)
     def _():
@@ -48,8 +42,8 @@
         others = pl.ds(pl.multiple_of((1 - core) * half, half), half)
         for k in range(n):
             at = pl.ds(pl.multiple_of(place_ref[1 + n + k] * rows, rows), rows)
-            x[at, mine] = own_ref[k]
-            x[at, others] = other_ref[k]
+            x[at, mine] = own[k][...].reshape(rows, half)
+            x[at, others] = other[k][...].reshape(rows, half)
 
     for which, (weight, keep) in enumerate(((gate_ref, gate_keep), (up_ref, up_keep))):
         product = masked_product(x, weight, keep)
@@ -62,11 +56,14 @@
                 outs[2 + which][p - n // 2] = term.astype(jnp.bfloat16)
 
 
-def gate_up(place, own, other, gate_weight, up_weight, gate_keep, up_keep):
-    n, rows, half = own.shape
+def gate_up(place, batch, own, other, gate_weight, up_weight, gate_keep, up_keep):
+    n = len(own)
+    _, whole, half = own[0].shape
+    piece = whole // BATCHES
+    rows = 2 * piece
     depth, width = gate_weight.shape
     tile = min(width, TILE)
-    whole = pl.BlockSpec((n, rows, half), lambda i, *_: (0, 0, 0))
+    part = pl.BlockSpec((2, piece, half), lambda i, *_: (0, batch, 0))
     strip = pl.BlockSpec((depth, tile), lambda i, *_: (0, i))
     mask = pl.BlockSpec((gate_keep.shape[0], tile), lambda i, *_: (0, i))
     out = pl.BlockSpec((n // 2, rows, tile), lambda i, *_: (0, 0, i))
@@ -75,7 +72,7 @@
         grid_spec=pltpu.PrefetchScalarGridSpec(
             num_scalar_prefetch=1,
             grid=(width // tile,),
-            in_specs=[whole, whole, strip, strip, mask, mask],
+            in_specs=[part] * (2 * n) + [strip, strip, mask, mask],
             out_specs=[out] * 4,
             scratch_shapes=[pltpu.VMEM((n * rows, depth), jnp.bfloat16)],
         ),
@@ -86,7 +83,7 @@
             flops=4 * n * rows * depth * width, bytes_accessed=4 * depth * width, transcendentals=0
         ),
         name="gate_up",
-    )(place, own, other, gate_weight, up_weight, gate_keep, up_keep)
+    )(place, *own, *other, gate_weight, up_weight, gate_keep, up_keep)
 
 
 def total_of(refs):
@@ -189,24 +186,6 @@
         ),
         name="down",
     )(place, *parts, weight, keep, *after)
-
-
-def join_kernel(n, *refs):
-    for k in range(n):
-        refs[-1][k] = refs[k][...]
-
-
-def join(blocks, after):
-    n = len(blocks)
-    spec = pl.BlockSpec(memory_space=pltpu.VMEM)
-    return pl.pallas_call(
-        functools.partial(join_kernel, n),
-        in_specs=[spec] * n + [pl.BlockSpec(memory_space=pl.ANY)] * len(after),
-        out_specs=spec,
-        out_shape=jax.ShapeDtypeStruct((n,) + blocks[0].shape, blocks[0].dtype),
-        compiler_params=pltpu.CompilerParams(vmem_limit_bytes=VMEM_BYTES),
-        name="join",
-    )(*blocks, *after)
 
 
 def mirror(p, n):
@@ -267,22 +246,17 @@
         return sums[0], [part.astype(jnp.bfloat16) for part in sums[1:]]
 
     rows, features = tokens.shape
-    piece = rows // (2 * BATCHES)
-    split = tokens.reshape(2, BATCHES, piece, features)
     gate_wide = widen(gate_keep, gate_weight.shape[1])
     up_wide = widen(up_keep, up_weight.shape[1])
     down_wide = widen(down_keep, down_weight.shape[1])
-    moved = []
-    for s in range(BATCHES):
-        block = split[:, s].reshape(2 * piece, features)
-        moved.append([send(block, lambda t, zz, c: (zz, t ^ k, c)) for k in range(n_z)])
-    sums, before_swap = [], []
-    for blocks in moved:
-        own = join(blocks, before_swap)
-        sums.append(gate_up(place, own, across_core(own), gate_weight, up_weight, gate_wide, up_wide))
-        before_swap = [sums[-1][2]]
+    moved = [send(tokens, lambda t, zz, c: (zz, t ^ k, c)) for k in range(n_z)]
+    swapped = [across_core(block) for block in moved]
+    own = [block.reshape(2, rows // 2, features) for block in moved]
+    other = [block.reshape(2, rows // 2, features) for block in swapped]
+    sums = [gate_up(place, s, own, other, gate_weight, up_weight, gate_wide, up_wide) for s in range(BATCHES)]
     out, before_add, before_hidden, before_down = [], [], [], []
-    for terms in sums:
+    for s, terms in enumerate(sums):
+        before_add += [later[2] for later in sums[s + 1 : s + 2]]
         parts = gather(activate(*halve(*terms, before_add), before_hidden))
         mine, theirs = down(place, parts, down_weight, down_wide, before_down)
         total, sent = combine(mine, theirs)

time: 151 us -> 146 us (0.967)
  starting transfers between devices: 52.3 us -> 45.4 us
  waiting for transfers between devices: 61.5 us -> 64.5 us
    ppermute x32 -> x30, starting transfers between devices: 52.3 us -> 45.4 us  [send(): return lax.ppermute(value, AXES, perm)]
    ppermute x32 -> x30, waiting for transfers between devices: 61.5 us -> 64.5 us  [send(): return lax.ppermute(value, AXES, perm)]
  transfers between devices with their start and end apart: 32 -> 30, of which waited for: 20 -> 20; matrix products, arithmetic and copies ran while one was open for 1% -> 1% of each run, Pallas kernels for 11% -> 11%
where the time goes in v5:
time: 146 us; the launch traced here: 145 us
  waiting for transfers between devices  64.5 us (44%)
  starting transfers between devices  45.4 us (31%)
  Pallas kernels  32.3 us (22%)
  other arithmetic  2.48 us (2%)
    ppermute x30, waiting for transfers between devices, send(): return lax.ppermute(value, AXES, perm)  64.5 us
    ppermute x30, starting transfers between devices, send(): return lax.ppermute(value, AXES, perm)  45.4 us
    pallas_call x2, Pallas kernels, gate_up(): pl.pallas_call(functools.partial(gate_up_kernel, n), grid_spec=pltpu.Pref...  18.7 us
    pallas_call x2, Pallas kernels, down(): pl.pallas_call(functools.partial(down_kernel, n), grid_spec=pltpu.Prefetc...  12.5 us
  transfers between devices with their start and end apart: 30, of which 20 were waited for; matrix products, arithmetic and copies ran while one was open for 1% of the time, Pallas kernels for 11%

profile of v5, /device:TPU:0, one launch (start us, length us, event | category | flops | bytes accessed | tf_op | source)
XLA Modules:
  0.0 145.4 jit_solution(9339151895997708255)
XLA Ops:
  0.0 1.6 %collective-permute-start = (bf16[128,1024]{1,0:T(8,128)(2,1)}, bf16[128,1024]{1,0:T(8,128)(2,1)S(1)}, u32[]{:S(2)}, u32[]{:S(2)}) collective-permute-start(bf16[128,1024]{1,0:T(8,128)(2,1)} %param.7), channel_id=1, source_target_pairs={{0,0},{1,1},{2,8},{3,9},{4,16},{5,17},{6,24},{7,25},{8,2},{9,3},{1... | collective-permute-start | bytes 786440 | tf_op jit(solution)/shard_map/ppermute | solution.py:213
  1.6 4.8 %collective-permute-start.1 = (bf16[128,1024]{1,0:T(8,128)(2,1)}, bf16[128,1024]{1,0:T(8,128)(2,1)S(1)}, u32[]{:S(2)}, u32[]{:S(2)}) collective-permute-start(bf16[128,1024]{1,0:T(8,128)(2,1)} %param.7), channel_id=1, source_target_pairs={{0,2},{1,3},{2,10},{3,11},{4,18},{5,19},{6,26},{7,27},{8,0},{9,1},... | collective-permute-start | bytes 786440 | tf_op jit(solution)/shard_map/ppermute | solution.py:213
  6.4 3.5 %collective-permute-start.2 = (bf16[128,1024]{1,0:T(8,128)(2,1)}, bf16[128,1024]{1,0:T(8,128)(2,1)S(1)}, u32[]{:S(2)}, u32[]{:S(2)}) collective-permute-start(bf16[128,1024]{1,0:T(8,128)(2,1)} %param.7), channel_id=1, source_target_pairs={{0,4},{1,5},{2,12},{3,13},{4,20},{5,21},{6,28},{7,29},{8,6},{9,7},... | collective-permute-start | bytes 786440 | tf_op jit(solution)/shard_map/ppermute | solution.py:213
  9.8 1.9 %collective-permute-start.3 = (bf16[128,1024]{1,0:T(8,128)(2,1)}, bf16[128,1024]{1,0:T(8,128)(2,1)S(1)}, u32[]{:S(2)}, u32[]{:S(2)}) collective-permute-start(bf16[128,1024]{1,0:T(8,128)(2,1)} %param.7), channel_id=1, source_target_pairs={{0,6},{1,7},{2,14},{3,15},{4,22},{5,23},{6,30},{7,31},{8,4},{9,5},... | collective-permute-start | bytes 786440 | tf_op jit(solution)/shard_map/ppermute | solution.py:213
  11.8 0.7 convert_element_type.98
  12.5 0.7 convert_element_type.99
  13.4 0.4 collective-permute-start.5
  13.8 8.4 %collective-permute-done.2 = bf16[128,1024]{1,0:T(8,128)(2,1)S(1)} collective-permute-done((bf16[128,1024]{1,0:T(8,128)(2,1)}, bf16[128,1024]{1,0:T(8,128)(2,1)S(1)}, u32[]{:S(2)}, u32[]{:S(2)}) %collective-permute-start.2) | collective-permute-done | bytes 262176 | tf_op jit(solution)/shard_map/ppermute | solution.py:213
  22.2 1.1 collective-permute-done.3
  23.7 1.1 collective-permute-done.7
  24.8 9.3 %gate_up.2 = (f32[2,64,2048]{2,1,0:T(8,128)S(1)}, f32[2,64,2048]{2,1,0:T(8,128)S(1)}, bf16[2,64,2048]{2,1,0:T(8,128)(2,1)S(1)}, bf16[2,64,2048]{2,1,0:T(8,128)(2,1)S(1)}) custom-call(s32[9]{0:T(128)S(1)} %stack.33.place_ref, bf16[2,64,1024]{2,1,0:T(8,128)(2,1)S(1)} %bitcast.55, bf16[2,64,1024]{2,1,0:T(8,128)(2,1)S(1)} %bitcast.57, ...), custom_call_target="tpu_custom_call" | custom-call | flops 4294967296 | bytes 16777216 | tf_op jit(solution)/shard_map/gate_up/pallas_call | solution.py:70
  34.1 13.0 %collective-permute-start.8 = (bf16[2,64,2048]{2,1,0:T(8,128)(2,1)S(1)}, bf16[2,64,2048]{2,1,0:T(8,128)(2,1)S(1)}, u32[]{:S(2)}, u32[]{:S(2)}) collective-permute-start(bf16[2,64,2048]{2,1,0:T(8,128)(2,1)S(1)} %get-tuple-element.22), channel_id=1, source_target_pairs={{0,16},{1,17},{2,18},{3,19},{4,20},{5,21},{6,22},{7,23},{8,24},{9,... | collective-permute-start | bytes 1572872 | tf_op jit(solution)/shard_map/ppermute | solution.py:213
  47.1 9.3 %gate_up.3 = (f32[2,64,2048]{2,1,0:T(8,128)S(1)}, f32[2,64,2048]{2,1,0:T(8,128)S(1)}, bf16[2,64,2048]{2,1,0:T(8,128)(2,1)S(1)}, bf16[2,64,2048]{2,1,0:T(8,128)(2,1)S(1)}) custom-call(s32[9]{0:T(128)S(1)} %stack.33.place_ref, bf16[2,64,1024]{2,1,0:T(8,128)(2,1)S(1)} %bitcast.56, bf16[2,64,1024]{2,1,0:T(8,128)(2,1)S(1)} %bitcast.58, ...), custom_call_target="tpu_custom_call" | custom-call | flops 4294967296 | bytes 16777216 | tf_op jit(solution)/shard_map/gate_up/pallas_call | solution.py:70
  56.4 2.9 %collective-permute-done.8.refs_1_ = bf16[2,64,2048]{2,1,0:T(8,128)(2,1)S(1)} collective-permute-done((bf16[2,64,2048]{2,1,0:T(8,128)(2,1)S(1)}, bf16[2,64,2048]{2,1,0:T(8,128)(2,1)S(1)}, u32[]{:S(2)}, u32[]{:S(2)}) %collective-permute-start.8) | collective-permute-done | bytes 524320 | tf_op jit(solution)/shard_map/ppermute | solution.py:213
  59.3 1.5 %collective-permute-done.9.refs_3_.refs_4_ = bf16[2,64,2048]{2,1,0:T(8,128)(2,1)S(1)} collective-permute-done((bf16[2,64,2048]{2,1,0:T(8,128)(2,1)S(1)}, bf16[2,64,2048]{2,1,0:T(8,128)(2,1)S(1)}, u32[]{:S(2)}, u32[]{:S(2)}) %collective-permute-start.9) | collective-permute-done | bytes 524320 | tf_op jit(solution)/shard_map/ppermute | solution.py:213
  60.9 0.3 collective-permute-start.10
  61.2 0.4 collective-permute-start.11
  61.6 6.5 %collective-permute-done.10.refs_2_ = bf16[1,64,2048]{2,1,0:T(8,128)(2,1)S(1)} collective-permute-done((bf16[1,64,2048]{2,1,0:T(8,128)(2,1)S(1)}, bf16[1,64,2048]{2,1,0:T(8,128)(2,1)S(1)}, u32[]{:S(2)}, u32[]{:S(2)}) %collective-permute-start.10) | collective-permute-done | bytes 262176 | tf_op jit(solution)/shard_map/ppermute | solution.py:213
  68.4 0.5 hidden.2.refs_0_
  69.0 1.5 %collective-permute-start.12 = (bf16[64,2048]{1,0:T(8,128)(2,1)S(1)}, bf16[64,2048]{1,0:T(8,128)(2,1)S(1)}, u32[]{:S(2)}, u32[]{:S(2)}) collective-permute-start(bf16[64,2048]{1,0:T(8,128)(2,1)S(1)} %hidden.2.refs_0_), channel_id=1, source_target_pairs={{0,8},{1,17},{2,10},{3,19},{4,12},{5,21},{6,14},{7,23},{8,0},{9,25... | collective-permute-start | bytes 786440 | tf_op jit(solution)/shard_map/ppermute | solution.py:213
  70.4 0.7 collective-permute-start.13
  71.1 6.0 %collective-permute-done.12.refs_1_.refs_4_ = bf16[64,2048]{1,0:T(8,128)(2,1)S(1)} collective-permute-done((bf16[64,2048]{1,0:T(8,128)(2,1)S(1)}, bf16[64,2048]{1,0:T(8,128)(2,1)S(1)}, u32[]{:S(2)}, u32[]{:S(2)}) %collective-permute-start.12) | collective-permute-done | bytes 262176 | tf_op jit(solution)/shard_map/ppermute | solution.py:213
  77.1 0.7 collective-permute-start.14
  78.0 1.4 collective-permute-start.19
  79.4 1.1 collective-permute-start.20
  80.5 4.8 %collective-permute-done.14.refs_3_ = bf16[64,2048]{1,0:T(8,128)(2,1)S(1)} collective-permute-done((bf16[64,2048]{1,0:T(8,128)(2,1)S(1)}, bf16[64,2048]{1,0:T(8,128)(2,1)S(1)}, u32[]{:S(2)}, u32[]{:S(2)}) %collective-permute-start.14) | collective-permute-done | bytes 262176 | tf_op jit(solution)/shard_map/ppermute | solution.py:213
  85.2 6.2 %down.2 = (f32[4,32,2048]{2,1,0:T(8,128)S(1)}, bf16[4,32,2048]{2,1,0:T(8,128)(2,1)S(1)}) custom-call(s32[9]{0:T(128)S(1)} %stack.33.place_ref, bf16[64,2048]{1,0:T(8,128)(2,1)S(1)} %hidden.2.refs_0_, bf16[64,2048]{1,0:T(8,128)(2,1)S(1)} %collective-permute-done.12.refs_1_.refs_4_, bf16[64,2048]{1,0:T(8,128)(2,1)S(1)} %collective-permute-done.13.refs_2_, ...), custom_call_target="tpu_custom_call" | custom-call | flops 2147483648 | bytes 8388608 | tf_op jit(solution)/shard_map/down/pallas_call | solution.py:167
  91.7 0.7 collective-permute-start.21
  92.4 0.8 collective-permute-start.22
  93.6 6.9 %collective-permute-done.21.refs_2_ = bf16[1,64,2048]{2,1,0:T(8,128)(2,1)S(1)} collective-permute-done((bf16[1,64,2048]{2,1,0:T(8,128)(2,1)S(1)}, bf16[1,64,2048]{2,1,0:T(8,128)(2,1)S(1)}, u32[]{:S(2)}, u32[]{:S(2)}) %collective-permute-start.21) | collective-permute-done | bytes 262176 | tf_op jit(solution)/shard_map/ppermute | solution.py:213
  100.5 0.3 collective-permute-done.22.refs_5_
  100.8 0.5 hidden.3.refs_0_
  101.3 1.5 %collective-permute-start.23 = (bf16[64,2048]{1,0:T(8,128)(2,1)S(1)}, bf16[64,2048]{1,0:T(8,128)(2,1)S(1)}, u32[]{:S(2)}, u32[]{:S(2)}) collective-permute-start(bf16[64,2048]{1,0:T(8,128)(2,1)S(1)} %hidden.3.refs_0_), channel_id=1, source_target_pairs={{0,8},{1,17},{2,10},{3,19},{4,12},{5,21},{6,14},{7,23},{8,0},{9,25... | collective-permute-start | bytes 786440 | tf_op jit(solution)/shard_map/ppermute | solution.py:213
  102.8 0.7 collective-permute-start.24
  103.5 6.3 %collective-permute-done.23.refs_1_ = bf16[64,2048]{1,0:T(8,128)(2,1)S(1)} collective-permute-done((bf16[64,2048]{1,0:T(8,128)(2,1)S(1)}, bf16[64,2048]{1,0:T(8,128)(2,1)S(1)}, u32[]{:S(2)}, u32[]{:S(2)}) %collective-permute-start.23) | collective-permute-done | bytes 262176 | tf_op jit(solution)/shard_map/ppermute | solution.py:213
  109.8 1.5 %collective-permute-start.25 = (bf16[64,2048]{1,0:T(8,128)(2,1)S(1)}, bf16[64,2048]{1,0:T(8,128)(2,1)S(1)}, u32[]{:S(2)}, u32[]{:S(2)}) collective-permute-start(bf16[64,2048]{1,0:T(8,128)(2,1)S(1)} %collective-permute-done.23.refs_1_), channel_id=1, source_target_pairs={{0,16},{1,9},{2,18},{3,11},{4,20},{5,13},{6,22},{7,15},{8,24},{9,1... | collective-permute-start | bytes 786440 | tf_op jit(solution)/shard_map/ppermute | solution.py:213
  111.3 0.5 collective-permute-start.16
  111.8 1.9 %collective-permute-start.17 = (bf16[32,2048]{1,0:T(8,128)(2,1)S(1)}, bf16[32,2048]{1,0:T(8,128)(2,1)S(1)}, u32[]{:S(2)}, u32[]{:S(2)}) collective-permute-start(bf16[32,2048]{1,0:T(8,128)(2,1)S(1)} %get-tuple-element.41.refs_7_), channel_id=1, source_target_pairs={{0,4},{1,5},{2,6},{3,7},{4,0},{5,1},{6,2},{7,3},{8,12},{9,13},{10,... | collective-permute-start | bytes 393224 | tf_op jit(solution)/shard_map/ppermute | solution.py:213
  113.7 2.0 %collective-permute-start.18 = (bf16[32,2048]{1,0:T(8,128)(2,1)S(1)}, bf16[32,2048]{1,0:T(8,128)(2,1)S(1)}, u32[]{:S(2)}, u32[]{:S(2)}) collective-permute-start(bf16[32,2048]{1,0:T(8,128)(2,1)S(1)} %get-tuple-element.40.refs_8_), channel_id=1, source_target_pairs={{0,6},{1,7},{2,4},{3,5},{4,2},{5,3},{6,0},{7,1},{8,14},{9,15},{10,... | collective-permute-start | bytes 393224 | tf_op jit(solution)/shard_map/ppermute | solution.py:213
  115.7 2.1 %collective-permute-done.16.refs_6_ = bf16[32,2048]{1,0:T(8,128)(2,1)S(1)} collective-permute-done((bf16[32,2048]{1,0:T(8,128)(2,1)S(1)}, bf16[32,2048]{1,0:T(8,128)(2,1)S(1)}, u32[]{:S(2)}, u32[]{:S(2)}) %collective-permute-start.16) | collective-permute-done | bytes 131104 | tf_op jit(solution)/shard_map/ppermute | solution.py:213
  117.8 3.7 %collective-permute-done.17.refs_7_ = bf16[32,2048]{1,0:T(8,128)(2,1)S(1)} collective-permute-done((bf16[32,2048]{1,0:T(8,128)(2,1)S(1)}, bf16[32,2048]{1,0:T(8,128)(2,1)S(1)}, u32[]{:S(2)}, u32[]{:S(2)}) %collective-permute-start.17) | collective-permute-done | bytes 131104 | tf_op jit(solution)/shard_map/ppermute | solution.py:213
  121.5 6.2 %down.3 = (f32[4,32,2048]{2,1,0:T(8,128)S(1)}, bf16[4,32,2048]{2,1,0:T(8,128)(2,1)S(1)}) custom-call(s32[9]{0:T(128)S(1)} %stack.33.place_ref, bf16[64,2048]{1,0:T(8,128)(2,1)S(1)} %hidden.3.refs_0_, bf16[64,2048]{1,0:T(8,128)(2,1)S(1)} %collective-permute-done.23.refs_1_, bf16[64,2048]{1,0:T(8,128)(2,1)S(1)} %collective-permute-done.24.refs_2_, ...), custom_call_target="tpu_custom_call" | custom-call | flops 2147483648 | bytes 8388608 | tf_op jit(solution)/shard_map/down/pallas_call | solution.py:167
  127.8 1.9 %collective-permute-done.26 = bf16[4,32,2048]{2,1,0:T(8,128)(2,1)S(1)} collective-permute-done((bf16[4,32,2048]{2,1,0:T(8,128)(2,1)S(1)}, bf16[4,32,2048]{2,1,0:T(8,128)(2,1)S(1)}, u32[]{:S(2)}, u32[]{:S(2)}) %collective-permute-start.26) | collective-permute-done | bytes 524320 | tf_op jit(solution)/shard_map/ppermute | solution.py:213
  129.8 2.0 %collective-permute-start.27 = (bf16[32,2048]{1,0:T(8,128)(2,1)S(1)}, bf16[32,2048]{1,0:T(8,128)(2,1)S(1)}, u32[]{:S(2)}, u32[]{:S(2)}) collective-permute-start(bf16[32,2048]{1,0:T(8,128)(2,1)S(1)} %get-tuple-element.37), channel_id=1, source_target_pairs={{0,2},{1,3},{2,0},{3,1},{4,6},{5,7},{6,4},{7,5},{8,10},{9,11},{10,... | collective-permute-start | bytes 393224 | tf_op jit(solution)/shard_map/ppermute | solution.py:213
  131.9 2.4 %collective-permute-start.29 = (bf16[32,2048]{1,0:T(8,128)(2,1)S(1)}, bf16[32,2048]{1,0:T(8,128)(2,1)S(1)}, u32[]{:S(2)}, u32[]{:S(2)}) collective-permute-start(bf16[32,2048]{1,0:T(8,128)(2,1)S(1)} %get-tuple-element.38), channel_id=1, source_target_pairs={{0,6},{1,7},{2,4},{3,5},{4,2},{5,3},{6,0},{7,1},{8,14},{9,15},{10,... | collective-permute-start | bytes 393224 | tf_op jit(solution)/shard_map/ppermute | solution.py:213
  134.4 2.5 %collective-permute-done.27 = bf16[32,2048]{1,0:T(8,128)(2,1)S(1)} collective-permute-done((bf16[32,2048]{1,0:T(8,128)(2,1)S(1)}, bf16[32,2048]{1,0:T(8,128)(2,1)S(1)}, u32[]{:S(2)}, u32[]{:S(2)}) %collective-permute-start.27) | collective-permute-done | bytes 131104 | tf_op jit(solution)/shard_map/ppermute | solution.py:213
  136.9 7.7 %collective-permute-done.28 = bf16[32,2048]{1,0:T(8,128)(2,1)S(1)} collective-permute-done((bf16[32,2048]{1,0:T(8,128)(2,1)S(1)}, bf16[32,2048]{1,0:T(8,128)(2,1)S(1)}, u32[]{:S(2)}, u32[]{:S(2)}) %collective-permute-start.28) | collective-permute-done | bytes 131104 | tf_op jit(solution)/shard_map/ppermute | solution.py:213
  144.7 0.7 pad_maximum_fusion
  (36 shorter events, 2.2 us)
Async XLA Ops:
  0.0 13.2 %collective-permute-start = (bf16[128,1024]{1,0:T(8,128)(2,1)}, bf16[128,1024]{1,0:T(8,128)(2,1)S(1)}, u32[]{:S(2)}, u32[]{:S(2)}) collective-permute-start(bf16[128,1024]{1,0:T(8,128)(2,1)} %param.7), channel_id=1, source_target_pairs={{0,0},{1,1},{2,8},{3,9},{4,16},{5,17},{6,24},{7,25},{8,2},{9,3},{1... | collective-permute-start | bytes 786440 | tf_op jit(solution)/shard_map/ppermute | solution.py:213
  1.6 11.8 %collective-permute-start.1 = (bf16[128,1024]{1,0:T(8,128)(2,1)}, bf16[128,1024]{1,0:T(8,128)(2,1)S(1)}, u32[]{:S(2)}, u32[]{:S(2)}) collective-permute-start(bf16[128,1024]{1,0:T(8,128)(2,1)} %param.7), channel_id=1, source_target_pairs={{0,2},{1,3},{2,10},{3,11},{4,18},{5,19},{6,26},{7,27},{8,0},{9,1},... | collective-permute-start | bytes 786440 | tf_op jit(solution)/shard_map/ppermute | solution.py:213
  6.4 15.8 %collective-permute-start.2 = (bf16[128,1024]{1,0:T(8,128)(2,1)}, bf16[128,1024]{1,0:T(8,128)(2,1)S(1)}, u32[]{:S(2)}, u32[]{:S(2)}) collective-permute-start(bf16[128,1024]{1,0:T(8,128)(2,1)} %param.7), channel_id=1, source_target_pairs={{0,4},{1,5},{2,12},{3,13},{4,20},{5,21},{6,28},{7,29},{8,6},{9,7},... | collective-permute-start | bytes 786440 | tf_op jit(solution)/shard_map/ppermute | solution.py:213
  9.8 13.4 %collective-permute-start.3 = (bf16[128,1024]{1,0:T(8,128)(2,1)}, bf16[128,1024]{1,0:T(8,128)(2,1)S(1)}, u32[]{:S(2)}, u32[]{:S(2)}) collective-permute-start(bf16[128,1024]{1,0:T(8,128)(2,1)} %param.7), channel_id=1, source_target_pairs={{0,6},{1,7},{2,14},{3,15},{4,22},{5,23},{6,30},{7,31},{8,4},{9,5},... | collective-permute-start | bytes 786440 | tf_op jit(solution)/shard_map/ppermute | solution.py:213
  13.2 10.3 %collective-permute-start.4 = (bf16[128,1024]{1,0:T(8,128)(2,1)S(1)}, bf16[128,1024]{1,0:T(8,128)(2,1)S(1)}, u32[]{:S(2)}, u32[]{:S(2)}) collective-permute-start(bf16[128,1024]{1,0:T(8,128)(2,1)S(1)} %collective-permute-done), channel_id=1, source_target_pairs={{0,1},{1,0},{2,3},{3,2},{4,5},{5,4},{6,7},{7,6},{8,9},{9,8},{10,11... | collective-permute-start | bytes 786440 | tf_op jit(solution)/shard_map/ppermute | solution.py:213
  13.4 10.1 %collective-permute-start.5 = (bf16[128,1024]{1,0:T(8,128)(2,1)S(1)}, bf16[128,1024]{1,0:T(8,128)(2,1)S(1)}, u32[]{:S(2)}, u32[]{:S(2)}) collective-permute-start(bf16[128,1024]{1,0:T(8,128)(2,1)S(1)} %collective-permute-done.1), channel_id=1, source_target_pairs={{0,1},{1,0},{2,3},{3,2},{4,5},{5,4},{6,7},{7,6},{8,9},{9,8},{10,11... | collective-permute-start | bytes 786440 | tf_op jit(solution)/shard_map/ppermute | solution.py:213
  22.2 1.5 %collective-permute-start.6 = (bf16[128,1024]{1,0:T(8,128)(2,1)S(1)}, bf16[128,1024]{1,0:T(8,128)(2,1)S(1)}, u32[]{:S(2)}, u32[]{:S(2)}) collective-permute-start(bf16[128,1024]{1,0:T(8,128)(2,1)S(1)} %collective-permute-done.2), channel_id=1, source_target_pairs={{0,1},{1,0},{2,3},{3,2},{4,5},{5,4},{6,7},{7,6},{8,9},{9,8},{10,11... | collective-permute-start | bytes 786440 | tf_op jit(solution)/shard_map/ppermute | solution.py:213
  23.2 1.5 %collective-permute-start.7 = (bf16[128,1024]{1,0:T(8,128)(2,1)S(1)}, bf16[128,1024]{1,0:T(8,128)(2,1)S(1)}, u32[]{:S(2)}, u32[]{:S(2)}) collective-permute-start(bf16[128,1024]{1,0:T(8,128)(2,1)S(1)} %collective-permute-done.3), channel_id=1, source_target_pairs={{0,1},{1,0},{2,3},{3,2},{4,5},{5,4},{6,7},{7,6},{8,9},{9,8},{10,11... | collective-permute-start | bytes 786440 | tf_op jit(solution)/shard_map/ppermute | solution.py:213
  34.1 25.2 %collective-permute-start.8 = (bf16[2,64,2048]{2,1,0:T(8,128)(2,1)S(1)}, bf16[2,64,2048]{2,1,0:T(8,128)(2,1)S(1)}, u32[]{:S(2)}, u32[]{:S(2)}) collective-permute-start(bf16[2,64,2048]{2,1,0:T(8,128)(2,1)S(1)} %get-tuple-element.22), channel_id=1, source_target_pairs={{0,16},{1,17},{2,18},{3,19},{4,20},{5,21},{6,22},{7,23},{8,24},{9,... | collective-permute-start | bytes 1572872 | tf_op jit(solution)/shard_map/ppermute | solution.py:213
  47.1 30.8 %copy-start = (s32[16,16]{1,0:T(8,128)S(1)}, s32[16,16]{1,0:T(8,128)}, u32[]{:S(2)}) copy-start(s32[16,16]{1,0:T(8,128)} %param.13) | copy-start | bytes 3076
  47.1 13.7 %collective-permute-start.9 = (bf16[2,64,2048]{2,1,0:T(8,128)(2,1)S(1)}, bf16[2,64,2048]{2,1,0:T(8,128)(2,1)S(1)}, u32[]{:S(2)}, u32[]{:S(2)}) collective-permute-start(bf16[2,64,2048]{2,1,0:T(8,128)(2,1)S(1)} %get-tuple-element.24), channel_id=1, source_target_pairs={{0,8},{1,9},{2,10},{3,11},{4,12},{5,13},{6,14},{7,15},{8,0},{9,1},... | collective-permute-start | bytes 1572872 | tf_op jit(solution)/shard_map/ppermute | solution.py:213
  60.9 7.3 %collective-permute-start.10 = (bf16[1,64,2048]{2,1,0:T(8,128)(2,1)S(1)}, bf16[1,64,2048]{2,1,0:T(8,128)(2,1)S(1)}, u32[]{:S(2)}, u32[]{:S(2)}) collective-permute-start(bf16[1,64,2048]{2,1,0:T(8,128)(2,1)S(1)} %get-tuple-element.26), channel_id=1, source_target_pairs={{0,8},{1,9},{2,10},{3,11},{4,12},{5,13},{6,14},{7,15},{8,0},{9,1},... | collective-permute-start | bytes 786440 | tf_op jit(solution)/shard_map/ppermute | solution.py:213
  61.2 7.2 %collective-permute-start.11 = (bf16[1,64,2048]{2,1,0:T(8,128)(2,1)S(1)}, bf16[1,64,2048]{2,1,0:T(8,128)(2,1)S(1)}, u32[]{:S(2)}, u32[]{:S(2)}) collective-permute-start(bf16[1,64,2048]{2,1,0:T(8,128)(2,1)S(1)} %get-tuple-element.27), channel_id=1, source_target_pairs={{0,16},{1,17},{2,18},{3,19},{4,20},{5,21},{6,22},{7,23},{8,24},{9,... | collective-permute-start | bytes 786440 | tf_op jit(solution)/shard_map/ppermute | solution.py:213
  69.0 8.2 %collective-permute-start.12 = (bf16[64,2048]{1,0:T(8,128)(2,1)S(1)}, bf16[64,2048]{1,0:T(8,128)(2,1)S(1)}, u32[]{:S(2)}, u32[]{:S(2)}) collective-permute-start(bf16[64,2048]{1,0:T(8,128)(2,1)S(1)} %hidden.2.refs_0_), channel_id=1, source_target_pairs={{0,8},{1,17},{2,10},{3,19},{4,12},{5,21},{6,14},{7,23},{8,0},{9,25... | collective-permute-start | bytes 786440 | tf_op jit(solution)/shard_map/ppermute | solution.py:213
  70.4 10.0 %collective-permute-start.13 = (bf16[64,2048]{1,0:T(8,128)(2,1)S(1)}, bf16[64,2048]{1,0:T(8,128)(2,1)S(1)}, u32[]{:S(2)}, u32[]{:S(2)}) collective-permute-start(bf16[64,2048]{1,0:T(8,128)(2,1)S(1)} %hidden.2.refs_0_), channel_id=1, source_target_pairs={{0,16},{1,9},{2,18},{3,11},{4,20},{5,13},{6,22},{7,15},{8,24},{9,1... | collective-permute-start | bytes 786440 | tf_op jit(solution)/shard_map/ppermute | solution.py:213
  77.1 8.1 %collective-permute-start.14 = (bf16[64,2048]{1,0:T(8,128)(2,1)S(1)}, bf16[64,2048]{1,0:T(8,128)(2,1)S(1)}, u32[]{:S(2)}, u32[]{:S(2)}) collective-permute-start(bf16[64,2048]{1,0:T(8,128)(2,1)S(1)} %collective-permute-done.12.refs_1_.refs_4_), channel_id=1, source_target_pairs={{0,16},{1,9},{2,18},{3,11},{4,20},{5,13},{6,22},{7,15},{8,24},{9,1... | collective-permute-start | bytes 786440 | tf_op jit(solution)/shard_map/ppermute | solution.py:213
  78.0 13.6 %collective-permute-start.19 = (bf16[2,64,2048]{2,1,0:T(8,128)(2,1)S(1)}, bf16[2,64,2048]{2,1,0:T(8,128)(2,1)S(1)}, u32[]{:S(2)}, u32[]{:S(2)}) collective-permute-start(bf16[2,64,2048]{2,1,0:T(8,128)(2,1)S(1)} %get-tuple-element.25.refs_4_), channel_id=1, source_target_pairs={{0,16},{1,17},{2,18},{3,19},{4,20},{5,21},{6,22},{7,23},{8,24},{9,... | collective-permute-start | bytes 1572872 | tf_op jit(solution)/shard_map/ppermute | solution.py:213
  79.4 12.2 %collective-permute-start.20 = (bf16[2,64,2048]{2,1,0:T(8,128)(2,1)S(1)}, bf16[2,64,2048]{2,1,0:T(8,128)(2,1)S(1)}, u32[]{:S(2)}, u32[]{:S(2)}) collective-permute-start(bf16[2,64,2048]{2,1,0:T(8,128)(2,1)S(1)} %get-tuple-element.32), channel_id=1, source_target_pairs={{0,8},{1,9},{2,10},{3,11},{4,12},{5,13},{6,14},{7,15},{8,0},{9,1},... | collective-permute-start | bytes 1572872 | tf_op jit(solution)/shard_map/ppermute | solution.py:213
  91.5 2.0 %collective-permute-start.15 = (bf16[4,32,2048]{2,1,0:T(8,128)(2,1)S(1)}, bf16[4,32,2048]{2,1,0:T(8,128)(2,1)S(1)}, u32[]{:S(2)}, u32[]{:S(2)}) collective-permute-start(bf16[4,32,2048]{2,1,0:T(8,128)(2,1)S(1)} %get-tuple-element.29), channel_id=1, source_target_pairs={{0,1},{1,0},{2,3},{3,2},{4,5},{5,4},{6,7},{7,6},{8,9},{9,8},{10,11... | collective-permute-start | bytes 1572872 | tf_op jit(solution)/shard_map/ppermute | solution.py:213
  91.7 8.8 %collective-permute-start.21 = (bf16[1,64,2048]{2,1,0:T(8,128)(2,1)S(1)}, bf16[1,64,2048]{2,1,0:T(8,128)(2,1)S(1)}, u32[]{:S(2)}, u32[]{:S(2)}) collective-permute-start(bf16[1,64,2048]{2,1,0:T(8,128)(2,1)S(1)} %get-tuple-element.33), channel_id=1, source_target_pairs={{0,8},{1,9},{2,10},{3,11},{4,12},{5,13},{6,14},{7,15},{8,0},{9,1},... | collective-permute-start | bytes 786440 | tf_op jit(solution)/shard_map/ppermute | solution.py:213
  92.4 8.4 %collective-permute-start.22 = (bf16[1,64,2048]{2,1,0:T(8,128)(2,1)S(1)}, bf16[1,64,2048]{2,1,0:T(8,128)(2,1)S(1)}, u32[]{:S(2)}, u32[]{:S(2)}) collective-permute-start(bf16[1,64,2048]{2,1,0:T(8,128)(2,1)S(1)} %get-tuple-element.34), channel_id=1, source_target_pairs={{0,16},{1,17},{2,18},{3,19},{4,20},{5,21},{6,22},{7,23},{8,24},{9,... | collective-permute-start | bytes 786440 | tf_op jit(solution)/shard_map/ppermute | solution.py:213
  101.3 8.5 %collective-permute-start.23 = (bf16[64,2048]{1,0:T(8,128)(2,1)S(1)}, bf16[64,2048]{1,0:T(8,128)(2,1)S(1)}, u32[]{:S(2)}, u32[]{:S(2)}) collective-permute-start(bf16[64,2048]{1,0:T(8,128)(2,1)S(1)} %hidden.3.refs_0_), channel_id=1, source_target_pairs={{0,8},{1,17},{2,10},{3,19},{4,12},{5,21},{6,14},{7,23},{8,0},{9,25... | collective-permute-start | bytes 786440 | tf_op jit(solution)/shard_map/ppermute | solution.py:213
  102.8 18.7 %collective-permute-start.24 = (bf16[64,2048]{1,0:T(8,128)(2,1)S(1)}, bf16[64,2048]{1,0:T(8,128)(2,1)S(1)}, u32[]{:S(2)}, u32[]{:S(2)}) collective-permute-start(bf16[64,2048]{1,0:T(8,128)(2,1)S(1)} %hidden.3.refs_0_), channel_id=1, source_target_pairs={{0,16},{1,9},{2,18},{3,11},{4,20},{5,13},{6,22},{7,15},{8,24},{9,1... | collective-permute-start | bytes 786440 | tf_op jit(solution)/shard_map/ppermute | solution.py:213
  109.8 11.7 %collective-permute-start.25 = (bf16[64,2048]{1,0:T(8,128)(2,1)S(1)}, bf16[64,2048]{1,0:T(8,128)(2,1)S(1)}, u32[]{:S(2)}, u32[]{:S(2)}) collective-permute-start(bf16[64,2048]{1,0:T(8,128)(2,1)S(1)} %collective-permute-done.23.refs_1_), channel_id=1, source_target_pairs={{0,16},{1,9},{2,18},{3,11},{4,20},{5,13},{6,22},{7,15},{8,24},{9,1... | collective-permute-start | bytes 786440 | tf_op jit(solution)/shard_map/ppermute | solution.py:213
  111.3 6.5 %collective-permute-start.16 = (bf16[32,2048]{1,0:T(8,128)(2,1)S(1)}, bf16[32,2048]{1,0:T(8,128)(2,1)S(1)}, u32[]{:S(2)}, u32[]{:S(2)}) collective-permute-start(bf16[32,2048]{1,0:T(8,128)(2,1)S(1)} %get-tuple-element.42.refs_6_), channel_id=1, source_target_pairs={{0,2},{1,3},{2,0},{3,1},{4,6},{5,7},{6,4},{7,5},{8,10},{9,11},{10,... | collective-permute-start | bytes 393224 | tf_op jit(solution)/shard_map/ppermute | solution.py:213
  111.8 9.7 %collective-permute-start.17 = (bf16[32,2048]{1,0:T(8,128)(2,1)S(1)}, bf16[32,2048]{1,0:T(8,128)(2,1)S(1)}, u32[]{:S(2)}, u32[]{:S(2)}) collective-permute-start(bf16[32,2048]{1,0:T(8,128)(2,1)S(1)} %get-tuple-element.41.refs_7_), channel_id=1, source_target_pairs={{0,4},{1,5},{2,6},{3,7},{4,0},{5,1},{6,2},{7,3},{8,12},{9,13},{10,... | collective-permute-start | bytes 393224 | tf_op jit(solution)/shard_map/ppermute | solution.py:213
  113.7 7.8 %collective-permute-start.18 = (bf16[32,2048]{1,0:T(8,128)(2,1)S(1)}, bf16[32,2048]{1,0:T(8,128)(2,1)S(1)}, u32[]{:S(2)}, u32[]{:S(2)}) collective-permute-start(bf16[32,2048]{1,0:T(8,128)(2,1)S(1)} %get-tuple-element.40.refs_8_), channel_id=1, source_target_pairs={{0,6},{1,7},{2,4},{3,5},{4,2},{5,3},{6,0},{7,1},{8,14},{9,15},{10,... | collective-permute-start | bytes 393224 | tf_op jit(solution)/shard_map/ppermute | solution.py:213
  127.7 2.0 %collective-permute-start.26 = (bf16[4,32,2048]{2,1,0:T(8,128)(2,1)S(1)}, bf16[4,32,2048]{2,1,0:T(8,128)(2,1)S(1)}, u32[]{:S(2)}, u32[]{:S(2)}) collective-permute-start(bf16[4,32,2048]{2,1,0:T(8,128)(2,1)S(1)} %get-tuple-element.36), channel_id=1, source_target_pairs={{0,1},{1,0},{2,3},{3,2},{4,5},{5,4},{6,7},{7,6},{8,9},{9,8},{10,11... | collective-permute-start | bytes 1572872 | tf_op jit(solution)/shard_map/ppermute | solution.py:213
  129.8 7.1 %collective-permute-start.27 = (bf16[32,2048]{1,0:T(8,128)(2,1)S(1)}, bf16[32,2048]{1,0:T(8,128)(2,1)S(1)}, u32[]{:S(2)}, u32[]{:S(2)}) collective-permute-start(bf16[32,2048]{1,0:T(8,128)(2,1)S(1)} %get-tuple-element.37), channel_id=1, source_target_pairs={{0,2},{1,3},{2,0},{3,1},{4,6},{5,7},{6,4},{7,5},{8,10},{9,11},{10,... | collective-permute-start | bytes 393224 | tf_op jit(solution)/shard_map/ppermute | solution.py:213
  131.9 12.8 %collective-permute-start.28 = (bf16[32,2048]{1,0:T(8,128)(2,1)S(1)}, bf16[32,2048]{1,0:T(8,128)(2,1)S(1)}, u32[]{:S(2)}, u32[]{:S(2)}) collective-permute-start(bf16[32,2048]{1,0:T(8,128)(2,1)S(1)} %get-tuple-element.39), channel_id=1, source_target_pairs={{0,4},{1,5},{2,6},{3,7},{4,0},{5,1},{6,2},{7,3},{8,12},{9,13},{10,... | collective-permute-start | bytes 393224 | tf_op jit(solution)/shard_map/ppermute | solution.py:213
  131.9 12.7 %collective-permute-start.29 = (bf16[32,2048]{1,0:T(8,128)(2,1)S(1)}, bf16[32,2048]{1,0:T(8,128)(2,1)S(1)}, u32[]{:S(2)}, u32[]{:S(2)}) collective-permute-start(bf16[32,2048]{1,0:T(8,128)(2,1)S(1)} %get-tuple-element.38), channel_id=1, source_target_pairs={{0,6},{1,7},{2,4},{3,5},{4,2},{5,3},{6,0},{7,1},{8,14},{9,15},{10,... | collective-permute-start | bytes 393224 | tf_op jit(solution)/shard_map/ppermute | solution.py:213

commit v6 on v4

--- a/solution.py
+++ b/solution.py
@@ -16,30 +16,21 @@
 def masked_product(x_ref, weight_ref, keep_ref):
     block_rows, width = keep_ref.shape
     side = weight_ref.shape[0] // block_rows
-    group = min(4, block_rows)
-    total = None
-    for first in range(0, block_rows, group):
-        strips = []
-        for i in range(first, first + group):
-            keep = jnp.broadcast_to(keep_ref[i : i + 1, :], (16, width)).astype(jnp.bfloat16)
-            block = weight_ref[i * side : (i + 1) * side, :].reshape(side // 16, 16, width)
-            strips.append((block * keep[None]).reshape(side, width))
-        term = jnp.dot(
-            x_ref[:, first * side : (first + group) * side],
-            jnp.concatenate(strips, axis=0),
-            preferred_element_type=jnp.float32,
-        )
-        total = term if total is None else total + term
-    return total
+    strips = []
+    for i in range(block_rows):
+        keep = jnp.broadcast_to(keep_ref[i : i + 1, :], (16, width)).astype(jnp.bfloat16)
+        block = weight_ref[i * side : (i + 1) * side, :].reshape(side // 16, 16, width)
+        strips.append((block * keep[None]).reshape(side, width))
+    return jnp.dot(x_ref[...], jnp.concatenate(strips, axis=0), preferred_element_type=jnp.float32)
 
 
 def widen(keep_mask, width):
     return jnp.repeat(keep_mask.astype(jnp.float32), width // keep_mask.shape[1], axis=1)
 
 
-def gate_up_kernel(n, place_ref, own_ref, other_ref, gate_ref, up_ref, gate_keep, up_keep, *refs):
+def gate_up_kernel(place_ref, own_ref, other_ref, gate_ref, up_ref, gate_keep, up_keep, *refs):
     outs, x = refs[:4], refs[4]
-    _, rows, half = own_ref.shape
+    n, rows, half = own_ref.shape
 
     @pl.when(pl.program_id(0) == 0)
     def _():
@@ -71,7 +62,7 @@
     mask = pl.BlockSpec((gate_keep.shape[0], tile), lambda i, *_: (0, i))
     out = pl.BlockSpec((n // 2, rows, tile), lambda i, *_: (0, 0, i))
     return pl.pallas_call(
-        functools.partial(gate_up_kernel, n),
+        gate_up_kernel,
         grid_spec=pltpu.PrefetchScalarGridSpec(
             num_scalar_prefetch=1,
             grid=(width // tile,),
@@ -207,6 +198,24 @@
         compiler_params=pltpu.CompilerParams(vmem_limit_bytes=VMEM_BYTES),
         name="join",
     )(*blocks, *after)
+
+
+def hold_kernel(value_ref, *refs):
+    refs[-1][...] = value_ref[...]
+
+
+def hold(value, after):
+    if not after:
+        return value
+    spec = pl.BlockSpec(memory_space=pltpu.VMEM)
+    return pl.pallas_call(
+        hold_kernel,
+        in_specs=[spec] + [pl.BlockSpec(memory_space=pl.ANY)] * len(after),
+        out_specs=spec,
+        out_shape=jax.ShapeDtypeStruct(value.shape, value.dtype),
+        compiler_params=pltpu.CompilerParams(vmem_limit_bytes=VMEM_BYTES),
+        name="hold",
+    )(value, *after)
 
 
 def mirror(p, n):
@@ -267,30 +276,33 @@
         return sums[0], [part.astype(jnp.bfloat16) for part in sums[1:]]
 
     rows, features = tokens.shape
-    piece = rows // (2 * BATCHES)
-    split = tokens.reshape(2, BATCHES, piece, features)
     gate_wide = widen(gate_keep, gate_weight.shape[1])
     up_wide = widen(up_keep, up_weight.shape[1])
     down_wide = widen(down_keep, down_weight.shape[1])
+    piece = rows // (2 * BATCHES)
+    split = tokens.reshape(2, BATCHES, piece, features)
     moved = []
     for s in range(BATCHES):
         block = split[:, s].reshape(2 * piece, features)
         moved.append([send(block, lambda t, zz, c: (zz, t ^ k, c)) for k in range(n_z)])
-    sums, before_swap = [], []
-    for blocks in moved:
-        own = join(blocks, before_swap)
-        sums.append(gate_up(place, own, across_core(own), gate_weight, up_weight, gate_wide, up_wide))
-        before_swap = [sums[-1][2]]
-    out, before_add, before_hidden, before_down = [], [], [], []
-    for terms in sums:
-        parts = gather(activate(*halve(*terms, before_add), before_hidden))
-        mine, theirs = down(place, parts, down_weight, down_wide, before_down)
-        total, sent = combine(mine, theirs)
+    sums, before = [], []
+    for s in range(BATCHES):
+        own = join(moved[s], before)
+        gate_kept, up_kept, gate_sent, up_sent = gate_up(
+            place, own, across_core(own), gate_weight, up_weight, gate_wide, up_wide
+        )
+        gate_sent = hold(gate_sent, [part for later in moved[s + 1 : s + 2] for part in later])
+        sums.append((gate_kept, up_kept, gate_sent, up_sent))
+        before = [gate_sent]
+    hidden = [gather(activate(*halve(*terms, ()), ())) for terms in sums]
+    out, arrived = [], []
+    for s, parts in enumerate(hidden):
+        mine, theirs = down(place, parts, down_weight, down_wide, [later[1] for later in hidden[s + 1 : s + 2]])
+        total, sent = combine(mine, hold(theirs, arrived))
         arrived = [across_z(sent[j - 1], j) for j in range(1, n_z)]
         for part in arrived:
             total += part.astype(jnp.float32)
         out.append(total.astype(jnp.bfloat16))
-        before_add, before_hidden, before_down = [parts[1]], sent, arrived
     return jnp.concatenate(out, axis=0)
 
 

time: 151 us -> 140 us (0.927)
  waiting for transfers between devices: 61.5 us -> 53.5 us
  starting transfers between devices: 52.3 us -> 49.9 us
    ppermute x32, waiting for transfers between devices: 61.5 us -> 53.5 us  [send(): return lax.ppermute(value, AXES, perm)]
    ppermute x32, starting transfers between devices: 52.3 us -> 49.9 us  [send(): return lax.ppermute(value, AXES, perm)]
    pallas_call x2 -> x4, Pallas kernels: 18.5 us -> 18.6 us  [the longest x2 18.6 us: gate_up(): pl.pallas_call(gate_up_kernel, grid_spec=pltpu.PrefetchScalarGridSpec(num...]
  transfers between devices with their start and end apart: 32 -> 32, of which waited for: 20 -> 13; matrix products, arithmetic and copies ran while one was open for 1% -> 1% of each run, Pallas kernels for 11% -> 19%
where the time goes in v6:
time: 140 us
  waiting for transfers between devices  53.5 us (38%)
  starting transfers between devices  49.9 us (36%)
  Pallas kernels  32.4 us (23%)
  other arithmetic  2.43 us (2%)
  local copies, waits for them, and re-layouts  1.48 us (1%)
    ppermute x32, waiting for transfers between devices, send(): return lax.ppermute(value, AXES, perm)  53.5 us
    ppermute x32, starting transfers between devices, send(): return lax.ppermute(value, AXES, perm)  49.9 us
    pallas_call x2, Pallas kernels, gate_up(): pl.pallas_call(gate_up_kernel, grid_spec=pltpu.PrefetchScalarGridSpec(num...  18.6 us
    pallas_call x2, Pallas kernels, down(): pl.pallas_call(functools.partial(down_kernel, n), grid_spec=pltpu.Prefetc...  12.5 us
  transfers between devices with their start and end apart: 32, of which 13 were waited for; matrix products, arithmetic and copies ran while one was open for 1% of the time, Pallas kernels for 19%

profile of v6, /device:TPU:0, one launch (start us, length us, event | category | flops | bytes accessed | tf_op | source)
XLA Modules:
  0.0 139.9 jit_solution(8481986473227366259)
XLA Ops:
  0.0 1.0 fusion.12
  1.0 0.7 collective-permute-start
  1.7 5.7 %collective-permute-start.1 = (bf16[64,1024]{1,0:T(8,128)(2,1)S(1)}, bf16[64,1024]{1,0:T(8,128)(2,1)S(1)}, u32[]{:S(2)}, u32[]{:S(2)}) collective-permute-start(bf16[64,1024]{1,0:T(8,128)(2,1)S(1)} %bitcast.63), channel_id=1, source_target_pairs={{0,2},{1,3},{2,10},{3,11},{4,18},{5,19},{6,26},{7,27},{8,0},{9,1},... | collective-permute-start | bytes 393224 | tf_op jit(solution)/shard_map/ppermute | solution.py:243
  7.4 3.5 %collective-permute-start.2 = (bf16[64,1024]{1,0:T(8,128)(2,1)S(1)}, bf16[64,1024]{1,0:T(8,128)(2,1)S(1)}, u32[]{:S(2)}, u32[]{:S(2)}) collective-permute-start(bf16[64,1024]{1,0:T(8,128)(2,1)S(1)} %bitcast.64), channel_id=1, source_target_pairs={{0,4},{1,5},{2,12},{3,13},{4,20},{5,21},{6,28},{7,29},{8,6},{9,7},... | collective-permute-start | bytes 393224 | tf_op jit(solution)/shard_map/ppermute | solution.py:243
  10.8 1.9 %collective-permute-start.3 = (bf16[64,1024]{1,0:T(8,128)(2,1)S(1)}, bf16[64,1024]{1,0:T(8,128)(2,1)S(1)}, u32[]{:S(2)}, u32[]{:S(2)}) collective-permute-start(bf16[64,1024]{1,0:T(8,128)(2,1)S(1)} %bitcast.65), channel_id=1, source_target_pairs={{0,6},{1,7},{2,14},{3,15},{4,22},{5,23},{6,30},{7,31},{8,4},{9,5},... | collective-permute-start | bytes 393224 | tf_op jit(solution)/shard_map/ppermute | solution.py:243
  12.8 4.6 %collective-permute-done.2.refs_2_ = bf16[64,1024]{1,0:T(8,128)(2,1)S(1)} collective-permute-done((bf16[64,1024]{1,0:T(8,128)(2,1)S(1)}, bf16[64,1024]{1,0:T(8,128)(2,1)S(1)}, u32[]{:S(2)}, u32[]{:S(2)}) %collective-permute-start.2) | collective-permute-done | bytes 131104 | tf_op jit(solution)/shard_map/ppermute | solution.py:243
  17.5 0.7 collective-permute-start.5
  18.1 8.4 %collective-permute-start.6 = (bf16[64,1024]{1,0:T(8,128)(2,1)S(1)}, bf16[64,1024]{1,0:T(8,128)(2,1)S(1)}, u32[]{:S(2)}, u32[]{:S(2)}) collective-permute-start(bf16[64,1024]{1,0:T(8,128)(2,1)S(1)} %bitcast.59), channel_id=1, source_target_pairs={{0,2},{1,3},{2,10},{3,11},{4,18},{5,19},{6,26},{7,27},{8,0},{9,1},... | collective-permute-start | bytes 393224 | tf_op jit(solution)/shard_map/ppermute | solution.py:243
  26.5 5.2 %collective-permute-start.7 = (bf16[64,1024]{1,0:T(8,128)(2,1)S(1)}, bf16[64,1024]{1,0:T(8,128)(2,1)S(1)}, u32[]{:S(2)}, u32[]{:S(2)}) collective-permute-start(bf16[64,1024]{1,0:T(8,128)(2,1)S(1)} %bitcast.60), channel_id=1, source_target_pairs={{0,4},{1,5},{2,12},{3,13},{4,20},{5,21},{6,28},{7,29},{8,6},{9,7},... | collective-permute-start | bytes 393224 | tf_op jit(solution)/shard_map/ppermute | solution.py:243
  31.7 1.1 collective-permute-start.8
  32.8 0.7 convert_element_type.101
  33.5 0.7 convert_element_type.102
  34.6 9.3 %gate_up.2 = (f32[2,64,2048]{2,1,0:T(8,128)S(1)}, f32[2,64,2048]{2,1,0:T(8,128)S(1)}, bf16[2,64,2048]{2,1,0:T(8,128)(2,1)S(1)}, bf16[2,64,2048]{2,1,0:T(8,128)(2,1)S(1)}) custom-call(s32[9]{0:T(128)S(1)} %stack.33.place_ref, bf16[4,64,1024]{2,1,0:T(8,128)(2,1)S(1)} %join.2.own_ref, bf16[4,64,1024]{2,1,0:T(8,128)(2,1)S(1)} %collective-permute-done.4.other_ref, ...), custom_call_target="tpu_custom_call" | custom-call | flops 4294967296 | bytes 16777216 | tf_op jit(solution)/shard_map/gate_up/pallas_call | solution.py:64
  44.1 1.8 %collective-permute-start.9 = (bf16[2,64,2048]{2,1,0:T(8,128)(2,1)S(1)}, bf16[2,64,2048]{2,1,0:T(8,128)(2,1)S(1)}, u32[]{:S(2)}, u32[]{:S(2)}) collective-permute-start(bf16[2,64,2048]{2,1,0:T(8,128)(2,1)S(1)} %hold.2.refs_4_), channel_id=1, source_target_pairs={{0,16},{1,17},{2,18},{3,19},{4,20},{5,21},{6,22},{7,23},{8,24},{9,... | collective-permute-start | bytes 1572872 | tf_op jit(solution)/shard_map/ppermute | solution.py:243
  45.9 0.7 collective-permute-start.10
  46.6 9.3 %gate_up.3 = (f32[2,64,2048]{2,1,0:T(8,128)S(1)}, f32[2,64,2048]{2,1,0:T(8,128)S(1)}, bf16[2,64,2048]{2,1,0:T(8,128)(2,1)S(1)}, bf16[2,64,2048]{2,1,0:T(8,128)(2,1)S(1)}) custom-call(s32[9]{0:T(128)S(1)} %stack.33.place_ref, bf16[4,64,1024]{2,1,0:T(8,128)(2,1)S(1)} %join.3.own_ref, bf16[4,64,1024]{2,1,0:T(8,128)(2,1)S(1)} %collective-permute-done.16.other_ref, ...), custom_call_target="tpu_custom_call" | custom-call | flops 4294967296 | bytes 16777216 | tf_op jit(solution)/shard_map/gate_up/pallas_call | solution.py:64
  55.9 1.2 collective-permute-start.17
  57.1 0.7 collective-permute-start.18
  57.8 0.7 collective-permute-done.9.refs_1_
  58.5 1.7 %collective-permute-done.10.refs_3_.refs_4_ = bf16[2,64,2048]{2,1,0:T(8,128)(2,1)S(1)} collective-permute-done((bf16[2,64,2048]{2,1,0:T(8,128)(2,1)S(1)}, bf16[2,64,2048]{2,1,0:T(8,128)(2,1)S(1)}, u32[]{:S(2)}, u32[]{:S(2)}) %collective-permute-start.10) | collective-permute-done | bytes 524320 | tf_op jit(solution)/shard_map/ppermute | solution.py:243
  60.3 0.7 collective-permute-start.11
  61.0 0.9 collective-permute-start.12
  61.9 14.9 %collective-permute-done.11.refs_2_ = bf16[1,64,2048]{2,1,0:T(8,128)(2,1)S(1)} collective-permute-done((bf16[1,64,2048]{2,1,0:T(8,128)(2,1)S(1)}, bf16[1,64,2048]{2,1,0:T(8,128)(2,1)S(1)}, u32[]{:S(2)}, u32[]{:S(2)}) %collective-permute-start.11) | collective-permute-done | bytes 262176 | tf_op jit(solution)/shard_map/ppermute | solution.py:243
  76.8 0.5 hidden.2.refs_0_
  77.3 0.7 collective-permute-start.13
  78.1 1.4 %collective-permute-start.19 = (bf16[1,64,2048]{2,1,0:T(8,128)(2,1)S(1)}, bf16[1,64,2048]{2,1,0:T(8,128)(2,1)S(1)}, u32[]{:S(2)}, u32[]{:S(2)}) collective-permute-start(bf16[1,64,2048]{2,1,0:T(8,128)(2,1)S(1)} %get-tuple-element.31), channel_id=1, source_target_pairs={{0,8},{1,9},{2,10},{3,11},{4,12},{5,13},{6,14},{7,15},{8,0},{9,1},... | collective-permute-start | bytes 786440 | tf_op jit(solution)/shard_map/ppermute | solution.py:243
  79.8 1.7 %collective-permute-start.14 = (bf16[64,2048]{1,0:T(8,128)(2,1)S(1)}, bf16[64,2048]{1,0:T(8,128)(2,1)S(1)}, u32[]{:S(2)}, u32[]{:S(2)}) collective-permute-start(bf16[64,2048]{1,0:T(8,128)(2,1)S(1)} %hidden.2.refs_0_), channel_id=1, source_target_pairs={{0,16},{1,9},{2,18},{3,11},{4,20},{5,13},{6,22},{7,15},{8,24},{9,1... | collective-permute-start | bytes 786440 | tf_op jit(solution)/shard_map/ppermute | solution.py:243
  81.6 5.0 %collective-permute-done.13.refs_1_ = bf16[64,2048]{1,0:T(8,128)(2,1)S(1)} collective-permute-done((bf16[64,2048]{1,0:T(8,128)(2,1)S(1)}, bf16[64,2048]{1,0:T(8,128)(2,1)S(1)}, u32[]{:S(2)}, u32[]{:S(2)}) %collective-permute-start.13) | collective-permute-done | bytes 262176 | tf_op jit(solution)/shard_map/ppermute | solution.py:243
  86.8 5.3 %collective-permute-done.19.refs_2_ = bf16[1,64,2048]{2,1,0:T(8,128)(2,1)S(1)} collective-permute-done((bf16[1,64,2048]{2,1,0:T(8,128)(2,1)S(1)}, bf16[1,64,2048]{2,1,0:T(8,128)(2,1)S(1)}, u32[]{:S(2)}, u32[]{:S(2)}) %collective-permute-start.19) | collective-permute-done | bytes 262176 | tf_op jit(solution)/shard_map/ppermute | solution.py:243
  92.2 0.5 hidden.3.refs_0_
  92.7 0.7 collective-permute-start.21
  93.6 2.5 %collective-permute-done.15.refs_3_ = bf16[64,2048]{1,0:T(8,128)(2,1)S(1)} collective-permute-done((bf16[64,2048]{1,0:T(8,128)(2,1)S(1)}, bf16[64,2048]{1,0:T(8,128)(2,1)S(1)}, u32[]{:S(2)}, u32[]{:S(2)}) %collective-permute-start.15) | collective-permute-done | bytes 262176 | tf_op jit(solution)/shard_map/ppermute | solution.py:243
  96.1 3.0 %collective-permute-done.21.refs_6_.refs_1_ = bf16[64,2048]{1,0:T(8,128)(2,1)S(1)} collective-permute-done((bf16[64,2048]{1,0:T(8,128)(2,1)S(1)}, bf16[64,2048]{1,0:T(8,128)(2,1)S(1)}, u32[]{:S(2)}, u32[]{:S(2)}) %collective-permute-start.21) | collective-permute-done | bytes 262176 | tf_op jit(solution)/shard_map/ppermute | solution.py:243
  99.1 6.2 %down.2 = (f32[4,32,2048]{2,1,0:T(8,128)S(1)}, bf16[4,32,2048]{2,1,0:T(8,128)(2,1)S(1)}) custom-call(s32[9]{0:T(128)S(1)} %stack.33.place_ref, bf16[64,2048]{1,0:T(8,128)(2,1)S(1)} %hidden.2.refs_0_, bf16[64,2048]{1,0:T(8,128)(2,1)S(1)} %collective-permute-done.13.refs_1_, bf16[64,2048]{1,0:T(8,128)(2,1)S(1)} %collective-permute-done.14.refs_2_, ...), custom_call_target="tpu_custom_call" | custom-call | flops 2147483648 | bytes 8388608 | tf_op jit(solution)/shard_map/down/pallas_call | solution.py:161
  105.8 1.8 %collective-permute-start.27 = (bf16[64,2048]{1,0:T(8,128)(2,1)S(1)}, bf16[64,2048]{1,0:T(8,128)(2,1)S(1)}, u32[]{:S(2)}, u32[]{:S(2)}) collective-permute-start(bf16[64,2048]{1,0:T(8,128)(2,1)S(1)} %collective-permute-done.21.refs_6_.refs_1_), channel_id=1, source_target_pairs={{0,16},{1,9},{2,18},{3,11},{4,20},{5,13},{6,22},{7,15},{8,24},{9,1... | collective-permute-start | bytes 786440 | tf_op jit(solution)/shard_map/ppermute | solution.py:243
  107.6 1.5 %collective-permute-start.23 = (bf16[32,2048]{1,0:T(8,128)(2,1)S(1)}, bf16[32,2048]{1,0:T(8,128)(2,1)S(1)}, u32[]{:S(2)}, u32[]{:S(2)}) collective-permute-start(bf16[32,2048]{1,0:T(8,128)(2,1)S(1)} %get-tuple-element.42), channel_id=1, source_target_pairs={{0,2},{1,3},{2,0},{3,1},{4,6},{5,7},{6,4},{7,5},{8,10},{9,11},{10,... | collective-permute-start | bytes 393224 | tf_op jit(solution)/shard_map/ppermute | solution.py:243
  109.1 1.1 collective-permute-start.24
  110.2 1.9 %collective-permute-start.25 = (bf16[32,2048]{1,0:T(8,128)(2,1)S(1)}, bf16[32,2048]{1,0:T(8,128)(2,1)S(1)}, u32[]{:S(2)}, u32[]{:S(2)}) collective-permute-start(bf16[32,2048]{1,0:T(8,128)(2,1)S(1)} %get-tuple-element.40), channel_id=1, source_target_pairs={{0,6},{1,7},{2,4},{3,5},{4,2},{5,3},{6,0},{7,1},{8,14},{9,15},{10,... | collective-permute-start | bytes 393224 | tf_op jit(solution)/shard_map/ppermute | solution.py:243
  112.1 2.6 %collective-permute-done.27.refs_3_ = bf16[64,2048]{1,0:T(8,128)(2,1)S(1)} collective-permute-done((bf16[64,2048]{1,0:T(8,128)(2,1)S(1)}, bf16[64,2048]{1,0:T(8,128)(2,1)S(1)}, u32[]{:S(2)}, u32[]{:S(2)}) %collective-permute-start.27) | collective-permute-done | bytes 262176 | tf_op jit(solution)/shard_map/ppermute | solution.py:243
  114.7 6.2 %down.3 = (f32[4,32,2048]{2,1,0:T(8,128)S(1)}, bf16[4,32,2048]{2,1,0:T(8,128)(2,1)S(1)}) custom-call(s32[9]{0:T(128)S(1)} %stack.33.place_ref, bf16[64,2048]{1,0:T(8,128)(2,1)S(1)} %hidden.3.refs_0_, bf16[64,2048]{1,0:T(8,128)(2,1)S(1)} %collective-permute-done.21.refs_6_.refs_1_, bf16[64,2048]{1,0:T(8,128)(2,1)S(1)} %collective-permute-done.26.refs_2_, ...), custom_call_target="tpu_custom_call" | custom-call | flops 2147483648 | bytes 8388608 | tf_op jit(solution)/shard_map/down/pallas_call | solution.py:161
  120.9 0.9 collective-permute-done.24.refs_1_
  122.0 1.9 %collective-permute-done.28 = bf16[4,32,2048]{2,1,0:T(8,128)(2,1)S(1)} collective-permute-done((bf16[4,32,2048]{2,1,0:T(8,128)(2,1)S(1)}, bf16[4,32,2048]{2,1,0:T(8,128)(2,1)S(1)}, u32[]{:S(2)}, u32[]{:S(2)}) %collective-permute-start.28) | collective-permute-done | bytes 524320 | tf_op jit(solution)/shard_map/ppermute | solution.py:243
  123.9 2.3 %collective-permute-start.29 = (bf16[32,2048]{1,0:T(8,128)(2,1)S(1)}, bf16[32,2048]{1,0:T(8,128)(2,1)S(1)}, u32[]{:S(2)}, u32[]{:S(2)}) collective-permute-start(bf16[32,2048]{1,0:T(8,128)(2,1)S(1)} %get-tuple-element.37), channel_id=1, source_target_pairs={{0,2},{1,3},{2,0},{3,1},{4,6},{5,7},{6,4},{7,5},{8,10},{9,11},{10,... | collective-permute-start | bytes 393224 | tf_op jit(solution)/shard_map/ppermute | solution.py:243
  126.2 0.4 collective-permute-start.30
  126.6 2.0 %collective-permute-start.31 = (bf16[32,2048]{1,0:T(8,128)(2,1)S(1)}, bf16[32,2048]{1,0:T(8,128)(2,1)S(1)}, u32[]{:S(2)}, u32[]{:S(2)}) collective-permute-start(bf16[32,2048]{1,0:T(8,128)(2,1)S(1)} %get-tuple-element.38), channel_id=1, source_target_pairs={{0,6},{1,7},{2,4},{3,5},{4,2},{5,3},{6,0},{7,1},{8,14},{9,15},{10,... | collective-permute-start | bytes 393224 | tf_op jit(solution)/shard_map/ppermute | solution.py:243
  128.8 2.8 %collective-permute-done.29 = bf16[32,2048]{1,0:T(8,128)(2,1)S(1)} collective-permute-done((bf16[32,2048]{1,0:T(8,128)(2,1)S(1)}, bf16[32,2048]{1,0:T(8,128)(2,1)S(1)}, u32[]{:S(2)}, u32[]{:S(2)}) %collective-permute-start.29) | collective-permute-done | bytes 131104 | tf_op jit(solution)/shard_map/ppermute | solution.py:243
  131.5 7.6 %collective-permute-done.30 = bf16[32,2048]{1,0:T(8,128)(2,1)S(1)} collective-permute-done((bf16[32,2048]{1,0:T(8,128)(2,1)S(1)}, bf16[32,2048]{1,0:T(8,128)(2,1)S(1)}, u32[]{:S(2)}, u32[]{:S(2)}) %collective-permute-start.30) | collective-permute-done | bytes 131104 | tf_op jit(solution)/shard_map/ppermute | solution.py:243
  139.2 0.7 pad_maximum_fusion
  (45 shorter events, 2.4 us)
Async XLA Ops:
  1.0 11.8 %collective-permute-start = (bf16[64,1024]{1,0:T(8,128)(2,1)S(1)}, bf16[64,1024]{1,0:T(8,128)(2,1)S(1)}, u32[]{:S(2)}, u32[]{:S(2)}) collective-permute-start(bf16[64,1024]{1,0:T(8,128)(2,1)S(1)} %bitcast.62), channel_id=1, source_target_pairs={{0,0},{1,1},{2,8},{3,9},{4,16},{5,17},{6,24},{7,25},{8,2},{9,3},{1... | collective-permute-start | bytes 393224 | tf_op jit(solution)/shard_map/ppermute | solution.py:243
  1.7 11.1 %collective-permute-start.1 = (bf16[64,1024]{1,0:T(8,128)(2,1)S(1)}, bf16[64,1024]{1,0:T(8,128)(2,1)S(1)}, u32[]{:S(2)}, u32[]{:S(2)}) collective-permute-start(bf16[64,1024]{1,0:T(8,128)(2,1)S(1)} %bitcast.63), channel_id=1, source_target_pairs={{0,2},{1,3},{2,10},{3,11},{4,18},{5,19},{6,26},{7,27},{8,0},{9,1},... | collective-permute-start | bytes 393224 | tf_op jit(solution)/shard_map/ppermute | solution.py:243
  7.4 10.0 %collective-permute-start.2 = (bf16[64,1024]{1,0:T(8,128)(2,1)S(1)}, bf16[64,1024]{1,0:T(8,128)(2,1)S(1)}, u32[]{:S(2)}, u32[]{:S(2)}) collective-permute-start(bf16[64,1024]{1,0:T(8,128)(2,1)S(1)} %bitcast.64), channel_id=1, source_target_pairs={{0,4},{1,5},{2,12},{3,13},{4,20},{5,21},{6,28},{7,29},{8,6},{9,7},... | collective-permute-start | bytes 393224 | tf_op jit(solution)/shard_map/ppermute | solution.py:243
  10.8 6.5 %collective-permute-start.3 = (bf16[64,1024]{1,0:T(8,128)(2,1)S(1)}, bf16[64,1024]{1,0:T(8,128)(2,1)S(1)}, u32[]{:S(2)}, u32[]{:S(2)}) collective-permute-start(bf16[64,1024]{1,0:T(8,128)(2,1)S(1)} %bitcast.65), channel_id=1, source_target_pairs={{0,6},{1,7},{2,14},{3,15},{4,22},{5,23},{6,30},{7,31},{8,4},{9,5},... | collective-permute-start | bytes 393224 | tf_op jit(solution)/shard_map/ppermute | solution.py:243
  17.4 17.2 %collective-permute-start.4 = (bf16[4,64,1024]{2,1,0:T(8,128)(2,1)S(1)}, bf16[4,64,1024]{2,1,0:T(8,128)(2,1)S(1)}, u32[]{:S(2)}, u32[]{:S(2)}) collective-permute-start(bf16[4,64,1024]{2,1,0:T(8,128)(2,1)S(1)} %join.2.own_ref), channel_id=1, source_target_pairs={{0,1},{1,0},{2,3},{3,2},{4,5},{5,4},{6,7},{7,6},{8,9},{9,8},{10,11... | collective-permute-start | bytes 1572872 | tf_op jit(solution)/shard_map/ppermute | solution.py:243
  17.5 26.4 %collective-permute-start.5 = (bf16[64,1024]{1,0:T(8,128)(2,1)S(1)}, bf16[64,1024]{1,0:T(8,128)(2,1)S(1)}, u32[]{:S(2)}, u32[]{:S(2)}) collective-permute-start(bf16[64,1024]{1,0:T(8,128)(2,1)S(1)} %bitcast.58), channel_id=1, source_target_pairs={{0,0},{1,1},{2,8},{3,9},{4,16},{5,17},{6,24},{7,25},{8,2},{9,3},{1... | collective-permute-start | bytes 393224 | tf_op jit(solution)/shard_map/ppermute | solution.py:243
  18.1 25.8 %collective-permute-start.6 = (bf16[64,1024]{1,0:T(8,128)(2,1)S(1)}, bf16[64,1024]{1,0:T(8,128)(2,1)S(1)}, u32[]{:S(2)}, u32[]{:S(2)}) collective-permute-start(bf16[64,1024]{1,0:T(8,128)(2,1)S(1)} %bitcast.59), channel_id=1, source_target_pairs={{0,2},{1,3},{2,10},{3,11},{4,18},{5,19},{6,26},{7,27},{8,0},{9,1},... | collective-permute-start | bytes 393224 | tf_op jit(solution)/shard_map/ppermute | solution.py:243
  26.5 17.4 %collective-permute-start.7 = (bf16[64,1024]{1,0:T(8,128)(2,1)S(1)}, bf16[64,1024]{1,0:T(8,128)(2,1)S(1)}, u32[]{:S(2)}, u32[]{:S(2)}) collective-permute-start(bf16[64,1024]{1,0:T(8,128)(2,1)S(1)} %bitcast.60), channel_id=1, source_target_pairs={{0,4},{1,5},{2,12},{3,13},{4,20},{5,21},{6,28},{7,29},{8,6},{9,7},... | collective-permute-start | bytes 393224 | tf_op jit(solution)/shard_map/ppermute | solution.py:243
  31.7 12.2 %collective-permute-start.8 = (bf16[64,1024]{1,0:T(8,128)(2,1)S(1)}, bf16[64,1024]{1,0:T(8,128)(2,1)S(1)}, u32[]{:S(2)}, u32[]{:S(2)}) collective-permute-start(bf16[64,1024]{1,0:T(8,128)(2,1)S(1)} %bitcast.61), channel_id=1, source_target_pairs={{0,6},{1,7},{2,14},{3,15},{4,22},{5,23},{6,30},{7,31},{8,4},{9,5},... | collective-permute-start | bytes 393224 | tf_op jit(solution)/shard_map/ppermute | solution.py:243
  44.0 2.6 %collective-permute-start.16 = (bf16[4,64,1024]{2,1,0:T(8,128)(2,1)S(1)}, bf16[4,64,1024]{2,1,0:T(8,128)(2,1)S(1)}, u32[]{:S(2)}, u32[]{:S(2)}) collective-permute-start(bf16[4,64,1024]{2,1,0:T(8,128)(2,1)S(1)} %join.3.own_ref), channel_id=1, source_target_pairs={{0,1},{1,0},{2,3},{3,2},{4,5},{5,4},{6,7},{7,6},{8,9},{9,8},{10,11... | collective-permute-start | bytes 1572872 | tf_op jit(solution)/shard_map/ppermute | solution.py:243
  44.1 14.3 %collective-permute-start.9 = (bf16[2,64,2048]{2,1,0:T(8,128)(2,1)S(1)}, bf16[2,64,2048]{2,1,0:T(8,128)(2,1)S(1)}, u32[]{:S(2)}, u32[]{:S(2)}) collective-permute-start(bf16[2,64,2048]{2,1,0:T(8,128)(2,1)S(1)} %hold.2.refs_4_), channel_id=1, source_target_pairs={{0,16},{1,17},{2,18},{3,19},{4,20},{5,21},{6,22},{7,23},{8,24},{9,... | collective-permute-start | bytes 1572872 | tf_op jit(solution)/shard_map/ppermute | solution.py:243
  45.9 14.3 %collective-permute-start.10 = (bf16[2,64,2048]{2,1,0:T(8,128)(2,1)S(1)}, bf16[2,64,2048]{2,1,0:T(8,128)(2,1)S(1)}, u32[]{:S(2)}, u32[]{:S(2)}) collective-permute-start(bf16[2,64,2048]{2,1,0:T(8,128)(2,1)S(1)} %get-tuple-element.24), channel_id=1, source_target_pairs={{0,8},{1,9},{2,10},{3,11},{4,12},{5,13},{6,14},{7,15},{8,0},{9,1},... | collective-permute-start | bytes 1572872 | tf_op jit(solution)/shard_map/ppermute | solution.py:243
  55.9 37.5 %copy-start = (s32[16,16]{1,0:T(8,128)S(1)}, s32[16,16]{1,0:T(8,128)}, u32[]{:S(2)}) copy-start(s32[16,16]{1,0:T(8,128)} %param.13) | copy-start | bytes 3076
  55.9 22.1 %collective-permute-start.17 = (bf16[2,64,2048]{2,1,0:T(8,128)(2,1)S(1)}, bf16[2,64,2048]{2,1,0:T(8,128)(2,1)S(1)}, u32[]{:S(2)}, u32[]{:S(2)}) collective-permute-start(bf16[2,64,2048]{2,1,0:T(8,128)(2,1)S(1)} %get-tuple-element.28), channel_id=1, source_target_pairs={{0,16},{1,17},{2,18},{3,19},{4,20},{5,21},{6,22},{7,23},{8,24},{9,... | collective-permute-start | bytes 1572872 | tf_op jit(solution)/shard_map/ppermute | solution.py:243
  57.1 20.9 %collective-permute-start.18 = (bf16[2,64,2048]{2,1,0:T(8,128)(2,1)S(1)}, bf16[2,64,2048]{2,1,0:T(8,128)(2,1)S(1)}, u32[]{:S(2)}, u32[]{:S(2)}) collective-permute-start(bf16[2,64,2048]{2,1,0:T(8,128)(2,1)S(1)} %get-tuple-element.30), channel_id=1, source_target_pairs={{0,8},{1,9},{2,10},{3,11},{4,12},{5,13},{6,14},{7,15},{8,0},{9,1},... | collective-permute-start | bytes 1572872 | tf_op jit(solution)/shard_map/ppermute | solution.py:243
  60.3 16.5 %collective-permute-start.11 = (bf16[1,64,2048]{2,1,0:T(8,128)(2,1)S(1)}, bf16[1,64,2048]{2,1,0:T(8,128)(2,1)S(1)}, u32[]{:S(2)}, u32[]{:S(2)}) collective-permute-start(bf16[1,64,2048]{2,1,0:T(8,128)(2,1)S(1)} %get-tuple-element.25), channel_id=1, source_target_pairs={{0,8},{1,9},{2,10},{3,11},{4,12},{5,13},{6,14},{7,15},{8,0},{9,1},... | collective-permute-start | bytes 786440 | tf_op jit(solution)/shard_map/ppermute | solution.py:243
  61.0 15.7 %collective-permute-start.12 = (bf16[1,64,2048]{2,1,0:T(8,128)(2,1)S(1)}, bf16[1,64,2048]{2,1,0:T(8,128)(2,1)S(1)}, u32[]{:S(2)}, u32[]{:S(2)}) collective-permute-start(bf16[1,64,2048]{2,1,0:T(8,128)(2,1)S(1)} %get-tuple-element.26), channel_id=1, source_target_pairs={{0,16},{1,17},{2,18},{3,19},{4,20},{5,21},{6,22},{7,23},{8,24},{9,... | collective-permute-start | bytes 786440 | tf_op jit(solution)/shard_map/ppermute | solution.py:243
  77.3 9.3 %collective-permute-start.13 = (bf16[64,2048]{1,0:T(8,128)(2,1)S(1)}, bf16[64,2048]{1,0:T(8,128)(2,1)S(1)}, u32[]{:S(2)}, u32[]{:S(2)}) collective-permute-start(bf16[64,2048]{1,0:T(8,128)(2,1)S(1)} %hidden.2.refs_0_), channel_id=1, source_target_pairs={{0,8},{1,17},{2,10},{3,19},{4,12},{5,21},{6,14},{7,23},{8,0},{9,25... | collective-permute-start | bytes 786440 | tf_op jit(solution)/shard_map/ppermute | solution.py:243
  78.1 14.0 %collective-permute-start.19 = (bf16[1,64,2048]{2,1,0:T(8,128)(2,1)S(1)}, bf16[1,64,2048]{2,1,0:T(8,128)(2,1)S(1)}, u32[]{:S(2)}, u32[]{:S(2)}) collective-permute-start(bf16[1,64,2048]{2,1,0:T(8,128)(2,1)S(1)} %get-tuple-element.31), channel_id=1, source_target_pairs={{0,8},{1,9},{2,10},{3,11},{4,12},{5,13},{6,14},{7,15},{8,0},{9,1},... | collective-permute-start | bytes 786440 | tf_op jit(solution)/shard_map/ppermute | solution.py:243
  79.5 12.6 %collective-permute-start.20 = (bf16[1,64,2048]{2,1,0:T(8,128)(2,1)S(1)}, bf16[1,64,2048]{2,1,0:T(8,128)(2,1)S(1)}, u32[]{:S(2)}, u32[]{:S(2)}) collective-permute-start(bf16[1,64,2048]{2,1,0:T(8,128)(2,1)S(1)} %get-tuple-element.32), channel_id=1, source_target_pairs={{0,16},{1,17},{2,18},{3,19},{4,20},{5,21},{6,22},{7,23},{8,24},{9,... | collective-permute-start | bytes 786440 | tf_op jit(solution)/shard_map/ppermute | solution.py:243
  79.8 13.7 %collective-permute-start.14 = (bf16[64,2048]{1,0:T(8,128)(2,1)S(1)}, bf16[64,2048]{1,0:T(8,128)(2,1)S(1)}, u32[]{:S(2)}, u32[]{:S(2)}) collective-permute-start(bf16[64,2048]{1,0:T(8,128)(2,1)S(1)} %hidden.2.refs_0_), channel_id=1, source_target_pairs={{0,16},{1,9},{2,18},{3,11},{4,20},{5,13},{6,22},{7,15},{8,24},{9,1... | collective-permute-start | bytes 786440 | tf_op jit(solution)/shard_map/ppermute | solution.py:243
  86.5 9.6 %collective-permute-start.15 = (bf16[64,2048]{1,0:T(8,128)(2,1)S(1)}, bf16[64,2048]{1,0:T(8,128)(2,1)S(1)}, u32[]{:S(2)}, u32[]{:S(2)}) collective-permute-start(bf16[64,2048]{1,0:T(8,128)(2,1)S(1)} %collective-permute-done.13.refs_1_), channel_id=1, source_target_pairs={{0,16},{1,9},{2,18},{3,11},{4,20},{5,13},{6,22},{7,15},{8,24},{9,1... | collective-permute-start | bytes 786440 | tf_op jit(solution)/shard_map/ppermute | solution.py:243
  92.7 6.4 %collective-permute-start.21 = (bf16[64,2048]{1,0:T(8,128)(2,1)S(1)}, bf16[64,2048]{1,0:T(8,128)(2,1)S(1)}, u32[]{:S(2)}, u32[]{:S(2)}) collective-permute-start(bf16[64,2048]{1,0:T(8,128)(2,1)S(1)} %hidden.3.refs_0_), channel_id=1, source_target_pairs={{0,8},{1,17},{2,10},{3,19},{4,12},{5,21},{6,14},{7,23},{8,0},{9,25... | collective-permute-start | bytes 786440 | tf_op jit(solution)/shard_map/ppermute | solution.py:243
  105.3 2.2 %collective-permute-start.22 = (bf16[4,32,2048]{2,1,0:T(8,128)(2,1)S(1)}, bf16[4,32,2048]{2,1,0:T(8,128)(2,1)S(1)}, u32[]{:S(2)}, u32[]{:S(2)}) collective-permute-start(bf16[4,32,2048]{2,1,0:T(8,128)(2,1)S(1)} %get-tuple-element.34), channel_id=1, source_target_pairs={{0,1},{1,0},{2,3},{3,2},{4,5},{5,4},{6,7},{7,6},{8,9},{9,8},{10,11... | collective-permute-start | bytes 1572872 | tf_op jit(solution)/shard_map/ppermute | solution.py:243
  105.4 6.6 %collective-permute-start.26 = (bf16[64,2048]{1,0:T(8,128)(2,1)S(1)}, bf16[64,2048]{1,0:T(8,128)(2,1)S(1)}, u32[]{:S(2)}, u32[]{:S(2)}) collective-permute-start(bf16[64,2048]{1,0:T(8,128)(2,1)S(1)} %hidden.3.refs_0_), channel_id=1, source_target_pairs={{0,16},{1,9},{2,18},{3,11},{4,20},{5,13},{6,22},{7,15},{8,24},{9,1... | collective-permute-start | bytes 786440 | tf_op jit(solution)/shard_map/ppermute | solution.py:243
  105.8 8.9 %collective-permute-start.27 = (bf16[64,2048]{1,0:T(8,128)(2,1)S(1)}, bf16[64,2048]{1,0:T(8,128)(2,1)S(1)}, u32[]{:S(2)}, u32[]{:S(2)}) collective-permute-start(bf16[64,2048]{1,0:T(8,128)(2,1)S(1)} %collective-permute-done.21.refs_6_.refs_1_), channel_id=1, source_target_pairs={{0,16},{1,9},{2,18},{3,11},{4,20},{5,13},{6,22},{7,15},{8,24},{9,1... | collective-permute-start | bytes 786440 | tf_op jit(solution)/shard_map/ppermute | solution.py:243
  107.6 13.3 %collective-permute-start.23 = (bf16[32,2048]{1,0:T(8,128)(2,1)S(1)}, bf16[32,2048]{1,0:T(8,128)(2,1)S(1)}, u32[]{:S(2)}, u32[]{:S(2)}) collective-permute-start(bf16[32,2048]{1,0:T(8,128)(2,1)S(1)} %get-tuple-element.42), channel_id=1, source_target_pairs={{0,2},{1,3},{2,0},{3,1},{4,6},{5,7},{6,4},{7,5},{8,10},{9,11},{10,... | collective-permute-start | bytes 393224 | tf_op jit(solution)/shard_map/ppermute | solution.py:243
  109.1 12.7 %collective-permute-start.24 = (bf16[32,2048]{1,0:T(8,128)(2,1)S(1)}, bf16[32,2048]{1,0:T(8,128)(2,1)S(1)}, u32[]{:S(2)}, u32[]{:S(2)}) collective-permute-start(bf16[32,2048]{1,0:T(8,128)(2,1)S(1)} %get-tuple-element.41), channel_id=1, source_target_pairs={{0,4},{1,5},{2,6},{3,7},{4,0},{5,1},{6,2},{7,3},{8,12},{9,13},{10,... | collective-permute-start | bytes 393224 | tf_op jit(solution)/shard_map/ppermute | solution.py:243
  110.2 11.7 %collective-permute-start.25 = (bf16[32,2048]{1,0:T(8,128)(2,1)S(1)}, bf16[32,2048]{1,0:T(8,128)(2,1)S(1)}, u32[]{:S(2)}, u32[]{:S(2)}) collective-permute-start(bf16[32,2048]{1,0:T(8,128)(2,1)S(1)} %get-tuple-element.40), channel_id=1, source_target_pairs={{0,6},{1,7},{2,4},{3,5},{4,2},{5,3},{6,0},{7,1},{8,14},{9,15},{10,... | collective-permute-start | bytes 393224 | tf_op jit(solution)/shard_map/ppermute | solution.py:243
  121.9 2.0 %collective-permute-start.28 = (bf16[4,32,2048]{2,1,0:T(8,128)(2,1)S(1)}, bf16[4,32,2048]{2,1,0:T(8,128)(2,1)S(1)}, u32[]{:S(2)}, u32[]{:S(2)}) collective-permute-start(bf16[4,32,2048]{2,1,0:T(8,128)(2,1)S(1)} %hold.3), channel_id=1, source_target_pairs={{0,1},{1,0},{2,3},{3,2},{4,5},{5,4},{6,7},{7,6},{8,9},{9,8},{10,11... | collective-permute-start | bytes 1572872 | tf_op jit(solution)/shard_map/ppermute | solution.py:243
  123.9 7.6 %collective-permute-start.29 = (bf16[32,2048]{1,0:T(8,128)(2,1)S(1)}, bf16[32,2048]{1,0:T(8,128)(2,1)S(1)}, u32[]{:S(2)}, u32[]{:S(2)}) collective-permute-start(bf16[32,2048]{1,0:T(8,128)(2,1)S(1)} %get-tuple-element.37), channel_id=1, source_target_pairs={{0,2},{1,3},{2,0},{3,1},{4,6},{5,7},{6,4},{7,5},{8,10},{9,11},{10,... | collective-permute-start | bytes 393224 | tf_op jit(solution)/shard_map/ppermute | solution.py:243
  126.2 12.9 %collective-permute-start.30 = (bf16[32,2048]{1,0:T(8,128)(2,1)S(1)}, bf16[32,2048]{1,0:T(8,128)(2,1)S(1)}, u32[]{:S(2)}, u32[]{:S(2)}) collective-permute-start(bf16[32,2048]{1,0:T(8,128)(2,1)S(1)} %get-tuple-element.39), channel_id=1, source_target_pairs={{0,4},{1,5},{2,6},{3,7},{4,0},{5,1},{6,2},{7,3},{8,12},{9,13},{10,... | collective-permute-start | bytes 393224 | tf_op jit(solution)/shard_map/ppermute | solution.py:243
  126.6 12.5 %collective-permute-start.31 = (bf16[32,2048]{1,0:T(8,128)(2,1)S(1)}, bf16[32,2048]{1,0:T(8,128)(2,1)S(1)}, u32[]{:S(2)}, u32[]{:S(2)}) collective-permute-start(bf16[32,2048]{1,0:T(8,128)(2,1)S(1)} %get-tuple-element.38), channel_id=1, source_target_pairs={{0,6},{1,7},{2,4},{3,5},{4,2},{5,3},{6,0},{7,1},{8,14},{9,15},{10,... | collective-permute-start | bytes 393224 | tf_op jit(solution)/shard_map/ppermute | solution.py:243

commit v7 on v6

--- a/solution.py
+++ b/solution.py
@@ -259,7 +259,7 @@
             gate_parts.append(send(gate_sent, lambda t, zz, c: (t ^ left, zz, c)))
             up_parts.append(send(up_sent, lambda t, zz, c: (t ^ turned, zz, c)))
             if left == 1:
-                return gate_parts, up_parts
+                return gate_parts, up_parts, gate_sent
             left //= 2
             gate_sent, up_sent = add_slots(gate_parts, up_parts, left, left, after)
 
@@ -294,13 +294,20 @@
         gate_sent = hold(gate_sent, [part for later in moved[s + 1 : s + 2] for part in later])
         sums.append((gate_kept, up_kept, gate_sent, up_sent))
         before = [gate_sent]
-    hidden = [gather(activate(*halve(*terms, ()), ())) for terms in sums]
-    out, arrived = [], []
-    for s, parts in enumerate(hidden):
-        mine, theirs = down(place, parts, down_weight, down_wide, [later[1] for later in hidden[s + 1 : s + 2]])
-        total, sent = combine(mine, hold(theirs, arrived))
-        arrived = [across_z(sent[j - 1], j) for j in range(1, n_z)]
-        for part in arrived:
+    out, beside = [], []
+    halved = halve(*sums[0], [later[2] for later in sums[1:2]])
+    for s in range(BATCHES):
+        gate_parts, up_parts, _ = halved
+        parts = gather(activate(gate_parts, up_parts, ()))
+        before_down = []
+        if s + 1 < BATCHES:
+            halved = halve(*sums[s + 1], [parts[1]] + [later[2] for later in sums[s + 2 : s + 3]])
+            before_down = [halved[2]]
+            beside = beside + [halved[0][-1], halved[1][-1]]
+        mine, theirs = down(place, parts, down_weight, down_wide, before_down)
+        total, sent = combine(mine, hold(theirs, beside))
+        beside = [across_z(sent[j - 1], j) for j in range(1, n_z)]
+        for part in beside:
             total += part.astype(jnp.float32)
         out.append(total.astype(jnp.bfloat16))
     return jnp.concatenate(out, axis=0)

time: 140 us -> 141 us (level)
  starting transfers between devices: 49.9 us -> 52.3 us
  waiting for transfers between devices: 53.5 us -> 52 us
    ppermute x32, starting transfers between devices: 49.9 us -> 52.3 us  [send(): return lax.ppermute(value, AXES, perm)]
    ppermute x32, waiting for transfers between devices: 53.5 us -> 52 us  [send(): return lax.ppermute(value, AXES, perm)]
  transfers between devices with their start and end apart: 32 -> 32, of which waited for: 13 -> 13; matrix products, arithmetic and copies ran while one was open for 1% -> 1% of each run, Pallas kernels for 19% -> 23%
where the time goes in v7:
time: 141 us
  starting transfers between devices  52.3 us (37%)
  waiting for transfers between devices  52 us (37%)
  Pallas kernels  32.4 us (23%)
  other arithmetic  2.45 us (2%)
  local copies, waits for them, and re-layouts  1.48 us (1%)
    ppermute x32, starting transfers between devices, send(): return lax.ppermute(value, AXES, perm)  52.3 us
    ppermute x32, waiting for transfers between devices, send(): return lax.ppermute(value, AXES, perm)  52 us
    pallas_call x2, Pallas kernels, gate_up(): pl.pallas_call(gate_up_kernel, grid_spec=pltpu.PrefetchScalarGridSpec(num...  18.6 us
    pallas_call x2, Pallas kernels, down(): pl.pallas_call(functools.partial(down_kernel, n), grid_spec=pltpu.Prefetc...  12.5 us
  transfers between devices with their start and end apart: 32, of which 13 were waited for; matrix products, arithmetic and copies ran while one was open for 1% of the time, Pallas kernels for 23%

profile of v7, /device:TPU:0, one launch (start us, length us, event | category | flops | bytes accessed | tf_op | source)
XLA Modules:
  0.0 140.9 jit_solution(17307953902860159779)
XLA Ops:
  0.0 1.0 fusion.12
  1.0 0.7 collective-permute-start
  1.7 5.7 %collective-permute-start.1 = (bf16[64,1024]{1,0:T(8,128)(2,1)S(1)}, bf16[64,1024]{1,0:T(8,128)(2,1)S(1)}, u32[]{:S(2)}, u32[]{:S(2)}) collective-permute-start(bf16[64,1024]{1,0:T(8,128)(2,1)S(1)} %bitcast.63), channel_id=1, source_target_pairs={{0,2},{1,3},{2,10},{3,11},{4,18},{5,19},{6,26},{7,27},{8,0},{9,1},... | collective-permute-start | bytes 393224 | tf_op jit(solution)/shard_map/ppermute | solution.py:243
  7.4 3.5 %collective-permute-start.2 = (bf16[64,1024]{1,0:T(8,128)(2,1)S(1)}, bf16[64,1024]{1,0:T(8,128)(2,1)S(1)}, u32[]{:S(2)}, u32[]{:S(2)}) collective-permute-start(bf16[64,1024]{1,0:T(8,128)(2,1)S(1)} %bitcast.64), channel_id=1, source_target_pairs={{0,4},{1,5},{2,12},{3,13},{4,20},{5,21},{6,28},{7,29},{8,6},{9,7},... | collective-permute-start | bytes 393224 | tf_op jit(solution)/shard_map/ppermute | solution.py:243
  10.8 1.9 %collective-permute-start.3 = (bf16[64,1024]{1,0:T(8,128)(2,1)S(1)}, bf16[64,1024]{1,0:T(8,128)(2,1)S(1)}, u32[]{:S(2)}, u32[]{:S(2)}) collective-permute-start(bf16[64,1024]{1,0:T(8,128)(2,1)S(1)} %bitcast.65), channel_id=1, source_target_pairs={{0,6},{1,7},{2,14},{3,15},{4,22},{5,23},{6,30},{7,31},{8,4},{9,5},... | collective-permute-start | bytes 393224 | tf_op jit(solution)/shard_map/ppermute | solution.py:243
  12.8 4.6 %collective-permute-done.2.refs_2_ = bf16[64,1024]{1,0:T(8,128)(2,1)S(1)} collective-permute-done((bf16[64,1024]{1,0:T(8,128)(2,1)S(1)}, bf16[64,1024]{1,0:T(8,128)(2,1)S(1)}, u32[]{:S(2)}, u32[]{:S(2)}) %collective-permute-start.2) | collective-permute-done | bytes 131104 | tf_op jit(solution)/shard_map/ppermute | solution.py:243
  17.5 0.7 collective-permute-start.5
  18.1 8.4 %collective-permute-start.6 = (bf16[64,1024]{1,0:T(8,128)(2,1)S(1)}, bf16[64,1024]{1,0:T(8,128)(2,1)S(1)}, u32[]{:S(2)}, u32[]{:S(2)}) collective-permute-start(bf16[64,1024]{1,0:T(8,128)(2,1)S(1)} %bitcast.59), channel_id=1, source_target_pairs={{0,2},{1,3},{2,10},{3,11},{4,18},{5,19},{6,26},{7,27},{8,0},{9,1},... | collective-permute-start | bytes 393224 | tf_op jit(solution)/shard_map/ppermute | solution.py:243
  26.5 5.2 %collective-permute-start.7 = (bf16[64,1024]{1,0:T(8,128)(2,1)S(1)}, bf16[64,1024]{1,0:T(8,128)(2,1)S(1)}, u32[]{:S(2)}, u32[]{:S(2)}) collective-permute-start(bf16[64,1024]{1,0:T(8,128)(2,1)S(1)} %bitcast.60), channel_id=1, source_target_pairs={{0,4},{1,5},{2,12},{3,13},{4,20},{5,21},{6,28},{7,29},{8,6},{9,7},... | collective-permute-start | bytes 393224 | tf_op jit(solution)/shard_map/ppermute | solution.py:243
  31.7 1.1 collective-permute-start.8
  32.8 0.7 convert_element_type.101
  33.5 0.7 convert_element_type.102
  34.6 9.3 %gate_up.2 = (f32[2,64,2048]{2,1,0:T(8,128)S(1)}, f32[2,64,2048]{2,1,0:T(8,128)S(1)}, bf16[2,64,2048]{2,1,0:T(8,128)(2,1)S(1)}, bf16[2,64,2048]{2,1,0:T(8,128)(2,1)S(1)}) custom-call(s32[9]{0:T(128)S(1)} %stack.33.place_ref, bf16[4,64,1024]{2,1,0:T(8,128)(2,1)S(1)} %join.2.own_ref, bf16[4,64,1024]{2,1,0:T(8,128)(2,1)S(1)} %collective-permute-done.4.other_ref, ...), custom_call_target="tpu_custom_call" | custom-call | flops 4294967296 | bytes 16777216 | tf_op jit(solution)/shard_map/gate_up/pallas_call | solution.py:64
  44.1 1.8 %collective-permute-start.9 = (bf16[2,64,2048]{2,1,0:T(8,128)(2,1)S(1)}, bf16[2,64,2048]{2,1,0:T(8,128)(2,1)S(1)}, u32[]{:S(2)}, u32[]{:S(2)}) collective-permute-start(bf16[2,64,2048]{2,1,0:T(8,128)(2,1)S(1)} %hold.3.refs_4_), channel_id=1, source_target_pairs={{0,16},{1,17},{2,18},{3,19},{4,20},{5,21},{6,22},{7,23},{8,24},{9,... | collective-permute-start | bytes 1572872 | tf_op jit(solution)/shard_map/ppermute | solution.py:243
  45.9 0.7 collective-permute-start.10
  46.6 9.3 %gate_up.3 = (f32[2,64,2048]{2,1,0:T(8,128)S(1)}, f32[2,64,2048]{2,1,0:T(8,128)S(1)}, bf16[2,64,2048]{2,1,0:T(8,128)(2,1)S(1)}, bf16[2,64,2048]{2,1,0:T(8,128)(2,1)S(1)}) custom-call(s32[9]{0:T(128)S(1)} %stack.33.place_ref, bf16[4,64,1024]{2,1,0:T(8,128)(2,1)S(1)} %join.3.own_ref, bf16[4,64,1024]{2,1,0:T(8,128)(2,1)S(1)} %collective-permute-done.11.other_ref, ...), custom_call_target="tpu_custom_call" | custom-call | flops 4294967296 | bytes 16777216 | tf_op jit(solution)/shard_map/gate_up/pallas_call | solution.py:64
  55.9 2.6 %collective-permute-done.9.refs_1_ = bf16[2,64,2048]{2,1,0:T(8,128)(2,1)S(1)} collective-permute-done((bf16[2,64,2048]{2,1,0:T(8,128)(2,1)S(1)}, bf16[2,64,2048]{2,1,0:T(8,128)(2,1)S(1)}, u32[]{:S(2)}, u32[]{:S(2)}) %collective-permute-start.9) | collective-permute-done | bytes 524320 | tf_op jit(solution)/shard_map/ppermute | solution.py:243
  58.5 1.5 %collective-permute-done.10.refs_3_.refs_4_ = bf16[2,64,2048]{2,1,0:T(8,128)(2,1)S(1)} collective-permute-done((bf16[2,64,2048]{2,1,0:T(8,128)(2,1)S(1)}, bf16[2,64,2048]{2,1,0:T(8,128)(2,1)S(1)}, u32[]{:S(2)}, u32[]{:S(2)}) %collective-permute-start.10) | collective-permute-done | bytes 524320 | tf_op jit(solution)/shard_map/ppermute | solution.py:243
  60.0 0.7 collective-permute-start.12
  60.7 1.1 collective-permute-start.13
  61.8 0.9 collective-permute-start.17
  62.8 1.3 collective-permute-start.18
  64.1 5.2 %collective-permute-done.12.refs_2_ = bf16[1,64,2048]{2,1,0:T(8,128)(2,1)S(1)} collective-permute-done((bf16[1,64,2048]{2,1,0:T(8,128)(2,1)S(1)}, bf16[1,64,2048]{2,1,0:T(8,128)(2,1)S(1)}, u32[]{:S(2)}, u32[]{:S(2)}) %collective-permute-start.12) | collective-permute-done | bytes 262176 | tf_op jit(solution)/shard_map/ppermute | solution.py:243
  69.3 0.7 collective-permute-done.13.refs_5_
  70.5 1.4 %collective-permute-start.14 = (bf16[64,2048]{1,0:T(8,128)(2,1)S(1)}, bf16[64,2048]{1,0:T(8,128)(2,1)S(1)}, u32[]{:S(2)}, u32[]{:S(2)}) collective-permute-start(bf16[64,2048]{1,0:T(8,128)(2,1)S(1)} %hidden.2.refs_0_), channel_id=1, source_target_pairs={{0,8},{1,17},{2,10},{3,19},{4,12},{5,21},{6,14},{7,23},{8,0},{9,25... | collective-permute-start | bytes 786440 | tf_op jit(solution)/shard_map/ppermute | solution.py:243
  72.2 12.3 %collective-permute-done.14.refs_4_.refs_1_ = bf16[64,2048]{1,0:T(8,128)(2,1)S(1)} collective-permute-done((bf16[64,2048]{1,0:T(8,128)(2,1)S(1)}, bf16[64,2048]{1,0:T(8,128)(2,1)S(1)}, u32[]{:S(2)}, u32[]{:S(2)}) %collective-permute-start.14) | collective-permute-done | bytes 262176 | tf_op jit(solution)/shard_map/ppermute | solution.py:243
  84.5 0.6 collective-permute-start.16
  85.2 1.2 collective-permute-start.19
  86.4 0.9 collective-permute-start.20
  87.5 5.3 %collective-permute-done.16.refs_3_ = bf16[64,2048]{1,0:T(8,128)(2,1)S(1)} collective-permute-done((bf16[64,2048]{1,0:T(8,128)(2,1)S(1)}, bf16[64,2048]{1,0:T(8,128)(2,1)S(1)}, u32[]{:S(2)}, u32[]{:S(2)}) %collective-permute-start.16) | collective-permute-done | bytes 262176 | tf_op jit(solution)/shard_map/ppermute | solution.py:243
  92.9 6.2 %down.2 = (f32[4,32,2048]{2,1,0:T(8,128)S(1)}, bf16[4,32,2048]{2,1,0:T(8,128)(2,1)S(1)}) custom-call(s32[9]{0:T(128)S(1)} %stack.33.place_ref, bf16[64,2048]{1,0:T(8,128)(2,1)S(1)} %hidden.2.refs_0_, bf16[64,2048]{1,0:T(8,128)(2,1)S(1)} %collective-permute-done.14.refs_4_.refs_1_, bf16[64,2048]{1,0:T(8,128)(2,1)S(1)} %collective-permute-done.15.refs_2_, ...), custom_call_target="tpu_custom_call" | custom-call | flops 2147483648 | bytes 8388608 | tf_op jit(solution)/shard_map/down/pallas_call | solution.py:161
  99.2 0.5 hidden.3.refs_0_
  99.8 1.4 %collective-permute-start.25 = (bf16[64,2048]{1,0:T(8,128)(2,1)S(1)}, bf16[64,2048]{1,0:T(8,128)(2,1)S(1)}, u32[]{:S(2)}, u32[]{:S(2)}) collective-permute-start(bf16[64,2048]{1,0:T(8,128)(2,1)S(1)} %hidden.3.refs_0_), channel_id=1, source_target_pairs={{0,8},{1,17},{2,10},{3,19},{4,12},{5,21},{6,14},{7,23},{8,0},{9,25... | collective-permute-start | bytes 786440 | tf_op jit(solution)/shard_map/ppermute | solution.py:243
  101.2 0.9 collective-permute-start.26
  102.1 6.6 %collective-permute-done.25.refs_1_ = bf16[64,2048]{1,0:T(8,128)(2,1)S(1)} collective-permute-done((bf16[64,2048]{1,0:T(8,128)(2,1)S(1)}, bf16[64,2048]{1,0:T(8,128)(2,1)S(1)}, u32[]{:S(2)}, u32[]{:S(2)}) %collective-permute-start.25) | collective-permute-done | bytes 262176 | tf_op jit(solution)/shard_map/ppermute | solution.py:243
  108.7 1.2 collective-permute-start.27
  110.0 1.3 collective-permute-start.22
  111.3 1.5 %collective-permute-start.23 = (bf16[32,2048]{1,0:T(8,128)(2,1)S(1)}, bf16[32,2048]{1,0:T(8,128)(2,1)S(1)}, u32[]{:S(2)}, u32[]{:S(2)}) collective-permute-start(bf16[32,2048]{1,0:T(8,128)(2,1)S(1)} %get-tuple-element.41), channel_id=1, source_target_pairs={{0,4},{1,5},{2,6},{3,7},{4,0},{5,1},{6,2},{7,3},{8,12},{9,13},{10,... | collective-permute-start | bytes 393224 | tf_op jit(solution)/shard_map/ppermute | solution.py:243
  112.8 1.7 %collective-permute-start.24 = (bf16[32,2048]{1,0:T(8,128)(2,1)S(1)}, bf16[32,2048]{1,0:T(8,128)(2,1)S(1)}, u32[]{:S(2)}, u32[]{:S(2)}) collective-permute-start(bf16[32,2048]{1,0:T(8,128)(2,1)S(1)} %get-tuple-element.40), channel_id=1, source_target_pairs={{0,6},{1,7},{2,4},{3,5},{4,2},{5,3},{6,0},{7,1},{8,14},{9,15},{10,... | collective-permute-start | bytes 393224 | tf_op jit(solution)/shard_map/ppermute | solution.py:243
  114.5 0.6 collective-permute-done.27.refs_3_
  115.1 6.2 %down.3 = (f32[4,32,2048]{2,1,0:T(8,128)S(1)}, bf16[4,32,2048]{2,1,0:T(8,128)(2,1)S(1)}) custom-call(s32[9]{0:T(128)S(1)} %stack.33.place_ref, bf16[64,2048]{1,0:T(8,128)(2,1)S(1)} %hidden.3.refs_0_, bf16[64,2048]{1,0:T(8,128)(2,1)S(1)} %collective-permute-done.25.refs_1_, bf16[64,2048]{1,0:T(8,128)(2,1)S(1)} %collective-permute-done.26.refs_2_, ...), custom_call_target="tpu_custom_call" | custom-call | flops 2147483648 | bytes 8388608 | tf_op jit(solution)/shard_map/down/pallas_call | solution.py:161
  121.3 0.6 collective-permute-done.23.refs_1_
  122.1 1.9 %collective-permute-done.28 = bf16[4,32,2048]{2,1,0:T(8,128)(2,1)S(1)} collective-permute-done((bf16[4,32,2048]{2,1,0:T(8,128)(2,1)S(1)}, bf16[4,32,2048]{2,1,0:T(8,128)(2,1)S(1)}, u32[]{:S(2)}, u32[]{:S(2)}) %collective-permute-start.28) | collective-permute-done | bytes 524320 | tf_op jit(solution)/shard_map/ppermute | solution.py:243
  124.1 3.3 %collective-permute-start.29 = (bf16[32,2048]{1,0:T(8,128)(2,1)S(1)}, bf16[32,2048]{1,0:T(8,128)(2,1)S(1)}, u32[]{:S(2)}, u32[]{:S(2)}) collective-permute-start(bf16[32,2048]{1,0:T(8,128)(2,1)S(1)} %get-tuple-element.37), channel_id=1, source_target_pairs={{0,2},{1,3},{2,0},{3,1},{4,6},{5,7},{6,4},{7,5},{8,10},{9,11},{10,... | collective-permute-start | bytes 393224 | tf_op jit(solution)/shard_map/ppermute | solution.py:243
  127.4 2.4 %collective-permute-start.31 = (bf16[32,2048]{1,0:T(8,128)(2,1)S(1)}, bf16[32,2048]{1,0:T(8,128)(2,1)S(1)}, u32[]{:S(2)}, u32[]{:S(2)}) collective-permute-start(bf16[32,2048]{1,0:T(8,128)(2,1)S(1)} %get-tuple-element.38), channel_id=1, source_target_pairs={{0,6},{1,7},{2,4},{3,5},{4,2},{5,3},{6,0},{7,1},{8,14},{9,15},{10,... | collective-permute-start | bytes 393224 | tf_op jit(solution)/shard_map/ppermute | solution.py:243
  129.9 2.4 %collective-permute-done.29 = bf16[32,2048]{1,0:T(8,128)(2,1)S(1)} collective-permute-done((bf16[32,2048]{1,0:T(8,128)(2,1)S(1)}, bf16[32,2048]{1,0:T(8,128)(2,1)S(1)}, u32[]{:S(2)}, u32[]{:S(2)}) %collective-permute-start.29) | collective-permute-done | bytes 131104 | tf_op jit(solution)/shard_map/ppermute | solution.py:243
  132.3 7.8 %collective-permute-done.30 = bf16[32,2048]{1,0:T(8,128)(2,1)S(1)} collective-permute-done((bf16[32,2048]{1,0:T(8,128)(2,1)S(1)}, bf16[32,2048]{1,0:T(8,128)(2,1)S(1)}, u32[]{:S(2)}, u32[]{:S(2)}) %collective-permute-start.30) | collective-permute-done | bytes 131104 | tf_op jit(solution)/shard_map/ppermute | solution.py:243
  140.2 0.7 pad_maximum_fusion
  (46 shorter events, 2.3 us)
Async XLA Ops:
  1.0 11.8 %collective-permute-start = (bf16[64,1024]{1,0:T(8,128)(2,1)S(1)}, bf16[64,1024]{1,0:T(8,128)(2,1)S(1)}, u32[]{:S(2)}, u32[]{:S(2)}) collective-permute-start(bf16[64,1024]{1,0:T(8,128)(2,1)S(1)} %bitcast.62), channel_id=1, source_target_pairs={{0,0},{1,1},{2,8},{3,9},{4,16},{5,17},{6,24},{7,25},{8,2},{9,3},{1... | collective-permute-start | bytes 393224 | tf_op jit(solution)/shard_map/ppermute | solution.py:243
  1.7 11.1 %collective-permute-start.1 = (bf16[64,1024]{1,0:T(8,128)(2,1)S(1)}, bf16[64,1024]{1,0:T(8,128)(2,1)S(1)}, u32[]{:S(2)}, u32[]{:S(2)}) collective-permute-start(bf16[64,1024]{1,0:T(8,128)(2,1)S(1)} %bitcast.63), channel_id=1, source_target_pairs={{0,2},{1,3},{2,10},{3,11},{4,18},{5,19},{6,26},{7,27},{8,0},{9,1},... | collective-permute-start | bytes 393224 | tf_op jit(solution)/shard_map/ppermute | solution.py:243
  7.4 10.0 %collective-permute-start.2 = (bf16[64,1024]{1,0:T(8,128)(2,1)S(1)}, bf16[64,1024]{1,0:T(8,128)(2,1)S(1)}, u32[]{:S(2)}, u32[]{:S(2)}) collective-permute-start(bf16[64,1024]{1,0:T(8,128)(2,1)S(1)} %bitcast.64), channel_id=1, source_target_pairs={{0,4},{1,5},{2,12},{3,13},{4,20},{5,21},{6,28},{7,29},{8,6},{9,7},... | collective-permute-start | bytes 393224 | tf_op jit(solution)/shard_map/ppermute | solution.py:243
  10.8 6.5 %collective-permute-start.3 = (bf16[64,1024]{1,0:T(8,128)(2,1)S(1)}, bf16[64,1024]{1,0:T(8,128)(2,1)S(1)}, u32[]{:S(2)}, u32[]{:S(2)}) collective-permute-start(bf16[64,1024]{1,0:T(8,128)(2,1)S(1)} %bitcast.65), channel_id=1, source_target_pairs={{0,6},{1,7},{2,14},{3,15},{4,22},{5,23},{6,30},{7,31},{8,4},{9,5},... | collective-permute-start | bytes 393224 | tf_op jit(solution)/shard_map/ppermute | solution.py:243
  17.4 17.2 %collective-permute-start.4 = (bf16[4,64,1024]{2,1,0:T(8,128)(2,1)S(1)}, bf16[4,64,1024]{2,1,0:T(8,128)(2,1)S(1)}, u32[]{:S(2)}, u32[]{:S(2)}) collective-permute-start(bf16[4,64,1024]{2,1,0:T(8,128)(2,1)S(1)} %join.2.own_ref), channel_id=1, source_target_pairs={{0,1},{1,0},{2,3},{3,2},{4,5},{5,4},{6,7},{7,6},{8,9},{9,8},{10,11... | collective-permute-start | bytes 1572872 | tf_op jit(solution)/shard_map/ppermute | solution.py:243
  17.5 26.4 %collective-permute-start.5 = (bf16[64,1024]{1,0:T(8,128)(2,1)S(1)}, bf16[64,1024]{1,0:T(8,128)(2,1)S(1)}, u32[]{:S(2)}, u32[]{:S(2)}) collective-permute-start(bf16[64,1024]{1,0:T(8,128)(2,1)S(1)} %bitcast.58), channel_id=1, source_target_pairs={{0,0},{1,1},{2,8},{3,9},{4,16},{5,17},{6,24},{7,25},{8,2},{9,3},{1... | collective-permute-start | bytes 393224 | tf_op jit(solution)/shard_map/ppermute | solution.py:243
  18.1 25.8 %collective-permute-start.6 = (bf16[64,1024]{1,0:T(8,128)(2,1)S(1)}, bf16[64,1024]{1,0:T(8,128)(2,1)S(1)}, u32[]{:S(2)}, u32[]{:S(2)}) collective-permute-start(bf16[64,1024]{1,0:T(8,128)(2,1)S(1)} %bitcast.59), channel_id=1, source_target_pairs={{0,2},{1,3},{2,10},{3,11},{4,18},{5,19},{6,26},{7,27},{8,0},{9,1},... | collective-permute-start | bytes 393224 | tf_op jit(solution)/shard_map/ppermute | solution.py:243
  26.5 17.4 %collective-permute-start.7 = (bf16[64,1024]{1,0:T(8,128)(2,1)S(1)}, bf16[64,1024]{1,0:T(8,128)(2,1)S(1)}, u32[]{:S(2)}, u32[]{:S(2)}) collective-permute-start(bf16[64,1024]{1,0:T(8,128)(2,1)S(1)} %bitcast.60), channel_id=1, source_target_pairs={{0,4},{1,5},{2,12},{3,13},{4,20},{5,21},{6,28},{7,29},{8,6},{9,7},... | collective-permute-start | bytes 393224 | tf_op jit(solution)/shard_map/ppermute | solution.py:243
  31.7 12.2 %collective-permute-start.8 = (bf16[64,1024]{1,0:T(8,128)(2,1)S(1)}, bf16[64,1024]{1,0:T(8,128)(2,1)S(1)}, u32[]{:S(2)}, u32[]{:S(2)}) collective-permute-start(bf16[64,1024]{1,0:T(8,128)(2,1)S(1)} %bitcast.61), channel_id=1, source_target_pairs={{0,6},{1,7},{2,14},{3,15},{4,22},{5,23},{6,30},{7,31},{8,4},{9,5},... | collective-permute-start | bytes 393224 | tf_op jit(solution)/shard_map/ppermute | solution.py:243
  44.0 2.6 %collective-permute-start.11 = (bf16[4,64,1024]{2,1,0:T(8,128)(2,1)S(1)}, bf16[4,64,1024]{2,1,0:T(8,128)(2,1)S(1)}, u32[]{:S(2)}, u32[]{:S(2)}) collective-permute-start(bf16[4,64,1024]{2,1,0:T(8,128)(2,1)S(1)} %join.3.own_ref), channel_id=1, source_target_pairs={{0,1},{1,0},{2,3},{3,2},{4,5},{5,4},{6,7},{7,6},{8,9},{9,8},{10,11... | collective-permute-start | bytes 1572872 | tf_op jit(solution)/shard_map/ppermute | solution.py:243
  44.1 14.3 %collective-permute-start.9 = (bf16[2,64,2048]{2,1,0:T(8,128)(2,1)S(1)}, bf16[2,64,2048]{2,1,0:T(8,128)(2,1)S(1)}, u32[]{:S(2)}, u32[]{:S(2)}) collective-permute-start(bf16[2,64,2048]{2,1,0:T(8,128)(2,1)S(1)} %hold.3.refs_4_), channel_id=1, source_target_pairs={{0,16},{1,17},{2,18},{3,19},{4,20},{5,21},{6,22},{7,23},{8,24},{9,... | collective-permute-start | bytes 1572872 | tf_op jit(solution)/shard_map/ppermute | solution.py:243
  45.9 14.0 %collective-permute-start.10 = (bf16[2,64,2048]{2,1,0:T(8,128)(2,1)S(1)}, bf16[2,64,2048]{2,1,0:T(8,128)(2,1)S(1)}, u32[]{:S(2)}, u32[]{:S(2)}) collective-permute-start(bf16[2,64,2048]{2,1,0:T(8,128)(2,1)S(1)} %get-tuple-element.24), channel_id=1, source_target_pairs={{0,8},{1,9},{2,10},{3,11},{4,12},{5,13},{6,14},{7,15},{8,0},{9,1},... | collective-permute-start | bytes 1572872 | tf_op jit(solution)/shard_map/ppermute | solution.py:243
  55.9 31.5 %copy-start = (s32[16,16]{1,0:T(8,128)S(1)}, s32[16,16]{1,0:T(8,128)}, u32[]{:S(2)}) copy-start(s32[16,16]{1,0:T(8,128)} %param.13) | copy-start | bytes 3076
  60.0 9.3 %collective-permute-start.12 = (bf16[1,64,2048]{2,1,0:T(8,128)(2,1)S(1)}, bf16[1,64,2048]{2,1,0:T(8,128)(2,1)S(1)}, u32[]{:S(2)}, u32[]{:S(2)}) collective-permute-start(bf16[1,64,2048]{2,1,0:T(8,128)(2,1)S(1)} %get-tuple-element.26), channel_id=1, source_target_pairs={{0,8},{1,9},{2,10},{3,11},{4,12},{5,13},{6,14},{7,15},{8,0},{9,1},... | collective-permute-start | bytes 786440 | tf_op jit(solution)/shard_map/ppermute | solution.py:243
  60.7 9.2 %collective-permute-start.13 = (bf16[1,64,2048]{2,1,0:T(8,128)(2,1)S(1)}, bf16[1,64,2048]{2,1,0:T(8,128)(2,1)S(1)}, u32[]{:S(2)}, u32[]{:S(2)}) collective-permute-start(bf16[1,64,2048]{2,1,0:T(8,128)(2,1)S(1)} %get-tuple-element.27), channel_id=1, source_target_pairs={{0,16},{1,17},{2,18},{3,19},{4,20},{5,21},{6,22},{7,23},{8,24},{9,... | collective-permute-start | bytes 786440 | tf_op jit(solution)/shard_map/ppermute | solution.py:243
  61.8 23.3 %collective-permute-start.17 = (bf16[2,64,2048]{2,1,0:T(8,128)(2,1)S(1)}, bf16[2,64,2048]{2,1,0:T(8,128)(2,1)S(1)}, u32[]{:S(2)}, u32[]{:S(2)}) collective-permute-start(bf16[2,64,2048]{2,1,0:T(8,128)(2,1)S(1)} %get-tuple-element.25.refs_4_), channel_id=1, source_target_pairs={{0,16},{1,17},{2,18},{3,19},{4,20},{5,21},{6,22},{7,23},{8,24},{9,... | collective-permute-start | bytes 1572872 | tf_op jit(solution)/shard_map/ppermute | solution.py:243
  62.8 22.3 %collective-permute-start.18 = (bf16[2,64,2048]{2,1,0:T(8,128)(2,1)S(1)}, bf16[2,64,2048]{2,1,0:T(8,128)(2,1)S(1)}, u32[]{:S(2)}, u32[]{:S(2)}) collective-permute-start(bf16[2,64,2048]{2,1,0:T(8,128)(2,1)S(1)} %get-tuple-element.30), channel_id=1, source_target_pairs={{0,8},{1,9},{2,10},{3,11},{4,12},{5,13},{6,14},{7,15},{8,0},{9,1},... | collective-permute-start | bytes 1572872 | tf_op jit(solution)/shard_map/ppermute | solution.py:243
  70.5 14.0 %collective-permute-start.14 = (bf16[64,2048]{1,0:T(8,128)(2,1)S(1)}, bf16[64,2048]{1,0:T(8,128)(2,1)S(1)}, u32[]{:S(2)}, u32[]{:S(2)}) collective-permute-start(bf16[64,2048]{1,0:T(8,128)(2,1)S(1)} %hidden.2.refs_0_), channel_id=1, source_target_pairs={{0,8},{1,17},{2,10},{3,19},{4,12},{5,21},{6,14},{7,23},{8,0},{9,25... | collective-permute-start | bytes 786440 | tf_op jit(solution)/shard_map/ppermute | solution.py:243
  71.9 15.6 %collective-permute-start.15 = (bf16[64,2048]{1,0:T(8,128)(2,1)S(1)}, bf16[64,2048]{1,0:T(8,128)(2,1)S(1)}, u32[]{:S(2)}, u32[]{:S(2)}) collective-permute-start(bf16[64,2048]{1,0:T(8,128)(2,1)S(1)} %hidden.2.refs_0_), channel_id=1, source_target_pairs={{0,16},{1,9},{2,18},{3,11},{4,20},{5,13},{6,22},{7,15},{8,24},{9,1... | collective-permute-start | bytes 786440 | tf_op jit(solution)/shard_map/ppermute | solution.py:243
  84.5 8.4 %collective-permute-start.16 = (bf16[64,2048]{1,0:T(8,128)(2,1)S(1)}, bf16[64,2048]{1,0:T(8,128)(2,1)S(1)}, u32[]{:S(2)}, u32[]{:S(2)}) collective-permute-start(bf16[64,2048]{1,0:T(8,128)(2,1)S(1)} %collective-permute-done.14.refs_4_.refs_1_), channel_id=1, source_target_pairs={{0,16},{1,9},{2,18},{3,11},{4,20},{5,13},{6,22},{7,15},{8,24},{9,1... | collective-permute-start | bytes 786440 | tf_op jit(solution)/shard_map/ppermute | solution.py:243
  85.2 13.9 %collective-permute-start.19 = (bf16[1,64,2048]{2,1,0:T(8,128)(2,1)S(1)}, bf16[1,64,2048]{2,1,0:T(8,128)(2,1)S(1)}, u32[]{:S(2)}, u32[]{:S(2)}) collective-permute-start(bf16[1,64,2048]{2,1,0:T(8,128)(2,1)S(1)} %get-tuple-element.31.refs_6_), channel_id=1, source_target_pairs={{0,8},{1,9},{2,10},{3,11},{4,12},{5,13},{6,14},{7,15},{8,0},{9,1},... | collective-permute-start | bytes 786440 | tf_op jit(solution)/shard_map/ppermute | solution.py:243
  86.4 12.7 %collective-permute-start.20 = (bf16[1,64,2048]{2,1,0:T(8,128)(2,1)S(1)}, bf16[1,64,2048]{2,1,0:T(8,128)(2,1)S(1)}, u32[]{:S(2)}, u32[]{:S(2)}) collective-permute-start(bf16[1,64,2048]{2,1,0:T(8,128)(2,1)S(1)} %get-tuple-element.34), channel_id=1, source_target_pairs={{0,16},{1,17},{2,18},{3,19},{4,20},{5,21},{6,22},{7,23},{8,24},{9,... | collective-permute-start | bytes 786440 | tf_op jit(solution)/shard_map/ppermute | solution.py:243
  99.2 10.7 %collective-permute-start.21 = (bf16[4,32,2048]{2,1,0:T(8,128)(2,1)S(1)}, bf16[4,32,2048]{2,1,0:T(8,128)(2,1)S(1)}, u32[]{:S(2)}, u32[]{:S(2)}) collective-permute-start(bf16[4,32,2048]{2,1,0:T(8,128)(2,1)S(1)} %hold.4), channel_id=1, source_target_pairs={{0,1},{1,0},{2,3},{3,2},{4,5},{5,4},{6,7},{7,6},{8,9},{9,8},{10,11... | collective-permute-start | bytes 1572872 | tf_op jit(solution)/shard_map/ppermute | solution.py:243
  99.8 8.9 %collective-permute-start.25 = (bf16[64,2048]{1,0:T(8,128)(2,1)S(1)}, bf16[64,2048]{1,0:T(8,128)(2,1)S(1)}, u32[]{:S(2)}, u32[]{:S(2)}) collective-permute-start(bf16[64,2048]{1,0:T(8,128)(2,1)S(1)} %hidden.3.refs_0_), channel_id=1, source_target_pairs={{0,8},{1,17},{2,10},{3,19},{4,12},{5,21},{6,14},{7,23},{8,0},{9,25... | collective-permute-start | bytes 786440 | tf_op jit(solution)/shard_map/ppermute | solution.py:243
  101.2 13.3 %collective-permute-start.26 = (bf16[64,2048]{1,0:T(8,128)(2,1)S(1)}, bf16[64,2048]{1,0:T(8,128)(2,1)S(1)}, u32[]{:S(2)}, u32[]{:S(2)}) collective-permute-start(bf16[64,2048]{1,0:T(8,128)(2,1)S(1)} %hidden.3.refs_0_), channel_id=1, source_target_pairs={{0,16},{1,9},{2,18},{3,11},{4,20},{5,13},{6,22},{7,15},{8,24},{9,1... | collective-permute-start | bytes 786440 | tf_op jit(solution)/shard_map/ppermute | solution.py:243
  108.7 6.4 %collective-permute-start.27 = (bf16[64,2048]{1,0:T(8,128)(2,1)S(1)}, bf16[64,2048]{1,0:T(8,128)(2,1)S(1)}, u32[]{:S(2)}, u32[]{:S(2)}) collective-permute-start(bf16[64,2048]{1,0:T(8,128)(2,1)S(1)} %collective-permute-done.25.refs_1_), channel_id=1, source_target_pairs={{0,16},{1,9},{2,18},{3,11},{4,20},{5,13},{6,22},{7,15},{8,24},{9,1... | collective-permute-start | bytes 786440 | tf_op jit(solution)/shard_map/ppermute | solution.py:243
  110.0 11.3 %collective-permute-start.22 = (bf16[32,2048]{1,0:T(8,128)(2,1)S(1)}, bf16[32,2048]{1,0:T(8,128)(2,1)S(1)}, u32[]{:S(2)}, u32[]{:S(2)}) collective-permute-start(bf16[32,2048]{1,0:T(8,128)(2,1)S(1)} %get-tuple-element.42), channel_id=1, source_target_pairs={{0,2},{1,3},{2,0},{3,1},{4,6},{5,7},{6,4},{7,5},{8,10},{9,11},{10,... | collective-permute-start | bytes 393224 | tf_op jit(solution)/shard_map/ppermute | solution.py:243
  111.3 10.6 %collective-permute-start.23 = (bf16[32,2048]{1,0:T(8,128)(2,1)S(1)}, bf16[32,2048]{1,0:T(8,128)(2,1)S(1)}, u32[]{:S(2)}, u32[]{:S(2)}) collective-permute-start(bf16[32,2048]{1,0:T(8,128)(2,1)S(1)} %get-tuple-element.41), channel_id=1, source_target_pairs={{0,4},{1,5},{2,6},{3,7},{4,0},{5,1},{6,2},{7,3},{8,12},{9,13},{10,... | collective-permute-start | bytes 393224 | tf_op jit(solution)/shard_map/ppermute | solution.py:243
  112.8 9.2 %collective-permute-start.24 = (bf16[32,2048]{1,0:T(8,128)(2,1)S(1)}, bf16[32,2048]{1,0:T(8,128)(2,1)S(1)}, u32[]{:S(2)}, u32[]{:S(2)}) collective-permute-start(bf16[32,2048]{1,0:T(8,128)(2,1)S(1)} %get-tuple-element.40), channel_id=1, source_target_pairs={{0,6},{1,7},{2,4},{3,5},{4,2},{5,3},{6,0},{7,1},{8,14},{9,15},{10,... | collective-permute-start | bytes 393224 | tf_op jit(solution)/shard_map/ppermute | solution.py:243
  122.0 2.0 %collective-permute-start.28 = (bf16[4,32,2048]{2,1,0:T(8,128)(2,1)S(1)}, bf16[4,32,2048]{2,1,0:T(8,128)(2,1)S(1)}, u32[]{:S(2)}, u32[]{:S(2)}) collective-permute-start(bf16[4,32,2048]{2,1,0:T(8,128)(2,1)S(1)} %hold.5), channel_id=1, source_target_pairs={{0,1},{1,0},{2,3},{3,2},{4,5},{5,4},{6,7},{7,6},{8,9},{9,8},{10,11... | collective-permute-start | bytes 1572872 | tf_op jit(solution)/shard_map/ppermute | solution.py:243
  124.1 8.3 %collective-permute-start.29 = (bf16[32,2048]{1,0:T(8,128)(2,1)S(1)}, bf16[32,2048]{1,0:T(8,128)(2,1)S(1)}, u32[]{:S(2)}, u32[]{:S(2)}) collective-permute-start(bf16[32,2048]{1,0:T(8,128)(2,1)S(1)} %get-tuple-element.37), channel_id=1, source_target_pairs={{0,2},{1,3},{2,0},{3,1},{4,6},{5,7},{6,4},{7,5},{8,10},{9,11},{10,... | collective-permute-start | bytes 393224 | tf_op jit(solution)/shard_map/ppermute | solution.py:243
  127.4 12.7 %collective-permute-start.30 = (bf16[32,2048]{1,0:T(8,128)(2,1)S(1)}, bf16[32,2048]{1,0:T(8,128)(2,1)S(1)}, u32[]{:S(2)}, u32[]{:S(2)}) collective-permute-start(bf16[32,2048]{1,0:T(8,128)(2,1)S(1)} %get-tuple-element.39), channel_id=1, source_target_pairs={{0,4},{1,5},{2,6},{3,7},{4,0},{5,1},{6,2},{7,3},{8,12},{9,13},{10,... | collective-permute-start | bytes 393224 | tf_op jit(solution)/shard_map/ppermute | solution.py:243
  127.4 12.7 %collective-permute-start.31 = (bf16[32,2048]{1,0:T(8,128)(2,1)S(1)}, bf16[32,2048]{1,0:T(8,128)(2,1)S(1)}, u32[]{:S(2)}, u32[]{:S(2)}) collective-permute-start(bf16[32,2048]{1,0:T(8,128)(2,1)S(1)} %get-tuple-element.38), channel_id=1, source_target_pairs={{0,6},{1,7},{2,4},{3,5},{4,2},{5,3},{6,0},{7,1},{8,14},{9,15},{10,... | collective-permute-start | bytes 393224 | tf_op jit(solution)/shard_map/ppermute | solution.py:243

commit v8 on v5

v8 whole, which is shorter than its diff:
```python
import functools

import jax
import jax.numpy as jnp
from jax import lax
from jax.experimental import pallas as pl
from jax.experimental.pallas import tpu as pltpu
from jax.sharding import PartitionSpec as P

AXES = ("tok", "hid")
BATCHES = 2
TILE = 512
VMEM_BYTES = 44 * 1024 * 1024


def masked_product(x_ref, weight_ref, keep_ref):
    block_rows, width = keep_ref.shape
    side = weight_ref.shape[0] // block_rows
    strips = []
    for i in range(block_rows):
        keep = jnp.broadcast_to(keep_ref[i : i + 1, :], (16, width)).astype(jnp.bfloat16)
        block = weight_ref[i * side : (i + 1) * side, :].reshape(side // 16, 16, width)
        strips.append((block * keep[None]).reshape(side, width))
    return jnp.dot(x_ref[...], jnp.concatenate(strips, axis=0), preferred_element_type=jnp.float32)


def widen(keep_mask, width):
    return jnp.repeat(keep_mask.astype(jnp.float32), width // keep_mask.shape[1], axis=1)


def project_kernel(n, place_ref, *refs):
    own, other = refs[:n], refs[n : 2 * n]
    weight_ref, mask_ref = refs[2 * n : 2 * n + 2]
    kept_ref, sent_ref, x = refs[-3:]
    rows, half = own[0].shape

    @pl.when(pl.program_id(0) == 0)
    def _():
        core = place_ref[0]
        mine = pl.ds(pl.multiple_of(core * half, half), half)
        others = pl.ds(pl.multiple_of((1 - core) * half, half), half)
        for k in range(n):
            at = pl.ds(pl.multiple_of(place_ref[1 + n + k] * rows, rows), rows)
            x[at, mine] = own[k][...]
            x[at, others] = other[k][...]

    product = masked_product(x, weight_ref, mask_ref)
    for p in range(n // 2):
        q = p + n // 2
        kept_ref[p] = product[p * rows : (p + 1) * rows]
        sent_ref[p] = product[q * rows : (q + 1) * rows].astype(jnp.bfloat16)


def project(place, own, other, weight, keep, after):
    n = len(own)
    rows, half = own[0].shape
    depth, width = weight.shape
    tile = min(width, TILE)
    part = pl.BlockSpec((rows, half), lambda i, *_: (0, 0))
    out = pl.BlockSpec((n // 2, rows, tile), lambda i, *_: (0, 0, i))
    return pl.pallas_call(
        functools.partial(project_kernel, n),
        grid_spec=pltpu.PrefetchScalarGridSpec(
            num_scalar_prefetch=1,
            grid=(width // tile,),
            in_specs=[part] * (2 * n)
            + [pl.BlockSpec((depth, tile), lambda i, *_: (0, i))]
            + [pl.BlockSpec((keep.shape[0], tile), lambda i, *_: (0, i))]
            + [pl.BlockSpec(memory_space=pl.ANY)] * len(after),
            out_specs=[out, out],
            scratch_shapes=[pltpu.VMEM((n * rows, depth), jnp.bfloat16)],
        ),
        out_shape=[
            jax.ShapeDtypeStruct((n // 2, rows, width), jnp.float32),
            jax.ShapeDtypeStruct((n // 2, rows, width), jnp.bfloat16),
        ],
        compiler_params=pltpu.CompilerParams(vmem_limit_bytes=VMEM_BYTES),
        cost_estimate=pl.CostEstimate(
            flops=2 * n * rows * depth * width, bytes_accessed=2 * depth * width, transcendentals=0
        ),
        name="project",
    )(place, *own, *other, weight, keep, *after)


def total_of(refs):
    total = refs[0][...].astype(jnp.float32)
    for ref in refs[1:]:
        total += ref[...].astype(jnp.float32)
    return total


def add_kernel(n, *refs):
    refs[-1][...] = total_of(refs[:n]).astype(jnp.bfloat16)


def add_slots(parts, first, count, after):
    _, rows, width = parts[0].shape
    n = len(parts)
    return pl.pallas_call(
        functools.partial(add_kernel, n),
        grid=(count,),
        in_specs=[pl.BlockSpec((1, rows, width), lambda i: (first + i, 0, 0))] * n
        + [pl.BlockSpec(memory_space=pl.ANY)] * len(after),
        out_specs=pl.BlockSpec((1, rows, width), lambda i: (i, 0, 0)),
        out_shape=jax.ShapeDtypeStruct((count, rows, width), jnp.bfloat16),
        compiler_params=pltpu.CompilerParams(vmem_limit_bytes=VMEM_BYTES),
        name="add_slots",
    )(*parts, *after)


def activate_kernel(n, *refs):
    gate = total_of(refs[:n])
    up = total_of(refs[n : 2 * n])
    result = gate / (1.0 + jnp.exp(-gate)) * up
    refs[-1][...] = result.reshape(refs[-1].shape).astype(jnp.bfloat16)


def activate(gate_parts, up_parts, batch):
    _, rows, width = gate_parts[0].shape
    tile = width // 2
    n = len(gate_parts)
    piece = rows // (2 * BATCHES)
    parts = [part.reshape(part.shape[0] * 2, rows // 2, width) for part in gate_parts + up_parts]
    return pl.pallas_call(
        functools.partial(activate_kernel, n),
        grid=(width // tile,),
        in_specs=[pl.BlockSpec((2, piece, tile), lambda i: (0, batch, i))] * (2 * n),
        out_specs=pl.BlockSpec((2 * piece, tile), lambda i: (0, i)),
        out_shape=jax.ShapeDtypeStruct((2 * piece, width), jnp.bfloat16),
        compiler_params=pltpu.CompilerParams(vmem_limit_bytes=VMEM_BYTES),
        name="hidden",
    )(*parts)


def down_kernel(n, place_ref, *refs):
    parts = refs[:n]
    weight_ref, keep_ref = refs[n : n + 2]
    mine_ref, other_ref, h = refs[-3:]
    rows = parts[0].shape[0]
    step = pl.program_id(0)

    @pl.when(step == 0)
    def _():
        for p in range(n):
            h[p * rows : (p + 1) * rows] = parts[p][...]

    product = masked_product(h, weight_ref, keep_ref)
    core = place_ref[0]
    half = rows // 2
    for p in range(n):
        slot = place_ref[1 + p]
        low = product[p * rows : p * rows + half]
        high = product[p * rows + half : (p + 1) * rows]
        mine_ref[slot] = jnp.where(core == 0, low, high)
        other_ref[slot] = jnp.where(core == 0, high, low).astype(jnp.bfloat16)


def down(place, parts, weight, keep, after):
    n = len(parts)
    rows = parts[0].shape[0]
    depth, width = weight.shape
    tile = min(width, TILE)
    out = pl.BlockSpec((n, rows // 2, tile), lambda i, *_: (0, 0, i))
    return pl.pallas_call(
        functools.partial(down_kernel, n),
        grid_spec=pltpu.PrefetchScalarGridSpec(
            num_scalar_prefetch=1,
            grid=(width // tile,),
            in_specs=[pl.BlockSpec((rows, depth), lambda i, *_: (0, 0))] * n
            + [pl.BlockSpec((depth, tile), lambda i, *_: (0, i))]
            + [pl.BlockSpec((keep.shape[0], tile), lambda i, *_: (0, i))]
            + [pl.BlockSpec(memory_space=pl.ANY)] * len(after),
            out_specs=[out, out],
            scratch_shapes=[pltpu.VMEM((n * rows, depth), jnp.bfloat16)],
        ),
        out_shape=[
            jax.ShapeDtypeStruct((n, rows // 2, width), jnp.float32),
            jax.ShapeDtypeStruct((n, rows // 2, width), jnp.bfloat16),
        ],
        compiler_params=pltpu.CompilerParams(vmem_limit_bytes=VMEM_BYTES),
        cost_estimate=pl.CostEstimate(
            flops=2 * n * rows * depth * width, bytes_accessed=2 * depth * width, transcendentals=0
        ),
        name="down",
    )(place, *parts, weight, keep, *after)


def hold_kernel(value_ref, *refs):
    refs[-1][...] = value_ref[...]


def hold(value, after):
    if not after:
        return value
    spec = pl.BlockSpec(memory_space=pltpu.VMEM)
    return pl.pallas_call(
        hold_kernel,
        in_specs=[spec] + [pl.BlockSpec(memory_space=pl.ANY)] * len(after),
        out_specs=spec,
        out_shape=jax.ShapeDtypeStruct(value.shape, value.dtype),
        compiler_params=pltpu.CompilerParams(vmem_limit_bytes=VMEM_BYTES),
        name="hold",
    )(value, *after)


def mirror(p, n):
    out = 0
    while n > 1:
        out, p, n = out * 2 + p % 2, p // 2, n // 2
    return out


def local(n_tok, n_hid, tokens, gate_weight, up_weight, down_weight, gate_keep, up_keep, down_keep):
    n_z = n_hid // 2
    tok, hid = lax.axis_index("tok"), lax.axis_index("hid")
    z, core = hid // 2, hid % 2
    offsets = [jnp.where(core == 0, p, mirror(p, n_tok)) for p in range(n_tok)]
    positions = [sum(jnp.where(off == tok ^ z ^ k, p, 0) for p, off in enumerate(offsets)) for k in range(n_tok)]
    place = jnp.stack([core] + [tok ^ z ^ off for off in offsets] + positions).astype(jnp.int32)

    def send(value, to):
        perm = []
        for t in range(n_tok):
            for zz in range(n_z):
                for c in range(2):
                    a, b, d = to(t, zz, c)
                    perm.append((t * n_hid + zz * 2 + c, a * n_hid + b * 2 + d))
        return lax.ppermute(value, AXES, perm)

    def across_tok(value, p):
        return send(value, lambda t, zz, c: (t ^ (p if c == 0 else mirror(p, n_tok)), zz, c))

    def across_z(value, j):
        return send(value, lambda t, zz, c: (t, zz ^ j, c))

    def across_core(value):
        return send(value, lambda t, zz, c: (t, zz, 1 - c))

    def halve(kept, sent, after):
        left = n_tok // 2
        parts = [kept]
        while True:
            parts.append(across_tok(sent, left))
            if left == 1:
                return parts, sent
            left //= 2
            sent = add_slots(parts, left, left, after)

    def gather(part):
        parts, left = [part], 1
        while left < n_tok:
            parts += [across_tok(part, left) for part in parts]
            left *= 2
        return parts

    def combine(mine, theirs):
        paired = across_core(theirs)
        sums = [mine[j] + paired[j].astype(jnp.float32) for j in range(n_z)]
        return sums[0], [part.astype(jnp.bfloat16) for part in sums[1:]]

    gate_wide = widen(gate_keep, gate_weight.shape[1])
    up_wide = widen(up_keep, up_weight.shape[1])
    down_wide = widen(down_keep, down_weight.shape[1])
    own = [send(tokens, lambda t, zz, c: (zz, t ^ k, c)) for k in range(n_z)]
    other = [across_core(block) for block in own]
    gate_kept, gate_sent = project(place, own, other, gate_weight, gate_wide, ())
    up_kept, up_sent = project(place, own, other, up_weight, up_wide, (gate_sent,))
    gate_parts, gate_last = halve(gate_kept, gate_sent, (up_sent,))
    up_parts, _ = halve(up_kept, up_sent, (gate_last,))
    hidden = [gather(activate(gate_parts, up_parts, s)) for s in range(BATCHES)]
    out, beside = [], []
    for s, parts in enumerate(hidden):
        for later in hidden[s + 1 : s + 2]:
            beside = beside + later[1:]
        mine, theirs = down(place, parts, down_weight, down_wide, ())
        total, sent = combine(mine, hold(theirs, beside))
        beside = [across_z(sent[j - 1], j) for j in range(1, n_z)]
        for part in beside:
            total += part.astype(jnp.float32)
        out.append(total.astype(jnp.bfloat16))
    return jnp.concatenate(out, axis=0)


def solution(mesh):
    n_tok, n_hid = mesh.shape["tok"], mesh.shape["hid"]
    return jax.shard_map(
        functools.partial(local, n_tok, n_hid),
        mesh=mesh,
        in_specs=(
            P("tok", "hid"),
            P("tok", "hid"),
            P("tok", "hid"),
            P("hid", "tok"),
            P("tok", "hid"),
            P("tok", "hid"),
            P("hid", "tok"),
        ),
        out_specs=P("hid", "tok"),
        check_vma=False,
    )
```

time: 146 us -> 143 us (0.979)
  starting transfers between devices: 45.4 us -> 41.1 us
  waiting for transfers between devices: 64.5 us -> 68.3 us
  Pallas kernels: 32.3 us -> 29.5 us
    ppermute x30 -> x26, starting transfers between devices: 45.4 us -> 41.1 us  [send(): return lax.ppermute(value, AXES, perm)]
    ppermute x30 -> x26, waiting for transfers between devices: 64.5 us -> 68.3 us  [send(): return lax.ppermute(value, AXES, perm)]
    pallas_call x2 -> x4, Pallas kernels: 18.7 us -> 15.8 us  [the longest x2 15.8 us: project(): pl.pallas_call(functools.partial(project_kernel, n), grid_spec=pltpu.Pref...]
  transfers between devices with their start and end apart: 30 -> 26, of which waited for: 20 -> 13; matrix products, arithmetic and copies ran while one was open for 1% -> 1% of each run, Pallas kernels for 11% -> 15%
where the time goes in v8:
time: 143 us; the launch traced here: 142 us
  waiting for transfers between devices  68.3 us (48%)
  starting transfers between devices  41.1 us (29%)
  Pallas kernels  29.5 us (21%)
  other arithmetic  2.48 us (2%)
    ppermute x26, waiting for transfers between devices, send(): return lax.ppermute(value, AXES, perm)  68.3 us
    ppermute x26, starting transfers between devices, send(): return lax.ppermute(value, AXES, perm)  41.1 us
    pallas_call x2, Pallas kernels, project(): pl.pallas_call(functools.partial(project_kernel, n), grid_spec=pltpu.Pref...  15.8 us
    pallas_call x2, Pallas kernels, down(): pl.pallas_call(functools.partial(down_kernel, n), grid_spec=pltpu.Prefetc...  12.5 us
  transfers between devices with their start and end apart: 26, of which 13 were waited for; matrix products, arithmetic and copies ran while one was open for 1% of the time, Pallas kernels for 15%

profile of v8, /device:TPU:0, one launch (start us, length us, event | category | flops | bytes accessed | tf_op | source)
XLA Modules:
  0.0 142.2 jit_solution(12761491473874746396)
XLA Ops:
  0.0 3.0 %collective-permute-start.1 = (bf16[128,1024]{1,0:T(8,128)(2,1)}, bf16[128,1024]{1,0:T(8,128)(2,1)S(1)}, u32[]{:S(2)}, u32[]{:S(2)}) collective-permute-start(bf16[128,1024]{1,0:T(8,128)(2,1)} %param.7), channel_id=1, source_target_pairs={{0,2},{1,3},{2,10},{3,11},{4,18},{5,19},{6,26},{7,27},{8,0},{9,1},... | collective-permute-start | bytes 786440 | tf_op jit(solution)/shard_map/ppermute | solution.py:228
  3.0 1.6 %collective-permute-start = (bf16[128,1024]{1,0:T(8,128)(2,1)}, bf16[128,1024]{1,0:T(8,128)(2,1)S(1)}, u32[]{:S(2)}, u32[]{:S(2)}) collective-permute-start(bf16[128,1024]{1,0:T(8,128)(2,1)} %param.7), channel_id=1, source_target_pairs={{0,0},{1,1},{2,8},{3,9},{4,16},{5,17},{6,24},{7,25},{8,2},{9,3},{1... | collective-permute-start | bytes 786440 | tf_op jit(solution)/shard_map/ppermute | solution.py:228
  4.6 7.0 %collective-permute-start.3 = (bf16[128,1024]{1,0:T(8,128)(2,1)}, bf16[128,1024]{1,0:T(8,128)(2,1)S(1)}, u32[]{:S(2)}, u32[]{:S(2)}) collective-permute-start(bf16[128,1024]{1,0:T(8,128)(2,1)} %param.7), channel_id=1, source_target_pairs={{0,6},{1,7},{2,14},{3,15},{4,22},{5,23},{6,30},{7,31},{8,4},{9,5},... | collective-permute-start | bytes 786440 | tf_op jit(solution)/shard_map/ppermute | solution.py:228
  11.6 0.5 collective-permute-start.4
  12.1 8.2 %collective-permute-done.3.refs_3_ = bf16[128,1024]{1,0:T(8,128)(2,1)S(1)} collective-permute-done((bf16[128,1024]{1,0:T(8,128)(2,1)}, bf16[128,1024]{1,0:T(8,128)(2,1)S(1)}, u32[]{:S(2)}, u32[]{:S(2)}) %collective-permute-start.3) | collective-permute-done | bytes 262176 | tf_op jit(solution)/shard_map/ppermute | solution.py:228
  20.4 3.9 %collective-permute-done.2.refs_2_ = bf16[128,1024]{1,0:T(8,128)(2,1)S(1)} collective-permute-done((bf16[128,1024]{1,0:T(8,128)(2,1)}, bf16[128,1024]{1,0:T(8,128)(2,1)S(1)}, u32[]{:S(2)}, u32[]{:S(2)}) %collective-permute-start.2) | collective-permute-done | bytes 262176 | tf_op jit(solution)/shard_map/ppermute | solution.py:228
  24.3 0.7 convert_element_type.101
  25.0 0.7 convert_element_type.102
  25.7 0.1 broadcast_in_dim.10
  25.8 0.1 broadcast_in_dim.9
  26.0 0.1 stack.39.place_ref
  26.2 7.9 %project.2 = (f32[2,128,2048]{2,1,0:T(8,128)S(1)}, bf16[2,128,2048]{2,1,0:T(8,128)(2,1)S(1)}) custom-call(s32[9]{0:T(128)S(1)} %stack.39.place_ref, bf16[128,1024]{1,0:T(8,128)(2,1)S(1)} %collective-permute-done.refs_0_, bf16[128,1024]{1,0:T(8,128)(2,1)S(1)} %collective-permute-done.1.refs_1_, bf16[128,1024]{1,0:T(8,128)(2,1)S(1)} %collective-permute-done.2.refs_2_, ...), custom_call_target="tpu_custom_call" | custom-call | flops 4294967296 | bytes 8388608 | tf_op jit(solution)/shard_map/project/pallas_call | solution.py:61
  34.1 10.0 %collective-permute-start.8 = (bf16[2,128,2048]{2,1,0:T(8,128)(2,1)S(1)}, bf16[2,128,2048]{2,1,0:T(8,128)(2,1)S(1)}, u32[]{:S(2)}, u32[]{:S(2)}) collective-permute-start(bf16[2,128,2048]{2,1,0:T(8,128)(2,1)S(1)} %get-tuple-element.14.refs_10_), channel_id=1, source_target_pairs={{0,16},{1,9},{2,18},{3,11},{4,20},{5,13},{6,22},{7,15},{8,24},{9,1... | collective-permute-start | bytes 3145736 | tf_op jit(solution)/shard_map/ppermute | solution.py:228
  44.1 7.9 %project.3 = (f32[2,128,2048]{2,1,0:T(8,128)S(1)}, bf16[2,128,2048]{2,1,0:T(8,128)(2,1)S(1)}) custom-call(s32[9]{0:T(128)S(1)} %stack.39.place_ref, bf16[128,1024]{1,0:T(8,128)(2,1)S(1)} %collective-permute-done.refs_0_, bf16[128,1024]{1,0:T(8,128)(2,1)S(1)} %collective-permute-done.1.refs_1_, bf16[128,1024]{1,0:T(8,128)(2,1)S(1)} %collective-permute-done.2.refs_2_, ...), custom_call_target="tpu_custom_call" | custom-call | flops 4294967296 | bytes 8388608 | tf_op jit(solution)/shard_map/project/pallas_call | solution.py:61
  52.0 0.1 collective-permute-start.10
  52.0 4.8 %collective-permute-done.8.refs_1_ = bf16[2,128,2048]{2,1,0:T(8,128)(2,1)S(1)} collective-permute-done((bf16[2,128,2048]{2,1,0:T(8,128)(2,1)S(1)}, bf16[2,128,2048]{2,1,0:T(8,128)(2,1)S(1)}, u32[]{:S(2)}, u32[]{:S(2)}) %collective-permute-start.8) | collective-permute-done | bytes 1048608 | tf_op jit(solution)/shard_map/ppermute | solution.py:228
  56.8 0.1 add_slots.2.refs_2_
  56.9 11.1 %collective-permute-done.10.refs_1_ = bf16[2,128,2048]{2,1,0:T(8,128)(2,1)S(1)} collective-permute-done((bf16[2,128,2048]{2,1,0:T(8,128)(2,1)S(1)}, bf16[2,128,2048]{2,1,0:T(8,128)(2,1)S(1)}, u32[]{:S(2)}, u32[]{:S(2)}) %collective-permute-start.10) | collective-permute-done | bytes 1048608 | tf_op jit(solution)/shard_map/ppermute | solution.py:228
  68.1 0.1 add_slots.3
  68.3 2.0 %collective-permute-start.9 = (bf16[1,128,2048]{2,1,0:T(8,128)(2,1)S(1)}, bf16[1,128,2048]{2,1,0:T(8,128)(2,1)S(1)}, u32[]{:S(2)}, u32[]{:S(2)}) collective-permute-start(bf16[1,128,2048]{2,1,0:T(8,128)(2,1)S(1)} %add_slots.2.refs_2_), channel_id=1, source_target_pairs={{0,8},{1,17},{2,10},{3,19},{4,12},{5,21},{6,14},{7,23},{8,0},{9,25... | collective-permute-start | bytes 1572872 | tf_op jit(solution)/shard_map/ppermute | solution.py:228
  70.3 7.2 %collective-permute-done.11 = bf16[1,128,2048]{2,1,0:T(8,128)(2,1)S(1)} collective-permute-done((bf16[1,128,2048]{2,1,0:T(8,128)(2,1)S(1)}, bf16[1,128,2048]{2,1,0:T(8,128)(2,1)S(1)}, u32[]{:S(2)}, u32[]{:S(2)}) %collective-permute-start.11) | collective-permute-done | bytes 524320 | tf_op jit(solution)/shard_map/ppermute | solution.py:228
  77.4 5.6 %collective-permute-done.9 = bf16[1,128,2048]{2,1,0:T(8,128)(2,1)S(1)} collective-permute-done((bf16[1,128,2048]{2,1,0:T(8,128)(2,1)S(1)}, bf16[1,128,2048]{2,1,0:T(8,128)(2,1)S(1)}, u32[]{:S(2)}, u32[]{:S(2)}) %collective-permute-start.9) | collective-permute-done | bytes 524320 | tf_op jit(solution)/shard_map/ppermute | solution.py:228
  83.0 0.5 hidden.2.refs_0_
  83.6 0.5 hidden.3.refs_0_
  84.2 2.1 %collective-permute-start.15 = (bf16[64,2048]{1,0:T(8,128)(2,1)S(1)}, bf16[64,2048]{1,0:T(8,128)(2,1)S(1)}, u32[]{:S(2)}, u32[]{:S(2)}) collective-permute-start(bf16[64,2048]{1,0:T(8,128)(2,1)S(1)} %hidden.3.refs_0_), channel_id=1, source_target_pairs={{0,8},{1,17},{2,10},{3,19},{4,12},{5,21},{6,14},{7,23},{8,0},{9,25... | collective-permute-start | bytes 786440 | tf_op jit(solution)/shard_map/ppermute | solution.py:228
  86.2 2.0 %collective-permute-start.13 = (bf16[64,2048]{1,0:T(8,128)(2,1)S(1)}, bf16[64,2048]{1,0:T(8,128)(2,1)S(1)}, u32[]{:S(2)}, u32[]{:S(2)}) collective-permute-start(bf16[64,2048]{1,0:T(8,128)(2,1)S(1)} %hidden.2.refs_0_), channel_id=1, source_target_pairs={{0,16},{1,9},{2,18},{3,11},{4,20},{5,13},{6,22},{7,15},{8,24},{9,1... | collective-permute-start | bytes 786440 | tf_op jit(solution)/shard_map/ppermute | solution.py:228
  88.2 4.3 %collective-permute-done.12.refs_1_ = bf16[64,2048]{1,0:T(8,128)(2,1)S(1)} collective-permute-done((bf16[64,2048]{1,0:T(8,128)(2,1)S(1)}, bf16[64,2048]{1,0:T(8,128)(2,1)S(1)}, u32[]{:S(2)}, u32[]{:S(2)}) %collective-permute-start.12) | collective-permute-done | bytes 262176 | tf_op jit(solution)/shard_map/ppermute | solution.py:228
  92.6 2.2 %collective-permute-start.14 = (bf16[64,2048]{1,0:T(8,128)(2,1)S(1)}, bf16[64,2048]{1,0:T(8,128)(2,1)S(1)}, u32[]{:S(2)}, u32[]{:S(2)}) collective-permute-start(bf16[64,2048]{1,0:T(8,128)(2,1)S(1)} %collective-permute-done.12.refs_1_), channel_id=1, source_target_pairs={{0,16},{1,9},{2,18},{3,11},{4,20},{5,13},{6,22},{7,15},{8,24},{9,1... | collective-permute-start | bytes 786440 | tf_op jit(solution)/shard_map/ppermute | solution.py:228
  94.9 3.3 %collective-permute-done.15.refs_0_.refs_1_ = bf16[64,2048]{1,0:T(8,128)(2,1)S(1)} collective-permute-done((bf16[64,2048]{1,0:T(8,128)(2,1)S(1)}, bf16[64,2048]{1,0:T(8,128)(2,1)S(1)}, u32[]{:S(2)}, u32[]{:S(2)}) %collective-permute-start.15) | collective-permute-done | bytes 262176 | tf_op jit(solution)/shard_map/ppermute | solution.py:228
  98.2 2.2 %collective-permute-start.17 = (bf16[64,2048]{1,0:T(8,128)(2,1)S(1)}, bf16[64,2048]{1,0:T(8,128)(2,1)S(1)}, u32[]{:S(2)}, u32[]{:S(2)}) collective-permute-start(bf16[64,2048]{1,0:T(8,128)(2,1)S(1)} %collective-permute-done.15.refs_0_.refs_1_), channel_id=1, source_target_pairs={{0,16},{1,9},{2,18},{3,11},{4,20},{5,13},{6,22},{7,15},{8,24},{9,1... | collective-permute-start | bytes 786440 | tf_op jit(solution)/shard_map/ppermute | solution.py:228
  100.4 0.1 broadcast_in_dim.11
  100.6 6.2 %down.2 = (f32[4,32,2048]{2,1,0:T(8,128)S(1)}, bf16[4,32,2048]{2,1,0:T(8,128)(2,1)S(1)}) custom-call(s32[9]{0:T(128)S(1)} %stack.39.place_ref, bf16[64,2048]{1,0:T(8,128)(2,1)S(1)} %hidden.2.refs_0_, bf16[64,2048]{1,0:T(8,128)(2,1)S(1)} %collective-permute-done.12.refs_1_, bf16[64,2048]{1,0:T(8,128)(2,1)S(1)} %collective-permute-done.13.refs_2_, ...), custom_call_target="tpu_custom_call" | custom-call | flops 2147483648 | bytes 8388608 | tf_op jit(solution)/shard_map/down/pallas_call | solution.py:164
  107.0 1.9 %collective-permute-done.18 = bf16[4,32,2048]{2,1,0:T(8,128)(2,1)S(1)} collective-permute-done((bf16[4,32,2048]{2,1,0:T(8,128)(2,1)S(1)}, bf16[4,32,2048]{2,1,0:T(8,128)(2,1)S(1)}, u32[]{:S(2)}, u32[]{:S(2)}) %collective-permute-start.18) | collective-permute-done | bytes 524320 | tf_op jit(solution)/shard_map/ppermute | solution.py:228
  108.9 0.1 fusion.8
  109.0 2.0 %collective-permute-start.21 = (bf16[32,2048]{1,0:T(8,128)(2,1)S(1)}, bf16[32,2048]{1,0:T(8,128)(2,1)S(1)}, u32[]{:S(2)}, u32[]{:S(2)}) collective-permute-start(bf16[32,2048]{1,0:T(8,128)(2,1)S(1)} %get-tuple-element.24), channel_id=1, source_target_pairs={{0,6},{1,7},{2,4},{3,5},{4,2},{5,3},{6,0},{7,1},{8,14},{9,15},{10,... | collective-permute-start | bytes 393224 | tf_op jit(solution)/shard_map/ppermute | solution.py:228
  111.0 1.1 collective-permute-start.20
  112.1 1.3 collective-permute-start.19
  113.5 6.2 %down.3 = (f32[4,32,2048]{2,1,0:T(8,128)S(1)}, bf16[4,32,2048]{2,1,0:T(8,128)(2,1)S(1)}) custom-call(s32[9]{0:T(128)S(1)} %stack.39.place_ref, bf16[64,2048]{1,0:T(8,128)(2,1)S(1)} %hidden.3.refs_0_, bf16[64,2048]{1,0:T(8,128)(2,1)S(1)} %collective-permute-done.15.refs_0_.refs_1_, bf16[64,2048]{1,0:T(8,128)(2,1)S(1)} %collective-permute-done.16.refs_1_.refs_2_, ...), custom_call_target="tpu_custom_call" | custom-call | flops 2147483648 | bytes 8388608 | tf_op jit(solution)/shard_map/down/pallas_call | solution.py:164
  119.7 4.3 %collective-permute-done.20.refs_1_ = bf16[32,2048]{1,0:T(8,128)(2,1)S(1)} collective-permute-done((bf16[32,2048]{1,0:T(8,128)(2,1)S(1)}, bf16[32,2048]{1,0:T(8,128)(2,1)S(1)}, u32[]{:S(2)}, u32[]{:S(2)}) %collective-permute-start.20) | collective-permute-done | bytes 131104 | tf_op jit(solution)/shard_map/ppermute | solution.py:228
  124.2 1.9 %collective-permute-done.22 = bf16[4,32,2048]{2,1,0:T(8,128)(2,1)S(1)} collective-permute-done((bf16[4,32,2048]{2,1,0:T(8,128)(2,1)S(1)}, bf16[4,32,2048]{2,1,0:T(8,128)(2,1)S(1)}, u32[]{:S(2)}, u32[]{:S(2)}) %collective-permute-start.22) | collective-permute-done | bytes 524320 | tf_op jit(solution)/shard_map/ppermute | solution.py:228
  126.1 0.1 fusion.9
  126.3 1.2 collective-permute-start.25
  127.5 2.2 %collective-permute-start.24 = (bf16[32,2048]{1,0:T(8,128)(2,1)S(1)}, bf16[32,2048]{1,0:T(8,128)(2,1)S(1)}, u32[]{:S(2)}, u32[]{:S(2)}) collective-permute-start(bf16[32,2048]{1,0:T(8,128)(2,1)S(1)} %get-tuple-element.23), channel_id=1, source_target_pairs={{0,4},{1,5},{2,6},{3,7},{4,0},{5,1},{6,2},{7,3},{8,12},{9,13},{10,... | collective-permute-start | bytes 393224 | tf_op jit(solution)/shard_map/ppermute | solution.py:228
  129.7 0.1 fusion.5
  129.8 4.8 %collective-permute-done.23 = bf16[32,2048]{1,0:T(8,128)(2,1)S(1)} collective-permute-done((bf16[32,2048]{1,0:T(8,128)(2,1)S(1)}, bf16[32,2048]{1,0:T(8,128)(2,1)S(1)}, u32[]{:S(2)}, u32[]{:S(2)}) %collective-permute-start.23) | collective-permute-done | bytes 131104 | tf_op jit(solution)/shard_map/ppermute | solution.py:228
  134.6 6.8 %collective-permute-done.24 = bf16[32,2048]{1,0:T(8,128)(2,1)S(1)} collective-permute-done((bf16[32,2048]{1,0:T(8,128)(2,1)S(1)}, bf16[32,2048]{1,0:T(8,128)(2,1)S(1)}, u32[]{:S(2)}, u32[]{:S(2)}) %collective-permute-start.24) | collective-permute-done | bytes 131104 | tf_op jit(solution)/shard_map/ppermute | solution.py:228
  141.4 0.1 fusion.2
  141.5 0.7 pad_maximum_fusion
  (31 shorter events, 0.6 us)
Async XLA Ops:
  0.0 11.6 %collective-permute-start.1 = (bf16[128,1024]{1,0:T(8,128)(2,1)}, bf16[128,1024]{1,0:T(8,128)(2,1)S(1)}, u32[]{:S(2)}, u32[]{:S(2)}) collective-permute-start(bf16[128,1024]{1,0:T(8,128)(2,1)} %param.7), channel_id=1, source_target_pairs={{0,2},{1,3},{2,10},{3,11},{4,18},{5,19},{6,26},{7,27},{8,0},{9,1},... | collective-permute-start | bytes 786440 | tf_op jit(solution)/shard_map/ppermute | solution.py:228
  3.0 8.6 %collective-permute-start = (bf16[128,1024]{1,0:T(8,128)(2,1)}, bf16[128,1024]{1,0:T(8,128)(2,1)S(1)}, u32[]{:S(2)}, u32[]{:S(2)}) collective-permute-start(bf16[128,1024]{1,0:T(8,128)(2,1)} %param.7), channel_id=1, source_target_pairs={{0,0},{1,1},{2,8},{3,9},{4,16},{5,17},{6,24},{7,25},{8,2},{9,3},{1... | collective-permute-start | bytes 786440 | tf_op jit(solution)/shard_map/ppermute | solution.py:228
  4.6 15.8 %collective-permute-start.3 = (bf16[128,1024]{1,0:T(8,128)(2,1)}, bf16[128,1024]{1,0:T(8,128)(2,1)S(1)}, u32[]{:S(2)}, u32[]{:S(2)}) collective-permute-start(bf16[128,1024]{1,0:T(8,128)(2,1)} %param.7), channel_id=1, source_target_pairs={{0,6},{1,7},{2,14},{3,15},{4,22},{5,23},{6,30},{7,31},{8,4},{9,5},... | collective-permute-start | bytes 786440 | tf_op jit(solution)/shard_map/ppermute | solution.py:228
  11.6 12.7 %collective-permute-start.2 = (bf16[128,1024]{1,0:T(8,128)(2,1)}, bf16[128,1024]{1,0:T(8,128)(2,1)S(1)}, u32[]{:S(2)}, u32[]{:S(2)}) collective-permute-start(bf16[128,1024]{1,0:T(8,128)(2,1)} %param.7), channel_id=1, source_target_pairs={{0,4},{1,5},{2,12},{3,13},{4,20},{5,21},{6,28},{7,29},{8,6},{9,7},... | collective-permute-start | bytes 786440 | tf_op jit(solution)/shard_map/ppermute | solution.py:228
  11.6 14.5 %collective-permute-start.5 = (bf16[128,1024]{1,0:T(8,128)(2,1)S(1)}, bf16[128,1024]{1,0:T(8,128)(2,1)S(1)}, u32[]{:S(2)}, u32[]{:S(2)}) collective-permute-start(bf16[128,1024]{1,0:T(8,128)(2,1)S(1)} %collective-permute-done.1.refs_1_), channel_id=1, source_target_pairs={{0,1},{1,0},{2,3},{3,2},{4,5},{5,4},{6,7},{7,6},{8,9},{9,8},{10,11... | collective-permute-start | bytes 786440 | tf_op jit(solution)/shard_map/ppermute | solution.py:228
  11.6 14.5 %collective-permute-start.4 = (bf16[128,1024]{1,0:T(8,128)(2,1)S(1)}, bf16[128,1024]{1,0:T(8,128)(2,1)S(1)}, u32[]{:S(2)}, u32[]{:S(2)}) collective-permute-start(bf16[128,1024]{1,0:T(8,128)(2,1)S(1)} %collective-permute-done.refs_0_), channel_id=1, source_target_pairs={{0,1},{1,0},{2,3},{3,2},{4,5},{5,4},{6,7},{7,6},{8,9},{9,8},{10,11... | collective-permute-start | bytes 786440 | tf_op jit(solution)/shard_map/ppermute | solution.py:228
  20.4 5.8 %collective-permute-start.7 = (bf16[128,1024]{1,0:T(8,128)(2,1)S(1)}, bf16[128,1024]{1,0:T(8,128)(2,1)S(1)}, u32[]{:S(2)}, u32[]{:S(2)}) collective-permute-start(bf16[128,1024]{1,0:T(8,128)(2,1)S(1)} %collective-permute-done.3.refs_3_), channel_id=1, source_target_pairs={{0,1},{1,0},{2,3},{3,2},{4,5},{5,4},{6,7},{7,6},{8,9},{9,8},{10,11... | collective-permute-start | bytes 786440 | tf_op jit(solution)/shard_map/ppermute | solution.py:228
  24.3 1.9 %collective-permute-start.6 = (bf16[128,1024]{1,0:T(8,128)(2,1)S(1)}, bf16[128,1024]{1,0:T(8,128)(2,1)S(1)}, u32[]{:S(2)}, u32[]{:S(2)}) collective-permute-start(bf16[128,1024]{1,0:T(8,128)(2,1)S(1)} %collective-permute-done.2.refs_2_), channel_id=1, source_target_pairs={{0,1},{1,0},{2,3},{3,2},{4,5},{5,4},{6,7},{7,6},{8,9},{9,8},{10,11... | collective-permute-start | bytes 786440 | tf_op jit(solution)/shard_map/ppermute | solution.py:228
  34.1 22.8 %collective-permute-start.8 = (bf16[2,128,2048]{2,1,0:T(8,128)(2,1)S(1)}, bf16[2,128,2048]{2,1,0:T(8,128)(2,1)S(1)}, u32[]{:S(2)}, u32[]{:S(2)}) collective-permute-start(bf16[2,128,2048]{2,1,0:T(8,128)(2,1)S(1)} %get-tuple-element.14.refs_10_), channel_id=1, source_target_pairs={{0,16},{1,9},{2,18},{3,11},{4,20},{5,13},{6,22},{7,15},{8,24},{9,1... | collective-permute-start | bytes 3145736 | tf_op jit(solution)/shard_map/ppermute | solution.py:228
  52.0 16.1 %collective-permute-start.10 = (bf16[2,128,2048]{2,1,0:T(8,128)(2,1)S(1)}, bf16[2,128,2048]{2,1,0:T(8,128)(2,1)S(1)}, u32[]{:S(2)}, u32[]{:S(2)}) collective-permute-start(bf16[2,128,2048]{2,1,0:T(8,128)(2,1)S(1)} %get-tuple-element.15.refs_2_), channel_id=1, source_target_pairs={{0,16},{1,9},{2,18},{3,11},{4,20},{5,13},{6,22},{7,15},{8,24},{9,1... | collective-permute-start | bytes 3145736 | tf_op jit(solution)/shard_map/ppermute | solution.py:228
  68.2 32.3 %copy-start = (s32[16,16]{1,0:T(8,128)S(1)}, s32[16,16]{1,0:T(8,128)}, u32[]{:S(2)}) copy-start(s32[16,16]{1,0:T(8,128)} %param.13) | copy-start | bytes 3076
  68.2 9.2 %collective-permute-start.11 = (bf16[1,128,2048]{2,1,0:T(8,128)(2,1)S(1)}, bf16[1,128,2048]{2,1,0:T(8,128)(2,1)S(1)}, u32[]{:S(2)}, u32[]{:S(2)}) collective-permute-start(bf16[1,128,2048]{2,1,0:T(8,128)(2,1)S(1)} %add_slots.3), channel_id=1, source_target_pairs={{0,8},{1,17},{2,10},{3,19},{4,12},{5,21},{6,14},{7,23},{8,0},{9,25... | collective-permute-start | bytes 1572872 | tf_op jit(solution)/shard_map/ppermute | solution.py:228
  68.3 14.8 %collective-permute-start.9 = (bf16[1,128,2048]{2,1,0:T(8,128)(2,1)S(1)}, bf16[1,128,2048]{2,1,0:T(8,128)(2,1)S(1)}, u32[]{:S(2)}, u32[]{:S(2)}) collective-permute-start(bf16[1,128,2048]{2,1,0:T(8,128)(2,1)S(1)} %add_slots.2.refs_2_), channel_id=1, source_target_pairs={{0,8},{1,17},{2,10},{3,19},{4,12},{5,21},{6,14},{7,23},{8,0},{9,25... | collective-permute-start | bytes 1572872 | tf_op jit(solution)/shard_map/ppermute | solution.py:228
  83.6 9.0 %collective-permute-start.12 = (bf16[64,2048]{1,0:T(8,128)(2,1)S(1)}, bf16[64,2048]{1,0:T(8,128)(2,1)S(1)}, u32[]{:S(2)}, u32[]{:S(2)}) collective-permute-start(bf16[64,2048]{1,0:T(8,128)(2,1)S(1)} %hidden.2.refs_0_), channel_id=1, source_target_pairs={{0,8},{1,17},{2,10},{3,19},{4,12},{5,21},{6,14},{7,23},{8,0},{9,25... | collective-permute-start | bytes 786440 | tf_op jit(solution)/shard_map/ppermute | solution.py:228
  84.2 14.0 %collective-permute-start.15 = (bf16[64,2048]{1,0:T(8,128)(2,1)S(1)}, bf16[64,2048]{1,0:T(8,128)(2,1)S(1)}, u32[]{:S(2)}, u32[]{:S(2)}) collective-permute-start(bf16[64,2048]{1,0:T(8,128)(2,1)S(1)} %hidden.3.refs_0_), channel_id=1, source_target_pairs={{0,8},{1,17},{2,10},{3,19},{4,12},{5,21},{6,14},{7,23},{8,0},{9,25... | collective-permute-start | bytes 786440 | tf_op jit(solution)/shard_map/ppermute | solution.py:228
  86.2 14.4 %collective-permute-start.13 = (bf16[64,2048]{1,0:T(8,128)(2,1)S(1)}, bf16[64,2048]{1,0:T(8,128)(2,1)S(1)}, u32[]{:S(2)}, u32[]{:S(2)}) collective-permute-start(bf16[64,2048]{1,0:T(8,128)(2,1)S(1)} %hidden.2.refs_0_), channel_id=1, source_target_pairs={{0,16},{1,9},{2,18},{3,11},{4,20},{5,13},{6,22},{7,15},{8,24},{9,1... | collective-permute-start | bytes 786440 | tf_op jit(solution)/shard_map/ppermute | solution.py:228
  92.6 8.0 %collective-permute-start.14 = (bf16[64,2048]{1,0:T(8,128)(2,1)S(1)}, bf16[64,2048]{1,0:T(8,128)(2,1)S(1)}, u32[]{:S(2)}, u32[]{:S(2)}) collective-permute-start(bf16[64,2048]{1,0:T(8,128)(2,1)S(1)} %collective-permute-done.12.refs_1_), channel_id=1, source_target_pairs={{0,16},{1,9},{2,18},{3,11},{4,20},{5,13},{6,22},{7,15},{8,24},{9,1... | collective-permute-start | bytes 786440 | tf_op jit(solution)/shard_map/ppermute | solution.py:228
  94.8 12.0 %collective-permute-start.16 = (bf16[64,2048]{1,0:T(8,128)(2,1)S(1)}, bf16[64,2048]{1,0:T(8,128)(2,1)S(1)}, u32[]{:S(2)}, u32[]{:S(2)}) collective-permute-start(bf16[64,2048]{1,0:T(8,128)(2,1)S(1)} %hidden.3.refs_0_), channel_id=1, source_target_pairs={{0,16},{1,9},{2,18},{3,11},{4,20},{5,13},{6,22},{7,15},{8,24},{9,1... | collective-permute-start | bytes 786440 | tf_op jit(solution)/shard_map/ppermute | solution.py:228
  98.2 8.7 %collective-permute-start.17 = (bf16[64,2048]{1,0:T(8,128)(2,1)S(1)}, bf16[64,2048]{1,0:T(8,128)(2,1)S(1)}, u32[]{:S(2)}, u32[]{:S(2)}) collective-permute-start(bf16[64,2048]{1,0:T(8,128)(2,1)S(1)} %collective-permute-done.15.refs_0_.refs_1_), channel_id=1, source_target_pairs={{0,16},{1,9},{2,18},{3,11},{4,20},{5,13},{6,22},{7,15},{8,24},{9,1... | collective-permute-start | bytes 786440 | tf_op jit(solution)/shard_map/ppermute | solution.py:228
  106.9 2.0 %collective-permute-start.18 = (bf16[4,32,2048]{2,1,0:T(8,128)(2,1)S(1)}, bf16[4,32,2048]{2,1,0:T(8,128)(2,1)S(1)}, u32[]{:S(2)}, u32[]{:S(2)}) collective-permute-start(bf16[4,32,2048]{2,1,0:T(8,128)(2,1)S(1)} %hold.2), channel_id=1, source_target_pairs={{0,1},{1,0},{2,3},{3,2},{4,5},{5,4},{6,7},{7,6},{8,9},{9,8},{10,11... | collective-permute-start | bytes 1572872 | tf_op jit(solution)/shard_map/ppermute | solution.py:228
  109.0 10.7 %collective-permute-start.21 = (bf16[32,2048]{1,0:T(8,128)(2,1)S(1)}, bf16[32,2048]{1,0:T(8,128)(2,1)S(1)}, u32[]{:S(2)}, u32[]{:S(2)}) collective-permute-start(bf16[32,2048]{1,0:T(8,128)(2,1)S(1)} %get-tuple-element.24), channel_id=1, source_target_pairs={{0,6},{1,7},{2,4},{3,5},{4,2},{5,3},{6,0},{7,1},{8,14},{9,15},{10,... | collective-permute-start | bytes 393224 | tf_op jit(solution)/shard_map/ppermute | solution.py:228
  111.0 13.0 %collective-permute-start.20 = (bf16[32,2048]{1,0:T(8,128)(2,1)S(1)}, bf16[32,2048]{1,0:T(8,128)(2,1)S(1)}, u32[]{:S(2)}, u32[]{:S(2)}) collective-permute-start(bf16[32,2048]{1,0:T(8,128)(2,1)S(1)} %get-tuple-element.25), channel_id=1, source_target_pairs={{0,4},{1,5},{2,6},{3,7},{4,0},{5,1},{6,2},{7,3},{8,12},{9,13},{10,... | collective-permute-start | bytes 393224 | tf_op jit(solution)/shard_map/ppermute | solution.py:228
  112.1 11.9 %collective-permute-start.19 = (bf16[32,2048]{1,0:T(8,128)(2,1)S(1)}, bf16[32,2048]{1,0:T(8,128)(2,1)S(1)}, u32[]{:S(2)}, u32[]{:S(2)}) collective-permute-start(bf16[32,2048]{1,0:T(8,128)(2,1)S(1)} %get-tuple-element.26), channel_id=1, source_target_pairs={{0,2},{1,3},{2,0},{3,1},{4,6},{5,7},{6,4},{7,5},{8,10},{9,11},{10,... | collective-permute-start | bytes 393224 | tf_op jit(solution)/shard_map/ppermute | solution.py:228
  124.1 2.0 %collective-permute-start.22 = (bf16[4,32,2048]{2,1,0:T(8,128)(2,1)S(1)}, bf16[4,32,2048]{2,1,0:T(8,128)(2,1)S(1)}, u32[]{:S(2)}, u32[]{:S(2)}) collective-permute-start(bf16[4,32,2048]{2,1,0:T(8,128)(2,1)S(1)} %hold.3), channel_id=1, source_target_pairs={{0,1},{1,0},{2,3},{3,2},{4,5},{5,4},{6,7},{7,6},{8,9},{9,8},{10,11... | collective-permute-start | bytes 1572872 | tf_op jit(solution)/shard_map/ppermute | solution.py:228
  126.2 8.4 %collective-permute-start.23 = (bf16[32,2048]{1,0:T(8,128)(2,1)S(1)}, bf16[32,2048]{1,0:T(8,128)(2,1)S(1)}, u32[]{:S(2)}, u32[]{:S(2)}) collective-permute-start(bf16[32,2048]{1,0:T(8,128)(2,1)S(1)} %get-tuple-element.21), channel_id=1, source_target_pairs={{0,2},{1,3},{2,0},{3,1},{4,6},{5,7},{6,4},{7,5},{8,10},{9,11},{10,... | collective-permute-start | bytes 393224 | tf_op jit(solution)/shard_map/ppermute | solution.py:228
  126.3 8.3 %collective-permute-start.25 = (bf16[32,2048]{1,0:T(8,128)(2,1)S(1)}, bf16[32,2048]{1,0:T(8,128)(2,1)S(1)}, u32[]{:S(2)}, u32[]{:S(2)}) collective-permute-start(bf16[32,2048]{1,0:T(8,128)(2,1)S(1)} %get-tuple-element.22), channel_id=1, source_target_pairs={{0,6},{1,7},{2,4},{3,5},{4,2},{5,3},{6,0},{7,1},{8,14},{9,15},{10,... | collective-permute-start | bytes 393224 | tf_op jit(solution)/shard_map/ppermute | solution.py:228
  127.5 13.9 %collective-permute-start.24 = (bf16[32,2048]{1,0:T(8,128)(2,1)S(1)}, bf16[32,2048]{1,0:T(8,128)(2,1)S(1)}, u32[]{:S(2)}, u32[]{:S(2)}) collective-permute-start(bf16[32,2048]{1,0:T(8,128)(2,1)S(1)} %get-tuple-element.23), channel_id=1, source_target_pairs={{0,4},{1,5},{2,6},{3,7},{4,0},{5,1},{6,2},{7,3},{8,12},{9,13},{10,... | collective-permute-start | bytes 393224 | tf_op jit(solution)/shard_map/ppermute | solution.py:228

commit v9 on v8

--- a/solution.py
+++ b/solution.py
@@ -9,6 +9,7 @@
 
 AXES = ("tok", "hid")
 BATCHES = 2
+STRIPS = 2
 TILE = 512
 VMEM_BYTES = 44 * 1024 * 1024
 
@@ -30,8 +31,8 @@
 
 def project_kernel(n, place_ref, *refs):
     own, other = refs[:n], refs[n : 2 * n]
-    weight_ref, mask_ref = refs[2 * n : 2 * n + 2]
-    kept_ref, sent_ref, x = refs[-3:]
+    gate_ref, up_ref, gate_mask, up_mask = refs[2 * n : 2 * n + 4]
+    outs, x = refs[-5:-1], refs[-1]
     rows, half = own[0].shape
 
     @pl.when(pl.program_id(0) == 0)
@@ -44,42 +45,46 @@
             x[at, mine] = own[k][...]
             x[at, others] = other[k][...]
 
-    product = masked_product(x, weight_ref, mask_ref)
-    for p in range(n // 2):
-        q = p + n // 2
-        kept_ref[p] = product[p * rows : (p + 1) * rows]
-        sent_ref[p] = product[q * rows : (q + 1) * rows].astype(jnp.bfloat16)
-
-
-def project(place, own, other, weight, keep, after):
+    for which, (weight, mask) in enumerate(((gate_ref, gate_mask), (up_ref, up_mask))):
+        product = masked_product(x, weight, mask)
+        for p in range(n):
+            offset = p if which == 0 else mirror(p, n)
+            term = product[offset * rows : (offset + 1) * rows]
+            if p < n // 2:
+                outs[which][p] = term
+            else:
+                outs[2 + which][p - n // 2] = term.astype(jnp.bfloat16)
+
+
+def project(place, own, other, weights, masks, strip, after):
     n = len(own)
     rows, half = own[0].shape
-    depth, width = weight.shape
-    tile = min(width, TILE)
+    depth, whole = weights[0].shape
+    width = whole // STRIPS
+    tile = min(width, TILE // 2)
+    steps = width // tile
     part = pl.BlockSpec((rows, half), lambda i, *_: (0, 0))
     out = pl.BlockSpec((n // 2, rows, tile), lambda i, *_: (0, 0, i))
     return pl.pallas_call(
         functools.partial(project_kernel, n),
         grid_spec=pltpu.PrefetchScalarGridSpec(
             num_scalar_prefetch=1,
-            grid=(width // tile,),
+            grid=(steps,),
             in_specs=[part] * (2 * n)
-            + [pl.BlockSpec((depth, tile), lambda i, *_: (0, i))]
-            + [pl.BlockSpec((keep.shape[0], tile), lambda i, *_: (0, i))]
+            + [pl.BlockSpec((depth, tile), lambda i, *_: (0, strip * steps + i))] * 2
+            + [pl.BlockSpec((masks[0].shape[0], tile), lambda i, *_: (0, strip * steps + i))] * 2
             + [pl.BlockSpec(memory_space=pl.ANY)] * len(after),
-            out_specs=[out, out],
+            out_specs=[out] * 4,
             scratch_shapes=[pltpu.VMEM((n * rows, depth), jnp.bfloat16)],
         ),
-        out_shape=[
-            jax.ShapeDtypeStruct((n // 2, rows, width), jnp.float32),
-            jax.ShapeDtypeStruct((n // 2, rows, width), jnp.bfloat16),
-        ],
+        out_shape=[jax.ShapeDtypeStruct((n // 2, rows, width), jnp.float32)] * 2
+        + [jax.ShapeDtypeStruct((n // 2, rows, width), jnp.bfloat16)] * 2,
         compiler_params=pltpu.CompilerParams(vmem_limit_bytes=VMEM_BYTES),
         cost_estimate=pl.CostEstimate(
-            flops=2 * n * rows * depth * width, bytes_accessed=2 * depth * width, transcendentals=0
+            flops=4 * n * rows * depth * width, bytes_accessed=4 * depth * width, transcendentals=0
         ),
         name="project",
-    )(place, *own, *other, weight, keep, *after)
+    )(place, *own, *other, *weights, *masks, *after)
 
 
 def total_of(refs):
@@ -90,43 +95,47 @@
 
 
 def add_kernel(n, *refs):
-    refs[-1][...] = total_of(refs[:n]).astype(jnp.bfloat16)
-
-
-def add_slots(parts, first, count, after):
-    _, rows, width = parts[0].shape
-    n = len(parts)
+    refs[-2][...] = total_of(refs[:n]).astype(jnp.bfloat16)
+    refs[-1][...] = total_of(refs[n : 2 * n]).astype(jnp.bfloat16)
+
+
+def add_slots(gate_parts, up_parts, first, count, after):
+    _, rows, width = gate_parts[0].shape
+    n = len(gate_parts)
     return pl.pallas_call(
         functools.partial(add_kernel, n),
         grid=(count,),
-        in_specs=[pl.BlockSpec((1, rows, width), lambda i: (first + i, 0, 0))] * n
+        in_specs=[pl.BlockSpec((1, rows, width), lambda i: (first + i, 0, 0))] * (2 * n)
         + [pl.BlockSpec(memory_space=pl.ANY)] * len(after),
-        out_specs=pl.BlockSpec((1, rows, width), lambda i: (i, 0, 0)),
-        out_shape=jax.ShapeDtypeStruct((count, rows, width), jnp.bfloat16),
+        out_specs=[pl.BlockSpec((1, rows, width), lambda i: (i, 0, 0))] * 2,
+        out_shape=[jax.ShapeDtypeStruct((count, rows, width), jnp.bfloat16)] * 2,
         compiler_params=pltpu.CompilerParams(vmem_limit_bytes=VMEM_BYTES),
         name="add_slots",
-    )(*parts, *after)
+    )(*gate_parts, *up_parts, *after)
 
 
 def activate_kernel(n, *refs):
-    gate = total_of(refs[:n])
-    up = total_of(refs[n : 2 * n])
-    result = gate / (1.0 + jnp.exp(-gate)) * up
-    refs[-1][...] = result.reshape(refs[-1].shape).astype(jnp.bfloat16)
-
-
-def activate(gate_parts, up_parts, batch):
-    _, rows, width = gate_parts[0].shape
-    tile = width // 2
-    n = len(gate_parts)
+    out_ref = refs[-1]
+    width = out_ref.shape[1] // STRIPS
+    for i in range(STRIPS):
+        gate = total_of(refs[2 * n * i : 2 * n * i + n])
+        up = total_of(refs[2 * n * i + n : 2 * n * (i + 1)])
+        result = gate / (1.0 + jnp.exp(-gate)) * up
+        out_ref[:, i * width : (i + 1) * width] = result.reshape(-1, width).astype(jnp.bfloat16)
+
+
+def activate(strips, batch):
+    n = len(strips[0][0])
+    _, rows, width = strips[0][0][0].shape
     piece = rows // (2 * BATCHES)
-    parts = [part.reshape(part.shape[0] * 2, rows // 2, width) for part in gate_parts + up_parts]
+    parts = [part for gate_parts, up_parts in strips for part in gate_parts + up_parts]
+    parts = [part.reshape(part.shape[0] * 2, rows // 2, width) for part in parts]
     return pl.pallas_call(
         functools.partial(activate_kernel, n),
-        grid=(width // tile,),
-        in_specs=[pl.BlockSpec((2, piece, tile), lambda i: (0, batch, i))] * (2 * n),
-        out_specs=pl.BlockSpec((2 * piece, tile), lambda i: (0, i)),
-        out_shape=jax.ShapeDtypeStruct((2 * piece, width), jnp.bfloat16),
+        grid=(1,),
+        in_specs=[pl.BlockSpec((2, piece, width), lambda i: (0, batch, 0))] * len(parts),
+        out_specs=pl.BlockSpec((2 * piece, width * STRIPS), lambda i: (0, 0)),
+        out_shape=jax.ShapeDtypeStruct((2 * piece, width * STRIPS), jnp.bfloat16),
         compiler_params=pltpu.CompilerParams(vmem_limit_bytes=VMEM_BYTES),
         name="hidden",
     )(*parts)
@@ -215,8 +224,8 @@
     tok, hid = lax.axis_index("tok"), lax.axis_index("hid")
     z, core = hid // 2, hid % 2
     offsets = [jnp.where(core == 0, p, mirror(p, n_tok)) for p in range(n_tok)]
-    positions = [sum(jnp.where(off == tok ^ z ^ k, p, 0) for p, off in enumerate(offsets)) for k in range(n_tok)]
-    place = jnp.stack([core] + [tok ^ z ^ off for off in offsets] + positions).astype(jnp.int32)
+    place = jnp.stack([core] + [tok ^ z ^ off for off in offsets] + [tok ^ z ^ k for k in range(n_z)])
+    place = place.astype(jnp.int32)
 
     def send(value, to):
         perm = []
@@ -236,15 +245,17 @@
     def across_core(value):
         return send(value, lambda t, zz, c: (t, zz, 1 - c))
 
-    def halve(kept, sent, after):
+    def halve(gate_kept, up_kept, gate_sent, up_sent, after):
         left = n_tok // 2
-        parts = [kept]
+        gate_parts, up_parts = [gate_kept], [up_kept]
         while True:
-            parts.append(across_tok(sent, left))
+            turned = mirror(left, n_tok)
+            gate_parts.append(send(gate_sent, lambda t, zz, c: (t ^ left, zz, c)))
+            up_parts.append(send(up_sent, lambda t, zz, c: (t ^ turned, zz, c)))
             if left == 1:
-                return parts, sent
+                return gate_parts, up_parts, gate_sent
             left //= 2
-            sent = add_slots(parts, left, left, after)
+            gate_sent, up_sent = add_slots(gate_parts, up_parts, left, left, after)
 
     def gather(part):
         parts, left = [part], 1
@@ -263,11 +274,17 @@
     down_wide = widen(down_keep, down_weight.shape[1])
     own = [send(tokens, lambda t, zz, c: (zz, t ^ k, c)) for k in range(n_z)]
     other = [across_core(block) for block in own]
-    gate_kept, gate_sent = project(place, own, other, gate_weight, gate_wide, ())
-    up_kept, up_sent = project(place, own, other, up_weight, up_wide, (gate_sent,))
-    gate_parts, gate_last = halve(gate_kept, gate_sent, (up_sent,))
-    up_parts, _ = halve(up_kept, up_sent, (gate_last,))
-    hidden = [gather(activate(gate_parts, up_parts, s)) for s in range(BATCHES)]
+    weights, masks = (gate_weight, up_weight), (gate_wide, up_wide)
+    sums, after = [], ()
+    for i in range(STRIPS):
+        sums.append(project(place, own, other, weights, masks, i, after))
+        after = (sums[i][2],)
+    strips = []
+    for i in range(STRIPS):
+        gate_parts, up_parts, last = halve(*sums[i], after)
+        strips.append((gate_parts, up_parts))
+        after = (last,)
+    hidden = [gather(activate(strips, s)) for s in range(BATCHES)]
     out, beside = [], []
     for s, parts in enumerate(hidden):
         for later in hidden[s + 1 : s + 2]:

time: 143 us -> 138 us (0.965)
  waiting for transfers between devices: 68.3 us -> 57.2 us
  starting transfers between devices: 41.1 us -> 47.8 us
    ppermute x26 -> x30, waiting for transfers between devices: 68.3 us -> 57.2 us  [send(): return lax.ppermute(value, AXES, perm)]
    ppermute x26 -> x30, starting transfers between devices: 41.1 us -> 47.8 us  [send(): return lax.ppermute(value, AXES, perm)]
  transfers between devices with their start and end apart: 26 -> 30, of which waited for: 13 -> 17; matrix products, arithmetic and copies ran while one was open for 1% -> 1% of each run, Pallas kernels for 15% -> 15%
where the time goes in v9:
time: 138 us; the launch traced here: 137 us
  waiting for transfers between devices  57.2 us (41%)
  starting transfers between devices  47.8 us (35%)
  Pallas kernels  29 us (21%)
  other arithmetic  2.48 us (2%)
    ppermute x30, waiting for transfers between devices, send(): return lax.ppermute(value, AXES, perm)  57.2 us
    ppermute x30, starting transfers between devices, send(): return lax.ppermute(value, AXES, perm)  47.8 us
    pallas_call x2, Pallas kernels, project(): pl.pallas_call(functools.partial(project_kernel, n), grid_spec=pltpu.Pref...  15.7 us
    pallas_call x2, Pallas kernels, down(): pl.pallas_call(functools.partial(down_kernel, n), grid_spec=pltpu.Prefetc...  12.5 us
  transfers between devices with their start and end apart: 30, of which 17 were waited for; matrix products, arithmetic and copies ran while one was open for 1% of the time, Pallas kernels for 15%

profile of v9, /device:TPU:0, one launch (start us, length us, event | category | flops | bytes accessed | tf_op | source)
XLA Modules:
  0.0 137.2 jit_solution(145409992816504022)
XLA Ops:
  0.0 3.0 %collective-permute-start.1 = (bf16[128,1024]{1,0:T(8,128)(2,1)}, bf16[128,1024]{1,0:T(8,128)(2,1)S(1)}, u32[]{:S(2)}, u32[]{:S(2)}) collective-permute-start(bf16[128,1024]{1,0:T(8,128)(2,1)} %param.7), channel_id=1, source_target_pairs={{0,2},{1,3},{2,10},{3,11},{4,18},{5,19},{6,26},{7,27},{8,0},{9,1},... | collective-permute-start | bytes 786440 | tf_op jit(solution)/shard_map/ppermute | solution.py:237
  3.0 1.6 %collective-permute-start = (bf16[128,1024]{1,0:T(8,128)(2,1)}, bf16[128,1024]{1,0:T(8,128)(2,1)S(1)}, u32[]{:S(2)}, u32[]{:S(2)}) collective-permute-start(bf16[128,1024]{1,0:T(8,128)(2,1)} %param.7), channel_id=1, source_target_pairs={{0,0},{1,1},{2,8},{3,9},{4,16},{5,17},{6,24},{7,25},{8,2},{9,3},{1... | collective-permute-start | bytes 786440 | tf_op jit(solution)/shard_map/ppermute | solution.py:237
  4.6 7.0 %collective-permute-start.3 = (bf16[128,1024]{1,0:T(8,128)(2,1)}, bf16[128,1024]{1,0:T(8,128)(2,1)S(1)}, u32[]{:S(2)}, u32[]{:S(2)}) collective-permute-start(bf16[128,1024]{1,0:T(8,128)(2,1)} %param.7), channel_id=1, source_target_pairs={{0,6},{1,7},{2,14},{3,15},{4,22},{5,23},{6,30},{7,31},{8,4},{9,5},... | collective-permute-start | bytes 786440 | tf_op jit(solution)/shard_map/ppermute | solution.py:237
  11.6 0.7 convert_element_type.101
  12.3 0.7 convert_element_type.102
  13.2 0.5 collective-permute-start.4
  13.7 6.7 %collective-permute-done.3.refs_3_ = bf16[128,1024]{1,0:T(8,128)(2,1)S(1)} collective-permute-done((bf16[128,1024]{1,0:T(8,128)(2,1)}, bf16[128,1024]{1,0:T(8,128)(2,1)S(1)}, u32[]{:S(2)}, u32[]{:S(2)}) %collective-permute-start.3) | collective-permute-done | bytes 262176 | tf_op jit(solution)/shard_map/ppermute | solution.py:237
  20.4 3.9 %collective-permute-done.2.refs_2_ = bf16[128,1024]{1,0:T(8,128)(2,1)S(1)} collective-permute-done((bf16[128,1024]{1,0:T(8,128)(2,1)}, bf16[128,1024]{1,0:T(8,128)(2,1)S(1)}, u32[]{:S(2)}, u32[]{:S(2)}) %collective-permute-start.2) | collective-permute-done | bytes 262176 | tf_op jit(solution)/shard_map/ppermute | solution.py:237
  24.4 0.1 broadcast_in_dim.9
  24.6 1.2 collective-permute-done.6.refs_6_
  25.8 7.9 %project.2 = (f32[2,128,1024]{2,1,0:T(8,128)S(1)}, f32[2,128,1024]{2,1,0:T(8,128)S(1)}, bf16[2,128,1024]{2,1,0:T(8,128)(2,1)S(1)}, bf16[2,128,1024]{2,1,0:T(8,128)(2,1)S(1)}) custom-call(s32[9]{0:T(128)S(1)} %stack.33.place_ref, bf16[128,1024]{1,0:T(8,128)(2,1)S(1)} %collective-permute-done.refs_0_, bf16[128,1024]{1,0:T(8,128)(2,1)S(1)} %collective-permute-done.1.refs_1_, ...), custom_call_target="tpu_custom_call" | custom-call | flops 4294967296 | bytes 8388608 | tf_op jit(solution)/shard_map/project/pallas_call | solution.py:68
  33.7 2.3 %collective-permute-start.9 = (bf16[2,128,1024]{2,1,0:T(8,128)(2,1)S(1)}, bf16[2,128,1024]{2,1,0:T(8,128)(2,1)S(1)}, u32[]{:S(2)}, u32[]{:S(2)}) collective-permute-start(bf16[2,128,1024]{2,1,0:T(8,128)(2,1)S(1)} %get-tuple-element.24), channel_id=1, source_target_pairs={{0,8},{1,9},{2,10},{3,11},{4,12},{5,13},{6,14},{7,15},{8,0},{9,1},... | collective-permute-start | bytes 1572872 | tf_op jit(solution)/shard_map/ppermute | solution.py:237
  36.0 7.8 %collective-permute-start.8 = (bf16[2,128,1024]{2,1,0:T(8,128)(2,1)S(1)}, bf16[2,128,1024]{2,1,0:T(8,128)(2,1)S(1)}, u32[]{:S(2)}, u32[]{:S(2)}) collective-permute-start(bf16[2,128,1024]{2,1,0:T(8,128)(2,1)S(1)} %get-tuple-element.22.refs_12_), channel_id=1, source_target_pairs={{0,16},{1,17},{2,18},{3,19},{4,20},{5,21},{6,22},{7,23},{8,24},{9,... | collective-permute-start | bytes 1572872 | tf_op jit(solution)/shard_map/ppermute | solution.py:237
  43.8 7.9 %project.3 = (f32[2,128,1024]{2,1,0:T(8,128)S(1)}, f32[2,128,1024]{2,1,0:T(8,128)S(1)}, bf16[2,128,1024]{2,1,0:T(8,128)(2,1)S(1)}, bf16[2,128,1024]{2,1,0:T(8,128)(2,1)S(1)}) custom-call(s32[9]{0:T(128)S(1)} %stack.33.place_ref, bf16[128,1024]{1,0:T(8,128)(2,1)S(1)} %collective-permute-done.refs_0_, bf16[128,1024]{1,0:T(8,128)(2,1)S(1)} %collective-permute-done.1.refs_1_, ...), custom_call_target="tpu_custom_call" | custom-call | flops 4294967296 | bytes 8388608 | tf_op jit(solution)/shard_map/project/pallas_call | solution.py:68
  51.7 2.0 %collective-permute-start.13 = (bf16[2,128,1024]{2,1,0:T(8,128)(2,1)S(1)}, bf16[2,128,1024]{2,1,0:T(8,128)(2,1)S(1)}, u32[]{:S(2)}, u32[]{:S(2)}) collective-permute-start(bf16[2,128,1024]{2,1,0:T(8,128)(2,1)S(1)} %get-tuple-element.30), channel_id=1, source_target_pairs={{0,8},{1,9},{2,10},{3,11},{4,12},{5,13},{6,14},{7,15},{8,0},{9,1},... | collective-permute-start | bytes 1572872 | tf_op jit(solution)/shard_map/ppermute | solution.py:237
  53.7 2.7 %collective-permute-done.8.refs_1_ = bf16[2,128,1024]{2,1,0:T(8,128)(2,1)S(1)} collective-permute-done((bf16[2,128,1024]{2,1,0:T(8,128)(2,1)S(1)}, bf16[2,128,1024]{2,1,0:T(8,128)(2,1)S(1)}, u32[]{:S(2)}, u32[]{:S(2)}) %collective-permute-start.8) | collective-permute-done | bytes 524320 | tf_op jit(solution)/shard_map/ppermute | solution.py:237
  56.5 2.2 %collective-permute-start.11 = (bf16[1,128,1024]{2,1,0:T(8,128)(2,1)S(1)}, bf16[1,128,1024]{2,1,0:T(8,128)(2,1)S(1)}, u32[]{:S(2)}, u32[]{:S(2)}) collective-permute-start(bf16[1,128,1024]{2,1,0:T(8,128)(2,1)S(1)} %get-tuple-element.27), channel_id=1, source_target_pairs={{0,16},{1,17},{2,18},{3,19},{4,20},{5,21},{6,22},{7,23},{8,24},{9,... | collective-permute-start | bytes 786440 | tf_op jit(solution)/shard_map/ppermute | solution.py:237
  58.7 2.0 %collective-permute-start.10 = (bf16[1,128,1024]{2,1,0:T(8,128)(2,1)S(1)}, bf16[1,128,1024]{2,1,0:T(8,128)(2,1)S(1)}, u32[]{:S(2)}, u32[]{:S(2)}) collective-permute-start(bf16[1,128,1024]{2,1,0:T(8,128)(2,1)S(1)} %get-tuple-element.26.refs_4_), channel_id=1, source_target_pairs={{0,8},{1,9},{2,10},{3,11},{4,12},{5,13},{6,14},{7,15},{8,0},{9,1},... | collective-permute-start | bytes 786440 | tf_op jit(solution)/shard_map/ppermute | solution.py:237
  60.7 5.8 %collective-permute-done.13.refs_3_ = bf16[2,128,1024]{2,1,0:T(8,128)(2,1)S(1)} collective-permute-done((bf16[2,128,1024]{2,1,0:T(8,128)(2,1)S(1)}, bf16[2,128,1024]{2,1,0:T(8,128)(2,1)S(1)}, u32[]{:S(2)}, u32[]{:S(2)}) %collective-permute-start.13) | collective-permute-done | bytes 524320 | tf_op jit(solution)/shard_map/ppermute | solution.py:237
  66.5 2.0 %collective-permute-done.12.refs_1_ = bf16[2,128,1024]{2,1,0:T(8,128)(2,1)S(1)} collective-permute-done((bf16[2,128,1024]{2,1,0:T(8,128)(2,1)S(1)}, bf16[2,128,1024]{2,1,0:T(8,128)(2,1)S(1)}, u32[]{:S(2)}, u32[]{:S(2)}) %collective-permute-start.12) | collective-permute-done | bytes 524320 | tf_op jit(solution)/shard_map/ppermute | solution.py:237
  68.6 1.2 collective-permute-start.14
  69.9 2.1 %collective-permute-start.15 = (bf16[1,128,1024]{2,1,0:T(8,128)(2,1)S(1)}, bf16[1,128,1024]{2,1,0:T(8,128)(2,1)S(1)}, u32[]{:S(2)}, u32[]{:S(2)}) collective-permute-start(bf16[1,128,1024]{2,1,0:T(8,128)(2,1)S(1)} %get-tuple-element.32), channel_id=1, source_target_pairs={{0,16},{1,17},{2,18},{3,19},{4,20},{5,21},{6,22},{7,23},{8,24},{9,... | collective-permute-start | bytes 786440 | tf_op jit(solution)/shard_map/ppermute | solution.py:237
  71.9 2.2 %collective-permute-done.11 = bf16[1,128,1024]{2,1,0:T(8,128)(2,1)S(1)} collective-permute-done((bf16[1,128,1024]{2,1,0:T(8,128)(2,1)S(1)}, bf16[1,128,1024]{2,1,0:T(8,128)(2,1)S(1)}, u32[]{:S(2)}, u32[]{:S(2)}) %collective-permute-start.11) | collective-permute-done | bytes 262176 | tf_op jit(solution)/shard_map/ppermute | solution.py:237
  74.2 2.5 %collective-permute-done.14 = bf16[1,128,1024]{2,1,0:T(8,128)(2,1)S(1)} collective-permute-done((bf16[1,128,1024]{2,1,0:T(8,128)(2,1)S(1)}, bf16[1,128,1024]{2,1,0:T(8,128)(2,1)S(1)}, u32[]{:S(2)}, u32[]{:S(2)}) %collective-permute-start.14) | collective-permute-done | bytes 262176 | tf_op jit(solution)/shard_map/ppermute | solution.py:237
  76.7 1.8 %collective-permute-done.15 = bf16[1,128,1024]{2,1,0:T(8,128)(2,1)S(1)} collective-permute-done((bf16[1,128,1024]{2,1,0:T(8,128)(2,1)S(1)}, bf16[1,128,1024]{2,1,0:T(8,128)(2,1)S(1)}, u32[]{:S(2)}, u32[]{:S(2)}) %collective-permute-start.15) | collective-permute-done | bytes 262176 | tf_op jit(solution)/shard_map/ppermute | solution.py:237
  78.5 0.3 hidden.2.refs_0_
  78.8 1.7 %collective-permute-start.16 = (bf16[64,2048]{1,0:T(8,128)(2,1)S(1)}, bf16[64,2048]{1,0:T(8,128)(2,1)S(1)}, u32[]{:S(2)}, u32[]{:S(2)}) collective-permute-start(bf16[64,2048]{1,0:T(8,128)(2,1)S(1)} %hidden.2.refs_0_), channel_id=1, source_target_pairs={{0,8},{1,17},{2,10},{3,19},{4,12},{5,21},{6,14},{7,23},{8,0},{9,25... | collective-permute-start | bytes 786440 | tf_op jit(solution)/shard_map/ppermute | solution.py:237
  80.5 0.3 hidden.3.refs_0_
  80.8 0.4 collective-permute-start.19
  81.2 1.7 %collective-permute-start.17 = (bf16[64,2048]{1,0:T(8,128)(2,1)S(1)}, bf16[64,2048]{1,0:T(8,128)(2,1)S(1)}, u32[]{:S(2)}, u32[]{:S(2)}) collective-permute-start(bf16[64,2048]{1,0:T(8,128)(2,1)S(1)} %hidden.2.refs_0_), channel_id=1, source_target_pairs={{0,16},{1,9},{2,18},{3,11},{4,20},{5,13},{6,22},{7,15},{8,24},{9,1... | collective-permute-start | bytes 786440 | tf_op jit(solution)/shard_map/ppermute | solution.py:237
  82.9 4.9 %collective-permute-done.16.refs_1_ = bf16[64,2048]{1,0:T(8,128)(2,1)S(1)} collective-permute-done((bf16[64,2048]{1,0:T(8,128)(2,1)S(1)}, bf16[64,2048]{1,0:T(8,128)(2,1)S(1)}, u32[]{:S(2)}, u32[]{:S(2)}) %collective-permute-start.16) | collective-permute-done | bytes 262176 | tf_op jit(solution)/shard_map/ppermute | solution.py:237
  87.9 1.8 %collective-permute-start.18 = (bf16[64,2048]{1,0:T(8,128)(2,1)S(1)}, bf16[64,2048]{1,0:T(8,128)(2,1)S(1)}, u32[]{:S(2)}, u32[]{:S(2)}) collective-permute-start(bf16[64,2048]{1,0:T(8,128)(2,1)S(1)} %collective-permute-done.16.refs_1_), channel_id=1, source_target_pairs={{0,16},{1,9},{2,18},{3,11},{4,20},{5,13},{6,22},{7,15},{8,24},{9,1... | collective-permute-start | bytes 786440 | tf_op jit(solution)/shard_map/ppermute | solution.py:237
  89.7 0.2 collective-permute-start.20
  89.9 3.6 %collective-permute-done.19.refs_0_.refs_1_ = bf16[64,2048]{1,0:T(8,128)(2,1)S(1)} collective-permute-done((bf16[64,2048]{1,0:T(8,128)(2,1)S(1)}, bf16[64,2048]{1,0:T(8,128)(2,1)S(1)}, u32[]{:S(2)}, u32[]{:S(2)}) %collective-permute-start.19) | collective-permute-done | bytes 262176 | tf_op jit(solution)/shard_map/ppermute | solution.py:237
  93.5 1.8 %collective-permute-start.21 = (bf16[64,2048]{1,0:T(8,128)(2,1)S(1)}, bf16[64,2048]{1,0:T(8,128)(2,1)S(1)}, u32[]{:S(2)}, u32[]{:S(2)}) collective-permute-start(bf16[64,2048]{1,0:T(8,128)(2,1)S(1)} %collective-permute-done.19.refs_0_.refs_1_), channel_id=1, source_target_pairs={{0,16},{1,9},{2,18},{3,11},{4,20},{5,13},{6,22},{7,15},{8,24},{9,1... | collective-permute-start | bytes 786440 | tf_op jit(solution)/shard_map/ppermute | solution.py:237
  95.5 6.2 %down.2 = (f32[4,32,2048]{2,1,0:T(8,128)S(1)}, bf16[4,32,2048]{2,1,0:T(8,128)(2,1)S(1)}) custom-call(s32[9]{0:T(128)S(1)} %stack.33.place_ref, bf16[64,2048]{1,0:T(8,128)(2,1)S(1)} %hidden.2.refs_0_, bf16[64,2048]{1,0:T(8,128)(2,1)S(1)} %collective-permute-done.16.refs_1_, bf16[64,2048]{1,0:T(8,128)(2,1)S(1)} %collective-permute-done.17.refs_2_, ...), custom_call_target="tpu_custom_call" | custom-call | flops 2147483648 | bytes 8388608 | tf_op jit(solution)/shard_map/down/pallas_call | solution.py:173
  101.9 1.9 %collective-permute-done.22 = bf16[4,32,2048]{2,1,0:T(8,128)(2,1)S(1)} collective-permute-done((bf16[4,32,2048]{2,1,0:T(8,128)(2,1)S(1)}, bf16[4,32,2048]{2,1,0:T(8,128)(2,1)S(1)}, u32[]{:S(2)}, u32[]{:S(2)}) %collective-permute-start.22) | collective-permute-done | bytes 524320 | tf_op jit(solution)/shard_map/ppermute | solution.py:237
  103.9 3.9 %collective-permute-start.25 = (bf16[32,2048]{1,0:T(8,128)(2,1)S(1)}, bf16[32,2048]{1,0:T(8,128)(2,1)S(1)}, u32[]{:S(2)}, u32[]{:S(2)}) collective-permute-start(bf16[32,2048]{1,0:T(8,128)(2,1)S(1)} %get-tuple-element.40), channel_id=1, source_target_pairs={{0,6},{1,7},{2,4},{3,5},{4,2},{5,3},{6,0},{7,1},{8,14},{9,15},{10,... | collective-permute-start | bytes 393224 | tf_op jit(solution)/shard_map/ppermute | solution.py:237
  107.8 0.6 collective-permute-start.23
  108.4 6.2 %down.3 = (f32[4,32,2048]{2,1,0:T(8,128)S(1)}, bf16[4,32,2048]{2,1,0:T(8,128)(2,1)S(1)}) custom-call(s32[9]{0:T(128)S(1)} %stack.33.place_ref, bf16[64,2048]{1,0:T(8,128)(2,1)S(1)} %hidden.3.refs_0_, bf16[64,2048]{1,0:T(8,128)(2,1)S(1)} %collective-permute-done.19.refs_0_.refs_1_, bf16[64,2048]{1,0:T(8,128)(2,1)S(1)} %collective-permute-done.20.refs_1_.refs_2_, ...), custom_call_target="tpu_custom_call" | custom-call | flops 2147483648 | bytes 8388608 | tf_op jit(solution)/shard_map/down/pallas_call | solution.py:173
  114.7 4.4 %collective-permute-done.24.refs_1_ = bf16[32,2048]{1,0:T(8,128)(2,1)S(1)} collective-permute-done((bf16[32,2048]{1,0:T(8,128)(2,1)S(1)}, bf16[32,2048]{1,0:T(8,128)(2,1)S(1)}, u32[]{:S(2)}, u32[]{:S(2)}) %collective-permute-start.24) | collective-permute-done | bytes 131104 | tf_op jit(solution)/shard_map/ppermute | solution.py:237
  119.1 1.9 %collective-permute-done.26 = bf16[4,32,2048]{2,1,0:T(8,128)(2,1)S(1)} collective-permute-done((bf16[4,32,2048]{2,1,0:T(8,128)(2,1)S(1)}, bf16[4,32,2048]{2,1,0:T(8,128)(2,1)S(1)}, u32[]{:S(2)}, u32[]{:S(2)}) %collective-permute-start.26) | collective-permute-done | bytes 524320 | tf_op jit(solution)/shard_map/ppermute | solution.py:237
  121.2 2.7 %collective-permute-start.29 = (bf16[32,2048]{1,0:T(8,128)(2,1)S(1)}, bf16[32,2048]{1,0:T(8,128)(2,1)S(1)}, u32[]{:S(2)}, u32[]{:S(2)}) collective-permute-start(bf16[32,2048]{1,0:T(8,128)(2,1)S(1)} %get-tuple-element.38), channel_id=1, source_target_pairs={{0,6},{1,7},{2,4},{3,5},{4,2},{5,3},{6,0},{7,1},{8,14},{9,15},{10,... | collective-permute-start | bytes 393224 | tf_op jit(solution)/shard_map/ppermute | solution.py:237
  123.9 0.8 collective-permute-start.28
  124.8 2.0 %collective-permute-done.27 = bf16[32,2048]{1,0:T(8,128)(2,1)S(1)} collective-permute-done((bf16[32,2048]{1,0:T(8,128)(2,1)S(1)}, bf16[32,2048]{1,0:T(8,128)(2,1)S(1)}, u32[]{:S(2)}, u32[]{:S(2)}) %collective-permute-start.27) | collective-permute-done | bytes 131104 | tf_op jit(solution)/shard_map/ppermute | solution.py:237
  126.7 4.3 %collective-permute-done.29 = bf16[32,2048]{1,0:T(8,128)(2,1)S(1)} collective-permute-done((bf16[32,2048]{1,0:T(8,128)(2,1)S(1)}, bf16[32,2048]{1,0:T(8,128)(2,1)S(1)}, u32[]{:S(2)}, u32[]{:S(2)}) %collective-permute-start.29) | collective-permute-done | bytes 131104 | tf_op jit(solution)/shard_map/ppermute | solution.py:237
  131.0 5.3 %collective-permute-done.28 = bf16[32,2048]{1,0:T(8,128)(2,1)S(1)} collective-permute-done((bf16[32,2048]{1,0:T(8,128)(2,1)S(1)}, bf16[32,2048]{1,0:T(8,128)(2,1)S(1)}, u32[]{:S(2)}, u32[]{:S(2)}) %collective-permute-start.28) | collective-permute-done | bytes 131104 | tf_op jit(solution)/shard_map/ppermute | solution.py:237
  136.4 0.7 pad_maximum_fusion
  (38 shorter events, 1.3 us)
Async XLA Ops:
  0.0 13.1 %collective-permute-start.1 = (bf16[128,1024]{1,0:T(8,128)(2,1)}, bf16[128,1024]{1,0:T(8,128)(2,1)S(1)}, u32[]{:S(2)}, u32[]{:S(2)}) collective-permute-start(bf16[128,1024]{1,0:T(8,128)(2,1)} %param.7), channel_id=1, source_target_pairs={{0,2},{1,3},{2,10},{3,11},{4,18},{5,19},{6,26},{7,27},{8,0},{9,1},... | collective-permute-start | bytes 786440 | tf_op jit(solution)/shard_map/ppermute | solution.py:237
  3.0 10.2 %collective-permute-start = (bf16[128,1024]{1,0:T(8,128)(2,1)}, bf16[128,1024]{1,0:T(8,128)(2,1)S(1)}, u32[]{:S(2)}, u32[]{:S(2)}) collective-permute-start(bf16[128,1024]{1,0:T(8,128)(2,1)} %param.7), channel_id=1, source_target_pairs={{0,0},{1,1},{2,8},{3,9},{4,16},{5,17},{6,24},{7,25},{8,2},{9,3},{1... | collective-permute-start | bytes 786440 | tf_op jit(solution)/shard_map/ppermute | solution.py:237
  4.6 15.8 %collective-permute-start.3 = (bf16[128,1024]{1,0:T(8,128)(2,1)}, bf16[128,1024]{1,0:T(8,128)(2,1)S(1)}, u32[]{:S(2)}, u32[]{:S(2)}) collective-permute-start(bf16[128,1024]{1,0:T(8,128)(2,1)} %param.7), channel_id=1, source_target_pairs={{0,6},{1,7},{2,14},{3,15},{4,22},{5,23},{6,30},{7,31},{8,4},{9,5},... | collective-permute-start | bytes 786440 | tf_op jit(solution)/shard_map/ppermute | solution.py:237
  11.6 12.7 %collective-permute-start.2 = (bf16[128,1024]{1,0:T(8,128)(2,1)}, bf16[128,1024]{1,0:T(8,128)(2,1)S(1)}, u32[]{:S(2)}, u32[]{:S(2)}) collective-permute-start(bf16[128,1024]{1,0:T(8,128)(2,1)} %param.7), channel_id=1, source_target_pairs={{0,4},{1,5},{2,12},{3,13},{4,20},{5,21},{6,28},{7,29},{8,6},{9,7},... | collective-permute-start | bytes 786440 | tf_op jit(solution)/shard_map/ppermute | solution.py:237
  13.1 11.5 %collective-permute-start.5 = (bf16[128,1024]{1,0:T(8,128)(2,1)S(1)}, bf16[128,1024]{1,0:T(8,128)(2,1)S(1)}, u32[]{:S(2)}, u32[]{:S(2)}) collective-permute-start(bf16[128,1024]{1,0:T(8,128)(2,1)S(1)} %collective-permute-done.1.refs_1_), channel_id=1, source_target_pairs={{0,1},{1,0},{2,3},{3,2},{4,5},{5,4},{6,7},{7,6},{8,9},{9,8},{10,11... | collective-permute-start | bytes 786440 | tf_op jit(solution)/shard_map/ppermute | solution.py:237
  13.2 11.4 %collective-permute-start.4 = (bf16[128,1024]{1,0:T(8,128)(2,1)S(1)}, bf16[128,1024]{1,0:T(8,128)(2,1)S(1)}, u32[]{:S(2)}, u32[]{:S(2)}) collective-permute-start(bf16[128,1024]{1,0:T(8,128)(2,1)S(1)} %collective-permute-done.refs_0_), channel_id=1, source_target_pairs={{0,1},{1,0},{2,3},{3,2},{4,5},{5,4},{6,7},{7,6},{8,9},{9,8},{10,11... | collective-permute-start | bytes 786440 | tf_op jit(solution)/shard_map/ppermute | solution.py:237
  20.4 4.2 %collective-permute-start.7 = (bf16[128,1024]{1,0:T(8,128)(2,1)S(1)}, bf16[128,1024]{1,0:T(8,128)(2,1)S(1)}, u32[]{:S(2)}, u32[]{:S(2)}) collective-permute-start(bf16[128,1024]{1,0:T(8,128)(2,1)S(1)} %collective-permute-done.3.refs_3_), channel_id=1, source_target_pairs={{0,1},{1,0},{2,3},{3,2},{4,5},{5,4},{6,7},{7,6},{8,9},{9,8},{10,11... | collective-permute-start | bytes 786440 | tf_op jit(solution)/shard_map/ppermute | solution.py:237
  24.3 1.5 %collective-permute-start.6 = (bf16[128,1024]{1,0:T(8,128)(2,1)S(1)}, bf16[128,1024]{1,0:T(8,128)(2,1)S(1)}, u32[]{:S(2)}, u32[]{:S(2)}) collective-permute-start(bf16[128,1024]{1,0:T(8,128)(2,1)S(1)} %collective-permute-done.2.refs_2_), channel_id=1, source_target_pairs={{0,1},{1,0},{2,3},{3,2},{4,5},{5,4},{6,7},{7,6},{8,9},{9,8},{10,11... | collective-permute-start | bytes 786440 | tf_op jit(solution)/shard_map/ppermute | solution.py:237
  33.7 20.0 %collective-permute-start.9 = (bf16[2,128,1024]{2,1,0:T(8,128)(2,1)S(1)}, bf16[2,128,1024]{2,1,0:T(8,128)(2,1)S(1)}, u32[]{:S(2)}, u32[]{:S(2)}) collective-permute-start(bf16[2,128,1024]{2,1,0:T(8,128)(2,1)S(1)} %get-tuple-element.24), channel_id=1, source_target_pairs={{0,8},{1,9},{2,10},{3,11},{4,12},{5,13},{6,14},{7,15},{8,0},{9,1},... | collective-permute-start | bytes 1572872 | tf_op jit(solution)/shard_map/ppermute | solution.py:237
  36.0 20.4 %collective-permute-start.8 = (bf16[2,128,1024]{2,1,0:T(8,128)(2,1)S(1)}, bf16[2,128,1024]{2,1,0:T(8,128)(2,1)S(1)}, u32[]{:S(2)}, u32[]{:S(2)}) collective-permute-start(bf16[2,128,1024]{2,1,0:T(8,128)(2,1)S(1)} %get-tuple-element.22.refs_12_), channel_id=1, source_target_pairs={{0,16},{1,17},{2,18},{3,19},{4,20},{5,21},{6,22},{7,23},{8,24},{9,... | collective-permute-start | bytes 1572872 | tf_op jit(solution)/shard_map/ppermute | solution.py:237
  51.7 14.9 %collective-permute-start.13 = (bf16[2,128,1024]{2,1,0:T(8,128)(2,1)S(1)}, bf16[2,128,1024]{2,1,0:T(8,128)(2,1)S(1)}, u32[]{:S(2)}, u32[]{:S(2)}) collective-permute-start(bf16[2,128,1024]{2,1,0:T(8,128)(2,1)S(1)} %get-tuple-element.30), channel_id=1, source_target_pairs={{0,8},{1,9},{2,10},{3,11},{4,12},{5,13},{6,14},{7,15},{8,0},{9,1},... | collective-permute-start | bytes 1572872 | tf_op jit(solution)/shard_map/ppermute | solution.py:237
  53.7 14.9 %collective-permute-start.12 = (bf16[2,128,1024]{2,1,0:T(8,128)(2,1)S(1)}, bf16[2,128,1024]{2,1,0:T(8,128)(2,1)S(1)}, u32[]{:S(2)}, u32[]{:S(2)}) collective-permute-start(bf16[2,128,1024]{2,1,0:T(8,128)(2,1)S(1)} %get-tuple-element.25.refs_4_), channel_id=1, source_target_pairs={{0,16},{1,17},{2,18},{3,19},{4,20},{5,21},{6,22},{7,23},{8,24},{9,... | collective-permute-start | bytes 1572872 | tf_op jit(solution)/shard_map/ppermute | solution.py:237
  56.5 17.7 %collective-permute-start.11 = (bf16[1,128,1024]{2,1,0:T(8,128)(2,1)S(1)}, bf16[1,128,1024]{2,1,0:T(8,128)(2,1)S(1)}, u32[]{:S(2)}, u32[]{:S(2)}) collective-permute-start(bf16[1,128,1024]{2,1,0:T(8,128)(2,1)S(1)} %get-tuple-element.27), channel_id=1, source_target_pairs={{0,16},{1,17},{2,18},{3,19},{4,20},{5,21},{6,22},{7,23},{8,24},{9,... | collective-permute-start | bytes 786440 | tf_op jit(solution)/shard_map/ppermute | solution.py:237
  58.7 15.4 %collective-permute-start.10 = (bf16[1,128,1024]{2,1,0:T(8,128)(2,1)S(1)}, bf16[1,128,1024]{2,1,0:T(8,128)(2,1)S(1)}, u32[]{:S(2)}, u32[]{:S(2)}) collective-permute-start(bf16[1,128,1024]{2,1,0:T(8,128)(2,1)S(1)} %get-tuple-element.26.refs_4_), channel_id=1, source_target_pairs={{0,8},{1,9},{2,10},{3,11},{4,12},{5,13},{6,14},{7,15},{8,0},{9,1},... | collective-permute-start | bytes 786440 | tf_op jit(solution)/shard_map/ppermute | solution.py:237
  68.6 26.7 %copy-start = (s32[16,16]{1,0:T(8,128)S(1)}, s32[16,16]{1,0:T(8,128)}, u32[]{:S(2)}) copy-start(s32[16,16]{1,0:T(8,128)} %param.13) | copy-start | bytes 3076
  68.6 8.0 %collective-permute-start.14 = (bf16[1,128,1024]{2,1,0:T(8,128)(2,1)S(1)}, bf16[1,128,1024]{2,1,0:T(8,128)(2,1)S(1)}, u32[]{:S(2)}, u32[]{:S(2)}) collective-permute-start(bf16[1,128,1024]{2,1,0:T(8,128)(2,1)S(1)} %get-tuple-element.31), channel_id=1, source_target_pairs={{0,8},{1,9},{2,10},{3,11},{4,12},{5,13},{6,14},{7,15},{8,0},{9,1},... | collective-permute-start | bytes 786440 | tf_op jit(solution)/shard_map/ppermute | solution.py:237
  69.9 8.6 %collective-permute-start.15 = (bf16[1,128,1024]{2,1,0:T(8,128)(2,1)S(1)}, bf16[1,128,1024]{2,1,0:T(8,128)(2,1)S(1)}, u32[]{:S(2)}, u32[]{:S(2)}) collective-permute-start(bf16[1,128,1024]{2,1,0:T(8,128)(2,1)S(1)} %get-tuple-element.32), channel_id=1, source_target_pairs={{0,16},{1,17},{2,18},{3,19},{4,20},{5,21},{6,22},{7,23},{8,24},{9,... | collective-permute-start | bytes 786440 | tf_op jit(solution)/shard_map/ppermute | solution.py:237
  78.8 9.1 %collective-permute-start.16 = (bf16[64,2048]{1,0:T(8,128)(2,1)S(1)}, bf16[64,2048]{1,0:T(8,128)(2,1)S(1)}, u32[]{:S(2)}, u32[]{:S(2)}) collective-permute-start(bf16[64,2048]{1,0:T(8,128)(2,1)S(1)} %hidden.2.refs_0_), channel_id=1, source_target_pairs={{0,8},{1,17},{2,10},{3,19},{4,12},{5,21},{6,14},{7,23},{8,0},{9,25... | collective-permute-start | bytes 786440 | tf_op jit(solution)/shard_map/ppermute | solution.py:237
  80.8 12.7 %collective-permute-start.19 = (bf16[64,2048]{1,0:T(8,128)(2,1)S(1)}, bf16[64,2048]{1,0:T(8,128)(2,1)S(1)}, u32[]{:S(2)}, u32[]{:S(2)}) collective-permute-start(bf16[64,2048]{1,0:T(8,128)(2,1)S(1)} %hidden.3.refs_0_), channel_id=1, source_target_pairs={{0,8},{1,17},{2,10},{3,19},{4,12},{5,21},{6,14},{7,23},{8,0},{9,25... | collective-permute-start | bytes 786440 | tf_op jit(solution)/shard_map/ppermute | solution.py:237
  81.2 14.3 %collective-permute-start.17 = (bf16[64,2048]{1,0:T(8,128)(2,1)S(1)}, bf16[64,2048]{1,0:T(8,128)(2,1)S(1)}, u32[]{:S(2)}, u32[]{:S(2)}) collective-permute-start(bf16[64,2048]{1,0:T(8,128)(2,1)S(1)} %hidden.2.refs_0_), channel_id=1, source_target_pairs={{0,16},{1,9},{2,18},{3,11},{4,20},{5,13},{6,22},{7,15},{8,24},{9,1... | collective-permute-start | bytes 786440 | tf_op jit(solution)/shard_map/ppermute | solution.py:237
  87.9 7.6 %collective-permute-start.18 = (bf16[64,2048]{1,0:T(8,128)(2,1)S(1)}, bf16[64,2048]{1,0:T(8,128)(2,1)S(1)}, u32[]{:S(2)}, u32[]{:S(2)}) collective-permute-start(bf16[64,2048]{1,0:T(8,128)(2,1)S(1)} %collective-permute-done.16.refs_1_), channel_id=1, source_target_pairs={{0,16},{1,9},{2,18},{3,11},{4,20},{5,13},{6,22},{7,15},{8,24},{9,1... | collective-permute-start | bytes 786440 | tf_op jit(solution)/shard_map/ppermute | solution.py:237
  89.7 12.1 %collective-permute-start.20 = (bf16[64,2048]{1,0:T(8,128)(2,1)S(1)}, bf16[64,2048]{1,0:T(8,128)(2,1)S(1)}, u32[]{:S(2)}, u32[]{:S(2)}) collective-permute-start(bf16[64,2048]{1,0:T(8,128)(2,1)S(1)} %hidden.3.refs_0_), channel_id=1, source_target_pairs={{0,16},{1,9},{2,18},{3,11},{4,20},{5,13},{6,22},{7,15},{8,24},{9,1... | collective-permute-start | bytes 786440 | tf_op jit(solution)/shard_map/ppermute | solution.py:237
  93.5 8.3 %collective-permute-start.21 = (bf16[64,2048]{1,0:T(8,128)(2,1)S(1)}, bf16[64,2048]{1,0:T(8,128)(2,1)S(1)}, u32[]{:S(2)}, u32[]{:S(2)}) collective-permute-start(bf16[64,2048]{1,0:T(8,128)(2,1)S(1)} %collective-permute-done.19.refs_0_.refs_1_), channel_id=1, source_target_pairs={{0,16},{1,9},{2,18},{3,11},{4,20},{5,13},{6,22},{7,15},{8,24},{9,1... | collective-permute-start | bytes 786440 | tf_op jit(solution)/shard_map/ppermute | solution.py:237
  101.8 2.0 %collective-permute-start.22 = (bf16[4,32,2048]{2,1,0:T(8,128)(2,1)S(1)}, bf16[4,32,2048]{2,1,0:T(8,128)(2,1)S(1)}, u32[]{:S(2)}, u32[]{:S(2)}) collective-permute-start(bf16[4,32,2048]{2,1,0:T(8,128)(2,1)S(1)} %hold.2), channel_id=1, source_target_pairs={{0,1},{1,0},{2,3},{3,2},{4,5},{5,4},{6,7},{7,6},{8,9},{9,8},{10,11... | collective-permute-start | bytes 1572872 | tf_op jit(solution)/shard_map/ppermute | solution.py:237
  103.9 10.8 %collective-permute-start.25 = (bf16[32,2048]{1,0:T(8,128)(2,1)S(1)}, bf16[32,2048]{1,0:T(8,128)(2,1)S(1)}, u32[]{:S(2)}, u32[]{:S(2)}) collective-permute-start(bf16[32,2048]{1,0:T(8,128)(2,1)S(1)} %get-tuple-element.40), channel_id=1, source_target_pairs={{0,6},{1,7},{2,4},{3,5},{4,2},{5,3},{6,0},{7,1},{8,14},{9,15},{10,... | collective-permute-start | bytes 393224 | tf_op jit(solution)/shard_map/ppermute | solution.py:237
  107.8 11.3 %collective-permute-start.24 = (bf16[32,2048]{1,0:T(8,128)(2,1)S(1)}, bf16[32,2048]{1,0:T(8,128)(2,1)S(1)}, u32[]{:S(2)}, u32[]{:S(2)}) collective-permute-start(bf16[32,2048]{1,0:T(8,128)(2,1)S(1)} %get-tuple-element.41), channel_id=1, source_target_pairs={{0,4},{1,5},{2,6},{3,7},{4,0},{5,1},{6,2},{7,3},{8,12},{9,13},{10,... | collective-permute-start | bytes 393224 | tf_op jit(solution)/shard_map/ppermute | solution.py:237
  107.8 11.3 %collective-permute-start.23 = (bf16[32,2048]{1,0:T(8,128)(2,1)S(1)}, bf16[32,2048]{1,0:T(8,128)(2,1)S(1)}, u32[]{:S(2)}, u32[]{:S(2)}) collective-permute-start(bf16[32,2048]{1,0:T(8,128)(2,1)S(1)} %get-tuple-element.42), channel_id=1, source_target_pairs={{0,2},{1,3},{2,0},{3,1},{4,6},{5,7},{6,4},{7,5},{8,10},{9,11},{10,... | collective-permute-start | bytes 393224 | tf_op jit(solution)/shard_map/ppermute | solution.py:237
  119.1 2.0 %collective-permute-start.26 = (bf16[4,32,2048]{2,1,0:T(8,128)(2,1)S(1)}, bf16[4,32,2048]{2,1,0:T(8,128)(2,1)S(1)}, u32[]{:S(2)}, u32[]{:S(2)}) collective-permute-start(bf16[4,32,2048]{2,1,0:T(8,128)(2,1)S(1)} %hold.3), channel_id=1, source_target_pairs={{0,1},{1,0},{2,3},{3,2},{4,5},{5,4},{6,7},{7,6},{8,9},{9,8},{10,11... | collective-permute-start | bytes 1572872 | tf_op jit(solution)/shard_map/ppermute | solution.py:237
  121.1 5.6 %collective-permute-start.27 = (bf16[32,2048]{1,0:T(8,128)(2,1)S(1)}, bf16[32,2048]{1,0:T(8,128)(2,1)S(1)}, u32[]{:S(2)}, u32[]{:S(2)}) collective-permute-start(bf16[32,2048]{1,0:T(8,128)(2,1)S(1)} %get-tuple-element.37), channel_id=1, source_target_pairs={{0,2},{1,3},{2,0},{3,1},{4,6},{5,7},{6,4},{7,5},{8,10},{9,11},{10,... | collective-permute-start | bytes 393224 | tf_op jit(solution)/shard_map/ppermute | solution.py:237
  121.2 9.8 %collective-permute-start.29 = (bf16[32,2048]{1,0:T(8,128)(2,1)S(1)}, bf16[32,2048]{1,0:T(8,128)(2,1)S(1)}, u32[]{:S(2)}, u32[]{:S(2)}) collective-permute-start(bf16[32,2048]{1,0:T(8,128)(2,1)S(1)} %get-tuple-element.38), channel_id=1, source_target_pairs={{0,6},{1,7},{2,4},{3,5},{4,2},{5,3},{6,0},{7,1},{8,14},{9,15},{10,... | collective-permute-start | bytes 393224 | tf_op jit(solution)/shard_map/ppermute | solution.py:237
  123.9 12.4 %collective-permute-start.28 = (bf16[32,2048]{1,0:T(8,128)(2,1)S(1)}, bf16[32,2048]{1,0:T(8,128)(2,1)S(1)}, u32[]{:S(2)}, u32[]{:S(2)}) collective-permute-start(bf16[32,2048]{1,0:T(8,128)(2,1)S(1)} %get-tuple-element.39), channel_id=1, source_target_pairs={{0,4},{1,5},{2,6},{3,7},{4,0},{5,1},{6,2},{7,3},{8,12},{9,13},{10,... | collective-permute-start | bytes 393224 | tf_op jit(solution)/shard_map/ppermute | solution.py:237

commit v10 on v9

--- a/solution.py
+++ b/solution.py
@@ -142,74 +142,57 @@
 
 
 def down_kernel(n, place_ref, *refs):
-    parts = refs[:n]
-    weight_ref, keep_ref = refs[n : n + 2]
-    mine_ref, other_ref, h = refs[-3:]
+    parts = refs[: n * BATCHES]
+    weight_ref, keep_ref, mine_ref, other_ref, h = refs[n * BATCHES :]
     rows = parts[0].shape[0]
-    step = pl.program_id(0)
-
-    @pl.when(step == 0)
+
+    @pl.when(pl.program_id(0) == 0)
     def _():
-        for p in range(n):
-            h[p * rows : (p + 1) * rows] = parts[p][...]
+        for i, part in enumerate(parts):
+            h[i * rows : (i + 1) * rows] = part[...]
 
     product = masked_product(h, weight_ref, keep_ref)
     core = place_ref[0]
     half = rows // 2
-    for p in range(n):
-        slot = place_ref[1 + p]
-        low = product[p * rows : p * rows + half]
-        high = product[p * rows + half : (p + 1) * rows]
-        mine_ref[slot] = jnp.where(core == 0, low, high)
-        other_ref[slot] = jnp.where(core == 0, high, low).astype(jnp.bfloat16)
-
-
-def down(place, parts, weight, keep, after):
-    n = len(parts)
+    for i in range(n * BATCHES):
+        batch, slot = i // n, place_ref[1 + i % n]
+        low = product[i * rows : i * rows + half]
+        high = product[i * rows + half : (i + 1) * rows]
+        mine_ref[slot, batch * half : (batch + 1) * half] = jnp.where(core == 0, low, high)
+        other_ref[slot, batch * half : (batch + 1) * half] = jnp.where(core == 0, high, low).astype(jnp.bfloat16)
+
+
+def down(place, hidden, weight, keep, strip):
+    n = len(hidden[0])
+    parts = [part for batch in hidden for part in batch]
     rows = parts[0].shape[0]
-    depth, width = weight.shape
-    tile = min(width, TILE)
-    out = pl.BlockSpec((n, rows // 2, tile), lambda i, *_: (0, 0, i))
+    depth, whole = weight.shape
+    width = whole // STRIPS
+    tile = min(width, TILE // 2)
+    steps = width // tile
+    height = rows // 2 * BATCHES
+    out = pl.BlockSpec((n, height, tile), lambda i, *_: (0, 0, i))
     return pl.pallas_call(
         functools.partial(down_kernel, n),
         grid_spec=pltpu.PrefetchScalarGridSpec(
             num_scalar_prefetch=1,
-            grid=(width // tile,),
-            in_specs=[pl.BlockSpec((rows, depth), lambda i, *_: (0, 0))] * n
-            + [pl.BlockSpec((depth, tile), lambda i, *_: (0, i))]
-            + [pl.BlockSpec((keep.shape[0], tile), lambda i, *_: (0, i))]
-            + [pl.BlockSpec(memory_space=pl.ANY)] * len(after),
+            grid=(steps,),
+            in_specs=[pl.BlockSpec((rows, depth), lambda i, *_: (0, 0))] * len(parts)
+            + [pl.BlockSpec((depth, tile), lambda i, *_: (0, strip * steps + i))]
+            + [pl.BlockSpec((keep.shape[0], tile), lambda i, *_: (0, strip * steps + i))],
             out_specs=[out, out],
-            scratch_shapes=[pltpu.VMEM((n * rows, depth), jnp.bfloat16)],
+            scratch_shapes=[pltpu.VMEM((len(parts) * rows, depth), jnp.bfloat16)],
         ),
         out_shape=[
-            jax.ShapeDtypeStruct((n, rows // 2, width), jnp.float32),
-            jax.ShapeDtypeStruct((n, rows // 2, width), jnp.bfloat16),
+            jax.ShapeDtypeStruct((n, height, width), jnp.float32),
+            jax.ShapeDtypeStruct((n, height, width), jnp.bfloat16),
         ],
         compiler_params=pltpu.CompilerParams(vmem_limit_bytes=VMEM_BYTES),
         cost_estimate=pl.CostEstimate(
-            flops=2 * n * rows * depth * width, bytes_accessed=2 * depth * width, transcendentals=0
+            flops=2 * len(parts) * rows * depth * width, bytes_accessed=2 * depth * width, transcendentals=0
         ),
         name="down",
-    )(place, *parts, weight, keep, *after)
-
-
-def hold_kernel(value_ref, *refs):
-    refs[-1][...] = value_ref[...]
-
-
-def hold(value, after):
-    if not after:
-        return value
-    spec = pl.BlockSpec(memory_space=pltpu.VMEM)
-    return pl.pallas_call(
-        hold_kernel,
-        in_specs=[spec] + [pl.BlockSpec(memory_space=pl.ANY)] * len(after),
-        out_specs=spec,
-        out_shape=jax.ShapeDtypeStruct(value.shape, value.dtype),
-        compiler_params=pltpu.CompilerParams(vmem_limit_bytes=VMEM_BYTES),
-        name="hold",
-    )(value, *after)
+    )(place, *parts, weight, keep)
 
 
 def mirror(p, n):
@@ -285,17 +268,13 @@
         strips.append((gate_parts, up_parts))
         after = (last,)
     hidden = [gather(activate(strips, s)) for s in range(BATCHES)]
-    out, beside = [], []
-    for s, parts in enumerate(hidden):
-        for later in hidden[s + 1 : s + 2]:
-            beside = beside + later[1:]
-        mine, theirs = down(place, parts, down_weight, down_wide, ())
-        total, sent = combine(mine, hold(theirs, beside))
-        beside = [across_z(sent[j - 1], j) for j in range(1, n_z)]
-        for part in beside:
-            total += part.astype(jnp.float32)
+    out = []
+    for i in range(STRIPS):
+        total, sent = combine(*down(place, hidden, down_weight, down_wide, i))
+        for j in range(1, n_z):
+            total += across_z(sent[j - 1], j).astype(jnp.float32)
         out.append(total.astype(jnp.bfloat16))
-    return jnp.concatenate(out, axis=0)
+    return jnp.concatenate(out, axis=1)
 
 
 def solution(mesh):

time: 138 us -> 143 us (1.036)
  waiting for transfers between devices: 57.2 us -> 66.5 us
  starting transfers between devices: 47.8 us -> 45.6 us
  Pallas kernels: 29 us -> 27.5 us
    ppermute x30, waiting for transfers between devices: 57.2 us -> 66.5 us  [send(): return lax.ppermute(value, AXES, perm)]
    ppermute x30, starting transfers between devices: 47.8 us -> 45.6 us  [send(): return lax.ppermute(value, AXES, perm)]
  transfers between devices with their start and end apart: 30 -> 30, of which waited for: 17 -> 20; matrix products, arithmetic and copies ran while one was open for 1% -> 2% of each run, Pallas kernels for 15% -> 10%
where the time goes in v10:
time: 143 us
  waiting for transfers between devices  66.5 us (47%)
  starting transfers between devices  45.6 us (32%)
  Pallas kernels  27.5 us (19%)
  other arithmetic  2.47 us (2%)
    ppermute x30, waiting for transfers between devices, send(): return lax.ppermute(value, AXES, perm)  66.5 us
    ppermute x30, starting transfers between devices, send(): return lax.ppermute(value, AXES, perm)  45.6 us
    pallas_call x2, Pallas kernels, project(): pl.pallas_call(functools.partial(project_kernel, n), grid_spec=pltpu.Pref...  15.7 us
    pallas_call x2, Pallas kernels, down(): pl.pallas_call(functools.partial(down_kernel, n), grid_spec=pltpu.Prefetc...  11.1 us
  transfers between devices with their start and end apart: 30, of which 20 were waited for; matrix products, arithmetic and copies ran while one was open for 2% of the time, Pallas kernels for 10%

profile of v10, /device:TPU:0, one launch (start us, length us, event | category | flops | bytes accessed | tf_op | source)
XLA Modules:
  0.0 142.7 jit_solution(618365236778031196)
XLA Ops:
  0.0 1.6 %collective-permute-start = (bf16[128,1024]{1,0:T(8,128)(2,1)}, bf16[128,1024]{1,0:T(8,128)(2,1)S(1)}, u32[]{:S(2)}, u32[]{:S(2)}) collective-permute-start(bf16[128,1024]{1,0:T(8,128)(2,1)} %param.7), channel_id=1, source_target_pairs={{0,0},{1,1},{2,8},{3,9},{4,16},{5,17},{6,24},{7,25},{8,2},{9,3},{1... | collective-permute-start | bytes 786440 | tf_op jit(solution)/shard_map/ppermute | solution.py:220
  1.6 4.8 %collective-permute-start.1 = (bf16[128,1024]{1,0:T(8,128)(2,1)}, bf16[128,1024]{1,0:T(8,128)(2,1)S(1)}, u32[]{:S(2)}, u32[]{:S(2)}) collective-permute-start(bf16[128,1024]{1,0:T(8,128)(2,1)} %param.7), channel_id=1, source_target_pairs={{0,2},{1,3},{2,10},{3,11},{4,18},{5,19},{6,26},{7,27},{8,0},{9,1},... | collective-permute-start | bytes 786440 | tf_op jit(solution)/shard_map/ppermute | solution.py:220
  6.4 3.5 %collective-permute-start.2 = (bf16[128,1024]{1,0:T(8,128)(2,1)}, bf16[128,1024]{1,0:T(8,128)(2,1)S(1)}, u32[]{:S(2)}, u32[]{:S(2)}) collective-permute-start(bf16[128,1024]{1,0:T(8,128)(2,1)} %param.7), channel_id=1, source_target_pairs={{0,4},{1,5},{2,12},{3,13},{4,20},{5,21},{6,28},{7,29},{8,6},{9,7},... | collective-permute-start | bytes 786440 | tf_op jit(solution)/shard_map/ppermute | solution.py:220
  9.8 1.9 %collective-permute-start.3 = (bf16[128,1024]{1,0:T(8,128)(2,1)}, bf16[128,1024]{1,0:T(8,128)(2,1)S(1)}, u32[]{:S(2)}, u32[]{:S(2)}) collective-permute-start(bf16[128,1024]{1,0:T(8,128)(2,1)} %param.7), channel_id=1, source_target_pairs={{0,6},{1,7},{2,14},{3,15},{4,22},{5,23},{6,30},{7,31},{8,4},{9,5},... | collective-permute-start | bytes 786440 | tf_op jit(solution)/shard_map/ppermute | solution.py:220
  11.8 0.7 convert_element_type.101
  12.5 0.7 convert_element_type.102
  13.4 0.4 collective-permute-start.5
  13.8 8.4 %collective-permute-done.2.refs_2_ = bf16[128,1024]{1,0:T(8,128)(2,1)S(1)} collective-permute-done((bf16[128,1024]{1,0:T(8,128)(2,1)}, bf16[128,1024]{1,0:T(8,128)(2,1)S(1)}, u32[]{:S(2)}, u32[]{:S(2)}) %collective-permute-start.2) | collective-permute-done | bytes 262176 | tf_op jit(solution)/shard_map/ppermute | solution.py:220
  22.2 1.1 collective-permute-done.3.refs_3_
  23.7 1.1 collective-permute-done.7.refs_7_
  24.8 7.9 %project.2 = (f32[2,128,1024]{2,1,0:T(8,128)S(1)}, f32[2,128,1024]{2,1,0:T(8,128)S(1)}, bf16[2,128,1024]{2,1,0:T(8,128)(2,1)S(1)}, bf16[2,128,1024]{2,1,0:T(8,128)(2,1)S(1)}) custom-call(s32[9]{0:T(128)S(1)} %stack.33.place_ref, bf16[128,1024]{1,0:T(8,128)(2,1)S(1)} %collective-permute-done.refs_0_, bf16[128,1024]{1,0:T(8,128)(2,1)S(1)} %collective-permute-done.1.refs_1_, ...), custom_call_target="tpu_custom_call" | custom-call | flops 4294967296 | bytes 8388608 | tf_op jit(solution)/shard_map/project/pallas_call | solution.py:68
  32.6 13.0 %collective-permute-start.8 = (bf16[2,128,1024]{2,1,0:T(8,128)(2,1)S(1)}, bf16[2,128,1024]{2,1,0:T(8,128)(2,1)S(1)}, u32[]{:S(2)}, u32[]{:S(2)}) collective-permute-start(bf16[2,128,1024]{2,1,0:T(8,128)(2,1)S(1)} %get-tuple-element.22.refs_12_), channel_id=1, source_target_pairs={{0,16},{1,17},{2,18},{3,19},{4,20},{5,21},{6,22},{7,23},{8,24},{9,... | collective-permute-start | bytes 1572872 | tf_op jit(solution)/shard_map/ppermute | solution.py:220
  45.6 7.9 %project.3 = (f32[2,128,1024]{2,1,0:T(8,128)S(1)}, f32[2,128,1024]{2,1,0:T(8,128)S(1)}, bf16[2,128,1024]{2,1,0:T(8,128)(2,1)S(1)}, bf16[2,128,1024]{2,1,0:T(8,128)(2,1)S(1)}) custom-call(s32[9]{0:T(128)S(1)} %stack.33.place_ref, bf16[128,1024]{1,0:T(8,128)(2,1)S(1)} %collective-permute-done.refs_0_, bf16[128,1024]{1,0:T(8,128)(2,1)S(1)} %collective-permute-done.1.refs_1_, ...), custom_call_target="tpu_custom_call" | custom-call | flops 4294967296 | bytes 8388608 | tf_op jit(solution)/shard_map/project/pallas_call | solution.py:68
  53.7 2.0 %collective-permute-start.13 = (bf16[2,128,1024]{2,1,0:T(8,128)(2,1)S(1)}, bf16[2,128,1024]{2,1,0:T(8,128)(2,1)S(1)}, u32[]{:S(2)}, u32[]{:S(2)}) collective-permute-start(bf16[2,128,1024]{2,1,0:T(8,128)(2,1)S(1)} %get-tuple-element.30), channel_id=1, source_target_pairs={{0,8},{1,9},{2,10},{3,11},{4,12},{5,13},{6,14},{7,15},{8,0},{9,1},... | collective-permute-start | bytes 1572872 | tf_op jit(solution)/shard_map/ppermute | solution.py:220
  55.7 2.7 %collective-permute-done.8.refs_1_ = bf16[2,128,1024]{2,1,0:T(8,128)(2,1)S(1)} collective-permute-done((bf16[2,128,1024]{2,1,0:T(8,128)(2,1)S(1)}, bf16[2,128,1024]{2,1,0:T(8,128)(2,1)S(1)}, u32[]{:S(2)}, u32[]{:S(2)}) %collective-permute-start.8) | collective-permute-done | bytes 524320 | tf_op jit(solution)/shard_map/ppermute | solution.py:220
  58.3 2.1 %collective-permute-done.9.refs_3_ = bf16[2,128,1024]{2,1,0:T(8,128)(2,1)S(1)} collective-permute-done((bf16[2,128,1024]{2,1,0:T(8,128)(2,1)S(1)}, bf16[2,128,1024]{2,1,0:T(8,128)(2,1)S(1)}, u32[]{:S(2)}, u32[]{:S(2)}) %collective-permute-start.9) | collective-permute-done | bytes 524320 | tf_op jit(solution)/shard_map/ppermute | solution.py:220
  60.5 8.6 %collective-permute-done.12.refs_1_ = bf16[2,128,1024]{2,1,0:T(8,128)(2,1)S(1)} collective-permute-done((bf16[2,128,1024]{2,1,0:T(8,128)(2,1)S(1)}, bf16[2,128,1024]{2,1,0:T(8,128)(2,1)S(1)}, u32[]{:S(2)}, u32[]{:S(2)}) %collective-permute-start.12) | collective-permute-done | bytes 524320 | tf_op jit(solution)/shard_map/ppermute | solution.py:220
  69.1 1.5 %collective-permute-done.13.refs_3_ = bf16[2,128,1024]{2,1,0:T(8,128)(2,1)S(1)} collective-permute-done((bf16[2,128,1024]{2,1,0:T(8,128)(2,1)S(1)}, bf16[2,128,1024]{2,1,0:T(8,128)(2,1)S(1)}, u32[]{:S(2)}, u32[]{:S(2)}) %collective-permute-start.13) | collective-permute-done | bytes 524320 | tf_op jit(solution)/shard_map/ppermute | solution.py:220
  70.6 0.3 collective-permute-start.14
  71.0 0.4 collective-permute-start.15
  71.3 1.7 %collective-permute-start.11 = (bf16[1,128,1024]{2,1,0:T(8,128)(2,1)S(1)}, bf16[1,128,1024]{2,1,0:T(8,128)(2,1)S(1)}, u32[]{:S(2)}, u32[]{:S(2)}) collective-permute-start(bf16[1,128,1024]{2,1,0:T(8,128)(2,1)S(1)} %get-tuple-element.27), channel_id=1, source_target_pairs={{0,16},{1,17},{2,18},{3,19},{4,20},{5,21},{6,22},{7,23},{8,24},{9,... | collective-permute-start | bytes 786440 | tf_op jit(solution)/shard_map/ppermute | solution.py:220
  73.0 1.7 %collective-permute-start.10 = (bf16[1,128,1024]{2,1,0:T(8,128)(2,1)S(1)}, bf16[1,128,1024]{2,1,0:T(8,128)(2,1)S(1)}, u32[]{:S(2)}, u32[]{:S(2)}) collective-permute-start(bf16[1,128,1024]{2,1,0:T(8,128)(2,1)S(1)} %get-tuple-element.26.refs_4_), channel_id=1, source_target_pairs={{0,8},{1,9},{2,10},{3,11},{4,12},{5,13},{6,14},{7,15},{8,0},{9,1},... | collective-permute-start | bytes 786440 | tf_op jit(solution)/shard_map/ppermute | solution.py:220
  74.8 5.2 %collective-permute-done.14 = bf16[1,128,1024]{2,1,0:T(8,128)(2,1)S(1)} collective-permute-done((bf16[1,128,1024]{2,1,0:T(8,128)(2,1)S(1)}, bf16[1,128,1024]{2,1,0:T(8,128)(2,1)S(1)}, u32[]{:S(2)}, u32[]{:S(2)}) %collective-permute-start.14) | collective-permute-done | bytes 262176 | tf_op jit(solution)/shard_map/ppermute | solution.py:220
  79.9 0.3 collective-permute-done.15
  80.2 3.6 %collective-permute-done.11 = bf16[1,128,1024]{2,1,0:T(8,128)(2,1)S(1)} collective-permute-done((bf16[1,128,1024]{2,1,0:T(8,128)(2,1)S(1)}, bf16[1,128,1024]{2,1,0:T(8,128)(2,1)S(1)}, u32[]{:S(2)}, u32[]{:S(2)}) %collective-permute-start.11) | collective-permute-done | bytes 262176 | tf_op jit(solution)/shard_map/ppermute | solution.py:220
  83.8 0.3 hidden.3.refs_4_
  84.1 1.5 %collective-permute-start.19 = (bf16[64,2048]{1,0:T(8,128)(2,1)S(1)}, bf16[64,2048]{1,0:T(8,128)(2,1)S(1)}, u32[]{:S(2)}, u32[]{:S(2)}) collective-permute-start(bf16[64,2048]{1,0:T(8,128)(2,1)S(1)} %hidden.3.refs_4_), channel_id=1, source_target_pairs={{0,8},{1,17},{2,10},{3,19},{4,12},{5,21},{6,14},{7,23},{8,0},{9,25... | collective-permute-start | bytes 786440 | tf_op jit(solution)/shard_map/ppermute | solution.py:220
  85.9 0.7 collective-permute-start.16
  86.5 0.4 collective-permute-start.20
  87.0 1.6 %collective-permute-start.17 = (bf16[64,2048]{1,0:T(8,128)(2,1)S(1)}, bf16[64,2048]{1,0:T(8,128)(2,1)S(1)}, u32[]{:S(2)}, u32[]{:S(2)}) collective-permute-start(bf16[64,2048]{1,0:T(8,128)(2,1)S(1)} %hidden.2.refs_0_), channel_id=1, source_target_pairs={{0,16},{1,9},{2,18},{3,11},{4,20},{5,13},{6,22},{7,15},{8,24},{9,1... | collective-permute-start | bytes 786440 | tf_op jit(solution)/shard_map/ppermute | solution.py:220
  88.6 4.8 %collective-permute-done.19.refs_5_ = bf16[64,2048]{1,0:T(8,128)(2,1)S(1)} collective-permute-done((bf16[64,2048]{1,0:T(8,128)(2,1)S(1)}, bf16[64,2048]{1,0:T(8,128)(2,1)S(1)}, u32[]{:S(2)}, u32[]{:S(2)}) %collective-permute-start.19) | collective-permute-done | bytes 262176 | tf_op jit(solution)/shard_map/ppermute | solution.py:220
  93.4 0.4 collective-permute-start.21
  93.8 5.2 %collective-permute-done.16.refs_1_ = bf16[64,2048]{1,0:T(8,128)(2,1)S(1)} collective-permute-done((bf16[64,2048]{1,0:T(8,128)(2,1)S(1)}, bf16[64,2048]{1,0:T(8,128)(2,1)S(1)}, u32[]{:S(2)}, u32[]{:S(2)}) %collective-permute-start.16) | collective-permute-done | bytes 262176 | tf_op jit(solution)/shard_map/ppermute | solution.py:220
  99.0 0.4 collective-permute-start.18
  99.7 5.6 %collective-permute-done.18.refs_3_ = bf16[64,2048]{1,0:T(8,128)(2,1)S(1)} collective-permute-done((bf16[64,2048]{1,0:T(8,128)(2,1)S(1)}, bf16[64,2048]{1,0:T(8,128)(2,1)S(1)}, u32[]{:S(2)}, u32[]{:S(2)}) %collective-permute-start.18) | collective-permute-done | bytes 262176 | tf_op jit(solution)/shard_map/ppermute | solution.py:220
  105.4 5.5 %down.2 = (f32[4,64,1024]{2,1,0:T(8,128)S(1)}, bf16[4,64,1024]{2,1,0:T(8,128)(2,1)S(1)}) custom-call(s32[9]{0:T(128)S(1)} %stack.33.place_ref, bf16[64,2048]{1,0:T(8,128)(2,1)S(1)} %hidden.2.refs_0_, bf16[64,2048]{1,0:T(8,128)(2,1)S(1)} %collective-permute-done.16.refs_1_, bf16[64,2048]{1,0:T(8,128)(2,1)S(1)} %collective-permute-done.17.refs_2_, ...), custom_call_target="tpu_custom_call" | custom-call | flops 2147483648 | bytes 4194304 | tf_op jit(solution)/shard_map/down/pallas_call | solution.py:175
  111.0 5.5 %down.3 = (f32[4,64,1024]{2,1,0:T(8,128)S(1)}, bf16[4,64,1024]{2,1,0:T(8,128)(2,1)S(1)}) custom-call(s32[9]{0:T(128)S(1)} %stack.33.place_ref, bf16[64,2048]{1,0:T(8,128)(2,1)S(1)} %hidden.2.refs_0_, bf16[64,2048]{1,0:T(8,128)(2,1)S(1)} %collective-permute-done.16.refs_1_, bf16[64,2048]{1,0:T(8,128)(2,1)S(1)} %collective-permute-done.17.refs_2_, ...), custom_call_target="tpu_custom_call" | custom-call | flops 2147483648 | bytes 4194304 | tf_op jit(solution)/shard_map/down/pallas_call | solution.py:175
  116.5 0.6 collective-permute-start.26
  117.2 0.6 collective-permute-start.23
  117.7 2.5 %collective-permute-start.24 = (bf16[64,1024]{1,0:T(8,128)(2,1)S(1)}, bf16[64,1024]{1,0:T(8,128)(2,1)S(1)}, u32[]{:S(2)}, u32[]{:S(2)}) collective-permute-start(bf16[64,1024]{1,0:T(8,128)(2,1)S(1)} %get-tuple-element.39), channel_id=1, source_target_pairs={{0,4},{1,5},{2,6},{3,7},{4,0},{5,1},{6,2},{7,3},{8,12},{9,13},{10,... | collective-permute-start | bytes 393224 | tf_op jit(solution)/shard_map/ppermute | solution.py:220
  120.2 1.4 collective-permute-start.25
  121.8 2.9 %collective-permute-start.28 = (bf16[64,1024]{1,0:T(8,128)(2,1)S(1)}, bf16[64,1024]{1,0:T(8,128)(2,1)S(1)}, u32[]{:S(2)}, u32[]{:S(2)}) collective-permute-start(bf16[64,1024]{1,0:T(8,128)(2,1)S(1)} %get-tuple-element.42), channel_id=1, source_target_pairs={{0,4},{1,5},{2,6},{3,7},{4,0},{5,1},{6,2},{7,3},{8,12},{9,13},{10,... | collective-permute-start | bytes 393224 | tf_op jit(solution)/shard_map/ppermute | solution.py:220
  124.8 1.1 collective-permute-done.23
  125.9 1.0 collective-permute-start.29
  126.9 3.8 %collective-permute-done.24 = bf16[64,1024]{1,0:T(8,128)(2,1)S(1)} collective-permute-done((bf16[64,1024]{1,0:T(8,128)(2,1)S(1)}, bf16[64,1024]{1,0:T(8,128)(2,1)S(1)}, u32[]{:S(2)}, u32[]{:S(2)}) %collective-permute-start.24) | collective-permute-done | bytes 131104 | tf_op jit(solution)/shard_map/ppermute | solution.py:220
  130.8 0.3 collective-permute-done.27
  131.1 10.8 %collective-permute-done.28 = bf16[64,1024]{1,0:T(8,128)(2,1)S(1)} collective-permute-done((bf16[64,1024]{1,0:T(8,128)(2,1)S(1)}, bf16[64,1024]{1,0:T(8,128)(2,1)S(1)}, u32[]{:S(2)}, u32[]{:S(2)}) %collective-permute-start.28) | collective-permute-done | bytes 131104 | tf_op jit(solution)/shard_map/ppermute | solution.py:220
  142.0 0.7 pad_maximum_fusion
  (36 shorter events, 2.1 us)
Async XLA Ops:
  0.0 13.2 %collective-permute-start = (bf16[128,1024]{1,0:T(8,128)(2,1)}, bf16[128,1024]{1,0:T(8,128)(2,1)S(1)}, u32[]{:S(2)}, u32[]{:S(2)}) collective-permute-start(bf16[128,1024]{1,0:T(8,128)(2,1)} %param.7), channel_id=1, source_target_pairs={{0,0},{1,1},{2,8},{3,9},{4,16},{5,17},{6,24},{7,25},{8,2},{9,3},{1... | collective-permute-start | bytes 786440 | tf_op jit(solution)/shard_map/ppermute | solution.py:220
  1.6 11.8 %collective-permute-start.1 = (bf16[128,1024]{1,0:T(8,128)(2,1)}, bf16[128,1024]{1,0:T(8,128)(2,1)S(1)}, u32[]{:S(2)}, u32[]{:S(2)}) collective-permute-start(bf16[128,1024]{1,0:T(8,128)(2,1)} %param.7), channel_id=1, source_target_pairs={{0,2},{1,3},{2,10},{3,11},{4,18},{5,19},{6,26},{7,27},{8,0},{9,1},... | collective-permute-start | bytes 786440 | tf_op jit(solution)/shard_map/ppermute | solution.py:220
  6.4 15.8 %collective-permute-start.2 = (bf16[128,1024]{1,0:T(8,128)(2,1)}, bf16[128,1024]{1,0:T(8,128)(2,1)S(1)}, u32[]{:S(2)}, u32[]{:S(2)}) collective-permute-start(bf16[128,1024]{1,0:T(8,128)(2,1)} %param.7), channel_id=1, source_target_pairs={{0,4},{1,5},{2,12},{3,13},{4,20},{5,21},{6,28},{7,29},{8,6},{9,7},... | collective-permute-start | bytes 786440 | tf_op jit(solution)/shard_map/ppermute | solution.py:220
  9.8 13.4 %collective-permute-start.3 = (bf16[128,1024]{1,0:T(8,128)(2,1)}, bf16[128,1024]{1,0:T(8,128)(2,1)S(1)}, u32[]{:S(2)}, u32[]{:S(2)}) collective-permute-start(bf16[128,1024]{1,0:T(8,128)(2,1)} %param.7), channel_id=1, source_target_pairs={{0,6},{1,7},{2,14},{3,15},{4,22},{5,23},{6,30},{7,31},{8,4},{9,5},... | collective-permute-start | bytes 786440 | tf_op jit(solution)/shard_map/ppermute | solution.py:220
  13.2 10.3 %collective-permute-start.4 = (bf16[128,1024]{1,0:T(8,128)(2,1)S(1)}, bf16[128,1024]{1,0:T(8,128)(2,1)S(1)}, u32[]{:S(2)}, u32[]{:S(2)}) collective-permute-start(bf16[128,1024]{1,0:T(8,128)(2,1)S(1)} %collective-permute-done.refs_0_), channel_id=1, source_target_pairs={{0,1},{1,0},{2,3},{3,2},{4,5},{5,4},{6,7},{7,6},{8,9},{9,8},{10,11... | collective-permute-start | bytes 786440 | tf_op jit(solution)/shard_map/ppermute | solution.py:220
  13.4 10.1 %collective-permute-start.5 = (bf16[128,1024]{1,0:T(8,128)(2,1)S(1)}, bf16[128,1024]{1,0:T(8,128)(2,1)S(1)}, u32[]{:S(2)}, u32[]{:S(2)}) collective-permute-start(bf16[128,1024]{1,0:T(8,128)(2,1)S(1)} %collective-permute-done.1.refs_1_), channel_id=1, source_target_pairs={{0,1},{1,0},{2,3},{3,2},{4,5},{5,4},{6,7},{7,6},{8,9},{9,8},{10,11... | collective-permute-start | bytes 786440 | tf_op jit(solution)/shard_map/ppermute | solution.py:220
  22.2 1.5 %collective-permute-start.6 = (bf16[128,1024]{1,0:T(8,128)(2,1)S(1)}, bf16[128,1024]{1,0:T(8,128)(2,1)S(1)}, u32[]{:S(2)}, u32[]{:S(2)}) collective-permute-start(bf16[128,1024]{1,0:T(8,128)(2,1)S(1)} %collective-permute-done.2.refs_2_), channel_id=1, source_target_pairs={{0,1},{1,0},{2,3},{3,2},{4,5},{5,4},{6,7},{7,6},{8,9},{9,8},{10,11... | collective-permute-start | bytes 786440 | tf_op jit(solution)/shard_map/ppermute | solution.py:220
  23.2 1.5 %collective-permute-start.7 = (bf16[128,1024]{1,0:T(8,128)(2,1)S(1)}, bf16[128,1024]{1,0:T(8,128)(2,1)S(1)}, u32[]{:S(2)}, u32[]{:S(2)}) collective-permute-start(bf16[128,1024]{1,0:T(8,128)(2,1)S(1)} %collective-permute-done.3.refs_3_), channel_id=1, source_target_pairs={{0,1},{1,0},{2,3},{3,2},{4,5},{5,4},{6,7},{7,6},{8,9},{9,8},{10,11... | collective-permute-start | bytes 786440 | tf_op jit(solution)/shard_map/ppermute | solution.py:220
  32.6 25.7 %collective-permute-start.8 = (bf16[2,128,1024]{2,1,0:T(8,128)(2,1)S(1)}, bf16[2,128,1024]{2,1,0:T(8,128)(2,1)S(1)}, u32[]{:S(2)}, u32[]{:S(2)}) collective-permute-start(bf16[2,128,1024]{2,1,0:T(8,128)(2,1)S(1)} %get-tuple-element.22.refs_12_), channel_id=1, source_target_pairs={{0,16},{1,17},{2,18},{3,19},{4,20},{5,21},{6,22},{7,23},{8,24},{9,... | collective-permute-start | bytes 1572872 | tf_op jit(solution)/shard_map/ppermute | solution.py:220
  45.6 14.8 %collective-permute-start.9 = (bf16[2,128,1024]{2,1,0:T(8,128)(2,1)S(1)}, bf16[2,128,1024]{2,1,0:T(8,128)(2,1)S(1)}, u32[]{:S(2)}, u32[]{:S(2)}) collective-permute-start(bf16[2,128,1024]{2,1,0:T(8,128)(2,1)S(1)} %get-tuple-element.24), channel_id=1, source_target_pairs={{0,8},{1,9},{2,10},{3,11},{4,12},{5,13},{6,14},{7,15},{8,0},{9,1},... | collective-permute-start | bytes 1572872 | tf_op jit(solution)/shard_map/ppermute | solution.py:220
  53.5 15.6 %collective-permute-start.12 = (bf16[2,128,1024]{2,1,0:T(8,128)(2,1)S(1)}, bf16[2,128,1024]{2,1,0:T(8,128)(2,1)S(1)}, u32[]{:S(2)}, u32[]{:S(2)}) collective-permute-start(bf16[2,128,1024]{2,1,0:T(8,128)(2,1)S(1)} %get-tuple-element.25.refs_4_), channel_id=1, source_target_pairs={{0,16},{1,17},{2,18},{3,19},{4,20},{5,21},{6,22},{7,23},{8,24},{9,... | collective-permute-start | bytes 1572872 | tf_op jit(solution)/shard_map/ppermute | solution.py:220
  53.7 16.9 %collective-permute-start.13 = (bf16[2,128,1024]{2,1,0:T(8,128)(2,1)S(1)}, bf16[2,128,1024]{2,1,0:T(8,128)(2,1)S(1)}, u32[]{:S(2)}, u32[]{:S(2)}) collective-permute-start(bf16[2,128,1024]{2,1,0:T(8,128)(2,1)S(1)} %get-tuple-element.30), channel_id=1, source_target_pairs={{0,8},{1,9},{2,10},{3,11},{4,12},{5,13},{6,14},{7,15},{8,0},{9,1},... | collective-permute-start | bytes 1572872 | tf_op jit(solution)/shard_map/ppermute | solution.py:220
  70.6 28.8 %copy-start = (s32[16,16]{1,0:T(8,128)S(1)}, s32[16,16]{1,0:T(8,128)}, u32[]{:S(2)}) copy-start(s32[16,16]{1,0:T(8,128)} %param.13) | copy-start | bytes 3076
  70.6 9.3 %collective-permute-start.14 = (bf16[1,128,1024]{2,1,0:T(8,128)(2,1)S(1)}, bf16[1,128,1024]{2,1,0:T(8,128)(2,1)S(1)}, u32[]{:S(2)}, u32[]{:S(2)}) collective-permute-start(bf16[1,128,1024]{2,1,0:T(8,128)(2,1)S(1)} %get-tuple-element.31), channel_id=1, source_target_pairs={{0,8},{1,9},{2,10},{3,11},{4,12},{5,13},{6,14},{7,15},{8,0},{9,1},... | collective-permute-start | bytes 786440 | tf_op jit(solution)/shard_map/ppermute | solution.py:220
  71.0 9.2 %collective-permute-start.15 = (bf16[1,128,1024]{2,1,0:T(8,128)(2,1)S(1)}, bf16[1,128,1024]{2,1,0:T(8,128)(2,1)S(1)}, u32[]{:S(2)}, u32[]{:S(2)}) collective-permute-start(bf16[1,128,1024]{2,1,0:T(8,128)(2,1)S(1)} %get-tuple-element.32), channel_id=1, source_target_pairs={{0,16},{1,17},{2,18},{3,19},{4,20},{5,21},{6,22},{7,23},{8,24},{9,... | collective-permute-start | bytes 786440 | tf_op jit(solution)/shard_map/ppermute | solution.py:220
  71.3 12.5 %collective-permute-start.11 = (bf16[1,128,1024]{2,1,0:T(8,128)(2,1)S(1)}, bf16[1,128,1024]{2,1,0:T(8,128)(2,1)S(1)}, u32[]{:S(2)}, u32[]{:S(2)}) collective-permute-start(bf16[1,128,1024]{2,1,0:T(8,128)(2,1)S(1)} %get-tuple-element.27), channel_id=1, source_target_pairs={{0,16},{1,17},{2,18},{3,19},{4,20},{5,21},{6,22},{7,23},{8,24},{9,... | collective-permute-start | bytes 786440 | tf_op jit(solution)/shard_map/ppermute | solution.py:220
  73.0 10.8 %collective-permute-start.10 = (bf16[1,128,1024]{2,1,0:T(8,128)(2,1)S(1)}, bf16[1,128,1024]{2,1,0:T(8,128)(2,1)S(1)}, u32[]{:S(2)}, u32[]{:S(2)}) collective-permute-start(bf16[1,128,1024]{2,1,0:T(8,128)(2,1)S(1)} %get-tuple-element.26.refs_4_), channel_id=1, source_target_pairs={{0,8},{1,9},{2,10},{3,11},{4,12},{5,13},{6,14},{7,15},{8,0},{9,1},... | collective-permute-start | bytes 786440 | tf_op jit(solution)/shard_map/ppermute | solution.py:220
  84.1 9.2 %collective-permute-start.19 = (bf16[64,2048]{1,0:T(8,128)(2,1)S(1)}, bf16[64,2048]{1,0:T(8,128)(2,1)S(1)}, u32[]{:S(2)}, u32[]{:S(2)}) collective-permute-start(bf16[64,2048]{1,0:T(8,128)(2,1)S(1)} %hidden.3.refs_4_), channel_id=1, source_target_pairs={{0,8},{1,17},{2,10},{3,19},{4,12},{5,21},{6,14},{7,23},{8,0},{9,25... | collective-permute-start | bytes 786440 | tf_op jit(solution)/shard_map/ppermute | solution.py:220
  85.9 13.1 %collective-permute-start.16 = (bf16[64,2048]{1,0:T(8,128)(2,1)S(1)}, bf16[64,2048]{1,0:T(8,128)(2,1)S(1)}, u32[]{:S(2)}, u32[]{:S(2)}) collective-permute-start(bf16[64,2048]{1,0:T(8,128)(2,1)S(1)} %hidden.2.refs_0_), channel_id=1, source_target_pairs={{0,8},{1,17},{2,10},{3,19},{4,12},{5,21},{6,14},{7,23},{8,0},{9,25... | collective-permute-start | bytes 786440 | tf_op jit(solution)/shard_map/ppermute | solution.py:220
  86.5 13.0 %collective-permute-start.20 = (bf16[64,2048]{1,0:T(8,128)(2,1)S(1)}, bf16[64,2048]{1,0:T(8,128)(2,1)S(1)}, u32[]{:S(2)}, u32[]{:S(2)}) collective-permute-start(bf16[64,2048]{1,0:T(8,128)(2,1)S(1)} %hidden.3.refs_4_), channel_id=1, source_target_pairs={{0,16},{1,9},{2,18},{3,11},{4,20},{5,13},{6,22},{7,15},{8,24},{9,1... | collective-permute-start | bytes 786440 | tf_op jit(solution)/shard_map/ppermute | solution.py:220
  87.0 12.6 %collective-permute-start.17 = (bf16[64,2048]{1,0:T(8,128)(2,1)S(1)}, bf16[64,2048]{1,0:T(8,128)(2,1)S(1)}, u32[]{:S(2)}, u32[]{:S(2)}) collective-permute-start(bf16[64,2048]{1,0:T(8,128)(2,1)S(1)} %hidden.2.refs_0_), channel_id=1, source_target_pairs={{0,16},{1,9},{2,18},{3,11},{4,20},{5,13},{6,22},{7,15},{8,24},{9,1... | collective-permute-start | bytes 786440 | tf_op jit(solution)/shard_map/ppermute | solution.py:220
  93.4 6.4 %collective-permute-start.21 = (bf16[64,2048]{1,0:T(8,128)(2,1)S(1)}, bf16[64,2048]{1,0:T(8,128)(2,1)S(1)}, u32[]{:S(2)}, u32[]{:S(2)}) collective-permute-start(bf16[64,2048]{1,0:T(8,128)(2,1)S(1)} %collective-permute-done.19.refs_5_), channel_id=1, source_target_pairs={{0,16},{1,9},{2,18},{3,11},{4,20},{5,13},{6,22},{7,15},{8,24},{9,1... | collective-permute-start | bytes 786440 | tf_op jit(solution)/shard_map/ppermute | solution.py:220
  99.0 6.4 %collective-permute-start.18 = (bf16[64,2048]{1,0:T(8,128)(2,1)S(1)}, bf16[64,2048]{1,0:T(8,128)(2,1)S(1)}, u32[]{:S(2)}, u32[]{:S(2)}) collective-permute-start(bf16[64,2048]{1,0:T(8,128)(2,1)S(1)} %collective-permute-done.16.refs_1_), channel_id=1, source_target_pairs={{0,16},{1,9},{2,18},{3,11},{4,20},{5,13},{6,22},{7,15},{8,24},{9,1... | collective-permute-start | bytes 786440 | tf_op jit(solution)/shard_map/ppermute | solution.py:220
  110.9 6.2 %collective-permute-start.22 = (bf16[4,64,1024]{2,1,0:T(8,128)(2,1)S(1)}, bf16[4,64,1024]{2,1,0:T(8,128)(2,1)S(1)}, u32[]{:S(2)}, u32[]{:S(2)}) collective-permute-start(bf16[4,64,1024]{2,1,0:T(8,128)(2,1)S(1)} %get-tuple-element.34), channel_id=1, source_target_pairs={{0,1},{1,0},{2,3},{3,2},{4,5},{5,4},{6,7},{7,6},{8,9},{9,8},{10,11... | collective-permute-start | bytes 1572872 | tf_op jit(solution)/shard_map/ppermute | solution.py:220
  116.5 5.1 %collective-permute-start.26 = (bf16[4,64,1024]{2,1,0:T(8,128)(2,1)S(1)}, bf16[4,64,1024]{2,1,0:T(8,128)(2,1)S(1)}, u32[]{:S(2)}, u32[]{:S(2)}) collective-permute-start(bf16[4,64,1024]{2,1,0:T(8,128)(2,1)S(1)} %get-tuple-element.36), channel_id=1, source_target_pairs={{0,1},{1,0},{2,3},{3,2},{4,5},{5,4},{6,7},{7,6},{8,9},{9,8},{10,11... | collective-permute-start | bytes 1572872 | tf_op jit(solution)/shard_map/ppermute | solution.py:220
  117.2 8.7 %collective-permute-start.23 = (bf16[64,1024]{1,0:T(8,128)(2,1)S(1)}, bf16[64,1024]{1,0:T(8,128)(2,1)S(1)}, u32[]{:S(2)}, u32[]{:S(2)}) collective-permute-start(bf16[64,1024]{1,0:T(8,128)(2,1)S(1)} %get-tuple-element.37), channel_id=1, source_target_pairs={{0,2},{1,3},{2,0},{3,1},{4,6},{5,7},{6,4},{7,5},{8,10},{9,11},{10,... | collective-permute-start | bytes 393224 | tf_op jit(solution)/shard_map/ppermute | solution.py:220
  117.7 13.0 %collective-permute-start.24 = (bf16[64,1024]{1,0:T(8,128)(2,1)S(1)}, bf16[64,1024]{1,0:T(8,128)(2,1)S(1)}, u32[]{:S(2)}, u32[]{:S(2)}) collective-permute-start(bf16[64,1024]{1,0:T(8,128)(2,1)S(1)} %get-tuple-element.39), channel_id=1, source_target_pairs={{0,4},{1,5},{2,6},{3,7},{4,0},{5,1},{6,2},{7,3},{8,12},{9,13},{10,... | collective-permute-start | bytes 393224 | tf_op jit(solution)/shard_map/ppermute | solution.py:220
  120.2 10.5 %collective-permute-start.25 = (bf16[64,1024]{1,0:T(8,128)(2,1)S(1)}, bf16[64,1024]{1,0:T(8,128)(2,1)S(1)}, u32[]{:S(2)}, u32[]{:S(2)}) collective-permute-start(bf16[64,1024]{1,0:T(8,128)(2,1)S(1)} %get-tuple-element.38), channel_id=1, source_target_pairs={{0,6},{1,7},{2,4},{3,5},{4,2},{5,3},{6,0},{7,1},{8,14},{9,15},{10,... | collective-permute-start | bytes 393224 | tf_op jit(solution)/shard_map/ppermute | solution.py:220
  121.7 9.4 %collective-permute-start.27 = (bf16[64,1024]{1,0:T(8,128)(2,1)S(1)}, bf16[64,1024]{1,0:T(8,128)(2,1)S(1)}, u32[]{:S(2)}, u32[]{:S(2)}) collective-permute-start(bf16[64,1024]{1,0:T(8,128)(2,1)S(1)} %get-tuple-element.40), channel_id=1, source_target_pairs={{0,2},{1,3},{2,0},{3,1},{4,6},{5,7},{6,4},{7,5},{8,10},{9,11},{10,... | collective-permute-start | bytes 393224 | tf_op jit(solution)/shard_map/ppermute | solution.py:220
  121.8 20.1 %collective-permute-start.28 = (bf16[64,1024]{1,0:T(8,128)(2,1)S(1)}, bf16[64,1024]{1,0:T(8,128)(2,1)S(1)}, u32[]{:S(2)}, u32[]{:S(2)}) collective-permute-start(bf16[64,1024]{1,0:T(8,128)(2,1)S(1)} %get-tuple-element.42), channel_id=1, source_target_pairs={{0,4},{1,5},{2,6},{3,7},{4,0},{5,1},{6,2},{7,3},{8,12},{9,13},{10,... | collective-permute-start | bytes 393224 | tf_op jit(solution)/shard_map/ppermute | solution.py:220
  125.9 16.0 %collective-permute-start.29 = (bf16[64,1024]{1,0:T(8,128)(2,1)S(1)}, bf16[64,1024]{1,0:T(8,128)(2,1)S(1)}, u32[]{:S(2)}, u32[]{:S(2)}) collective-permute-start(bf16[64,1024]{1,0:T(8,128)(2,1)S(1)} %get-tuple-element.41), channel_id=1, source_target_pairs={{0,6},{1,7},{2,4},{3,5},{4,2},{5,3},{6,0},{7,1},{8,14},{9,15},{10,... | collective-permute-start | bytes 393224 | tf_op jit(solution)/shard_map/ppermute | solution.py:220

commit v11 on v9

--- a/solution.py
+++ b/solution.py
@@ -124,7 +124,7 @@
         out_ref[:, i * width : (i + 1) * width] = result.reshape(-1, width).astype(jnp.bfloat16)
 
 
-def activate(strips, batch):
+def activate(strips, batch, after):
     n = len(strips[0][0])
     _, rows, width = strips[0][0][0].shape
     piece = rows // (2 * BATCHES)
@@ -133,12 +133,13 @@
     return pl.pallas_call(
         functools.partial(activate_kernel, n),
         grid=(1,),
-        in_specs=[pl.BlockSpec((2, piece, width), lambda i: (0, batch, 0))] * len(parts),
+        in_specs=[pl.BlockSpec((2, piece, width), lambda i: (0, batch, 0))] * len(parts)
+        + [pl.BlockSpec(memory_space=pl.ANY)] * len(after),
         out_specs=pl.BlockSpec((2 * piece, width * STRIPS), lambda i: (0, 0)),
         out_shape=jax.ShapeDtypeStruct((2 * piece, width * STRIPS), jnp.bfloat16),
         compiler_params=pltpu.CompilerParams(vmem_limit_bytes=VMEM_BYTES),
         name="hidden",
-    )(*parts)
+    )(*parts, *after)
 
 
 def down_kernel(n, place_ref, *refs):
@@ -210,6 +211,27 @@
         compiler_params=pltpu.CompilerParams(vmem_limit_bytes=VMEM_BYTES),
         name="hold",
     )(value, *after)
+
+
+def finish_kernel(n, *refs):
+    out_ref = refs[-1]
+    rows = refs[0].shape[0]
+    for s in range(BATCHES):
+        out_ref[s * rows : (s + 1) * rows] = total_of(refs[n * s : n * (s + 1)]).astype(jnp.bfloat16)
+
+
+def finish(batches):
+    parts = [part for batch in batches for part in batch]
+    rows, width = parts[0].shape
+    spec = pl.BlockSpec(memory_space=pltpu.VMEM)
+    return pl.pallas_call(
+        functools.partial(finish_kernel, len(batches[0])),
+        in_specs=[spec] * len(parts),
+        out_specs=spec,
+        out_shape=jax.ShapeDtypeStruct((rows * len(batches), width), jnp.bfloat16),
+        compiler_params=pltpu.CompilerParams(vmem_limit_bytes=VMEM_BYTES),
+        name="finish",
+    )(*parts)
 
 
 def mirror(p, n):
@@ -283,8 +305,11 @@
     for i in range(STRIPS):
         gate_parts, up_parts, last = halve(*sums[i], after)
         strips.append((gate_parts, up_parts))
-        after = (last,)
-    hidden = [gather(activate(strips, s)) for s in range(BATCHES)]
+        after = (gate_parts[-1],)
+    hidden, after = [], ()
+    for s in range(BATCHES):
+        hidden.append(gather(activate(strips, s, after)))
+        after = tuple(hidden[s][1 << i] for i in range(n_tok.bit_length() - 1))
     out, beside = [], []
     for s, parts in enumerate(hidden):
         for later in hidden[s + 1 : s + 2]:
@@ -292,10 +317,8 @@
         mine, theirs = down(place, parts, down_weight, down_wide, ())
         total, sent = combine(mine, hold(theirs, beside))
         beside = [across_z(sent[j - 1], j) for j in range(1, n_z)]
-        for part in beside:
-            total += part.astype(jnp.float32)
-        out.append(total.astype(jnp.bfloat16))
-    return jnp.concatenate(out, axis=0)
+        out.append([total] + beside)
+    return finish(out)
 
 
 def solution(mesh):

time: 138 us -> 143 us (1.036)
  waiting for transfers between devices: 57.2 us -> 67.1 us
  starting transfers between devices: 47.8 us -> 43.2 us
    ppermute x30, waiting for transfers between devices: 57.2 us -> 67.1 us  [send(): return lax.ppermute(value, AXES, perm)]
    ppermute x30, starting transfers between devices: 47.8 us -> 43.2 us  [send(): return lax.ppermute(value, AXES, perm)]
  transfers between devices with their start and end apart: 30 -> 30, of which waited for: 17 -> 20; matrix products, arithmetic and copies ran while one was open for 1% -> 1% of each run, Pallas kernels for 15% -> 14%
where the time goes in v11:
time: 143 us; the launch traced here: 142 us
  waiting for transfers between devices  67.1 us (47%)
  starting transfers between devices  43.2 us (30%)
  Pallas kernels  29.8 us (21%)
  other arithmetic  1.62 us (1%)
    ppermute x30, waiting for transfers between devices, send(): return lax.ppermute(value, AXES, perm)  67.1 us
    ppermute x30, starting transfers between devices, send(): return lax.ppermute(value, AXES, perm)  43.2 us
    pallas_call x2, Pallas kernels, project(): pl.pallas_call(functools.partial(project_kernel, n), grid_spec=pltpu.Pref...  15.7 us
    pallas_call x2, Pallas kernels, down(): pl.pallas_call(functools.partial(down_kernel, n), grid_spec=pltpu.Prefetc...  12.5 us
  transfers between devices with their start and end apart: 30, of which 20 were waited for; matrix products, arithmetic and copies ran while one was open for 1% of the time, Pallas kernels for 14%

profile of v11, /device:TPU:0, one launch (start us, length us, event | category | flops | bytes accessed | tf_op | source)
XLA Modules:
  0.0 142.5 jit_solution(1833672651505982196)
XLA Ops:
  0.0 1.6 %collective-permute-start = (bf16[128,1024]{1,0:T(8,128)(2,1)}, bf16[128,1024]{1,0:T(8,128)(2,1)S(1)}, u32[]{:S(2)}, u32[]{:S(2)}) collective-permute-start(bf16[128,1024]{1,0:T(8,128)(2,1)} %param.7), channel_id=1, source_target_pairs={{0,0},{1,1},{2,8},{3,9},{4,16},{5,17},{6,24},{7,25},{8,2},{9,3},{1... | collective-permute-start | bytes 786440 | tf_op jit(solution)/shard_map/ppermute | solution.py:259
  1.6 4.8 %collective-permute-start.1 = (bf16[128,1024]{1,0:T(8,128)(2,1)}, bf16[128,1024]{1,0:T(8,128)(2,1)S(1)}, u32[]{:S(2)}, u32[]{:S(2)}) collective-permute-start(bf16[128,1024]{1,0:T(8,128)(2,1)} %param.7), channel_id=1, source_target_pairs={{0,2},{1,3},{2,10},{3,11},{4,18},{5,19},{6,26},{7,27},{8,0},{9,1},... | collective-permute-start | bytes 786440 | tf_op jit(solution)/shard_map/ppermute | solution.py:259
  6.4 3.5 %collective-permute-start.2 = (bf16[128,1024]{1,0:T(8,128)(2,1)}, bf16[128,1024]{1,0:T(8,128)(2,1)S(1)}, u32[]{:S(2)}, u32[]{:S(2)}) collective-permute-start(bf16[128,1024]{1,0:T(8,128)(2,1)} %param.7), channel_id=1, source_target_pairs={{0,4},{1,5},{2,12},{3,13},{4,20},{5,21},{6,28},{7,29},{8,6},{9,7},... | collective-permute-start | bytes 786440 | tf_op jit(solution)/shard_map/ppermute | solution.py:259
  9.8 1.9 %collective-permute-start.3 = (bf16[128,1024]{1,0:T(8,128)(2,1)}, bf16[128,1024]{1,0:T(8,128)(2,1)S(1)}, u32[]{:S(2)}, u32[]{:S(2)}) collective-permute-start(bf16[128,1024]{1,0:T(8,128)(2,1)} %param.7), channel_id=1, source_target_pairs={{0,6},{1,7},{2,14},{3,15},{4,22},{5,23},{6,30},{7,31},{8,4},{9,5},... | collective-permute-start | bytes 786440 | tf_op jit(solution)/shard_map/ppermute | solution.py:259
  11.8 0.7 convert_element_type.77
  12.5 0.7 convert_element_type.78
  13.4 0.4 collective-permute-start.5
  13.8 8.4 %collective-permute-done.2.refs_2_ = bf16[128,1024]{1,0:T(8,128)(2,1)S(1)} collective-permute-done((bf16[128,1024]{1,0:T(8,128)(2,1)}, bf16[128,1024]{1,0:T(8,128)(2,1)S(1)}, u32[]{:S(2)}, u32[]{:S(2)}) %collective-permute-start.2) | collective-permute-done | bytes 262176 | tf_op jit(solution)/shard_map/ppermute | solution.py:259
  22.2 1.1 collective-permute-done.3.refs_3_
  23.7 1.1 collective-permute-done.7.refs_7_
  24.8 7.9 %project.2 = (f32[2,128,1024]{2,1,0:T(8,128)S(1)}, f32[2,128,1024]{2,1,0:T(8,128)S(1)}, bf16[2,128,1024]{2,1,0:T(8,128)(2,1)S(1)}, bf16[2,128,1024]{2,1,0:T(8,128)(2,1)S(1)}) custom-call(s32[9]{0:T(128)S(1)} %stack.33.place_ref, bf16[128,1024]{1,0:T(8,128)(2,1)S(1)} %collective-permute-done.refs_0_, bf16[128,1024]{1,0:T(8,128)(2,1)S(1)} %collective-permute-done.1.refs_1_, ...), custom_call_target="tpu_custom_call" | custom-call | flops 4294967296 | bytes 8388608 | tf_op jit(solution)/shard_map/project/pallas_call | solution.py:68
  32.6 13.0 %collective-permute-start.8 = (bf16[2,128,1024]{2,1,0:T(8,128)(2,1)S(1)}, bf16[2,128,1024]{2,1,0:T(8,128)(2,1)S(1)}, u32[]{:S(2)}, u32[]{:S(2)}) collective-permute-start(bf16[2,128,1024]{2,1,0:T(8,128)(2,1)S(1)} %get-tuple-element.22.refs_12_), channel_id=1, source_target_pairs={{0,16},{1,17},{2,18},{3,19},{4,20},{5,21},{6,22},{7,23},{8,24},{9,... | collective-permute-start | bytes 1572872 | tf_op jit(solution)/shard_map/ppermute | solution.py:259
  45.6 7.9 %project.3 = (f32[2,128,1024]{2,1,0:T(8,128)S(1)}, f32[2,128,1024]{2,1,0:T(8,128)S(1)}, bf16[2,128,1024]{2,1,0:T(8,128)(2,1)S(1)}, bf16[2,128,1024]{2,1,0:T(8,128)(2,1)S(1)}) custom-call(s32[9]{0:T(128)S(1)} %stack.33.place_ref, bf16[128,1024]{1,0:T(8,128)(2,1)S(1)} %collective-permute-done.refs_0_, bf16[128,1024]{1,0:T(8,128)(2,1)S(1)} %collective-permute-done.1.refs_1_, ...), custom_call_target="tpu_custom_call" | custom-call | flops 4294967296 | bytes 8388608 | tf_op jit(solution)/shard_map/project/pallas_call | solution.py:68
  53.7 2.0 %collective-permute-start.13 = (bf16[2,128,1024]{2,1,0:T(8,128)(2,1)S(1)}, bf16[2,128,1024]{2,1,0:T(8,128)(2,1)S(1)}, u32[]{:S(2)}, u32[]{:S(2)}) collective-permute-start(bf16[2,128,1024]{2,1,0:T(8,128)(2,1)S(1)} %get-tuple-element.30), channel_id=1, source_target_pairs={{0,8},{1,9},{2,10},{3,11},{4,12},{5,13},{6,14},{7,15},{8,0},{9,1},... | collective-permute-start | bytes 1572872 | tf_op jit(solution)/shard_map/ppermute | solution.py:259
  55.7 2.7 %collective-permute-done.8.refs_1_ = bf16[2,128,1024]{2,1,0:T(8,128)(2,1)S(1)} collective-permute-done((bf16[2,128,1024]{2,1,0:T(8,128)(2,1)S(1)}, bf16[2,128,1024]{2,1,0:T(8,128)(2,1)S(1)}, u32[]{:S(2)}, u32[]{:S(2)}) %collective-permute-start.8) | collective-permute-done | bytes 524320 | tf_op jit(solution)/shard_map/ppermute | solution.py:259
  58.3 2.1 %collective-permute-done.9.refs_3_ = bf16[2,128,1024]{2,1,0:T(8,128)(2,1)S(1)} collective-permute-done((bf16[2,128,1024]{2,1,0:T(8,128)(2,1)S(1)}, bf16[2,128,1024]{2,1,0:T(8,128)(2,1)S(1)}, u32[]{:S(2)}, u32[]{:S(2)}) %collective-permute-start.9) | collective-permute-done | bytes 524320 | tf_op jit(solution)/shard_map/ppermute | solution.py:259
  60.7 8.9 %collective-permute-done.12.refs_1_ = bf16[2,128,1024]{2,1,0:T(8,128)(2,1)S(1)} collective-permute-done((bf16[2,128,1024]{2,1,0:T(8,128)(2,1)S(1)}, bf16[2,128,1024]{2,1,0:T(8,128)(2,1)S(1)}, u32[]{:S(2)}, u32[]{:S(2)}) %collective-permute-start.12) | collective-permute-done | bytes 524320 | tf_op jit(solution)/shard_map/ppermute | solution.py:259
  69.6 2.1 %collective-permute-done.13.refs_3_ = bf16[2,128,1024]{2,1,0:T(8,128)(2,1)S(1)} collective-permute-done((bf16[2,128,1024]{2,1,0:T(8,128)(2,1)S(1)}, bf16[2,128,1024]{2,1,0:T(8,128)(2,1)S(1)}, u32[]{:S(2)}, u32[]{:S(2)}) %collective-permute-start.13) | collective-permute-done | bytes 524320 | tf_op jit(solution)/shard_map/ppermute | solution.py:259
  71.7 4.5 %collective-permute-done.10.refs_4_ = bf16[1,128,1024]{2,1,0:T(8,128)(2,1)S(1)} collective-permute-done((bf16[1,128,1024]{2,1,0:T(8,128)(2,1)S(1)}, bf16[1,128,1024]{2,1,0:T(8,128)(2,1)S(1)}, u32[]{:S(2)}, u32[]{:S(2)}) %collective-permute-start.10) | collective-permute-done | bytes 262176 | tf_op jit(solution)/shard_map/ppermute | solution.py:259
  76.3 0.3 collective-permute-start.14
  76.6 0.4 collective-permute-start.15
  77.0 6.5 %collective-permute-done.14 = bf16[1,128,1024]{2,1,0:T(8,128)(2,1)S(1)} collective-permute-done((bf16[1,128,1024]{2,1,0:T(8,128)(2,1)S(1)}, bf16[1,128,1024]{2,1,0:T(8,128)(2,1)S(1)}, u32[]{:S(2)}, u32[]{:S(2)}) %collective-permute-start.14) | collective-permute-done | bytes 262176 | tf_op jit(solution)/shard_map/ppermute | solution.py:259
  83.5 0.3 collective-permute-done.15
  83.8 0.3 hidden.2.refs_0_
  84.1 1.5 %collective-permute-start.16 = (bf16[64,2048]{1,0:T(8,128)(2,1)S(1)}, bf16[64,2048]{1,0:T(8,128)(2,1)S(1)}, u32[]{:S(2)}, u32[]{:S(2)}) collective-permute-start(bf16[64,2048]{1,0:T(8,128)(2,1)S(1)} %hidden.2.refs_0_), channel_id=1, source_target_pairs={{0,8},{1,17},{2,10},{3,19},{4,12},{5,21},{6,14},{7,23},{8,0},{9,25... | collective-permute-start | bytes 786440 | tf_op jit(solution)/shard_map/ppermute | solution.py:259
  85.6 0.7 collective-permute-start.17
  86.3 4.6 %collective-permute-done.16.refs_1_.refs_12_ = bf16[64,2048]{1,0:T(8,128)(2,1)S(1)} collective-permute-done((bf16[64,2048]{1,0:T(8,128)(2,1)S(1)}, bf16[64,2048]{1,0:T(8,128)(2,1)S(1)}, u32[]{:S(2)}, u32[]{:S(2)}) %collective-permute-start.16) | collective-permute-done | bytes 262176 | tf_op jit(solution)/shard_map/ppermute | solution.py:259
  90.8 1.1 collective-permute-done.17.refs_2_.refs_13_
  92.0 0.3 hidden.3.refs_0_
  92.2 0.7 collective-permute-start.19
  92.9 0.8 collective-permute-start.18
  93.7 1.3 collective-permute-start.20
  94.9 6.6 %collective-permute-done.19.refs_0_.refs_1_ = bf16[64,2048]{1,0:T(8,128)(2,1)S(1)} collective-permute-done((bf16[64,2048]{1,0:T(8,128)(2,1)S(1)}, bf16[64,2048]{1,0:T(8,128)(2,1)S(1)}, u32[]{:S(2)}, u32[]{:S(2)}) %collective-permute-start.19) | collective-permute-done | bytes 262176 | tf_op jit(solution)/shard_map/ppermute | solution.py:259
  101.6 0.7 collective-permute-start.21
  102.4 6.2 %down.2 = (f32[4,32,2048]{2,1,0:T(8,128)S(1)}, bf16[4,32,2048]{2,1,0:T(8,128)(2,1)S(1)}) custom-call(s32[9]{0:T(128)S(1)} %stack.33.place_ref, bf16[64,2048]{1,0:T(8,128)(2,1)S(1)} %hidden.2.refs_0_, bf16[64,2048]{1,0:T(8,128)(2,1)S(1)} %collective-permute-done.16.refs_1_.refs_12_, bf16[64,2048]{1,0:T(8,128)(2,1)S(1)} %collective-permute-done.17.refs_2_.refs_13_, ...), custom_call_target="tpu_custom_call" | custom-call | flops 2147483648 | bytes 8388608 | tf_op jit(solution)/shard_map/down/pallas_call | solution.py:174
  108.8 1.9 %collective-permute-done.22 = bf16[4,32,2048]{2,1,0:T(8,128)(2,1)S(1)} collective-permute-done((bf16[4,32,2048]{2,1,0:T(8,128)(2,1)S(1)}, bf16[4,32,2048]{2,1,0:T(8,128)(2,1)S(1)}, u32[]{:S(2)}, u32[]{:S(2)}) %collective-permute-start.22) | collective-permute-done | bytes 524320 | tf_op jit(solution)/shard_map/ppermute | solution.py:259
  110.8 0.6 collective-permute-start.23
  111.4 2.3 %collective-permute-start.24 = (bf16[32,2048]{1,0:T(8,128)(2,1)S(1)}, bf16[32,2048]{1,0:T(8,128)(2,1)S(1)}, u32[]{:S(2)}, u32[]{:S(2)}) collective-permute-start(bf16[32,2048]{1,0:T(8,128)(2,1)S(1)} %get-tuple-element.42), channel_id=1, source_target_pairs={{0,4},{1,5},{2,6},{3,7},{4,0},{5,1},{6,2},{7,3},{8,12},{9,13},{10,... | collective-permute-start | bytes 393224 | tf_op jit(solution)/shard_map/ppermute | solution.py:259
  113.7 1.6 %collective-permute-start.25 = (bf16[32,2048]{1,0:T(8,128)(2,1)S(1)}, bf16[32,2048]{1,0:T(8,128)(2,1)S(1)}, u32[]{:S(2)}, u32[]{:S(2)}) collective-permute-start(bf16[32,2048]{1,0:T(8,128)(2,1)S(1)} %get-tuple-element.41), channel_id=1, source_target_pairs={{0,6},{1,7},{2,4},{3,5},{4,2},{5,3},{6,0},{7,1},{8,14},{9,15},{10,... | collective-permute-start | bytes 393224 | tf_op jit(solution)/shard_map/ppermute | solution.py:259
  115.3 6.2 %down.3 = (f32[4,32,2048]{2,1,0:T(8,128)S(1)}, bf16[4,32,2048]{2,1,0:T(8,128)(2,1)S(1)}) custom-call(s32[9]{0:T(128)S(1)} %stack.33.place_ref, bf16[64,2048]{1,0:T(8,128)(2,1)S(1)} %hidden.3.refs_0_, bf16[64,2048]{1,0:T(8,128)(2,1)S(1)} %collective-permute-done.19.refs_0_.refs_1_, bf16[64,2048]{1,0:T(8,128)(2,1)S(1)} %collective-permute-done.20.refs_1_.refs_2_, ...), custom_call_target="tpu_custom_call" | custom-call | flops 2147483648 | bytes 8388608 | tf_op jit(solution)/shard_map/down/pallas_call | solution.py:174
  121.5 2.8 %collective-permute-done.24.refs_1_.refs_2_ = bf16[32,2048]{1,0:T(8,128)(2,1)S(1)} collective-permute-done((bf16[32,2048]{1,0:T(8,128)(2,1)S(1)}, bf16[32,2048]{1,0:T(8,128)(2,1)S(1)}, u32[]{:S(2)}, u32[]{:S(2)}) %collective-permute-start.24) | collective-permute-done | bytes 131104 | tf_op jit(solution)/shard_map/ppermute | solution.py:259
  124.4 1.9 %collective-permute-done.26 = bf16[4,32,2048]{2,1,0:T(8,128)(2,1)S(1)} collective-permute-done((bf16[4,32,2048]{2,1,0:T(8,128)(2,1)S(1)}, bf16[4,32,2048]{2,1,0:T(8,128)(2,1)S(1)}, u32[]{:S(2)}, u32[]{:S(2)}) %collective-permute-start.26) | collective-permute-done | bytes 524320 | tf_op jit(solution)/shard_map/ppermute | solution.py:259
  126.4 2.4 %collective-permute-start.27 = (bf16[32,2048]{1,0:T(8,128)(2,1)S(1)}, bf16[32,2048]{1,0:T(8,128)(2,1)S(1)}, u32[]{:S(2)}, u32[]{:S(2)}) collective-permute-start(bf16[32,2048]{1,0:T(8,128)(2,1)S(1)} %get-tuple-element.39), channel_id=1, source_target_pairs={{0,2},{1,3},{2,0},{3,1},{4,6},{5,7},{6,4},{7,5},{8,10},{9,11},{10,... | collective-permute-start | bytes 393224 | tf_op jit(solution)/shard_map/ppermute | solution.py:259
  128.8 1.1 collective-permute-start.28
  129.9 1.4 collective-permute-start.29
  131.3 3.2 %collective-permute-done.27.refs_5_ = bf16[32,2048]{1,0:T(8,128)(2,1)S(1)} collective-permute-done((bf16[32,2048]{1,0:T(8,128)(2,1)S(1)}, bf16[32,2048]{1,0:T(8,128)(2,1)S(1)}, u32[]{:S(2)}, u32[]{:S(2)}) %collective-permute-start.27) | collective-permute-done | bytes 131104 | tf_op jit(solution)/shard_map/ppermute | solution.py:259
  134.5 7.2 %collective-permute-done.28.refs_6_ = bf16[32,2048]{1,0:T(8,128)(2,1)S(1)} collective-permute-done((bf16[32,2048]{1,0:T(8,128)(2,1)S(1)}, bf16[32,2048]{1,0:T(8,128)(2,1)S(1)}, u32[]{:S(2)}, u32[]{:S(2)}) %collective-permute-start.28) | collective-permute-done | bytes 131104 | tf_op jit(solution)/shard_map/ppermute | solution.py:259
  141.7 0.8 finish.1
  (36 shorter events, 1.8 us)
Async XLA Ops:
  0.0 13.2 %collective-permute-start = (bf16[128,1024]{1,0:T(8,128)(2,1)}, bf16[128,1024]{1,0:T(8,128)(2,1)S(1)}, u32[]{:S(2)}, u32[]{:S(2)}) collective-permute-start(bf16[128,1024]{1,0:T(8,128)(2,1)} %param.7), channel_id=1, source_target_pairs={{0,0},{1,1},{2,8},{3,9},{4,16},{5,17},{6,24},{7,25},{8,2},{9,3},{1... | collective-permute-start | bytes 786440 | tf_op jit(solution)/shard_map/ppermute | solution.py:259
  1.6 11.8 %collective-permute-start.1 = (bf16[128,1024]{1,0:T(8,128)(2,1)}, bf16[128,1024]{1,0:T(8,128)(2,1)S(1)}, u32[]{:S(2)}, u32[]{:S(2)}) collective-permute-start(bf16[128,1024]{1,0:T(8,128)(2,1)} %param.7), channel_id=1, source_target_pairs={{0,2},{1,3},{2,10},{3,11},{4,18},{5,19},{6,26},{7,27},{8,0},{9,1},... | collective-permute-start | bytes 786440 | tf_op jit(solution)/shard_map/ppermute | solution.py:259
  6.4 15.8 %collective-permute-start.2 = (bf16[128,1024]{1,0:T(8,128)(2,1)}, bf16[128,1024]{1,0:T(8,128)(2,1)S(1)}, u32[]{:S(2)}, u32[]{:S(2)}) collective-permute-start(bf16[128,1024]{1,0:T(8,128)(2,1)} %param.7), channel_id=1, source_target_pairs={{0,4},{1,5},{2,12},{3,13},{4,20},{5,21},{6,28},{7,29},{8,6},{9,7},... | collective-permute-start | bytes 786440 | tf_op jit(solution)/shard_map/ppermute | solution.py:259
  9.8 13.4 %collective-permute-start.3 = (bf16[128,1024]{1,0:T(8,128)(2,1)}, bf16[128,1024]{1,0:T(8,128)(2,1)S(1)}, u32[]{:S(2)}, u32[]{:S(2)}) collective-permute-start(bf16[128,1024]{1,0:T(8,128)(2,1)} %param.7), channel_id=1, source_target_pairs={{0,6},{1,7},{2,14},{3,15},{4,22},{5,23},{6,30},{7,31},{8,4},{9,5},... | collective-permute-start | bytes 786440 | tf_op jit(solution)/shard_map/ppermute | solution.py:259
  13.2 10.3 %collective-permute-start.4 = (bf16[128,1024]{1,0:T(8,128)(2,1)S(1)}, bf16[128,1024]{1,0:T(8,128)(2,1)S(1)}, u32[]{:S(2)}, u32[]{:S(2)}) collective-permute-start(bf16[128,1024]{1,0:T(8,128)(2,1)S(1)} %collective-permute-done.refs_0_), channel_id=1, source_target_pairs={{0,1},{1,0},{2,3},{3,2},{4,5},{5,4},{6,7},{7,6},{8,9},{9,8},{10,11... | collective-permute-start | bytes 786440 | tf_op jit(solution)/shard_map/ppermute | solution.py:259
  13.4 10.1 %collective-permute-start.5 = (bf16[128,1024]{1,0:T(8,128)(2,1)S(1)}, bf16[128,1024]{1,0:T(8,128)(2,1)S(1)}, u32[]{:S(2)}, u32[]{:S(2)}) collective-permute-start(bf16[128,1024]{1,0:T(8,128)(2,1)S(1)} %collective-permute-done.1.refs_1_), channel_id=1, source_target_pairs={{0,1},{1,0},{2,3},{3,2},{4,5},{5,4},{6,7},{7,6},{8,9},{9,8},{10,11... | collective-permute-start | bytes 786440 | tf_op jit(solution)/shard_map/ppermute | solution.py:259
  22.2 1.5 %collective-permute-start.6 = (bf16[128,1024]{1,0:T(8,128)(2,1)S(1)}, bf16[128,1024]{1,0:T(8,128)(2,1)S(1)}, u32[]{:S(2)}, u32[]{:S(2)}) collective-permute-start(bf16[128,1024]{1,0:T(8,128)(2,1)S(1)} %collective-permute-done.2.refs_2_), channel_id=1, source_target_pairs={{0,1},{1,0},{2,3},{3,2},{4,5},{5,4},{6,7},{7,6},{8,9},{9,8},{10,11... | collective-permute-start | bytes 786440 | tf_op jit(solution)/shard_map/ppermute | solution.py:259
  23.2 1.5 %collective-permute-start.7 = (bf16[128,1024]{1,0:T(8,128)(2,1)S(1)}, bf16[128,1024]{1,0:T(8,128)(2,1)S(1)}, u32[]{:S(2)}, u32[]{:S(2)}) collective-permute-start(bf16[128,1024]{1,0:T(8,128)(2,1)S(1)} %collective-permute-done.3.refs_3_), channel_id=1, source_target_pairs={{0,1},{1,0},{2,3},{3,2},{4,5},{5,4},{6,7},{7,6},{8,9},{9,8},{10,11... | collective-permute-start | bytes 786440 | tf_op jit(solution)/shard_map/ppermute | solution.py:259
  32.6 25.7 %collective-permute-start.8 = (bf16[2,128,1024]{2,1,0:T(8,128)(2,1)S(1)}, bf16[2,128,1024]{2,1,0:T(8,128)(2,1)S(1)}, u32[]{:S(2)}, u32[]{:S(2)}) collective-permute-start(bf16[2,128,1024]{2,1,0:T(8,128)(2,1)S(1)} %get-tuple-element.22.refs_12_), channel_id=1, source_target_pairs={{0,16},{1,17},{2,18},{3,19},{4,20},{5,21},{6,22},{7,23},{8,24},{9,... | collective-permute-start | bytes 1572872 | tf_op jit(solution)/shard_map/ppermute | solution.py:259
  45.6 14.8 %collective-permute-start.9 = (bf16[2,128,1024]{2,1,0:T(8,128)(2,1)S(1)}, bf16[2,128,1024]{2,1,0:T(8,128)(2,1)S(1)}, u32[]{:S(2)}, u32[]{:S(2)}) collective-permute-start(bf16[2,128,1024]{2,1,0:T(8,128)(2,1)S(1)} %get-tuple-element.24), channel_id=1, source_target_pairs={{0,8},{1,9},{2,10},{3,11},{4,12},{5,13},{6,14},{7,15},{8,0},{9,1},... | collective-permute-start | bytes 1572872 | tf_op jit(solution)/shard_map/ppermute | solution.py:259
  53.5 16.1 %collective-permute-start.12 = (bf16[2,128,1024]{2,1,0:T(8,128)(2,1)S(1)}, bf16[2,128,1024]{2,1,0:T(8,128)(2,1)S(1)}, u32[]{:S(2)}, u32[]{:S(2)}) collective-permute-start(bf16[2,128,1024]{2,1,0:T(8,128)(2,1)S(1)} %get-tuple-element.25.refs_4_), channel_id=1, source_target_pairs={{0,16},{1,17},{2,18},{3,19},{4,20},{5,21},{6,22},{7,23},{8,24},{9,... | collective-permute-start | bytes 1572872 | tf_op jit(solution)/shard_map/ppermute | solution.py:259
  53.7 18.0 %collective-permute-start.13 = (bf16[2,128,1024]{2,1,0:T(8,128)(2,1)S(1)}, bf16[2,128,1024]{2,1,0:T(8,128)(2,1)S(1)}, u32[]{:S(2)}, u32[]{:S(2)}) collective-permute-start(bf16[2,128,1024]{2,1,0:T(8,128)(2,1)S(1)} %get-tuple-element.30), channel_id=1, source_target_pairs={{0,8},{1,9},{2,10},{3,11},{4,12},{5,13},{6,14},{7,15},{8,0},{9,1},... | collective-permute-start | bytes 1572872 | tf_op jit(solution)/shard_map/ppermute | solution.py:259
  60.5 15.6 %collective-permute-start.10 = (bf16[1,128,1024]{2,1,0:T(8,128)(2,1)S(1)}, bf16[1,128,1024]{2,1,0:T(8,128)(2,1)S(1)}, u32[]{:S(2)}, u32[]{:S(2)}) collective-permute-start(bf16[1,128,1024]{2,1,0:T(8,128)(2,1)S(1)} %get-tuple-element.26), channel_id=1, source_target_pairs={{0,8},{1,9},{2,10},{3,11},{4,12},{5,13},{6,14},{7,15},{8,0},{9,1},... | collective-permute-start | bytes 786440 | tf_op jit(solution)/shard_map/ppermute | solution.py:259
  60.6 16.4 %collective-permute-start.11 = (bf16[1,128,1024]{2,1,0:T(8,128)(2,1)S(1)}, bf16[1,128,1024]{2,1,0:T(8,128)(2,1)S(1)}, u32[]{:S(2)}, u32[]{:S(2)}) collective-permute-start(bf16[1,128,1024]{2,1,0:T(8,128)(2,1)S(1)} %get-tuple-element.27), channel_id=1, source_target_pairs={{0,16},{1,17},{2,18},{3,19},{4,20},{5,21},{6,22},{7,23},{8,24},{9,... | collective-permute-start | bytes 786440 | tf_op jit(solution)/shard_map/ppermute | solution.py:259
  76.2 26.0 %copy-start = (s32[16,16]{1,0:T(8,128)S(1)}, s32[16,16]{1,0:T(8,128)}, u32[]{:S(2)}) copy-start(s32[16,16]{1,0:T(8,128)} %param.13) | copy-start | bytes 3076
  76.3 7.3 %collective-permute-start.14 = (bf16[1,128,1024]{2,1,0:T(8,128)(2,1)S(1)}, bf16[1,128,1024]{2,1,0:T(8,128)(2,1)S(1)}, u32[]{:S(2)}, u32[]{:S(2)}) collective-permute-start(bf16[1,128,1024]{2,1,0:T(8,128)(2,1)S(1)} %get-tuple-element.31), channel_id=1, source_target_pairs={{0,8},{1,9},{2,10},{3,11},{4,12},{5,13},{6,14},{7,15},{8,0},{9,1},... | collective-permute-start | bytes 786440 | tf_op jit(solution)/shard_map/ppermute | solution.py:259
  76.6 7.2 %collective-permute-start.15 = (bf16[1,128,1024]{2,1,0:T(8,128)(2,1)S(1)}, bf16[1,128,1024]{2,1,0:T(8,128)(2,1)S(1)}, u32[]{:S(2)}, u32[]{:S(2)}) collective-permute-start(bf16[1,128,1024]{2,1,0:T(8,128)(2,1)S(1)} %get-tuple-element.32), channel_id=1, source_target_pairs={{0,16},{1,17},{2,18},{3,19},{4,20},{5,21},{6,22},{7,23},{8,24},{9,... | collective-permute-start | bytes 786440 | tf_op jit(solution)/shard_map/ppermute | solution.py:259
  84.1 6.7 %collective-permute-start.16 = (bf16[64,2048]{1,0:T(8,128)(2,1)S(1)}, bf16[64,2048]{1,0:T(8,128)(2,1)S(1)}, u32[]{:S(2)}, u32[]{:S(2)}) collective-permute-start(bf16[64,2048]{1,0:T(8,128)(2,1)S(1)} %hidden.2.refs_0_), channel_id=1, source_target_pairs={{0,8},{1,17},{2,10},{3,19},{4,12},{5,21},{6,14},{7,23},{8,0},{9,25... | collective-permute-start | bytes 786440 | tf_op jit(solution)/shard_map/ppermute | solution.py:259
  85.6 6.4 %collective-permute-start.17 = (bf16[64,2048]{1,0:T(8,128)(2,1)S(1)}, bf16[64,2048]{1,0:T(8,128)(2,1)S(1)}, u32[]{:S(2)}, u32[]{:S(2)}) collective-permute-start(bf16[64,2048]{1,0:T(8,128)(2,1)S(1)} %hidden.2.refs_0_), channel_id=1, source_target_pairs={{0,16},{1,9},{2,18},{3,11},{4,20},{5,13},{6,22},{7,15},{8,24},{9,1... | collective-permute-start | bytes 786440 | tf_op jit(solution)/shard_map/ppermute | solution.py:259
  92.2 9.3 %collective-permute-start.19 = (bf16[64,2048]{1,0:T(8,128)(2,1)S(1)}, bf16[64,2048]{1,0:T(8,128)(2,1)S(1)}, u32[]{:S(2)}, u32[]{:S(2)}) collective-permute-start(bf16[64,2048]{1,0:T(8,128)(2,1)S(1)} %hidden.3.refs_0_), channel_id=1, source_target_pairs={{0,8},{1,17},{2,10},{3,19},{4,12},{5,21},{6,14},{7,23},{8,0},{9,25... | collective-permute-start | bytes 786440 | tf_op jit(solution)/shard_map/ppermute | solution.py:259
  92.9 9.5 %collective-permute-start.18 = (bf16[64,2048]{1,0:T(8,128)(2,1)S(1)}, bf16[64,2048]{1,0:T(8,128)(2,1)S(1)}, u32[]{:S(2)}, u32[]{:S(2)}) collective-permute-start(bf16[64,2048]{1,0:T(8,128)(2,1)S(1)} %collective-permute-done.16.refs_1_.refs_12_), channel_id=1, source_target_pairs={{0,16},{1,9},{2,18},{3,11},{4,20},{5,13},{6,22},{7,15},{8,24},{9,1... | collective-permute-start | bytes 786440 | tf_op jit(solution)/shard_map/ppermute | solution.py:259
  93.7 15.0 %collective-permute-start.20 = (bf16[64,2048]{1,0:T(8,128)(2,1)S(1)}, bf16[64,2048]{1,0:T(8,128)(2,1)S(1)}, u32[]{:S(2)}, u32[]{:S(2)}) collective-permute-start(bf16[64,2048]{1,0:T(8,128)(2,1)S(1)} %hidden.3.refs_0_), channel_id=1, source_target_pairs={{0,16},{1,9},{2,18},{3,11},{4,20},{5,13},{6,22},{7,15},{8,24},{9,1... | collective-permute-start | bytes 786440 | tf_op jit(solution)/shard_map/ppermute | solution.py:259
  101.6 7.1 %collective-permute-start.21 = (bf16[64,2048]{1,0:T(8,128)(2,1)S(1)}, bf16[64,2048]{1,0:T(8,128)(2,1)S(1)}, u32[]{:S(2)}, u32[]{:S(2)}) collective-permute-start(bf16[64,2048]{1,0:T(8,128)(2,1)S(1)} %collective-permute-done.19.refs_0_.refs_1_), channel_id=1, source_target_pairs={{0,16},{1,9},{2,18},{3,11},{4,20},{5,13},{6,22},{7,15},{8,24},{9,1... | collective-permute-start | bytes 786440 | tf_op jit(solution)/shard_map/ppermute | solution.py:259
  108.7 2.0 %collective-permute-start.22 = (bf16[4,32,2048]{2,1,0:T(8,128)(2,1)S(1)}, bf16[4,32,2048]{2,1,0:T(8,128)(2,1)S(1)}, u32[]{:S(2)}, u32[]{:S(2)}) collective-permute-start(bf16[4,32,2048]{2,1,0:T(8,128)(2,1)S(1)} %hold.2), channel_id=1, source_target_pairs={{0,1},{1,0},{2,3},{3,2},{4,5},{5,4},{6,7},{7,6},{8,9},{9,8},{10,11... | collective-permute-start | bytes 1572872 | tf_op jit(solution)/shard_map/ppermute | solution.py:259
  110.8 10.7 %collective-permute-start.23 = (bf16[32,2048]{1,0:T(8,128)(2,1)S(1)}, bf16[32,2048]{1,0:T(8,128)(2,1)S(1)}, u32[]{:S(2)}, u32[]{:S(2)}) collective-permute-start(bf16[32,2048]{1,0:T(8,128)(2,1)S(1)} %get-tuple-element.43), channel_id=1, source_target_pairs={{0,2},{1,3},{2,0},{3,1},{4,6},{5,7},{6,4},{7,5},{8,10},{9,11},{10,... | collective-permute-start | bytes 393224 | tf_op jit(solution)/shard_map/ppermute | solution.py:259
  111.4 12.9 %collective-permute-start.24 = (bf16[32,2048]{1,0:T(8,128)(2,1)S(1)}, bf16[32,2048]{1,0:T(8,128)(2,1)S(1)}, u32[]{:S(2)}, u32[]{:S(2)}) collective-permute-start(bf16[32,2048]{1,0:T(8,128)(2,1)S(1)} %get-tuple-element.42), channel_id=1, source_target_pairs={{0,4},{1,5},{2,6},{3,7},{4,0},{5,1},{6,2},{7,3},{8,12},{9,13},{10,... | collective-permute-start | bytes 393224 | tf_op jit(solution)/shard_map/ppermute | solution.py:259
  113.7 10.6 %collective-permute-start.25 = (bf16[32,2048]{1,0:T(8,128)(2,1)S(1)}, bf16[32,2048]{1,0:T(8,128)(2,1)S(1)}, u32[]{:S(2)}, u32[]{:S(2)}) collective-permute-start(bf16[32,2048]{1,0:T(8,128)(2,1)S(1)} %get-tuple-element.41), channel_id=1, source_target_pairs={{0,6},{1,7},{2,4},{3,5},{4,2},{5,3},{6,0},{7,1},{8,14},{9,15},{10,... | collective-permute-start | bytes 393224 | tf_op jit(solution)/shard_map/ppermute | solution.py:259
  124.3 2.0 %collective-permute-start.26 = (bf16[4,32,2048]{2,1,0:T(8,128)(2,1)S(1)}, bf16[4,32,2048]{2,1,0:T(8,128)(2,1)S(1)}, u32[]{:S(2)}, u32[]{:S(2)}) collective-permute-start(bf16[4,32,2048]{2,1,0:T(8,128)(2,1)S(1)} %hold.3), channel_id=1, source_target_pairs={{0,1},{1,0},{2,3},{3,2},{4,5},{5,4},{6,7},{7,6},{8,9},{9,8},{10,11... | collective-permute-start | bytes 1572872 | tf_op jit(solution)/shard_map/ppermute | solution.py:259
  126.4 8.0 %collective-permute-start.27 = (bf16[32,2048]{1,0:T(8,128)(2,1)S(1)}, bf16[32,2048]{1,0:T(8,128)(2,1)S(1)}, u32[]{:S(2)}, u32[]{:S(2)}) collective-permute-start(bf16[32,2048]{1,0:T(8,128)(2,1)S(1)} %get-tuple-element.39), channel_id=1, source_target_pairs={{0,2},{1,3},{2,0},{3,1},{4,6},{5,7},{6,4},{7,5},{8,10},{9,11},{10,... | collective-permute-start | bytes 393224 | tf_op jit(solution)/shard_map/ppermute | solution.py:259
  128.8 12.9 %collective-permute-start.28 = (bf16[32,2048]{1,0:T(8,128)(2,1)S(1)}, bf16[32,2048]{1,0:T(8,128)(2,1)S(1)}, u32[]{:S(2)}, u32[]{:S(2)}) collective-permute-start(bf16[32,2048]{1,0:T(8,128)(2,1)S(1)} %get-tuple-element.38), channel_id=1, source_target_pairs={{0,4},{1,5},{2,6},{3,7},{4,0},{5,1},{6,2},{7,3},{8,12},{9,13},{10,... | collective-permute-start | bytes 393224 | tf_op jit(solution)/shard_map/ppermute | solution.py:259
  129.9 11.8 %collective-permute-start.29 = (bf16[32,2048]{1,0:T(8,128)(2,1)S(1)}, bf16[32,2048]{1,0:T(8,128)(2,1)S(1)}, u32[]{:S(2)}, u32[]{:S(2)}) collective-permute-start(bf16[32,2048]{1,0:T(8,128)(2,1)S(1)} %get-tuple-element.37), channel_id=1, source_target_pairs={{0,6},{1,7},{2,4},{3,5},{4,2},{5,3},{6,0},{7,1},{8,14},{9,15},{10,... | collective-permute-start | bytes 393224 | tf_op jit(solution)/shard_map/ppermute | solution.py:259

commit v12 on v9

--- a/solution.py
+++ b/solution.py
@@ -9,7 +9,7 @@
 
 AXES = ("tok", "hid")
 BATCHES = 2
-STRIPS = 2
+STRIPS = 4
 TILE = 512
 VMEM_BYTES = 44 * 1024 * 1024
 

time: 138 us -> 141 us (1.022)
  Pallas kernels: 29 us -> 33 us
  starting transfers between devices: 47.8 us -> 45.5 us
    pallas_call x2 -> x4, Pallas kernels: 15.7 us -> 19.6 us  [project(): pl.pallas_call(functools.partial(project_kernel, n), grid_spec=pltpu.Pref...]
    ppermute x30 -> x38, starting transfers between devices: 47.8 us -> 45.5 us  [send(): return lax.ppermute(value, AXES, perm)]
    ppermute x30 -> x38, waiting for transfers between devices: 57.2 us -> 58.6 us  [send(): return lax.ppermute(value, AXES, perm)]
  transfers between devices with their start and end apart: 30 -> 38, of which waited for: 17 -> 17; matrix products, arithmetic and copies ran while one was open for 1% -> 1% of each run, Pallas kernels for 15% -> 20%
where the time goes in v12:
time: 141 us; the launch traced here: 140 us
  waiting for transfers between devices  58.6 us (42%)
  starting transfers between devices  45.5 us (32%)
  Pallas kernels  33 us (23%)
  other arithmetic  2.48 us (2%)
    ppermute x38, waiting for transfers between devices, send(): return lax.ppermute(value, AXES, perm)  58.6 us
    ppermute x38, starting transfers between devices, send(): return lax.ppermute(value, AXES, perm)  45.5 us
    pallas_call x4, Pallas kernels, project(): pl.pallas_call(functools.partial(project_kernel, n), grid_spec=pltpu.Pref...  19.6 us
    pallas_call x2, Pallas kernels, down(): pl.pallas_call(functools.partial(down_kernel, n), grid_spec=pltpu.Prefetc...  12.5 us
  transfers between devices with their start and end apart: 38, of which 17 were waited for; matrix products, arithmetic and copies ran while one was open for 1% of the time, Pallas kernels for 20%

profile of v12, /device:TPU:0, one launch (start us, length us, event | category | flops | bytes accessed | tf_op | source)
XLA Modules:
  0.0 140.3 jit_solution(3569640144410829449)
XLA Ops:
  0.0 3.0 %collective-permute-start.1 = (bf16[128,1024]{1,0:T(8,128)(2,1)}, bf16[128,1024]{1,0:T(8,128)(2,1)S(1)}, u32[]{:S(2)}, u32[]{:S(2)}) collective-permute-start(bf16[128,1024]{1,0:T(8,128)(2,1)} %param.7), channel_id=1, source_target_pairs={{0,2},{1,3},{2,10},{3,11},{4,18},{5,19},{6,26},{7,27},{8,0},{9,1},... | collective-permute-start | bytes 786440 | tf_op jit(solution)/shard_map/ppermute | solution.py:237
  3.0 1.6 %collective-permute-start = (bf16[128,1024]{1,0:T(8,128)(2,1)}, bf16[128,1024]{1,0:T(8,128)(2,1)S(1)}, u32[]{:S(2)}, u32[]{:S(2)}) collective-permute-start(bf16[128,1024]{1,0:T(8,128)(2,1)} %param.7), channel_id=1, source_target_pairs={{0,0},{1,1},{2,8},{3,9},{4,16},{5,17},{6,24},{7,25},{8,2},{9,3},{1... | collective-permute-start | bytes 786440 | tf_op jit(solution)/shard_map/ppermute | solution.py:237
  4.6 7.0 %collective-permute-start.3 = (bf16[128,1024]{1,0:T(8,128)(2,1)}, bf16[128,1024]{1,0:T(8,128)(2,1)S(1)}, u32[]{:S(2)}, u32[]{:S(2)}) collective-permute-start(bf16[128,1024]{1,0:T(8,128)(2,1)} %param.7), channel_id=1, source_target_pairs={{0,6},{1,7},{2,14},{3,15},{4,22},{5,23},{6,30},{7,31},{8,4},{9,5},... | collective-permute-start | bytes 786440 | tf_op jit(solution)/shard_map/ppermute | solution.py:237
  11.6 0.7 convert_element_type.101
  12.3 0.7 convert_element_type.102
  13.2 0.5 collective-permute-start.4
  13.7 6.7 %collective-permute-done.3.refs_3_ = bf16[128,1024]{1,0:T(8,128)(2,1)S(1)} collective-permute-done((bf16[128,1024]{1,0:T(8,128)(2,1)}, bf16[128,1024]{1,0:T(8,128)(2,1)S(1)}, u32[]{:S(2)}, u32[]{:S(2)}) %collective-permute-start.3) | collective-permute-done | bytes 262176 | tf_op jit(solution)/shard_map/ppermute | solution.py:237
  20.4 3.9 %collective-permute-done.2.refs_2_ = bf16[128,1024]{1,0:T(8,128)(2,1)S(1)} collective-permute-done((bf16[128,1024]{1,0:T(8,128)(2,1)}, bf16[128,1024]{1,0:T(8,128)(2,1)S(1)}, u32[]{:S(2)}, u32[]{:S(2)}) %collective-permute-start.2) | collective-permute-done | bytes 262176 | tf_op jit(solution)/shard_map/ppermute | solution.py:237
  24.6 1.2 collective-permute-done.6.refs_6_
  25.8 4.9 %project.4 = (f32[2,128,512]{2,1,0:T(8,128)S(1)}, f32[2,128,512]{2,1,0:T(8,128)S(1)}, bf16[2,128,512]{2,1,0:T(8,128)(2,1)S(1)}, bf16[2,128,512]{2,1,0:T(8,128)(2,1)S(1)}) custom-call(s32[9]{0:T(128)S(1)} %stack.33.place_ref, bf16[128,1024]{1,0:T(8,128)(2,1)S(1)} %collective-permute-done.refs_0_, bf16[128,1024]{1,0:T(8,128)(2,1)S(1)} %collective-permute-done.1.refs_1_, ...), custom_call_target="tpu_custom_call" | custom-call | flops 2147483648 | bytes 4194304 | tf_op jit(solution)/shard_map/project/pallas_call | solution.py:68
  30.7 2.3 %collective-permute-start.9 = (bf16[2,128,512]{2,1,0:T(8,128)(2,1)S(1)}, bf16[2,128,512]{2,1,0:T(8,128)(2,1)S(1)}, u32[]{:S(2)}, u32[]{:S(2)}) collective-permute-start(bf16[2,128,512]{2,1,0:T(8,128)(2,1)S(1)} %get-tuple-element.36), channel_id=1, source_target_pairs={{0,8},{1,9},{2,10},{3,11},{4,12},{5,13},{6,14},{7,15},{8,0},{9,1},... | collective-permute-start | bytes 786440 | tf_op jit(solution)/shard_map/ppermute | solution.py:237
  33.0 7.8 %collective-permute-start.8 = (bf16[2,128,512]{2,1,0:T(8,128)(2,1)S(1)}, bf16[2,128,512]{2,1,0:T(8,128)(2,1)S(1)}, u32[]{:S(2)}, u32[]{:S(2)}) collective-permute-start(bf16[2,128,512]{2,1,0:T(8,128)(2,1)S(1)} %get-tuple-element.34.refs_12_), channel_id=1, source_target_pairs={{0,16},{1,17},{2,18},{3,19},{4,20},{5,21},{6,22},{7,23},{8,24},{9,... | collective-permute-start | bytes 786440 | tf_op jit(solution)/shard_map/ppermute | solution.py:237
  40.8 4.9 %project.5 = (f32[2,128,512]{2,1,0:T(8,128)S(1)}, f32[2,128,512]{2,1,0:T(8,128)S(1)}, bf16[2,128,512]{2,1,0:T(8,128)(2,1)S(1)}, bf16[2,128,512]{2,1,0:T(8,128)(2,1)S(1)}) custom-call(s32[9]{0:T(128)S(1)} %stack.33.place_ref, bf16[128,1024]{1,0:T(8,128)(2,1)S(1)} %collective-permute-done.refs_0_, bf16[128,1024]{1,0:T(8,128)(2,1)S(1)} %collective-permute-done.1.refs_1_, ...), custom_call_target="tpu_custom_call" | custom-call | flops 2147483648 | bytes 4194304 | tf_op jit(solution)/shard_map/project/pallas_call | solution.py:68
  45.8 2.0 %collective-permute-start.13 = (bf16[2,128,512]{2,1,0:T(8,128)(2,1)S(1)}, bf16[2,128,512]{2,1,0:T(8,128)(2,1)S(1)}, u32[]{:S(2)}, u32[]{:S(2)}) collective-permute-start(bf16[2,128,512]{2,1,0:T(8,128)(2,1)S(1)} %get-tuple-element.44), channel_id=1, source_target_pairs={{0,8},{1,9},{2,10},{3,11},{4,12},{5,13},{6,14},{7,15},{8,0},{9,1},... | collective-permute-start | bytes 786440 | tf_op jit(solution)/shard_map/ppermute | solution.py:237
  47.8 4.9 %project.6 = (f32[2,128,512]{2,1,0:T(8,128)S(1)}, f32[2,128,512]{2,1,0:T(8,128)S(1)}, bf16[2,128,512]{2,1,0:T(8,128)(2,1)S(1)}, bf16[2,128,512]{2,1,0:T(8,128)(2,1)S(1)}) custom-call(s32[9]{0:T(128)S(1)} %stack.33.place_ref, bf16[128,1024]{1,0:T(8,128)(2,1)S(1)} %collective-permute-done.refs_0_, bf16[128,1024]{1,0:T(8,128)(2,1)S(1)} %collective-permute-done.1.refs_1_, ...), custom_call_target="tpu_custom_call" | custom-call | flops 2147483648 | bytes 4194304 | tf_op jit(solution)/shard_map/project/pallas_call | solution.py:68
  52.7 0.2 collective-permute-start.17
  52.9 2.0 %collective-permute-start.16 = (bf16[2,128,512]{2,1,0:T(8,128)(2,1)S(1)}, bf16[2,128,512]{2,1,0:T(8,128)(2,1)S(1)}, u32[]{:S(2)}, u32[]{:S(2)}) collective-permute-start(bf16[2,128,512]{2,1,0:T(8,128)(2,1)S(1)} %get-tuple-element.38.refs_12_), channel_id=1, source_target_pairs={{0,16},{1,17},{2,18},{3,19},{4,20},{5,21},{6,22},{7,23},{8,24},{9,... | collective-permute-start | bytes 786440 | tf_op jit(solution)/shard_map/ppermute | solution.py:237
  54.9 4.9 %project.7 = (f32[2,128,512]{2,1,0:T(8,128)S(1)}, f32[2,128,512]{2,1,0:T(8,128)S(1)}, bf16[2,128,512]{2,1,0:T(8,128)(2,1)S(1)}, bf16[2,128,512]{2,1,0:T(8,128)(2,1)S(1)}) custom-call(s32[9]{0:T(128)S(1)} %stack.33.place_ref, bf16[128,1024]{1,0:T(8,128)(2,1)S(1)} %collective-permute-done.refs_0_, bf16[128,1024]{1,0:T(8,128)(2,1)S(1)} %collective-permute-done.1.refs_1_, ...), custom_call_target="tpu_custom_call" | custom-call | flops 2147483648 | bytes 4194304 | tf_op jit(solution)/shard_map/project/pallas_call | solution.py:68
  59.8 2.0 %collective-permute-start.21 = (bf16[2,128,512]{2,1,0:T(8,128)(2,1)S(1)}, bf16[2,128,512]{2,1,0:T(8,128)(2,1)S(1)}, u32[]{:S(2)}, u32[]{:S(2)}) collective-permute-start(bf16[2,128,512]{2,1,0:T(8,128)(2,1)S(1)} %get-tuple-element.54), channel_id=1, source_target_pairs={{0,8},{1,9},{2,10},{3,11},{4,12},{5,13},{6,14},{7,15},{8,0},{9,1},... | collective-permute-start | bytes 786440 | tf_op jit(solution)/shard_map/ppermute | solution.py:237
  61.9 2.1 %collective-permute-start.11 = (bf16[1,128,512]{2,1,0:T(8,128)(2,1)S(1)}, bf16[1,128,512]{2,1,0:T(8,128)(2,1)S(1)}, u32[]{:S(2)}, u32[]{:S(2)}) collective-permute-start(bf16[1,128,512]{2,1,0:T(8,128)(2,1)S(1)} %get-tuple-element.41), channel_id=1, source_target_pairs={{0,16},{1,17},{2,18},{3,19},{4,20},{5,21},{6,22},{7,23},{8,24},{9,... | collective-permute-start | bytes 393224 | tf_op jit(solution)/shard_map/ppermute | solution.py:237
  64.1 0.2 collective-permute-start.10
  64.3 4.8 %collective-permute-done.21.refs_3_ = bf16[2,128,512]{2,1,0:T(8,128)(2,1)S(1)} collective-permute-done((bf16[2,128,512]{2,1,0:T(8,128)(2,1)S(1)}, bf16[2,128,512]{2,1,0:T(8,128)(2,1)S(1)}, u32[]{:S(2)}, u32[]{:S(2)}) %collective-permute-start.21) | collective-permute-done | bytes 262176 | tf_op jit(solution)/shard_map/ppermute | solution.py:237
  69.1 1.9 %collective-permute-start.14 = (bf16[1,128,512]{2,1,0:T(8,128)(2,1)S(1)}, bf16[1,128,512]{2,1,0:T(8,128)(2,1)S(1)}, u32[]{:S(2)}, u32[]{:S(2)}) collective-permute-start(bf16[1,128,512]{2,1,0:T(8,128)(2,1)S(1)} %get-tuple-element.45.refs_4_), channel_id=1, source_target_pairs={{0,8},{1,9},{2,10},{3,11},{4,12},{5,13},{6,14},{7,15},{8,0},{9,1},... | collective-permute-start | bytes 393224 | tf_op jit(solution)/shard_map/ppermute | solution.py:237
  71.2 2.7 %collective-permute-done.11 = bf16[1,128,512]{2,1,0:T(8,128)(2,1)S(1)} collective-permute-done((bf16[1,128,512]{2,1,0:T(8,128)(2,1)S(1)}, bf16[1,128,512]{2,1,0:T(8,128)(2,1)S(1)}, u32[]{:S(2)}, u32[]{:S(2)}) %collective-permute-start.11) | collective-permute-done | bytes 131104 | tf_op jit(solution)/shard_map/ppermute | solution.py:237
  74.0 2.6 %collective-permute-done.15 = bf16[1,128,512]{2,1,0:T(8,128)(2,1)S(1)} collective-permute-done((bf16[1,128,512]{2,1,0:T(8,128)(2,1)S(1)}, bf16[1,128,512]{2,1,0:T(8,128)(2,1)S(1)}, u32[]{:S(2)}, u32[]{:S(2)}) %collective-permute-start.15) | collective-permute-done | bytes 131104 | tf_op jit(solution)/shard_map/ppermute | solution.py:237
  76.7 2.2 %collective-permute-done.19 = bf16[1,128,512]{2,1,0:T(8,128)(2,1)S(1)} collective-permute-done((bf16[1,128,512]{2,1,0:T(8,128)(2,1)S(1)}, bf16[1,128,512]{2,1,0:T(8,128)(2,1)S(1)}, u32[]{:S(2)}, u32[]{:S(2)}) %collective-permute-start.19) | collective-permute-done | bytes 131104 | tf_op jit(solution)/shard_map/ppermute | solution.py:237
  78.8 4.1 %collective-permute-done.23 = bf16[1,128,512]{2,1,0:T(8,128)(2,1)S(1)} collective-permute-done((bf16[1,128,512]{2,1,0:T(8,128)(2,1)S(1)}, bf16[1,128,512]{2,1,0:T(8,128)(2,1)S(1)}, u32[]{:S(2)}, u32[]{:S(2)}) %collective-permute-start.23) | collective-permute-done | bytes 131104 | tf_op jit(solution)/shard_map/ppermute | solution.py:237
  82.9 0.3 hidden.2.refs_0_
  83.2 0.3 collective-permute-start.24
  83.5 0.3 hidden.3.refs_0_
  83.8 1.9 %collective-permute-start.27 = (bf16[64,2048]{1,0:T(8,128)(2,1)S(1)}, bf16[64,2048]{1,0:T(8,128)(2,1)S(1)}, u32[]{:S(2)}, u32[]{:S(2)}) collective-permute-start(bf16[64,2048]{1,0:T(8,128)(2,1)S(1)} %hidden.3.refs_0_), channel_id=1, source_target_pairs={{0,8},{1,17},{2,10},{3,19},{4,12},{5,21},{6,14},{7,23},{8,0},{9,25... | collective-permute-start | bytes 786440 | tf_op jit(solution)/shard_map/ppermute | solution.py:237
  85.8 6.6 %collective-permute-done.24.refs_1_ = bf16[64,2048]{1,0:T(8,128)(2,1)S(1)} collective-permute-done((bf16[64,2048]{1,0:T(8,128)(2,1)S(1)}, bf16[64,2048]{1,0:T(8,128)(2,1)S(1)}, u32[]{:S(2)}, u32[]{:S(2)}) %collective-permute-start.24) | collective-permute-done | bytes 262176 | tf_op jit(solution)/shard_map/ppermute | solution.py:237
  92.5 1.9 %collective-permute-start.28 = (bf16[64,2048]{1,0:T(8,128)(2,1)S(1)}, bf16[64,2048]{1,0:T(8,128)(2,1)S(1)}, u32[]{:S(2)}, u32[]{:S(2)}) collective-permute-start(bf16[64,2048]{1,0:T(8,128)(2,1)S(1)} %hidden.3.refs_0_), channel_id=1, source_target_pairs={{0,16},{1,9},{2,18},{3,11},{4,20},{5,13},{6,22},{7,15},{8,24},{9,1... | collective-permute-start | bytes 786440 | tf_op jit(solution)/shard_map/ppermute | solution.py:237
  94.4 3.6 %collective-permute-done.27.refs_0_.refs_1_ = bf16[64,2048]{1,0:T(8,128)(2,1)S(1)} collective-permute-done((bf16[64,2048]{1,0:T(8,128)(2,1)S(1)}, bf16[64,2048]{1,0:T(8,128)(2,1)S(1)}, u32[]{:S(2)}, u32[]{:S(2)}) %collective-permute-start.27) | collective-permute-done | bytes 262176 | tf_op jit(solution)/shard_map/ppermute | solution.py:237
  98.3 0.5 collective-permute-done.26.refs_3_
  98.8 6.2 %down.2 = (f32[4,32,2048]{2,1,0:T(8,128)S(1)}, bf16[4,32,2048]{2,1,0:T(8,128)(2,1)S(1)}) custom-call(s32[9]{0:T(128)S(1)} %stack.33.place_ref, bf16[64,2048]{1,0:T(8,128)(2,1)S(1)} %hidden.2.refs_0_, bf16[64,2048]{1,0:T(8,128)(2,1)S(1)} %collective-permute-done.24.refs_1_, bf16[64,2048]{1,0:T(8,128)(2,1)S(1)} %collective-permute-done.25.refs_2_, ...), custom_call_target="tpu_custom_call" | custom-call | flops 2147483648 | bytes 8388608 | tf_op jit(solution)/shard_map/down/pallas_call | solution.py:173
  105.2 1.9 %collective-permute-done.30 = bf16[4,32,2048]{2,1,0:T(8,128)(2,1)S(1)} collective-permute-done((bf16[4,32,2048]{2,1,0:T(8,128)(2,1)S(1)}, bf16[4,32,2048]{2,1,0:T(8,128)(2,1)S(1)}, u32[]{:S(2)}, u32[]{:S(2)}) %collective-permute-start.30) | collective-permute-done | bytes 524320 | tf_op jit(solution)/shard_map/ppermute | solution.py:237
  107.2 3.2 %collective-permute-start.33 = (bf16[32,2048]{1,0:T(8,128)(2,1)S(1)}, bf16[32,2048]{1,0:T(8,128)(2,1)S(1)}, u32[]{:S(2)}, u32[]{:S(2)}) collective-permute-start(bf16[32,2048]{1,0:T(8,128)(2,1)S(1)} %get-tuple-element.64), channel_id=1, source_target_pairs={{0,6},{1,7},{2,4},{3,5},{4,2},{5,3},{6,0},{7,1},{8,14},{9,15},{10,... | collective-permute-start | bytes 393224 | tf_op jit(solution)/shard_map/ppermute | solution.py:237
  110.4 1.3 collective-permute-start.31
  111.6 6.2 %down.3 = (f32[4,32,2048]{2,1,0:T(8,128)S(1)}, bf16[4,32,2048]{2,1,0:T(8,128)(2,1)S(1)}) custom-call(s32[9]{0:T(128)S(1)} %stack.33.place_ref, bf16[64,2048]{1,0:T(8,128)(2,1)S(1)} %hidden.3.refs_0_, bf16[64,2048]{1,0:T(8,128)(2,1)S(1)} %collective-permute-done.27.refs_0_.refs_1_, bf16[64,2048]{1,0:T(8,128)(2,1)S(1)} %collective-permute-done.28.refs_1_.refs_2_, ...), custom_call_target="tpu_custom_call" | custom-call | flops 2147483648 | bytes 8388608 | tf_op jit(solution)/shard_map/down/pallas_call | solution.py:173
  117.9 4.3 %collective-permute-done.32.refs_1_ = bf16[32,2048]{1,0:T(8,128)(2,1)S(1)} collective-permute-done((bf16[32,2048]{1,0:T(8,128)(2,1)S(1)}, bf16[32,2048]{1,0:T(8,128)(2,1)S(1)}, u32[]{:S(2)}, u32[]{:S(2)}) %collective-permute-start.32) | collective-permute-done | bytes 131104 | tf_op jit(solution)/shard_map/ppermute | solution.py:237
  122.3 1.9 %collective-permute-done.34 = bf16[4,32,2048]{2,1,0:T(8,128)(2,1)S(1)} collective-permute-done((bf16[4,32,2048]{2,1,0:T(8,128)(2,1)S(1)}, bf16[4,32,2048]{2,1,0:T(8,128)(2,1)S(1)}, u32[]{:S(2)}, u32[]{:S(2)}) %collective-permute-start.34) | collective-permute-done | bytes 524320 | tf_op jit(solution)/shard_map/ppermute | solution.py:237
  124.4 2.1 %collective-permute-start.37 = (bf16[32,2048]{1,0:T(8,128)(2,1)S(1)}, bf16[32,2048]{1,0:T(8,128)(2,1)S(1)}, u32[]{:S(2)}, u32[]{:S(2)}) collective-permute-start(bf16[32,2048]{1,0:T(8,128)(2,1)S(1)} %get-tuple-element.62), channel_id=1, source_target_pairs={{0,6},{1,7},{2,4},{3,5},{4,2},{5,3},{6,0},{7,1},{8,14},{9,15},{10,... | collective-permute-start | bytes 393224 | tf_op jit(solution)/shard_map/ppermute | solution.py:237
  126.5 1.4 collective-permute-start.36
  128.0 2.1 %collective-permute-done.35 = bf16[32,2048]{1,0:T(8,128)(2,1)S(1)} collective-permute-done((bf16[32,2048]{1,0:T(8,128)(2,1)S(1)}, bf16[32,2048]{1,0:T(8,128)(2,1)S(1)}, u32[]{:S(2)}, u32[]{:S(2)}) %collective-permute-start.35) | collective-permute-done | bytes 131104 | tf_op jit(solution)/shard_map/ppermute | solution.py:237
  130.1 3.5 %collective-permute-done.37 = bf16[32,2048]{1,0:T(8,128)(2,1)S(1)} collective-permute-done((bf16[32,2048]{1,0:T(8,128)(2,1)S(1)}, bf16[32,2048]{1,0:T(8,128)(2,1)S(1)}, u32[]{:S(2)}, u32[]{:S(2)}) %collective-permute-start.37) | collective-permute-done | bytes 131104 | tf_op jit(solution)/shard_map/ppermute | solution.py:237
  133.6 5.9 %collective-permute-done.36 = bf16[32,2048]{1,0:T(8,128)(2,1)S(1)} collective-permute-done((bf16[32,2048]{1,0:T(8,128)(2,1)S(1)}, bf16[32,2048]{1,0:T(8,128)(2,1)S(1)}, u32[]{:S(2)}, u32[]{:S(2)}) %collective-permute-start.36) | collective-permute-done | bytes 131104 | tf_op jit(solution)/shard_map/ppermute | solution.py:237
  139.6 0.7 pad_maximum_fusion
  (58 shorter events, 2.1 us)
Async XLA Ops:
  0.0 13.1 %collective-permute-start.1 = (bf16[128,1024]{1,0:T(8,128)(2,1)}, bf16[128,1024]{1,0:T(8,128)(2,1)S(1)}, u32[]{:S(2)}, u32[]{:S(2)}) collective-permute-start(bf16[128,1024]{1,0:T(8,128)(2,1)} %param.7), channel_id=1, source_target_pairs={{0,2},{1,3},{2,10},{3,11},{4,18},{5,19},{6,26},{7,27},{8,0},{9,1},... | collective-permute-start | bytes 786440 | tf_op jit(solution)/shard_map/ppermute | solution.py:237
  3.0 10.2 %collective-permute-start = (bf16[128,1024]{1,0:T(8,128)(2,1)}, bf16[128,1024]{1,0:T(8,128)(2,1)S(1)}, u32[]{:S(2)}, u32[]{:S(2)}) collective-permute-start(bf16[128,1024]{1,0:T(8,128)(2,1)} %param.7), channel_id=1, source_target_pairs={{0,0},{1,1},{2,8},{3,9},{4,16},{5,17},{6,24},{7,25},{8,2},{9,3},{1... | collective-permute-start | bytes 786440 | tf_op jit(solution)/shard_map/ppermute | solution.py:237
  4.6 15.8 %collective-permute-start.3 = (bf16[128,1024]{1,0:T(8,128)(2,1)}, bf16[128,1024]{1,0:T(8,128)(2,1)S(1)}, u32[]{:S(2)}, u32[]{:S(2)}) collective-permute-start(bf16[128,1024]{1,0:T(8,128)(2,1)} %param.7), channel_id=1, source_target_pairs={{0,6},{1,7},{2,14},{3,15},{4,22},{5,23},{6,30},{7,31},{8,4},{9,5},... | collective-permute-start | bytes 786440 | tf_op jit(solution)/shard_map/ppermute | solution.py:237
  11.6 12.7 %collective-permute-start.2 = (bf16[128,1024]{1,0:T(8,128)(2,1)}, bf16[128,1024]{1,0:T(8,128)(2,1)S(1)}, u32[]{:S(2)}, u32[]{:S(2)}) collective-permute-start(bf16[128,1024]{1,0:T(8,128)(2,1)} %param.7), channel_id=1, source_target_pairs={{0,4},{1,5},{2,12},{3,13},{4,20},{5,21},{6,28},{7,29},{8,6},{9,7},... | collective-permute-start | bytes 786440 | tf_op jit(solution)/shard_map/ppermute | solution.py:237
  13.1 11.5 %collective-permute-start.5 = (bf16[128,1024]{1,0:T(8,128)(2,1)S(1)}, bf16[128,1024]{1,0:T(8,128)(2,1)S(1)}, u32[]{:S(2)}, u32[]{:S(2)}) collective-permute-start(bf16[128,1024]{1,0:T(8,128)(2,1)S(1)} %collective-permute-done.1.refs_1_), channel_id=1, source_target_pairs={{0,1},{1,0},{2,3},{3,2},{4,5},{5,4},{6,7},{7,6},{8,9},{9,8},{10,11... | collective-permute-start | bytes 786440 | tf_op jit(solution)/shard_map/ppermute | solution.py:237
  13.2 11.4 %collective-permute-start.4 = (bf16[128,1024]{1,0:T(8,128)(2,1)S(1)}, bf16[128,1024]{1,0:T(8,128)(2,1)S(1)}, u32[]{:S(2)}, u32[]{:S(2)}) collective-permute-start(bf16[128,1024]{1,0:T(8,128)(2,1)S(1)} %collective-permute-done.refs_0_), channel_id=1, source_target_pairs={{0,1},{1,0},{2,3},{3,2},{4,5},{5,4},{6,7},{7,6},{8,9},{9,8},{10,11... | collective-permute-start | bytes 786440 | tf_op jit(solution)/shard_map/ppermute | solution.py:237
  20.4 4.2 %collective-permute-start.7 = (bf16[128,1024]{1,0:T(8,128)(2,1)S(1)}, bf16[128,1024]{1,0:T(8,128)(2,1)S(1)}, u32[]{:S(2)}, u32[]{:S(2)}) collective-permute-start(bf16[128,1024]{1,0:T(8,128)(2,1)S(1)} %collective-permute-done.3.refs_3_), channel_id=1, source_target_pairs={{0,1},{1,0},{2,3},{3,2},{4,5},{5,4},{6,7},{7,6},{8,9},{9,8},{10,11... | collective-permute-start | bytes 786440 | tf_op jit(solution)/shard_map/ppermute | solution.py:237
  24.3 1.5 %collective-permute-start.6 = (bf16[128,1024]{1,0:T(8,128)(2,1)S(1)}, bf16[128,1024]{1,0:T(8,128)(2,1)S(1)}, u32[]{:S(2)}, u32[]{:S(2)}) collective-permute-start(bf16[128,1024]{1,0:T(8,128)(2,1)S(1)} %collective-permute-done.2.refs_2_), channel_id=1, source_target_pairs={{0,1},{1,0},{2,3},{3,2},{4,5},{5,4},{6,7},{7,6},{8,9},{9,8},{10,11... | collective-permute-start | bytes 786440 | tf_op jit(solution)/shard_map/ppermute | solution.py:237
  30.7 22.1 %collective-permute-start.9 = (bf16[2,128,512]{2,1,0:T(8,128)(2,1)S(1)}, bf16[2,128,512]{2,1,0:T(8,128)(2,1)S(1)}, u32[]{:S(2)}, u32[]{:S(2)}) collective-permute-start(bf16[2,128,512]{2,1,0:T(8,128)(2,1)S(1)} %get-tuple-element.36), channel_id=1, source_target_pairs={{0,8},{1,9},{2,10},{3,11},{4,12},{5,13},{6,14},{7,15},{8,0},{9,1},... | collective-permute-start | bytes 786440 | tf_op jit(solution)/shard_map/ppermute | solution.py:237
  33.0 26.8 %collective-permute-start.8 = (bf16[2,128,512]{2,1,0:T(8,128)(2,1)S(1)}, bf16[2,128,512]{2,1,0:T(8,128)(2,1)S(1)}, u32[]{:S(2)}, u32[]{:S(2)}) collective-permute-start(bf16[2,128,512]{2,1,0:T(8,128)(2,1)S(1)} %get-tuple-element.34.refs_12_), channel_id=1, source_target_pairs={{0,16},{1,17},{2,18},{3,19},{4,20},{5,21},{6,22},{7,23},{8,24},{9,... | collective-permute-start | bytes 786440 | tf_op jit(solution)/shard_map/ppermute | solution.py:237
  45.8 16.1 %collective-permute-start.13 = (bf16[2,128,512]{2,1,0:T(8,128)(2,1)S(1)}, bf16[2,128,512]{2,1,0:T(8,128)(2,1)S(1)}, u32[]{:S(2)}, u32[]{:S(2)}) collective-permute-start(bf16[2,128,512]{2,1,0:T(8,128)(2,1)S(1)} %get-tuple-element.44), channel_id=1, source_target_pairs={{0,8},{1,9},{2,10},{3,11},{4,12},{5,13},{6,14},{7,15},{8,0},{9,1},... | collective-permute-start | bytes 786440 | tf_op jit(solution)/shard_map/ppermute | solution.py:237
  47.8 14.1 %collective-permute-start.12 = (bf16[2,128,512]{2,1,0:T(8,128)(2,1)S(1)}, bf16[2,128,512]{2,1,0:T(8,128)(2,1)S(1)}, u32[]{:S(2)}, u32[]{:S(2)}) collective-permute-start(bf16[2,128,512]{2,1,0:T(8,128)(2,1)S(1)} %get-tuple-element.37.refs_12_), channel_id=1, source_target_pairs={{0,16},{1,17},{2,18},{3,19},{4,20},{5,21},{6,22},{7,23},{8,24},{9,... | collective-permute-start | bytes 786440 | tf_op jit(solution)/shard_map/ppermute | solution.py:237
  52.7 11.4 %collective-permute-start.17 = (bf16[2,128,512]{2,1,0:T(8,128)(2,1)S(1)}, bf16[2,128,512]{2,1,0:T(8,128)(2,1)S(1)}, u32[]{:S(2)}, u32[]{:S(2)}) collective-permute-start(bf16[2,128,512]{2,1,0:T(8,128)(2,1)S(1)} %get-tuple-element.49), channel_id=1, source_target_pairs={{0,8},{1,9},{2,10},{3,11},{4,12},{5,13},{6,14},{7,15},{8,0},{9,1},... | collective-permute-start | bytes 786440 | tf_op jit(solution)/shard_map/ppermute | solution.py:237
  52.9 11.3 %collective-permute-start.16 = (bf16[2,128,512]{2,1,0:T(8,128)(2,1)S(1)}, bf16[2,128,512]{2,1,0:T(8,128)(2,1)S(1)}, u32[]{:S(2)}, u32[]{:S(2)}) collective-permute-start(bf16[2,128,512]{2,1,0:T(8,128)(2,1)S(1)} %get-tuple-element.38.refs_12_), channel_id=1, source_target_pairs={{0,16},{1,17},{2,18},{3,19},{4,20},{5,21},{6,22},{7,23},{8,24},{9,... | collective-permute-start | bytes 786440 | tf_op jit(solution)/shard_map/ppermute | solution.py:237
  59.8 9.3 %collective-permute-start.21 = (bf16[2,128,512]{2,1,0:T(8,128)(2,1)S(1)}, bf16[2,128,512]{2,1,0:T(8,128)(2,1)S(1)}, u32[]{:S(2)}, u32[]{:S(2)}) collective-permute-start(bf16[2,128,512]{2,1,0:T(8,128)(2,1)S(1)} %get-tuple-element.54), channel_id=1, source_target_pairs={{0,8},{1,9},{2,10},{3,11},{4,12},{5,13},{6,14},{7,15},{8,0},{9,1},... | collective-permute-start | bytes 786440 | tf_op jit(solution)/shard_map/ppermute | solution.py:237
  61.8 9.2 %collective-permute-start.20 = (bf16[2,128,512]{2,1,0:T(8,128)(2,1)S(1)}, bf16[2,128,512]{2,1,0:T(8,128)(2,1)S(1)}, u32[]{:S(2)}, u32[]{:S(2)}) collective-permute-start(bf16[2,128,512]{2,1,0:T(8,128)(2,1)S(1)} %get-tuple-element.39.refs_4_), channel_id=1, source_target_pairs={{0,16},{1,17},{2,18},{3,19},{4,20},{5,21},{6,22},{7,23},{8,24},{9,... | collective-permute-start | bytes 786440 | tf_op jit(solution)/shard_map/ppermute | solution.py:237
  61.9 12.0 %collective-permute-start.11 = (bf16[1,128,512]{2,1,0:T(8,128)(2,1)S(1)}, bf16[1,128,512]{2,1,0:T(8,128)(2,1)S(1)}, u32[]{:S(2)}, u32[]{:S(2)}) collective-permute-start(bf16[1,128,512]{2,1,0:T(8,128)(2,1)S(1)} %get-tuple-element.41), channel_id=1, source_target_pairs={{0,16},{1,17},{2,18},{3,19},{4,20},{5,21},{6,22},{7,23},{8,24},{9,... | collective-permute-start | bytes 393224 | tf_op jit(solution)/shard_map/ppermute | solution.py:237
  64.1 9.8 %collective-permute-start.10 = (bf16[1,128,512]{2,1,0:T(8,128)(2,1)S(1)}, bf16[1,128,512]{2,1,0:T(8,128)(2,1)S(1)}, u32[]{:S(2)}, u32[]{:S(2)}) collective-permute-start(bf16[1,128,512]{2,1,0:T(8,128)(2,1)S(1)} %get-tuple-element.40.refs_4_), channel_id=1, source_target_pairs={{0,8},{1,9},{2,10},{3,11},{4,12},{5,13},{6,14},{7,15},{8,0},{9,1},... | collective-permute-start | bytes 393224 | tf_op jit(solution)/shard_map/ppermute | solution.py:237
  64.2 12.4 %collective-permute-start.15 = (bf16[1,128,512]{2,1,0:T(8,128)(2,1)S(1)}, bf16[1,128,512]{2,1,0:T(8,128)(2,1)S(1)}, u32[]{:S(2)}, u32[]{:S(2)}) collective-permute-start(bf16[1,128,512]{2,1,0:T(8,128)(2,1)S(1)} %get-tuple-element.46), channel_id=1, source_target_pairs={{0,16},{1,17},{2,18},{3,19},{4,20},{5,21},{6,22},{7,23},{8,24},{9,... | collective-permute-start | bytes 393224 | tf_op jit(solution)/shard_map/ppermute | solution.py:237
  69.1 7.6 %collective-permute-start.14 = (bf16[1,128,512]{2,1,0:T(8,128)(2,1)S(1)}, bf16[1,128,512]{2,1,0:T(8,128)(2,1)S(1)}, u32[]{:S(2)}, u32[]{:S(2)}) collective-permute-start(bf16[1,128,512]{2,1,0:T(8,128)(2,1)S(1)} %get-tuple-element.45.refs_4_), channel_id=1, source_target_pairs={{0,8},{1,9},{2,10},{3,11},{4,12},{5,13},{6,14},{7,15},{8,0},{9,1},... | collective-permute-start | bytes 393224 | tf_op jit(solution)/shard_map/ppermute | solution.py:237
  71.1 7.8 %collective-permute-start.18 = (bf16[1,128,512]{2,1,0:T(8,128)(2,1)S(1)}, bf16[1,128,512]{2,1,0:T(8,128)(2,1)S(1)}, u32[]{:S(2)}, u32[]{:S(2)}) collective-permute-start(bf16[1,128,512]{2,1,0:T(8,128)(2,1)S(1)} %get-tuple-element.50.refs_4_), channel_id=1, source_target_pairs={{0,8},{1,9},{2,10},{3,11},{4,12},{5,13},{6,14},{7,15},{8,0},{9,1},... | collective-permute-start | bytes 393224 | tf_op jit(solution)/shard_map/ppermute | solution.py:237
  71.1 27.0 %copy-start = (s32[16,16]{1,0:T(8,128)S(1)}, s32[16,16]{1,0:T(8,128)}, u32[]{:S(2)}) copy-start(s32[16,16]{1,0:T(8,128)} %param.13) | copy-start | bytes 3076
  73.9 5.0 %collective-permute-start.19 = (bf16[1,128,512]{2,1,0:T(8,128)(2,1)S(1)}, bf16[1,128,512]{2,1,0:T(8,128)(2,1)S(1)}, u32[]{:S(2)}, u32[]{:S(2)}) collective-permute-start(bf16[1,128,512]{2,1,0:T(8,128)(2,1)S(1)} %get-tuple-element.51), channel_id=1, source_target_pairs={{0,16},{1,17},{2,18},{3,19},{4,20},{5,21},{6,22},{7,23},{8,24},{9,... | collective-permute-start | bytes 393224 | tf_op jit(solution)/shard_map/ppermute | solution.py:237
  73.9 5.0 %collective-permute-start.22 = (bf16[1,128,512]{2,1,0:T(8,128)(2,1)S(1)}, bf16[1,128,512]{2,1,0:T(8,128)(2,1)S(1)}, u32[]{:S(2)}, u32[]{:S(2)}) collective-permute-start(bf16[1,128,512]{2,1,0:T(8,128)(2,1)S(1)} %get-tuple-element.55), channel_id=1, source_target_pairs={{0,8},{1,9},{2,10},{3,11},{4,12},{5,13},{6,14},{7,15},{8,0},{9,1},... | collective-permute-start | bytes 393224 | tf_op jit(solution)/shard_map/ppermute | solution.py:237
  76.6 6.3 %collective-permute-start.23 = (bf16[1,128,512]{2,1,0:T(8,128)(2,1)S(1)}, bf16[1,128,512]{2,1,0:T(8,128)(2,1)S(1)}, u32[]{:S(2)}, u32[]{:S(2)}) collective-permute-start(bf16[1,128,512]{2,1,0:T(8,128)(2,1)S(1)} %get-tuple-element.56), channel_id=1, source_target_pairs={{0,16},{1,17},{2,18},{3,19},{4,20},{5,21},{6,22},{7,23},{8,24},{9,... | collective-permute-start | bytes 393224 | tf_op jit(solution)/shard_map/ppermute | solution.py:237
  83.2 9.2 %collective-permute-start.24 = (bf16[64,2048]{1,0:T(8,128)(2,1)S(1)}, bf16[64,2048]{1,0:T(8,128)(2,1)S(1)}, u32[]{:S(2)}, u32[]{:S(2)}) collective-permute-start(bf16[64,2048]{1,0:T(8,128)(2,1)S(1)} %hidden.2.refs_0_), channel_id=1, source_target_pairs={{0,8},{1,17},{2,10},{3,19},{4,12},{5,21},{6,14},{7,23},{8,0},{9,25... | collective-permute-start | bytes 786440 | tf_op jit(solution)/shard_map/ppermute | solution.py:237
  83.8 14.2 %collective-permute-start.27 = (bf16[64,2048]{1,0:T(8,128)(2,1)S(1)}, bf16[64,2048]{1,0:T(8,128)(2,1)S(1)}, u32[]{:S(2)}, u32[]{:S(2)}) collective-permute-start(bf16[64,2048]{1,0:T(8,128)(2,1)S(1)} %hidden.3.refs_0_), channel_id=1, source_target_pairs={{0,8},{1,17},{2,10},{3,19},{4,12},{5,21},{6,14},{7,23},{8,0},{9,25... | collective-permute-start | bytes 786440 | tf_op jit(solution)/shard_map/ppermute | solution.py:237
  85.7 12.6 %collective-permute-start.25 = (bf16[64,2048]{1,0:T(8,128)(2,1)S(1)}, bf16[64,2048]{1,0:T(8,128)(2,1)S(1)}, u32[]{:S(2)}, u32[]{:S(2)}) collective-permute-start(bf16[64,2048]{1,0:T(8,128)(2,1)S(1)} %hidden.2.refs_0_), channel_id=1, source_target_pairs={{0,16},{1,9},{2,18},{3,11},{4,20},{5,13},{6,22},{7,15},{8,24},{9,1... | collective-permute-start | bytes 786440 | tf_op jit(solution)/shard_map/ppermute | solution.py:237
  92.4 6.4 %collective-permute-start.26 = (bf16[64,2048]{1,0:T(8,128)(2,1)S(1)}, bf16[64,2048]{1,0:T(8,128)(2,1)S(1)}, u32[]{:S(2)}, u32[]{:S(2)}) collective-permute-start(bf16[64,2048]{1,0:T(8,128)(2,1)S(1)} %collective-permute-done.24.refs_1_), channel_id=1, source_target_pairs={{0,16},{1,9},{2,18},{3,11},{4,20},{5,13},{6,22},{7,15},{8,24},{9,1... | collective-permute-start | bytes 786440 | tf_op jit(solution)/shard_map/ppermute | solution.py:237
  92.5 12.5 %collective-permute-start.28 = (bf16[64,2048]{1,0:T(8,128)(2,1)S(1)}, bf16[64,2048]{1,0:T(8,128)(2,1)S(1)}, u32[]{:S(2)}, u32[]{:S(2)}) collective-permute-start(bf16[64,2048]{1,0:T(8,128)(2,1)S(1)} %hidden.3.refs_0_), channel_id=1, source_target_pairs={{0,16},{1,9},{2,18},{3,11},{4,20},{5,13},{6,22},{7,15},{8,24},{9,1... | collective-permute-start | bytes 786440 | tf_op jit(solution)/shard_map/ppermute | solution.py:237
  98.0 7.0 %collective-permute-start.29 = (bf16[64,2048]{1,0:T(8,128)(2,1)S(1)}, bf16[64,2048]{1,0:T(8,128)(2,1)S(1)}, u32[]{:S(2)}, u32[]{:S(2)}) collective-permute-start(bf16[64,2048]{1,0:T(8,128)(2,1)S(1)} %collective-permute-done.27.refs_0_.refs_1_), channel_id=1, source_target_pairs={{0,16},{1,9},{2,18},{3,11},{4,20},{5,13},{6,22},{7,15},{8,24},{9,1... | collective-permute-start | bytes 786440 | tf_op jit(solution)/shard_map/ppermute | solution.py:237
  105.1 2.0 %collective-permute-start.30 = (bf16[4,32,2048]{2,1,0:T(8,128)(2,1)S(1)}, bf16[4,32,2048]{2,1,0:T(8,128)(2,1)S(1)}, u32[]{:S(2)}, u32[]{:S(2)}) collective-permute-start(bf16[4,32,2048]{2,1,0:T(8,128)(2,1)S(1)} %hold.2), channel_id=1, source_target_pairs={{0,1},{1,0},{2,3},{3,2},{4,5},{5,4},{6,7},{7,6},{8,9},{9,8},{10,11... | collective-permute-start | bytes 1572872 | tf_op jit(solution)/shard_map/ppermute | solution.py:237
  107.2 10.7 %collective-permute-start.33 = (bf16[32,2048]{1,0:T(8,128)(2,1)S(1)}, bf16[32,2048]{1,0:T(8,128)(2,1)S(1)}, u32[]{:S(2)}, u32[]{:S(2)}) collective-permute-start(bf16[32,2048]{1,0:T(8,128)(2,1)S(1)} %get-tuple-element.64), channel_id=1, source_target_pairs={{0,6},{1,7},{2,4},{3,5},{4,2},{5,3},{6,0},{7,1},{8,14},{9,15},{10,... | collective-permute-start | bytes 393224 | tf_op jit(solution)/shard_map/ppermute | solution.py:237
  110.4 11.9 %collective-permute-start.32 = (bf16[32,2048]{1,0:T(8,128)(2,1)S(1)}, bf16[32,2048]{1,0:T(8,128)(2,1)S(1)}, u32[]{:S(2)}, u32[]{:S(2)}) collective-permute-start(bf16[32,2048]{1,0:T(8,128)(2,1)S(1)} %get-tuple-element.65), channel_id=1, source_target_pairs={{0,4},{1,5},{2,6},{3,7},{4,0},{5,1},{6,2},{7,3},{8,12},{9,13},{10,... | collective-permute-start | bytes 393224 | tf_op jit(solution)/shard_map/ppermute | solution.py:237
  110.4 11.9 %collective-permute-start.31 = (bf16[32,2048]{1,0:T(8,128)(2,1)S(1)}, bf16[32,2048]{1,0:T(8,128)(2,1)S(1)}, u32[]{:S(2)}, u32[]{:S(2)}) collective-permute-start(bf16[32,2048]{1,0:T(8,128)(2,1)S(1)} %get-tuple-element.66), channel_id=1, source_target_pairs={{0,2},{1,3},{2,0},{3,1},{4,6},{5,7},{6,4},{7,5},{8,10},{9,11},{10,... | collective-permute-start | bytes 393224 | tf_op jit(solution)/shard_map/ppermute | solution.py:237
  122.2 2.0 %collective-permute-start.34 = (bf16[4,32,2048]{2,1,0:T(8,128)(2,1)S(1)}, bf16[4,32,2048]{2,1,0:T(8,128)(2,1)S(1)}, u32[]{:S(2)}, u32[]{:S(2)}) collective-permute-start(bf16[4,32,2048]{2,1,0:T(8,128)(2,1)S(1)} %hold.3), channel_id=1, source_target_pairs={{0,1},{1,0},{2,3},{3,2},{4,5},{5,4},{6,7},{7,6},{8,9},{9,8},{10,11... | collective-permute-start | bytes 1572872 | tf_op jit(solution)/shard_map/ppermute | solution.py:237
  124.3 5.8 %collective-permute-start.35 = (bf16[32,2048]{1,0:T(8,128)(2,1)S(1)}, bf16[32,2048]{1,0:T(8,128)(2,1)S(1)}, u32[]{:S(2)}, u32[]{:S(2)}) collective-permute-start(bf16[32,2048]{1,0:T(8,128)(2,1)S(1)} %get-tuple-element.61), channel_id=1, source_target_pairs={{0,2},{1,3},{2,0},{3,1},{4,6},{5,7},{6,4},{7,5},{8,10},{9,11},{10,... | collective-permute-start | bytes 393224 | tf_op jit(solution)/shard_map/ppermute | solution.py:237
  124.4 9.2 %collective-permute-start.37 = (bf16[32,2048]{1,0:T(8,128)(2,1)S(1)}, bf16[32,2048]{1,0:T(8,128)(2,1)S(1)}, u32[]{:S(2)}, u32[]{:S(2)}) collective-permute-start(bf16[32,2048]{1,0:T(8,128)(2,1)S(1)} %get-tuple-element.62), channel_id=1, source_target_pairs={{0,6},{1,7},{2,4},{3,5},{4,2},{5,3},{6,0},{7,1},{8,14},{9,15},{10,... | collective-permute-start | bytes 393224 | tf_op jit(solution)/shard_map/ppermute | solution.py:237
  126.5 13.0 %collective-permute-start.36 = (bf16[32,2048]{1,0:T(8,128)(2,1)S(1)}, bf16[32,2048]{1,0:T(8,128)(2,1)S(1)}, u32[]{:S(2)}, u32[]{:S(2)}) collective-permute-start(bf16[32,2048]{1,0:T(8,128)(2,1)S(1)} %get-tuple-element.63), channel_id=1, source_target_pairs={{0,4},{1,5},{2,6},{3,7},{4,0},{5,1},{6,2},{7,3},{8,12},{9,13},{10,... | collective-permute-start | bytes 393224 | tf_op jit(solution)/shard_map/ppermute | solution.py:237

commit v13 on v9

--- a/solution.py
+++ b/solution.py
@@ -290,7 +290,7 @@
         for later in hidden[s + 1 : s + 2]:
             beside = beside + later[1:]
         mine, theirs = down(place, parts, down_weight, down_wide, ())
-        total, sent = combine(mine, hold(theirs, beside))
+        total, sent = combine(mine, hold(theirs, beside[:2] if s else beside))
         beside = [across_z(sent[j - 1], j) for j in range(1, n_z)]
         for part in beside:
             total += part.astype(jnp.float32)

time: 138 us -> 136 us (0.986)
  waiting for transfers between devices: 57.2 us -> 53.2 us
  starting transfers between devices: 47.8 us -> 50.1 us
    ppermute x30, waiting for transfers between devices: 57.2 us -> 53.2 us  [send(): return lax.ppermute(value, AXES, perm)]
    ppermute x30, starting transfers between devices: 47.8 us -> 50.1 us  [send(): return lax.ppermute(value, AXES, perm)]
  transfers between devices with their start and end apart: 30 -> 30, of which waited for: 17 -> 16; matrix products, arithmetic and copies ran while one was open for 1% -> 2% of each run, Pallas kernels for 15% -> 15%
where the time goes in v13:
time: 136 us; the launch traced here: 135 us
  waiting for transfers between devices  53.2 us (39%)
  starting transfers between devices  50.1 us (37%)
  Pallas kernels  29 us (21%)
  other arithmetic  2.48 us (2%)
    ppermute x30, waiting for transfers between devices, send(): return lax.ppermute(value, AXES, perm)  53.2 us
    ppermute x30, starting transfers between devices, send(): return lax.ppermute(value, AXES, perm)  50.1 us
    pallas_call x2, Pallas kernels, project(): pl.pallas_call(functools.partial(project_kernel, n), grid_spec=pltpu.Pref...  15.7 us
    pallas_call x2, Pallas kernels, down(): pl.pallas_call(functools.partial(down_kernel, n), grid_spec=pltpu.Prefetc...  12.5 us
  transfers between devices with their start and end apart: 30, of which 16 were waited for; matrix products, arithmetic and copies ran while one was open for 2% of the time, Pallas kernels for 15%

profile of v13, /device:TPU:0, one launch (start us, length us, event | category | flops | bytes accessed | tf_op | source)
XLA Modules:
  0.0 135.5 jit_solution(16784331854345006148)
XLA Ops:
  0.0 3.0 %collective-permute-start.1 = (bf16[128,1024]{1,0:T(8,128)(2,1)}, bf16[128,1024]{1,0:T(8,128)(2,1)S(1)}, u32[]{:S(2)}, u32[]{:S(2)}) collective-permute-start(bf16[128,1024]{1,0:T(8,128)(2,1)} %param.7), channel_id=1, source_target_pairs={{0,2},{1,3},{2,10},{3,11},{4,18},{5,19},{6,26},{7,27},{8,0},{9,1},... | collective-permute-start | bytes 786440 | tf_op jit(solution)/shard_map/ppermute | solution.py:237
  3.0 1.6 %collective-permute-start = (bf16[128,1024]{1,0:T(8,128)(2,1)}, bf16[128,1024]{1,0:T(8,128)(2,1)S(1)}, u32[]{:S(2)}, u32[]{:S(2)}) collective-permute-start(bf16[128,1024]{1,0:T(8,128)(2,1)} %param.7), channel_id=1, source_target_pairs={{0,0},{1,1},{2,8},{3,9},{4,16},{5,17},{6,24},{7,25},{8,2},{9,3},{1... | collective-permute-start | bytes 786440 | tf_op jit(solution)/shard_map/ppermute | solution.py:237
  4.6 7.0 %collective-permute-start.3 = (bf16[128,1024]{1,0:T(8,128)(2,1)}, bf16[128,1024]{1,0:T(8,128)(2,1)S(1)}, u32[]{:S(2)}, u32[]{:S(2)}) collective-permute-start(bf16[128,1024]{1,0:T(8,128)(2,1)} %param.7), channel_id=1, source_target_pairs={{0,6},{1,7},{2,14},{3,15},{4,22},{5,23},{6,30},{7,31},{8,4},{9,5},... | collective-permute-start | bytes 786440 | tf_op jit(solution)/shard_map/ppermute | solution.py:237
  11.6 0.7 convert_element_type.101
  12.3 0.7 convert_element_type.102
  13.2 0.5 collective-permute-start.4
  13.7 6.7 %collective-permute-done.3.refs_3_ = bf16[128,1024]{1,0:T(8,128)(2,1)S(1)} collective-permute-done((bf16[128,1024]{1,0:T(8,128)(2,1)}, bf16[128,1024]{1,0:T(8,128)(2,1)S(1)}, u32[]{:S(2)}, u32[]{:S(2)}) %collective-permute-start.3) | collective-permute-done | bytes 262176 | tf_op jit(solution)/shard_map/ppermute | solution.py:237
  20.4 3.9 %collective-permute-done.2.refs_2_ = bf16[128,1024]{1,0:T(8,128)(2,1)S(1)} collective-permute-done((bf16[128,1024]{1,0:T(8,128)(2,1)}, bf16[128,1024]{1,0:T(8,128)(2,1)S(1)}, u32[]{:S(2)}, u32[]{:S(2)}) %collective-permute-start.2) | collective-permute-done | bytes 262176 | tf_op jit(solution)/shard_map/ppermute | solution.py:237
  24.6 1.2 collective-permute-done.6.refs_6_
  25.8 7.9 %project.2 = (f32[2,128,1024]{2,1,0:T(8,128)S(1)}, f32[2,128,1024]{2,1,0:T(8,128)S(1)}, bf16[2,128,1024]{2,1,0:T(8,128)(2,1)S(1)}, bf16[2,128,1024]{2,1,0:T(8,128)(2,1)S(1)}) custom-call(s32[9]{0:T(128)S(1)} %stack.33.place_ref, bf16[128,1024]{1,0:T(8,128)(2,1)S(1)} %collective-permute-done.refs_0_, bf16[128,1024]{1,0:T(8,128)(2,1)S(1)} %collective-permute-done.1.refs_1_, ...), custom_call_target="tpu_custom_call" | custom-call | flops 4294967296 | bytes 8388608 | tf_op jit(solution)/shard_map/project/pallas_call | solution.py:68
  33.7 2.3 %collective-permute-start.9 = (bf16[2,128,1024]{2,1,0:T(8,128)(2,1)S(1)}, bf16[2,128,1024]{2,1,0:T(8,128)(2,1)S(1)}, u32[]{:S(2)}, u32[]{:S(2)}) collective-permute-start(bf16[2,128,1024]{2,1,0:T(8,128)(2,1)S(1)} %get-tuple-element.24), channel_id=1, source_target_pairs={{0,8},{1,9},{2,10},{3,11},{4,12},{5,13},{6,14},{7,15},{8,0},{9,1},... | collective-permute-start | bytes 1572872 | tf_op jit(solution)/shard_map/ppermute | solution.py:237
  36.0 7.8 %collective-permute-start.8 = (bf16[2,128,1024]{2,1,0:T(8,128)(2,1)S(1)}, bf16[2,128,1024]{2,1,0:T(8,128)(2,1)S(1)}, u32[]{:S(2)}, u32[]{:S(2)}) collective-permute-start(bf16[2,128,1024]{2,1,0:T(8,128)(2,1)S(1)} %get-tuple-element.22.refs_12_), channel_id=1, source_target_pairs={{0,16},{1,17},{2,18},{3,19},{4,20},{5,21},{6,22},{7,23},{8,24},{9,... | collective-permute-start | bytes 1572872 | tf_op jit(solution)/shard_map/ppermute | solution.py:237
  43.8 7.9 %project.3 = (f32[2,128,1024]{2,1,0:T(8,128)S(1)}, f32[2,128,1024]{2,1,0:T(8,128)S(1)}, bf16[2,128,1024]{2,1,0:T(8,128)(2,1)S(1)}, bf16[2,128,1024]{2,1,0:T(8,128)(2,1)S(1)}) custom-call(s32[9]{0:T(128)S(1)} %stack.33.place_ref, bf16[128,1024]{1,0:T(8,128)(2,1)S(1)} %collective-permute-done.refs_0_, bf16[128,1024]{1,0:T(8,128)(2,1)S(1)} %collective-permute-done.1.refs_1_, ...), custom_call_target="tpu_custom_call" | custom-call | flops 4294967296 | bytes 8388608 | tf_op jit(solution)/shard_map/project/pallas_call | solution.py:68
  51.7 2.0 %collective-permute-start.13 = (bf16[2,128,1024]{2,1,0:T(8,128)(2,1)S(1)}, bf16[2,128,1024]{2,1,0:T(8,128)(2,1)S(1)}, u32[]{:S(2)}, u32[]{:S(2)}) collective-permute-start(bf16[2,128,1024]{2,1,0:T(8,128)(2,1)S(1)} %get-tuple-element.30), channel_id=1, source_target_pairs={{0,8},{1,9},{2,10},{3,11},{4,12},{5,13},{6,14},{7,15},{8,0},{9,1},... | collective-permute-start | bytes 1572872 | tf_op jit(solution)/shard_map/ppermute | solution.py:237
  53.7 2.7 %collective-permute-done.8.refs_1_ = bf16[2,128,1024]{2,1,0:T(8,128)(2,1)S(1)} collective-permute-done((bf16[2,128,1024]{2,1,0:T(8,128)(2,1)S(1)}, bf16[2,128,1024]{2,1,0:T(8,128)(2,1)S(1)}, u32[]{:S(2)}, u32[]{:S(2)}) %collective-permute-start.8) | collective-permute-done | bytes 524320 | tf_op jit(solution)/shard_map/ppermute | solution.py:237
  56.5 2.2 %collective-permute-start.11 = (bf16[1,128,1024]{2,1,0:T(8,128)(2,1)S(1)}, bf16[1,128,1024]{2,1,0:T(8,128)(2,1)S(1)}, u32[]{:S(2)}, u32[]{:S(2)}) collective-permute-start(bf16[1,128,1024]{2,1,0:T(8,128)(2,1)S(1)} %get-tuple-element.27), channel_id=1, source_target_pairs={{0,16},{1,17},{2,18},{3,19},{4,20},{5,21},{6,22},{7,23},{8,24},{9,... | collective-permute-start | bytes 786440 | tf_op jit(solution)/shard_map/ppermute | solution.py:237
  58.7 2.0 %collective-permute-start.10 = (bf16[1,128,1024]{2,1,0:T(8,128)(2,1)S(1)}, bf16[1,128,1024]{2,1,0:T(8,128)(2,1)S(1)}, u32[]{:S(2)}, u32[]{:S(2)}) collective-permute-start(bf16[1,128,1024]{2,1,0:T(8,128)(2,1)S(1)} %get-tuple-element.26.refs_4_), channel_id=1, source_target_pairs={{0,8},{1,9},{2,10},{3,11},{4,12},{5,13},{6,14},{7,15},{8,0},{9,1},... | collective-permute-start | bytes 786440 | tf_op jit(solution)/shard_map/ppermute | solution.py:237
  60.7 5.8 %collective-permute-done.13.refs_3_ = bf16[2,128,1024]{2,1,0:T(8,128)(2,1)S(1)} collective-permute-done((bf16[2,128,1024]{2,1,0:T(8,128)(2,1)S(1)}, bf16[2,128,1024]{2,1,0:T(8,128)(2,1)S(1)}, u32[]{:S(2)}, u32[]{:S(2)}) %collective-permute-start.13) | collective-permute-done | bytes 524320 | tf_op jit(solution)/shard_map/ppermute | solution.py:237
  66.5 2.0 %collective-permute-done.12.refs_1_ = bf16[2,128,1024]{2,1,0:T(8,128)(2,1)S(1)} collective-permute-done((bf16[2,128,1024]{2,1,0:T(8,128)(2,1)S(1)}, bf16[2,128,1024]{2,1,0:T(8,128)(2,1)S(1)}, u32[]{:S(2)}, u32[]{:S(2)}) %collective-permute-start.12) | collective-permute-done | bytes 524320 | tf_op jit(solution)/shard_map/ppermute | solution.py:237
  68.6 1.2 collective-permute-start.14
  69.9 2.1 %collective-permute-start.15 = (bf16[1,128,1024]{2,1,0:T(8,128)(2,1)S(1)}, bf16[1,128,1024]{2,1,0:T(8,128)(2,1)S(1)}, u32[]{:S(2)}, u32[]{:S(2)}) collective-permute-start(bf16[1,128,1024]{2,1,0:T(8,128)(2,1)S(1)} %get-tuple-element.32), channel_id=1, source_target_pairs={{0,16},{1,17},{2,18},{3,19},{4,20},{5,21},{6,22},{7,23},{8,24},{9,... | collective-permute-start | bytes 786440 | tf_op jit(solution)/shard_map/ppermute | solution.py:237
  71.9 2.2 %collective-permute-done.11 = bf16[1,128,1024]{2,1,0:T(8,128)(2,1)S(1)} collective-permute-done((bf16[1,128,1024]{2,1,0:T(8,128)(2,1)S(1)}, bf16[1,128,1024]{2,1,0:T(8,128)(2,1)S(1)}, u32[]{:S(2)}, u32[]{:S(2)}) %collective-permute-start.11) | collective-permute-done | bytes 262176 | tf_op jit(solution)/shard_map/ppermute | solution.py:237
  74.2 2.5 %collective-permute-done.14 = bf16[1,128,1024]{2,1,0:T(8,128)(2,1)S(1)} collective-permute-done((bf16[1,128,1024]{2,1,0:T(8,128)(2,1)S(1)}, bf16[1,128,1024]{2,1,0:T(8,128)(2,1)S(1)}, u32[]{:S(2)}, u32[]{:S(2)}) %collective-permute-start.14) | collective-permute-done | bytes 262176 | tf_op jit(solution)/shard_map/ppermute | solution.py:237
  76.7 1.8 %collective-permute-done.15 = bf16[1,128,1024]{2,1,0:T(8,128)(2,1)S(1)} collective-permute-done((bf16[1,128,1024]{2,1,0:T(8,128)(2,1)S(1)}, bf16[1,128,1024]{2,1,0:T(8,128)(2,1)S(1)}, u32[]{:S(2)}, u32[]{:S(2)}) %collective-permute-start.15) | collective-permute-done | bytes 262176 | tf_op jit(solution)/shard_map/ppermute | solution.py:237
  78.5 0.3 hidden.2.refs_0_
  78.8 1.7 %collective-permute-start.16 = (bf16[64,2048]{1,0:T(8,128)(2,1)S(1)}, bf16[64,2048]{1,0:T(8,128)(2,1)S(1)}, u32[]{:S(2)}, u32[]{:S(2)}) collective-permute-start(bf16[64,2048]{1,0:T(8,128)(2,1)S(1)} %hidden.2.refs_0_), channel_id=1, source_target_pairs={{0,8},{1,17},{2,10},{3,19},{4,12},{5,21},{6,14},{7,23},{8,0},{9,25... | collective-permute-start | bytes 786440 | tf_op jit(solution)/shard_map/ppermute | solution.py:237
  80.5 0.3 hidden.3.refs_0_
  80.8 0.4 collective-permute-start.19
  81.2 1.7 %collective-permute-start.17 = (bf16[64,2048]{1,0:T(8,128)(2,1)S(1)}, bf16[64,2048]{1,0:T(8,128)(2,1)S(1)}, u32[]{:S(2)}, u32[]{:S(2)}) collective-permute-start(bf16[64,2048]{1,0:T(8,128)(2,1)S(1)} %hidden.2.refs_0_), channel_id=1, source_target_pairs={{0,16},{1,9},{2,18},{3,11},{4,20},{5,13},{6,22},{7,15},{8,24},{9,1... | collective-permute-start | bytes 786440 | tf_op jit(solution)/shard_map/ppermute | solution.py:237
  82.9 4.9 %collective-permute-done.16.refs_1_ = bf16[64,2048]{1,0:T(8,128)(2,1)S(1)} collective-permute-done((bf16[64,2048]{1,0:T(8,128)(2,1)S(1)}, bf16[64,2048]{1,0:T(8,128)(2,1)S(1)}, u32[]{:S(2)}, u32[]{:S(2)}) %collective-permute-start.16) | collective-permute-done | bytes 262176 | tf_op jit(solution)/shard_map/ppermute | solution.py:237
  87.9 1.8 %collective-permute-start.18 = (bf16[64,2048]{1,0:T(8,128)(2,1)S(1)}, bf16[64,2048]{1,0:T(8,128)(2,1)S(1)}, u32[]{:S(2)}, u32[]{:S(2)}) collective-permute-start(bf16[64,2048]{1,0:T(8,128)(2,1)S(1)} %collective-permute-done.16.refs_1_), channel_id=1, source_target_pairs={{0,16},{1,9},{2,18},{3,11},{4,20},{5,13},{6,22},{7,15},{8,24},{9,1... | collective-permute-start | bytes 786440 | tf_op jit(solution)/shard_map/ppermute | solution.py:237
  89.7 0.2 collective-permute-start.20
  89.9 3.6 %collective-permute-done.19.refs_0_.refs_1_ = bf16[64,2048]{1,0:T(8,128)(2,1)S(1)} collective-permute-done((bf16[64,2048]{1,0:T(8,128)(2,1)S(1)}, bf16[64,2048]{1,0:T(8,128)(2,1)S(1)}, u32[]{:S(2)}, u32[]{:S(2)}) %collective-permute-start.19) | collective-permute-done | bytes 262176 | tf_op jit(solution)/shard_map/ppermute | solution.py:237
  93.5 1.8 %collective-permute-start.21 = (bf16[64,2048]{1,0:T(8,128)(2,1)S(1)}, bf16[64,2048]{1,0:T(8,128)(2,1)S(1)}, u32[]{:S(2)}, u32[]{:S(2)}) collective-permute-start(bf16[64,2048]{1,0:T(8,128)(2,1)S(1)} %collective-permute-done.19.refs_0_.refs_1_), channel_id=1, source_target_pairs={{0,16},{1,9},{2,18},{3,11},{4,20},{5,13},{6,22},{7,15},{8,24},{9,1... | collective-permute-start | bytes 786440 | tf_op jit(solution)/shard_map/ppermute | solution.py:237
  95.5 6.2 %down.2 = (f32[4,32,2048]{2,1,0:T(8,128)S(1)}, bf16[4,32,2048]{2,1,0:T(8,128)(2,1)S(1)}) custom-call(s32[9]{0:T(128)S(1)} %stack.33.place_ref, bf16[64,2048]{1,0:T(8,128)(2,1)S(1)} %hidden.2.refs_0_, bf16[64,2048]{1,0:T(8,128)(2,1)S(1)} %collective-permute-done.16.refs_1_, bf16[64,2048]{1,0:T(8,128)(2,1)S(1)} %collective-permute-done.17.refs_2_, ...), custom_call_target="tpu_custom_call" | custom-call | flops 2147483648 | bytes 8388608 | tf_op jit(solution)/shard_map/down/pallas_call | solution.py:173
  101.9 1.9 %collective-permute-done.22 = bf16[4,32,2048]{2,1,0:T(8,128)(2,1)S(1)} collective-permute-done((bf16[4,32,2048]{2,1,0:T(8,128)(2,1)S(1)}, bf16[4,32,2048]{2,1,0:T(8,128)(2,1)S(1)}, u32[]{:S(2)}, u32[]{:S(2)}) %collective-permute-start.22) | collective-permute-done | bytes 524320 | tf_op jit(solution)/shard_map/ppermute | solution.py:237
  103.9 2.9 %collective-permute-start.24 = (bf16[32,2048]{1,0:T(8,128)(2,1)S(1)}, bf16[32,2048]{1,0:T(8,128)(2,1)S(1)}, u32[]{:S(2)}, u32[]{:S(2)}) collective-permute-start(bf16[32,2048]{1,0:T(8,128)(2,1)S(1)} %get-tuple-element.38), channel_id=1, source_target_pairs={{0,4},{1,5},{2,6},{3,7},{4,0},{5,1},{6,2},{7,3},{8,12},{9,13},{10,... | collective-permute-start | bytes 393224 | tf_op jit(solution)/shard_map/ppermute | solution.py:237
  106.8 1.5 %collective-permute-start.23 = (bf16[32,2048]{1,0:T(8,128)(2,1)S(1)}, bf16[32,2048]{1,0:T(8,128)(2,1)S(1)}, u32[]{:S(2)}, u32[]{:S(2)}) collective-permute-start(bf16[32,2048]{1,0:T(8,128)(2,1)S(1)} %get-tuple-element.39), channel_id=1, source_target_pairs={{0,2},{1,3},{2,0},{3,1},{4,6},{5,7},{6,4},{7,5},{8,10},{9,11},{10,... | collective-permute-start | bytes 393224 | tf_op jit(solution)/shard_map/ppermute | solution.py:237
  108.3 6.2 %down.3 = (f32[4,32,2048]{2,1,0:T(8,128)S(1)}, bf16[4,32,2048]{2,1,0:T(8,128)(2,1)S(1)}) custom-call(s32[9]{0:T(128)S(1)} %stack.33.place_ref, bf16[64,2048]{1,0:T(8,128)(2,1)S(1)} %hidden.3.refs_0_, bf16[64,2048]{1,0:T(8,128)(2,1)S(1)} %collective-permute-done.19.refs_0_.refs_1_, bf16[64,2048]{1,0:T(8,128)(2,1)S(1)} %collective-permute-done.20.refs_1_.refs_2_, ...), custom_call_target="tpu_custom_call" | custom-call | flops 2147483648 | bytes 8388608 | tf_op jit(solution)/shard_map/down/pallas_call | solution.py:173
  114.7 2.4 %collective-permute-start.25 = (bf16[32,2048]{1,0:T(8,128)(2,1)S(1)}, bf16[32,2048]{1,0:T(8,128)(2,1)S(1)}, u32[]{:S(2)}, u32[]{:S(2)}) collective-permute-start(bf16[32,2048]{1,0:T(8,128)(2,1)S(1)} %get-tuple-element.37), channel_id=1, source_target_pairs={{0,6},{1,7},{2,4},{3,5},{4,2},{5,3},{6,0},{7,1},{8,14},{9,15},{10,... | collective-permute-start | bytes 393224 | tf_op jit(solution)/shard_map/ppermute | solution.py:237
  117.2 0.1 collective-permute-start.27
  117.4 1.8 %collective-permute-start.29 = (bf16[32,2048]{1,0:T(8,128)(2,1)S(1)}, bf16[32,2048]{1,0:T(8,128)(2,1)S(1)}, u32[]{:S(2)}, u32[]{:S(2)}) collective-permute-start(bf16[32,2048]{1,0:T(8,128)(2,1)S(1)} %get-tuple-element.41), channel_id=1, source_target_pairs={{0,6},{1,7},{2,4},{3,5},{4,2},{5,3},{6,0},{7,1},{8,14},{9,15},{10,... | collective-permute-start | bytes 393224 | tf_op jit(solution)/shard_map/ppermute | solution.py:237
  119.2 1.6 %collective-permute-start.28 = (bf16[32,2048]{1,0:T(8,128)(2,1)S(1)}, bf16[32,2048]{1,0:T(8,128)(2,1)S(1)}, u32[]{:S(2)}, u32[]{:S(2)}) collective-permute-start(bf16[32,2048]{1,0:T(8,128)(2,1)S(1)} %get-tuple-element.42), channel_id=1, source_target_pairs={{0,4},{1,5},{2,6},{3,7},{4,0},{5,1},{6,2},{7,3},{8,12},{9,13},{10,... | collective-permute-start | bytes 393224 | tf_op jit(solution)/shard_map/ppermute | solution.py:237
  120.8 2.1 %collective-permute-done.25 = bf16[32,2048]{1,0:T(8,128)(2,1)S(1)} collective-permute-done((bf16[32,2048]{1,0:T(8,128)(2,1)S(1)}, bf16[32,2048]{1,0:T(8,128)(2,1)S(1)}, u32[]{:S(2)}, u32[]{:S(2)}) %collective-permute-start.25) | collective-permute-done | bytes 131104 | tf_op jit(solution)/shard_map/ppermute | solution.py:237
  123.0 2.8 %collective-permute-done.27 = bf16[32,2048]{1,0:T(8,128)(2,1)S(1)} collective-permute-done((bf16[32,2048]{1,0:T(8,128)(2,1)S(1)}, bf16[32,2048]{1,0:T(8,128)(2,1)S(1)}, u32[]{:S(2)}, u32[]{:S(2)}) %collective-permute-start.27) | collective-permute-done | bytes 131104 | tf_op jit(solution)/shard_map/ppermute | solution.py:237
  125.8 2.8 %collective-permute-done.29 = bf16[32,2048]{1,0:T(8,128)(2,1)S(1)} collective-permute-done((bf16[32,2048]{1,0:T(8,128)(2,1)S(1)}, bf16[32,2048]{1,0:T(8,128)(2,1)S(1)}, u32[]{:S(2)}, u32[]{:S(2)}) %collective-permute-start.29) | collective-permute-done | bytes 131104 | tf_op jit(solution)/shard_map/ppermute | solution.py:237
  128.6 6.1 %collective-permute-done.28 = bf16[32,2048]{1,0:T(8,128)(2,1)S(1)} collective-permute-done((bf16[32,2048]{1,0:T(8,128)(2,1)S(1)}, bf16[32,2048]{1,0:T(8,128)(2,1)S(1)}, u32[]{:S(2)}, u32[]{:S(2)}) %collective-permute-start.28) | collective-permute-done | bytes 131104 | tf_op jit(solution)/shard_map/ppermute | solution.py:237
  134.8 0.7 pad_maximum_fusion
  (38 shorter events, 1.4 us)
Async XLA Ops:
  0.0 13.1 %collective-permute-start.1 = (bf16[128,1024]{1,0:T(8,128)(2,1)}, bf16[128,1024]{1,0:T(8,128)(2,1)S(1)}, u32[]{:S(2)}, u32[]{:S(2)}) collective-permute-start(bf16[128,1024]{1,0:T(8,128)(2,1)} %param.7), channel_id=1, source_target_pairs={{0,2},{1,3},{2,10},{3,11},{4,18},{5,19},{6,26},{7,27},{8,0},{9,1},... | collective-permute-start | bytes 786440 | tf_op jit(solution)/shard_map/ppermute | solution.py:237
  3.0 10.2 %collective-permute-start = (bf16[128,1024]{1,0:T(8,128)(2,1)}, bf16[128,1024]{1,0:T(8,128)(2,1)S(1)}, u32[]{:S(2)}, u32[]{:S(2)}) collective-permute-start(bf16[128,1024]{1,0:T(8,128)(2,1)} %param.7), channel_id=1, source_target_pairs={{0,0},{1,1},{2,8},{3,9},{4,16},{5,17},{6,24},{7,25},{8,2},{9,3},{1... | collective-permute-start | bytes 786440 | tf_op jit(solution)/shard_map/ppermute | solution.py:237
  4.6 15.8 %collective-permute-start.3 = (bf16[128,1024]{1,0:T(8,128)(2,1)}, bf16[128,1024]{1,0:T(8,128)(2,1)S(1)}, u32[]{:S(2)}, u32[]{:S(2)}) collective-permute-start(bf16[128,1024]{1,0:T(8,128)(2,1)} %param.7), channel_id=1, source_target_pairs={{0,6},{1,7},{2,14},{3,15},{4,22},{5,23},{6,30},{7,31},{8,4},{9,5},... | collective-permute-start | bytes 786440 | tf_op jit(solution)/shard_map/ppermute | solution.py:237
  11.6 12.7 %collective-permute-start.2 = (bf16[128,1024]{1,0:T(8,128)(2,1)}, bf16[128,1024]{1,0:T(8,128)(2,1)S(1)}, u32[]{:S(2)}, u32[]{:S(2)}) collective-permute-start(bf16[128,1024]{1,0:T(8,128)(2,1)} %param.7), channel_id=1, source_target_pairs={{0,4},{1,5},{2,12},{3,13},{4,20},{5,21},{6,28},{7,29},{8,6},{9,7},... | collective-permute-start | bytes 786440 | tf_op jit(solution)/shard_map/ppermute | solution.py:237
  13.1 11.5 %collective-permute-start.5 = (bf16[128,1024]{1,0:T(8,128)(2,1)S(1)}, bf16[128,1024]{1,0:T(8,128)(2,1)S(1)}, u32[]{:S(2)}, u32[]{:S(2)}) collective-permute-start(bf16[128,1024]{1,0:T(8,128)(2,1)S(1)} %collective-permute-done.1.refs_1_), channel_id=1, source_target_pairs={{0,1},{1,0},{2,3},{3,2},{4,5},{5,4},{6,7},{7,6},{8,9},{9,8},{10,11... | collective-permute-start | bytes 786440 | tf_op jit(solution)/shard_map/ppermute | solution.py:237
  13.2 11.4 %collective-permute-start.4 = (bf16[128,1024]{1,0:T(8,128)(2,1)S(1)}, bf16[128,1024]{1,0:T(8,128)(2,1)S(1)}, u32[]{:S(2)}, u32[]{:S(2)}) collective-permute-start(bf16[128,1024]{1,0:T(8,128)(2,1)S(1)} %collective-permute-done.refs_0_), channel_id=1, source_target_pairs={{0,1},{1,0},{2,3},{3,2},{4,5},{5,4},{6,7},{7,6},{8,9},{9,8},{10,11... | collective-permute-start | bytes 786440 | tf_op jit(solution)/shard_map/ppermute | solution.py:237
  20.4 4.2 %collective-permute-start.7 = (bf16[128,1024]{1,0:T(8,128)(2,1)S(1)}, bf16[128,1024]{1,0:T(8,128)(2,1)S(1)}, u32[]{:S(2)}, u32[]{:S(2)}) collective-permute-start(bf16[128,1024]{1,0:T(8,128)(2,1)S(1)} %collective-permute-done.3.refs_3_), channel_id=1, source_target_pairs={{0,1},{1,0},{2,3},{3,2},{4,5},{5,4},{6,7},{7,6},{8,9},{9,8},{10,11... | collective-permute-start | bytes 786440 | tf_op jit(solution)/shard_map/ppermute | solution.py:237
  24.3 1.5 %collective-permute-start.6 = (bf16[128,1024]{1,0:T(8,128)(2,1)S(1)}, bf16[128,1024]{1,0:T(8,128)(2,1)S(1)}, u32[]{:S(2)}, u32[]{:S(2)}) collective-permute-start(bf16[128,1024]{1,0:T(8,128)(2,1)S(1)} %collective-permute-done.2.refs_2_), channel_id=1, source_target_pairs={{0,1},{1,0},{2,3},{3,2},{4,5},{5,4},{6,7},{7,6},{8,9},{9,8},{10,11... | collective-permute-start | bytes 786440 | tf_op jit(solution)/shard_map/ppermute | solution.py:237
  33.7 20.0 %collective-permute-start.9 = (bf16[2,128,1024]{2,1,0:T(8,128)(2,1)S(1)}, bf16[2,128,1024]{2,1,0:T(8,128)(2,1)S(1)}, u32[]{:S(2)}, u32[]{:S(2)}) collective-permute-start(bf16[2,128,1024]{2,1,0:T(8,128)(2,1)S(1)} %get-tuple-element.24), channel_id=1, source_target_pairs={{0,8},{1,9},{2,10},{3,11},{4,12},{5,13},{6,14},{7,15},{8,0},{9,1},... | collective-permute-start | bytes 1572872 | tf_op jit(solution)/shard_map/ppermute | solution.py:237
  36.0 20.4 %collective-permute-start.8 = (bf16[2,128,1024]{2,1,0:T(8,128)(2,1)S(1)}, bf16[2,128,1024]{2,1,0:T(8,128)(2,1)S(1)}, u32[]{:S(2)}, u32[]{:S(2)}) collective-permute-start(bf16[2,128,1024]{2,1,0:T(8,128)(2,1)S(1)} %get-tuple-element.22.refs_12_), channel_id=1, source_target_pairs={{0,16},{1,17},{2,18},{3,19},{4,20},{5,21},{6,22},{7,23},{8,24},{9,... | collective-permute-start | bytes 1572872 | tf_op jit(solution)/shard_map/ppermute | solution.py:237
  51.7 14.9 %collective-permute-start.13 = (bf16[2,128,1024]{2,1,0:T(8,128)(2,1)S(1)}, bf16[2,128,1024]{2,1,0:T(8,128)(2,1)S(1)}, u32[]{:S(2)}, u32[]{:S(2)}) collective-permute-start(bf16[2,128,1024]{2,1,0:T(8,128)(2,1)S(1)} %get-tuple-element.30), channel_id=1, source_target_pairs={{0,8},{1,9},{2,10},{3,11},{4,12},{5,13},{6,14},{7,15},{8,0},{9,1},... | collective-permute-start | bytes 1572872 | tf_op jit(solution)/shard_map/ppermute | solution.py:237
  53.7 14.9 %collective-permute-start.12 = (bf16[2,128,1024]{2,1,0:T(8,128)(2,1)S(1)}, bf16[2,128,1024]{2,1,0:T(8,128)(2,1)S(1)}, u32[]{:S(2)}, u32[]{:S(2)}) collective-permute-start(bf16[2,128,1024]{2,1,0:T(8,128)(2,1)S(1)} %get-tuple-element.25.refs_4_), channel_id=1, source_target_pairs={{0,16},{1,17},{2,18},{3,19},{4,20},{5,21},{6,22},{7,23},{8,24},{9,... | collective-permute-start | bytes 1572872 | tf_op jit(solution)/shard_map/ppermute | solution.py:237
  56.5 17.7 %collective-permute-start.11 = (bf16[1,128,1024]{2,1,0:T(8,128)(2,1)S(1)}, bf16[1,128,1024]{2,1,0:T(8,128)(2,1)S(1)}, u32[]{:S(2)}, u32[]{:S(2)}) collective-permute-start(bf16[1,128,1024]{2,1,0:T(8,128)(2,1)S(1)} %get-tuple-element.27), channel_id=1, source_target_pairs={{0,16},{1,17},{2,18},{3,19},{4,20},{5,21},{6,22},{7,23},{8,24},{9,... | collective-permute-start | bytes 786440 | tf_op jit(solution)/shard_map/ppermute | solution.py:237
  58.7 15.4 %collective-permute-start.10 = (bf16[1,128,1024]{2,1,0:T(8,128)(2,1)S(1)}, bf16[1,128,1024]{2,1,0:T(8,128)(2,1)S(1)}, u32[]{:S(2)}, u32[]{:S(2)}) collective-permute-start(bf16[1,128,1024]{2,1,0:T(8,128)(2,1)S(1)} %get-tuple-element.26.refs_4_), channel_id=1, source_target_pairs={{0,8},{1,9},{2,10},{3,11},{4,12},{5,13},{6,14},{7,15},{8,0},{9,1},... | collective-permute-start | bytes 786440 | tf_op jit(solution)/shard_map/ppermute | solution.py:237
  68.6 26.7 %copy-start = (s32[16,16]{1,0:T(8,128)S(1)}, s32[16,16]{1,0:T(8,128)}, u32[]{:S(2)}) copy-start(s32[16,16]{1,0:T(8,128)} %param.13) | copy-start | bytes 3076
  68.6 8.0 %collective-permute-start.14 = (bf16[1,128,1024]{2,1,0:T(8,128)(2,1)S(1)}, bf16[1,128,1024]{2,1,0:T(8,128)(2,1)S(1)}, u32[]{:S(2)}, u32[]{:S(2)}) collective-permute-start(bf16[1,128,1024]{2,1,0:T(8,128)(2,1)S(1)} %get-tuple-element.31), channel_id=1, source_target_pairs={{0,8},{1,9},{2,10},{3,11},{4,12},{5,13},{6,14},{7,15},{8,0},{9,1},... | collective-permute-start | bytes 786440 | tf_op jit(solution)/shard_map/ppermute | solution.py:237
  69.9 8.6 %collective-permute-start.15 = (bf16[1,128,1024]{2,1,0:T(8,128)(2,1)S(1)}, bf16[1,128,1024]{2,1,0:T(8,128)(2,1)S(1)}, u32[]{:S(2)}, u32[]{:S(2)}) collective-permute-start(bf16[1,128,1024]{2,1,0:T(8,128)(2,1)S(1)} %get-tuple-element.32), channel_id=1, source_target_pairs={{0,16},{1,17},{2,18},{3,19},{4,20},{5,21},{6,22},{7,23},{8,24},{9,... | collective-permute-start | bytes 786440 | tf_op jit(solution)/shard_map/ppermute | solution.py:237
  78.8 9.1 %collective-permute-start.16 = (bf16[64,2048]{1,0:T(8,128)(2,1)S(1)}, bf16[64,2048]{1,0:T(8,128)(2,1)S(1)}, u32[]{:S(2)}, u32[]{:S(2)}) collective-permute-start(bf16[64,2048]{1,0:T(8,128)(2,1)S(1)} %hidden.2.refs_0_), channel_id=1, source_target_pairs={{0,8},{1,17},{2,10},{3,19},{4,12},{5,21},{6,14},{7,23},{8,0},{9,25... | collective-permute-start | bytes 786440 | tf_op jit(solution)/shard_map/ppermute | solution.py:237
  80.8 12.7 %collective-permute-start.19 = (bf16[64,2048]{1,0:T(8,128)(2,1)S(1)}, bf16[64,2048]{1,0:T(8,128)(2,1)S(1)}, u32[]{:S(2)}, u32[]{:S(2)}) collective-permute-start(bf16[64,2048]{1,0:T(8,128)(2,1)S(1)} %hidden.3.refs_0_), channel_id=1, source_target_pairs={{0,8},{1,17},{2,10},{3,19},{4,12},{5,21},{6,14},{7,23},{8,0},{9,25... | collective-permute-start | bytes 786440 | tf_op jit(solution)/shard_map/ppermute | solution.py:237
  81.2 14.3 %collective-permute-start.17 = (bf16[64,2048]{1,0:T(8,128)(2,1)S(1)}, bf16[64,2048]{1,0:T(8,128)(2,1)S(1)}, u32[]{:S(2)}, u32[]{:S(2)}) collective-permute-start(bf16[64,2048]{1,0:T(8,128)(2,1)S(1)} %hidden.2.refs_0_), channel_id=1, source_target_pairs={{0,16},{1,9},{2,18},{3,11},{4,20},{5,13},{6,22},{7,15},{8,24},{9,1... | collective-permute-start | bytes 786440 | tf_op jit(solution)/shard_map/ppermute | solution.py:237
  87.9 7.6 %collective-permute-start.18 = (bf16[64,2048]{1,0:T(8,128)(2,1)S(1)}, bf16[64,2048]{1,0:T(8,128)(2,1)S(1)}, u32[]{:S(2)}, u32[]{:S(2)}) collective-permute-start(bf16[64,2048]{1,0:T(8,128)(2,1)S(1)} %collective-permute-done.16.refs_1_), channel_id=1, source_target_pairs={{0,16},{1,9},{2,18},{3,11},{4,20},{5,13},{6,22},{7,15},{8,24},{9,1... | collective-permute-start | bytes 786440 | tf_op jit(solution)/shard_map/ppermute | solution.py:237
  89.7 12.1 %collective-permute-start.20 = (bf16[64,2048]{1,0:T(8,128)(2,1)S(1)}, bf16[64,2048]{1,0:T(8,128)(2,1)S(1)}, u32[]{:S(2)}, u32[]{:S(2)}) collective-permute-start(bf16[64,2048]{1,0:T(8,128)(2,1)S(1)} %hidden.3.refs_0_), channel_id=1, source_target_pairs={{0,16},{1,9},{2,18},{3,11},{4,20},{5,13},{6,22},{7,15},{8,24},{9,1... | collective-permute-start | bytes 786440 | tf_op jit(solution)/shard_map/ppermute | solution.py:237
  93.5 8.3 %collective-permute-start.21 = (bf16[64,2048]{1,0:T(8,128)(2,1)S(1)}, bf16[64,2048]{1,0:T(8,128)(2,1)S(1)}, u32[]{:S(2)}, u32[]{:S(2)}) collective-permute-start(bf16[64,2048]{1,0:T(8,128)(2,1)S(1)} %collective-permute-done.19.refs_0_.refs_1_), channel_id=1, source_target_pairs={{0,16},{1,9},{2,18},{3,11},{4,20},{5,13},{6,22},{7,15},{8,24},{9,1... | collective-permute-start | bytes 786440 | tf_op jit(solution)/shard_map/ppermute | solution.py:237
  101.8 2.0 %collective-permute-start.22 = (bf16[4,32,2048]{2,1,0:T(8,128)(2,1)S(1)}, bf16[4,32,2048]{2,1,0:T(8,128)(2,1)S(1)}, u32[]{:S(2)}, u32[]{:S(2)}) collective-permute-start(bf16[4,32,2048]{2,1,0:T(8,128)(2,1)S(1)} %hold.2), channel_id=1, source_target_pairs={{0,1},{1,0},{2,3},{3,2},{4,5},{5,4},{6,7},{7,6},{8,9},{9,8},{10,11... | collective-permute-start | bytes 1572872 | tf_op jit(solution)/shard_map/ppermute | solution.py:237
  103.9 10.7 %collective-permute-start.24 = (bf16[32,2048]{1,0:T(8,128)(2,1)S(1)}, bf16[32,2048]{1,0:T(8,128)(2,1)S(1)}, u32[]{:S(2)}, u32[]{:S(2)}) collective-permute-start(bf16[32,2048]{1,0:T(8,128)(2,1)S(1)} %get-tuple-element.38), channel_id=1, source_target_pairs={{0,4},{1,5},{2,6},{3,7},{4,0},{5,1},{6,2},{7,3},{8,12},{9,13},{10,... | collective-permute-start | bytes 393224 | tf_op jit(solution)/shard_map/ppermute | solution.py:237
  106.8 7.8 %collective-permute-start.23 = (bf16[32,2048]{1,0:T(8,128)(2,1)S(1)}, bf16[32,2048]{1,0:T(8,128)(2,1)S(1)}, u32[]{:S(2)}, u32[]{:S(2)}) collective-permute-start(bf16[32,2048]{1,0:T(8,128)(2,1)S(1)} %get-tuple-element.39), channel_id=1, source_target_pairs={{0,2},{1,3},{2,0},{3,1},{4,6},{5,7},{6,4},{7,5},{8,10},{9,11},{10,... | collective-permute-start | bytes 393224 | tf_op jit(solution)/shard_map/ppermute | solution.py:237
  114.6 2.5 %collective-permute-start.26 = (bf16[4,32,2048]{2,1,0:T(8,128)(2,1)S(1)}, bf16[4,32,2048]{2,1,0:T(8,128)(2,1)S(1)}, u32[]{:S(2)}, u32[]{:S(2)}) collective-permute-start(bf16[4,32,2048]{2,1,0:T(8,128)(2,1)S(1)} %hold.3), channel_id=1, source_target_pairs={{0,1},{1,0},{2,3},{3,2},{4,5},{5,4},{6,7},{7,6},{8,9},{9,8},{10,11... | collective-permute-start | bytes 1572872 | tf_op jit(solution)/shard_map/ppermute | solution.py:237
  114.7 8.2 %collective-permute-start.25 = (bf16[32,2048]{1,0:T(8,128)(2,1)S(1)}, bf16[32,2048]{1,0:T(8,128)(2,1)S(1)}, u32[]{:S(2)}, u32[]{:S(2)}) collective-permute-start(bf16[32,2048]{1,0:T(8,128)(2,1)S(1)} %get-tuple-element.37), channel_id=1, source_target_pairs={{0,6},{1,7},{2,4},{3,5},{4,2},{5,3},{6,0},{7,1},{8,14},{9,15},{10,... | collective-permute-start | bytes 393224 | tf_op jit(solution)/shard_map/ppermute | solution.py:237
  117.2 8.6 %collective-permute-start.27 = (bf16[32,2048]{1,0:T(8,128)(2,1)S(1)}, bf16[32,2048]{1,0:T(8,128)(2,1)S(1)}, u32[]{:S(2)}, u32[]{:S(2)}) collective-permute-start(bf16[32,2048]{1,0:T(8,128)(2,1)S(1)} %get-tuple-element.40), channel_id=1, source_target_pairs={{0,2},{1,3},{2,0},{3,1},{4,6},{5,7},{6,4},{7,5},{8,10},{9,11},{10,... | collective-permute-start | bytes 393224 | tf_op jit(solution)/shard_map/ppermute | solution.py:237
  117.4 11.3 %collective-permute-start.29 = (bf16[32,2048]{1,0:T(8,128)(2,1)S(1)}, bf16[32,2048]{1,0:T(8,128)(2,1)S(1)}, u32[]{:S(2)}, u32[]{:S(2)}) collective-permute-start(bf16[32,2048]{1,0:T(8,128)(2,1)S(1)} %get-tuple-element.41), channel_id=1, source_target_pairs={{0,6},{1,7},{2,4},{3,5},{4,2},{5,3},{6,0},{7,1},{8,14},{9,15},{10,... | collective-permute-start | bytes 393224 | tf_op jit(solution)/shard_map/ppermute | solution.py:237
  119.2 15.5 %collective-permute-start.28 = (bf16[32,2048]{1,0:T(8,128)(2,1)S(1)}, bf16[32,2048]{1,0:T(8,128)(2,1)S(1)}, u32[]{:S(2)}, u32[]{:S(2)}) collective-permute-start(bf16[32,2048]{1,0:T(8,128)(2,1)S(1)} %get-tuple-element.42), channel_id=1, source_target_pairs={{0,4},{1,5},{2,6},{3,7},{4,0},{5,1},{6,2},{7,3},{8,12},{9,13},{10,... | collective-permute-start | bytes 393224 | tf_op jit(solution)/shard_map/ppermute | solution.py:237

commit v14 on v13

--- a/solution.py
+++ b/solution.py
@@ -290,7 +290,7 @@
         for later in hidden[s + 1 : s + 2]:
             beside = beside + later[1:]
         mine, theirs = down(place, parts, down_weight, down_wide, ())
-        total, sent = combine(mine, hold(theirs, beside[:2] if s else beside))
+        total, sent = combine(mine, hold(theirs, beside[1:2] if s else beside))
         beside = [across_z(sent[j - 1], j) for j in range(1, n_z)]
         for part in beside:
             total += part.astype(jnp.float32)

time: 136 us -> 137 us (level)
  transfers between devices with their start and end apart: 30 -> 30, of which waited for: 16 -> 17; matrix products, arithmetic and copies ran while one was open for 2% -> 1% of each run, Pallas kernels for 15% -> 15%
where the time goes in v14:
time: 137 us; the launch traced here: 136 us
  waiting for transfers between devices  54.3 us (40%)
  starting transfers between devices  49.8 us (36%)
  Pallas kernels  29 us (21%)
  other arithmetic  2.43 us (2%)
    ppermute x30, waiting for transfers between devices, send(): return lax.ppermute(value, AXES, perm)  54.3 us
    ppermute x30, starting transfers between devices, send(): return lax.ppermute(value, AXES, perm)  49.8 us
    pallas_call x2, Pallas kernels, project(): pl.pallas_call(functools.partial(project_kernel, n), grid_spec=pltpu.Pref...  15.7 us
    pallas_call x2, Pallas kernels, down(): pl.pallas_call(functools.partial(down_kernel, n), grid_spec=pltpu.Prefetc...  12.5 us
  transfers between devices with their start and end apart: 30, of which 17 were waited for; matrix products, arithmetic and copies ran while one was open for 1% of the time, Pallas kernels for 15%

profile of v14, /device:TPU:0, one launch (start us, length us, event | category | flops | bytes accessed | tf_op | source)
XLA Modules:
  0.0 136.3 jit_solution(8303951518369380912)
XLA Ops:
  0.0 3.0 %collective-permute-start.1 = (bf16[128,1024]{1,0:T(8,128)(2,1)}, bf16[128,1024]{1,0:T(8,128)(2,1)S(1)}, u32[]{:S(2)}, u32[]{:S(2)}) collective-permute-start(bf16[128,1024]{1,0:T(8,128)(2,1)} %param.7), channel_id=1, source_target_pairs={{0,2},{1,3},{2,10},{3,11},{4,18},{5,19},{6,26},{7,27},{8,0},{9,1},... | collective-permute-start | bytes 786440 | tf_op jit(solution)/shard_map/ppermute | solution.py:237
  3.0 1.6 %collective-permute-start = (bf16[128,1024]{1,0:T(8,128)(2,1)}, bf16[128,1024]{1,0:T(8,128)(2,1)S(1)}, u32[]{:S(2)}, u32[]{:S(2)}) collective-permute-start(bf16[128,1024]{1,0:T(8,128)(2,1)} %param.7), channel_id=1, source_target_pairs={{0,0},{1,1},{2,8},{3,9},{4,16},{5,17},{6,24},{7,25},{8,2},{9,3},{1... | collective-permute-start | bytes 786440 | tf_op jit(solution)/shard_map/ppermute | solution.py:237
  4.6 7.0 %collective-permute-start.3 = (bf16[128,1024]{1,0:T(8,128)(2,1)}, bf16[128,1024]{1,0:T(8,128)(2,1)S(1)}, u32[]{:S(2)}, u32[]{:S(2)}) collective-permute-start(bf16[128,1024]{1,0:T(8,128)(2,1)} %param.7), channel_id=1, source_target_pairs={{0,6},{1,7},{2,14},{3,15},{4,22},{5,23},{6,30},{7,31},{8,4},{9,5},... | collective-permute-start | bytes 786440 | tf_op jit(solution)/shard_map/ppermute | solution.py:237
  11.6 0.7 convert_element_type.101
  12.3 0.7 convert_element_type.102
  13.2 0.5 collective-permute-start.4
  13.7 6.7 %collective-permute-done.3.refs_3_ = bf16[128,1024]{1,0:T(8,128)(2,1)S(1)} collective-permute-done((bf16[128,1024]{1,0:T(8,128)(2,1)}, bf16[128,1024]{1,0:T(8,128)(2,1)S(1)}, u32[]{:S(2)}, u32[]{:S(2)}) %collective-permute-start.3) | collective-permute-done | bytes 262176 | tf_op jit(solution)/shard_map/ppermute | solution.py:237
  20.4 3.9 %collective-permute-done.2.refs_2_ = bf16[128,1024]{1,0:T(8,128)(2,1)S(1)} collective-permute-done((bf16[128,1024]{1,0:T(8,128)(2,1)}, bf16[128,1024]{1,0:T(8,128)(2,1)S(1)}, u32[]{:S(2)}, u32[]{:S(2)}) %collective-permute-start.2) | collective-permute-done | bytes 262176 | tf_op jit(solution)/shard_map/ppermute | solution.py:237
  24.6 1.2 collective-permute-done.6.refs_6_
  25.8 7.9 %project.2 = (f32[2,128,1024]{2,1,0:T(8,128)S(1)}, f32[2,128,1024]{2,1,0:T(8,128)S(1)}, bf16[2,128,1024]{2,1,0:T(8,128)(2,1)S(1)}, bf16[2,128,1024]{2,1,0:T(8,128)(2,1)S(1)}) custom-call(s32[9]{0:T(128)S(1)} %stack.33.place_ref, bf16[128,1024]{1,0:T(8,128)(2,1)S(1)} %collective-permute-done.refs_0_, bf16[128,1024]{1,0:T(8,128)(2,1)S(1)} %collective-permute-done.1.refs_1_, ...), custom_call_target="tpu_custom_call" | custom-call | flops 4294967296 | bytes 8388608 | tf_op jit(solution)/shard_map/project/pallas_call | solution.py:68
  33.7 2.3 %collective-permute-start.9 = (bf16[2,128,1024]{2,1,0:T(8,128)(2,1)S(1)}, bf16[2,128,1024]{2,1,0:T(8,128)(2,1)S(1)}, u32[]{:S(2)}, u32[]{:S(2)}) collective-permute-start(bf16[2,128,1024]{2,1,0:T(8,128)(2,1)S(1)} %get-tuple-element.24), channel_id=1, source_target_pairs={{0,8},{1,9},{2,10},{3,11},{4,12},{5,13},{6,14},{7,15},{8,0},{9,1},... | collective-permute-start | bytes 1572872 | tf_op jit(solution)/shard_map/ppermute | solution.py:237
  36.0 7.8 %collective-permute-start.8 = (bf16[2,128,1024]{2,1,0:T(8,128)(2,1)S(1)}, bf16[2,128,1024]{2,1,0:T(8,128)(2,1)S(1)}, u32[]{:S(2)}, u32[]{:S(2)}) collective-permute-start(bf16[2,128,1024]{2,1,0:T(8,128)(2,1)S(1)} %get-tuple-element.22.refs_12_), channel_id=1, source_target_pairs={{0,16},{1,17},{2,18},{3,19},{4,20},{5,21},{6,22},{7,23},{8,24},{9,... | collective-permute-start | bytes 1572872 | tf_op jit(solution)/shard_map/ppermute | solution.py:237
  43.8 7.9 %project.3 = (f32[2,128,1024]{2,1,0:T(8,128)S(1)}, f32[2,128,1024]{2,1,0:T(8,128)S(1)}, bf16[2,128,1024]{2,1,0:T(8,128)(2,1)S(1)}, bf16[2,128,1024]{2,1,0:T(8,128)(2,1)S(1)}) custom-call(s32[9]{0:T(128)S(1)} %stack.33.place_ref, bf16[128,1024]{1,0:T(8,128)(2,1)S(1)} %collective-permute-done.refs_0_, bf16[128,1024]{1,0:T(8,128)(2,1)S(1)} %collective-permute-done.1.refs_1_, ...), custom_call_target="tpu_custom_call" | custom-call | flops 4294967296 | bytes 8388608 | tf_op jit(solution)/shard_map/project/pallas_call | solution.py:68
  51.7 2.0 %collective-permute-start.13 = (bf16[2,128,1024]{2,1,0:T(8,128)(2,1)S(1)}, bf16[2,128,1024]{2,1,0:T(8,128)(2,1)S(1)}, u32[]{:S(2)}, u32[]{:S(2)}) collective-permute-start(bf16[2,128,1024]{2,1,0:T(8,128)(2,1)S(1)} %get-tuple-element.30), channel_id=1, source_target_pairs={{0,8},{1,9},{2,10},{3,11},{4,12},{5,13},{6,14},{7,15},{8,0},{9,1},... | collective-permute-start | bytes 1572872 | tf_op jit(solution)/shard_map/ppermute | solution.py:237
  53.7 2.7 %collective-permute-done.8.refs_1_ = bf16[2,128,1024]{2,1,0:T(8,128)(2,1)S(1)} collective-permute-done((bf16[2,128,1024]{2,1,0:T(8,128)(2,1)S(1)}, bf16[2,128,1024]{2,1,0:T(8,128)(2,1)S(1)}, u32[]{:S(2)}, u32[]{:S(2)}) %collective-permute-start.8) | collective-permute-done | bytes 524320 | tf_op jit(solution)/shard_map/ppermute | solution.py:237
  56.5 2.2 %collective-permute-start.11 = (bf16[1,128,1024]{2,1,0:T(8,128)(2,1)S(1)}, bf16[1,128,1024]{2,1,0:T(8,128)(2,1)S(1)}, u32[]{:S(2)}, u32[]{:S(2)}) collective-permute-start(bf16[1,128,1024]{2,1,0:T(8,128)(2,1)S(1)} %get-tuple-element.27), channel_id=1, source_target_pairs={{0,16},{1,17},{2,18},{3,19},{4,20},{5,21},{6,22},{7,23},{8,24},{9,... | collective-permute-start | bytes 786440 | tf_op jit(solution)/shard_map/ppermute | solution.py:237
  58.7 2.0 %collective-permute-start.10 = (bf16[1,128,1024]{2,1,0:T(8,128)(2,1)S(1)}, bf16[1,128,1024]{2,1,0:T(8,128)(2,1)S(1)}, u32[]{:S(2)}, u32[]{:S(2)}) collective-permute-start(bf16[1,128,1024]{2,1,0:T(8,128)(2,1)S(1)} %get-tuple-element.26.refs_4_), channel_id=1, source_target_pairs={{0,8},{1,9},{2,10},{3,11},{4,12},{5,13},{6,14},{7,15},{8,0},{9,1},... | collective-permute-start | bytes 786440 | tf_op jit(solution)/shard_map/ppermute | solution.py:237
  60.7 5.8 %collective-permute-done.13.refs_3_ = bf16[2,128,1024]{2,1,0:T(8,128)(2,1)S(1)} collective-permute-done((bf16[2,128,1024]{2,1,0:T(8,128)(2,1)S(1)}, bf16[2,128,1024]{2,1,0:T(8,128)(2,1)S(1)}, u32[]{:S(2)}, u32[]{:S(2)}) %collective-permute-start.13) | collective-permute-done | bytes 524320 | tf_op jit(solution)/shard_map/ppermute | solution.py:237
  66.5 2.0 %collective-permute-done.12.refs_1_ = bf16[2,128,1024]{2,1,0:T(8,128)(2,1)S(1)} collective-permute-done((bf16[2,128,1024]{2,1,0:T(8,128)(2,1)S(1)}, bf16[2,128,1024]{2,1,0:T(8,128)(2,1)S(1)}, u32[]{:S(2)}, u32[]{:S(2)}) %collective-permute-start.12) | collective-permute-done | bytes 524320 | tf_op jit(solution)/shard_map/ppermute | solution.py:237
  68.6 1.2 collective-permute-start.14
  69.9 2.1 %collective-permute-start.15 = (bf16[1,128,1024]{2,1,0:T(8,128)(2,1)S(1)}, bf16[1,128,1024]{2,1,0:T(8,128)(2,1)S(1)}, u32[]{:S(2)}, u32[]{:S(2)}) collective-permute-start(bf16[1,128,1024]{2,1,0:T(8,128)(2,1)S(1)} %get-tuple-element.32), channel_id=1, source_target_pairs={{0,16},{1,17},{2,18},{3,19},{4,20},{5,21},{6,22},{7,23},{8,24},{9,... | collective-permute-start | bytes 786440 | tf_op jit(solution)/shard_map/ppermute | solution.py:237
  71.9 2.2 %collective-permute-done.11 = bf16[1,128,1024]{2,1,0:T(8,128)(2,1)S(1)} collective-permute-done((bf16[1,128,1024]{2,1,0:T(8,128)(2,1)S(1)}, bf16[1,128,1024]{2,1,0:T(8,128)(2,1)S(1)}, u32[]{:S(2)}, u32[]{:S(2)}) %collective-permute-start.11) | collective-permute-done | bytes 262176 | tf_op jit(solution)/shard_map/ppermute | solution.py:237
  74.2 2.5 %collective-permute-done.14 = bf16[1,128,1024]{2,1,0:T(8,128)(2,1)S(1)} collective-permute-done((bf16[1,128,1024]{2,1,0:T(8,128)(2,1)S(1)}, bf16[1,128,1024]{2,1,0:T(8,128)(2,1)S(1)}, u32[]{:S(2)}, u32[]{:S(2)}) %collective-permute-start.14) | collective-permute-done | bytes 262176 | tf_op jit(solution)/shard_map/ppermute | solution.py:237
  76.7 1.8 %collective-permute-done.15 = bf16[1,128,1024]{2,1,0:T(8,128)(2,1)S(1)} collective-permute-done((bf16[1,128,1024]{2,1,0:T(8,128)(2,1)S(1)}, bf16[1,128,1024]{2,1,0:T(8,128)(2,1)S(1)}, u32[]{:S(2)}, u32[]{:S(2)}) %collective-permute-start.15) | collective-permute-done | bytes 262176 | tf_op jit(solution)/shard_map/ppermute | solution.py:237
  78.5 0.3 hidden.2.refs_0_
  78.8 1.7 %collective-permute-start.16 = (bf16[64,2048]{1,0:T(8,128)(2,1)S(1)}, bf16[64,2048]{1,0:T(8,128)(2,1)S(1)}, u32[]{:S(2)}, u32[]{:S(2)}) collective-permute-start(bf16[64,2048]{1,0:T(8,128)(2,1)S(1)} %hidden.2.refs_0_), channel_id=1, source_target_pairs={{0,8},{1,17},{2,10},{3,19},{4,12},{5,21},{6,14},{7,23},{8,0},{9,25... | collective-permute-start | bytes 786440 | tf_op jit(solution)/shard_map/ppermute | solution.py:237
  80.5 0.3 hidden.3.refs_0_
  80.8 0.4 collective-permute-start.19
  81.2 1.7 %collective-permute-start.17 = (bf16[64,2048]{1,0:T(8,128)(2,1)S(1)}, bf16[64,2048]{1,0:T(8,128)(2,1)S(1)}, u32[]{:S(2)}, u32[]{:S(2)}) collective-permute-start(bf16[64,2048]{1,0:T(8,128)(2,1)S(1)} %hidden.2.refs_0_), channel_id=1, source_target_pairs={{0,16},{1,9},{2,18},{3,11},{4,20},{5,13},{6,22},{7,15},{8,24},{9,1... | collective-permute-start | bytes 786440 | tf_op jit(solution)/shard_map/ppermute | solution.py:237
  82.9 4.9 %collective-permute-done.16.refs_1_ = bf16[64,2048]{1,0:T(8,128)(2,1)S(1)} collective-permute-done((bf16[64,2048]{1,0:T(8,128)(2,1)S(1)}, bf16[64,2048]{1,0:T(8,128)(2,1)S(1)}, u32[]{:S(2)}, u32[]{:S(2)}) %collective-permute-start.16) | collective-permute-done | bytes 262176 | tf_op jit(solution)/shard_map/ppermute | solution.py:237
  87.9 1.8 %collective-permute-start.18 = (bf16[64,2048]{1,0:T(8,128)(2,1)S(1)}, bf16[64,2048]{1,0:T(8,128)(2,1)S(1)}, u32[]{:S(2)}, u32[]{:S(2)}) collective-permute-start(bf16[64,2048]{1,0:T(8,128)(2,1)S(1)} %collective-permute-done.16.refs_1_), channel_id=1, source_target_pairs={{0,16},{1,9},{2,18},{3,11},{4,20},{5,13},{6,22},{7,15},{8,24},{9,1... | collective-permute-start | bytes 786440 | tf_op jit(solution)/shard_map/ppermute | solution.py:237
  89.9 3.6 %collective-permute-done.19.refs_0_.refs_1_ = bf16[64,2048]{1,0:T(8,128)(2,1)S(1)} collective-permute-done((bf16[64,2048]{1,0:T(8,128)(2,1)S(1)}, bf16[64,2048]{1,0:T(8,128)(2,1)S(1)}, u32[]{:S(2)}, u32[]{:S(2)}) %collective-permute-start.19) | collective-permute-done | bytes 262176 | tf_op jit(solution)/shard_map/ppermute | solution.py:237
  93.5 1.8 %collective-permute-start.21 = (bf16[64,2048]{1,0:T(8,128)(2,1)S(1)}, bf16[64,2048]{1,0:T(8,128)(2,1)S(1)}, u32[]{:S(2)}, u32[]{:S(2)}) collective-permute-start(bf16[64,2048]{1,0:T(8,128)(2,1)S(1)} %collective-permute-done.19.refs_0_.refs_1_), channel_id=1, source_target_pairs={{0,16},{1,9},{2,18},{3,11},{4,20},{5,13},{6,22},{7,15},{8,24},{9,1... | collective-permute-start | bytes 786440 | tf_op jit(solution)/shard_map/ppermute | solution.py:237
  95.5 6.2 %down.2 = (f32[4,32,2048]{2,1,0:T(8,128)S(1)}, bf16[4,32,2048]{2,1,0:T(8,128)(2,1)S(1)}) custom-call(s32[9]{0:T(128)S(1)} %stack.33.place_ref, bf16[64,2048]{1,0:T(8,128)(2,1)S(1)} %hidden.2.refs_0_, bf16[64,2048]{1,0:T(8,128)(2,1)S(1)} %collective-permute-done.16.refs_1_, bf16[64,2048]{1,0:T(8,128)(2,1)S(1)} %collective-permute-done.17.refs_2_, ...), custom_call_target="tpu_custom_call" | custom-call | flops 2147483648 | bytes 8388608 | tf_op jit(solution)/shard_map/down/pallas_call | solution.py:173
  101.9 1.9 %collective-permute-done.22 = bf16[4,32,2048]{2,1,0:T(8,128)(2,1)S(1)} collective-permute-done((bf16[4,32,2048]{2,1,0:T(8,128)(2,1)S(1)}, bf16[4,32,2048]{2,1,0:T(8,128)(2,1)S(1)}, u32[]{:S(2)}, u32[]{:S(2)}) %collective-permute-start.22) | collective-permute-done | bytes 524320 | tf_op jit(solution)/shard_map/ppermute | solution.py:237
  103.8 2.9 %collective-permute-start.24 = (bf16[32,2048]{1,0:T(8,128)(2,1)S(1)}, bf16[32,2048]{1,0:T(8,128)(2,1)S(1)}, u32[]{:S(2)}, u32[]{:S(2)}) collective-permute-start(bf16[32,2048]{1,0:T(8,128)(2,1)S(1)} %get-tuple-element.39), channel_id=1, source_target_pairs={{0,4},{1,5},{2,6},{3,7},{4,0},{5,1},{6,2},{7,3},{8,12},{9,13},{10,... | collective-permute-start | bytes 393224 | tf_op jit(solution)/shard_map/ppermute | solution.py:237
  106.8 6.2 %down.3 = (f32[4,32,2048]{2,1,0:T(8,128)S(1)}, bf16[4,32,2048]{2,1,0:T(8,128)(2,1)S(1)}) custom-call(s32[9]{0:T(128)S(1)} %stack.33.place_ref, bf16[64,2048]{1,0:T(8,128)(2,1)S(1)} %hidden.3.refs_0_, bf16[64,2048]{1,0:T(8,128)(2,1)S(1)} %collective-permute-done.19.refs_0_.refs_1_, bf16[64,2048]{1,0:T(8,128)(2,1)S(1)} %collective-permute-done.20.refs_1_.refs_2_, ...), custom_call_target="tpu_custom_call" | custom-call | flops 2147483648 | bytes 8388608 | tf_op jit(solution)/shard_map/down/pallas_call | solution.py:173
  113.0 0.4 collective-permute-done.24.refs_0_
  113.5 1.3 collective-permute-start.23
  114.7 2.4 %collective-permute-start.25 = (bf16[32,2048]{1,0:T(8,128)(2,1)S(1)}, bf16[32,2048]{1,0:T(8,128)(2,1)S(1)}, u32[]{:S(2)}, u32[]{:S(2)}) collective-permute-start(bf16[32,2048]{1,0:T(8,128)(2,1)S(1)} %get-tuple-element.38), channel_id=1, source_target_pairs={{0,6},{1,7},{2,4},{3,5},{4,2},{5,3},{6,0},{7,1},{8,14},{9,15},{10,... | collective-permute-start | bytes 393224 | tf_op jit(solution)/shard_map/ppermute | solution.py:237
  117.3 1.1 collective-permute-start.27
  118.4 0.9 collective-permute-start.29
  119.3 1.5 %collective-permute-start.28 = (bf16[32,2048]{1,0:T(8,128)(2,1)S(1)}, bf16[32,2048]{1,0:T(8,128)(2,1)S(1)}, u32[]{:S(2)}, u32[]{:S(2)}) collective-permute-start(bf16[32,2048]{1,0:T(8,128)(2,1)S(1)} %get-tuple-element.42), channel_id=1, source_target_pairs={{0,4},{1,5},{2,6},{3,7},{4,0},{5,1},{6,2},{7,3},{8,12},{9,13},{10,... | collective-permute-start | bytes 393224 | tf_op jit(solution)/shard_map/ppermute | solution.py:237
  120.8 3.5 %collective-permute-done.25 = bf16[32,2048]{1,0:T(8,128)(2,1)S(1)} collective-permute-done((bf16[32,2048]{1,0:T(8,128)(2,1)S(1)}, bf16[32,2048]{1,0:T(8,128)(2,1)S(1)}, u32[]{:S(2)}, u32[]{:S(2)}) %collective-permute-start.25) | collective-permute-done | bytes 131104 | tf_op jit(solution)/shard_map/ppermute | solution.py:237
  124.4 1.2 collective-permute-done.27
  125.6 4.4 %collective-permute-done.29 = bf16[32,2048]{1,0:T(8,128)(2,1)S(1)} collective-permute-done((bf16[32,2048]{1,0:T(8,128)(2,1)S(1)}, bf16[32,2048]{1,0:T(8,128)(2,1)S(1)}, u32[]{:S(2)}, u32[]{:S(2)}) %collective-permute-start.29) | collective-permute-done | bytes 131104 | tf_op jit(solution)/shard_map/ppermute | solution.py:237
  130.0 5.5 %collective-permute-done.28 = bf16[32,2048]{1,0:T(8,128)(2,1)S(1)} collective-permute-done((bf16[32,2048]{1,0:T(8,128)(2,1)S(1)}, bf16[32,2048]{1,0:T(8,128)(2,1)S(1)}, u32[]{:S(2)}, u32[]{:S(2)}) %collective-permute-start.28) | collective-permute-done | bytes 131104 | tf_op jit(solution)/shard_map/ppermute | solution.py:237
  135.6 0.7 pad_maximum_fusion
  (38 shorter events, 1.5 us)
Async XLA Ops:
  0.0 13.1 %collective-permute-start.1 = (bf16[128,1024]{1,0:T(8,128)(2,1)}, bf16[128,1024]{1,0:T(8,128)(2,1)S(1)}, u32[]{:S(2)}, u32[]{:S(2)}) collective-permute-start(bf16[128,1024]{1,0:T(8,128)(2,1)} %param.7), channel_id=1, source_target_pairs={{0,2},{1,3},{2,10},{3,11},{4,18},{5,19},{6,26},{7,27},{8,0},{9,1},... | collective-permute-start | bytes 786440 | tf_op jit(solution)/shard_map/ppermute | solution.py:237
  3.0 10.2 %collective-permute-start = (bf16[128,1024]{1,0:T(8,128)(2,1)}, bf16[128,1024]{1,0:T(8,128)(2,1)S(1)}, u32[]{:S(2)}, u32[]{:S(2)}) collective-permute-start(bf16[128,1024]{1,0:T(8,128)(2,1)} %param.7), channel_id=1, source_target_pairs={{0,0},{1,1},{2,8},{3,9},{4,16},{5,17},{6,24},{7,25},{8,2},{9,3},{1... | collective-permute-start | bytes 786440 | tf_op jit(solution)/shard_map/ppermute | solution.py:237
  4.6 15.8 %collective-permute-start.3 = (bf16[128,1024]{1,0:T(8,128)(2,1)}, bf16[128,1024]{1,0:T(8,128)(2,1)S(1)}, u32[]{:S(2)}, u32[]{:S(2)}) collective-permute-start(bf16[128,1024]{1,0:T(8,128)(2,1)} %param.7), channel_id=1, source_target_pairs={{0,6},{1,7},{2,14},{3,15},{4,22},{5,23},{6,30},{7,31},{8,4},{9,5},... | collective-permute-start | bytes 786440 | tf_op jit(solution)/shard_map/ppermute | solution.py:237
  11.6 12.7 %collective-permute-start.2 = (bf16[128,1024]{1,0:T(8,128)(2,1)}, bf16[128,1024]{1,0:T(8,128)(2,1)S(1)}, u32[]{:S(2)}, u32[]{:S(2)}) collective-permute-start(bf16[128,1024]{1,0:T(8,128)(2,1)} %param.7), channel_id=1, source_target_pairs={{0,4},{1,5},{2,12},{3,13},{4,20},{5,21},{6,28},{7,29},{8,6},{9,7},... | collective-permute-start | bytes 786440 | tf_op jit(solution)/shard_map/ppermute | solution.py:237
  13.1 11.5 %collective-permute-start.5 = (bf16[128,1024]{1,0:T(8,128)(2,1)S(1)}, bf16[128,1024]{1,0:T(8,128)(2,1)S(1)}, u32[]{:S(2)}, u32[]{:S(2)}) collective-permute-start(bf16[128,1024]{1,0:T(8,128)(2,1)S(1)} %collective-permute-done.1.refs_1_), channel_id=1, source_target_pairs={{0,1},{1,0},{2,3},{3,2},{4,5},{5,4},{6,7},{7,6},{8,9},{9,8},{10,11... | collective-permute-start | bytes 786440 | tf_op jit(solution)/shard_map/ppermute | solution.py:237
  13.2 11.4 %collective-permute-start.4 = (bf16[128,1024]{1,0:T(8,128)(2,1)S(1)}, bf16[128,1024]{1,0:T(8,128)(2,1)S(1)}, u32[]{:S(2)}, u32[]{:S(2)}) collective-permute-start(bf16[128,1024]{1,0:T(8,128)(2,1)S(1)} %collective-permute-done.refs_0_), channel_id=1, source_target_pairs={{0,1},{1,0},{2,3},{3,2},{4,5},{5,4},{6,7},{7,6},{8,9},{9,8},{10,11... | collective-permute-start | bytes 786440 | tf_op jit(solution)/shard_map/ppermute | solution.py:237
  20.4 4.2 %collective-permute-start.7 = (bf16[128,1024]{1,0:T(8,128)(2,1)S(1)}, bf16[128,1024]{1,0:T(8,128)(2,1)S(1)}, u32[]{:S(2)}, u32[]{:S(2)}) collective-permute-start(bf16[128,1024]{1,0:T(8,128)(2,1)S(1)} %collective-permute-done.3.refs_3_), channel_id=1, source_target_pairs={{0,1},{1,0},{2,3},{3,2},{4,5},{5,4},{6,7},{7,6},{8,9},{9,8},{10,11... | collective-permute-start | bytes 786440 | tf_op jit(solution)/shard_map/ppermute | solution.py:237
  24.3 1.5 %collective-permute-start.6 = (bf16[128,1024]{1,0:T(8,128)(2,1)S(1)}, bf16[128,1024]{1,0:T(8,128)(2,1)S(1)}, u32[]{:S(2)}, u32[]{:S(2)}) collective-permute-start(bf16[128,1024]{1,0:T(8,128)(2,1)S(1)} %collective-permute-done.2.refs_2_), channel_id=1, source_target_pairs={{0,1},{1,0},{2,3},{3,2},{4,5},{5,4},{6,7},{7,6},{8,9},{9,8},{10,11... | collective-permute-start | bytes 786440 | tf_op jit(solution)/shard_map/ppermute | solution.py:237
  33.7 20.0 %collective-permute-start.9 = (bf16[2,128,1024]{2,1,0:T(8,128)(2,1)S(1)}, bf16[2,128,1024]{2,1,0:T(8,128)(2,1)S(1)}, u32[]{:S(2)}, u32[]{:S(2)}) collective-permute-start(bf16[2,128,1024]{2,1,0:T(8,128)(2,1)S(1)} %get-tuple-element.24), channel_id=1, source_target_pairs={{0,8},{1,9},{2,10},{3,11},{4,12},{5,13},{6,14},{7,15},{8,0},{9,1},... | collective-permute-start | bytes 1572872 | tf_op jit(solution)/shard_map/ppermute | solution.py:237
  36.0 20.4 %collective-permute-start.8 = (bf16[2,128,1024]{2,1,0:T(8,128)(2,1)S(1)}, bf16[2,128,1024]{2,1,0:T(8,128)(2,1)S(1)}, u32[]{:S(2)}, u32[]{:S(2)}) collective-permute-start(bf16[2,128,1024]{2,1,0:T(8,128)(2,1)S(1)} %get-tuple-element.22.refs_12_), channel_id=1, source_target_pairs={{0,16},{1,17},{2,18},{3,19},{4,20},{5,21},{6,22},{7,23},{8,24},{9,... | collective-permute-start | bytes 1572872 | tf_op jit(solution)/shard_map/ppermute | solution.py:237
  51.7 14.9 %collective-permute-start.13 = (bf16[2,128,1024]{2,1,0:T(8,128)(2,1)S(1)}, bf16[2,128,1024]{2,1,0:T(8,128)(2,1)S(1)}, u32[]{:S(2)}, u32[]{:S(2)}) collective-permute-start(bf16[2,128,1024]{2,1,0:T(8,128)(2,1)S(1)} %get-tuple-element.30), channel_id=1, source_target_pairs={{0,8},{1,9},{2,10},{3,11},{4,12},{5,13},{6,14},{7,15},{8,0},{9,1},... | collective-permute-start | bytes 1572872 | tf_op jit(solution)/shard_map/ppermute | solution.py:237
  53.7 14.9 %collective-permute-start.12 = (bf16[2,128,1024]{2,1,0:T(8,128)(2,1)S(1)}, bf16[2,128,1024]{2,1,0:T(8,128)(2,1)S(1)}, u32[]{:S(2)}, u32[]{:S(2)}) collective-permute-start(bf16[2,128,1024]{2,1,0:T(8,128)(2,1)S(1)} %get-tuple-element.25.refs_4_), channel_id=1, source_target_pairs={{0,16},{1,17},{2,18},{3,19},{4,20},{5,21},{6,22},{7,23},{8,24},{9,... | collective-permute-start | bytes 1572872 | tf_op jit(solution)/shard_map/ppermute | solution.py:237
  56.5 17.7 %collective-permute-start.11 = (bf16[1,128,1024]{2,1,0:T(8,128)(2,1)S(1)}, bf16[1,128,1024]{2,1,0:T(8,128)(2,1)S(1)}, u32[]{:S(2)}, u32[]{:S(2)}) collective-permute-start(bf16[1,128,1024]{2,1,0:T(8,128)(2,1)S(1)} %get-tuple-element.27), channel_id=1, source_target_pairs={{0,16},{1,17},{2,18},{3,19},{4,20},{5,21},{6,22},{7,23},{8,24},{9,... | collective-permute-start | bytes 786440 | tf_op jit(solution)/shard_map/ppermute | solution.py:237
  58.7 15.4 %collective-permute-start.10 = (bf16[1,128,1024]{2,1,0:T(8,128)(2,1)S(1)}, bf16[1,128,1024]{2,1,0:T(8,128)(2,1)S(1)}, u32[]{:S(2)}, u32[]{:S(2)}) collective-permute-start(bf16[1,128,1024]{2,1,0:T(8,128)(2,1)S(1)} %get-tuple-element.26.refs_4_), channel_id=1, source_target_pairs={{0,8},{1,9},{2,10},{3,11},{4,12},{5,13},{6,14},{7,15},{8,0},{9,1},... | collective-permute-start | bytes 786440 | tf_op jit(solution)/shard_map/ppermute | solution.py:237
  68.6 26.7 %copy-start = (s32[16,16]{1,0:T(8,128)S(1)}, s32[16,16]{1,0:T(8,128)}, u32[]{:S(2)}) copy-start(s32[16,16]{1,0:T(8,128)} %param.13) | copy-start | bytes 3076
  68.6 8.0 %collective-permute-start.14 = (bf16[1,128,1024]{2,1,0:T(8,128)(2,1)S(1)}, bf16[1,128,1024]{2,1,0:T(8,128)(2,1)S(1)}, u32[]{:S(2)}, u32[]{:S(2)}) collective-permute-start(bf16[1,128,1024]{2,1,0:T(8,128)(2,1)S(1)} %get-tuple-element.31), channel_id=1, source_target_pairs={{0,8},{1,9},{2,10},{3,11},{4,12},{5,13},{6,14},{7,15},{8,0},{9,1},... | collective-permute-start | bytes 786440 | tf_op jit(solution)/shard_map/ppermute | solution.py:237
  69.9 8.6 %collective-permute-start.15 = (bf16[1,128,1024]{2,1,0:T(8,128)(2,1)S(1)}, bf16[1,128,1024]{2,1,0:T(8,128)(2,1)S(1)}, u32[]{:S(2)}, u32[]{:S(2)}) collective-permute-start(bf16[1,128,1024]{2,1,0:T(8,128)(2,1)S(1)} %get-tuple-element.32), channel_id=1, source_target_pairs={{0,16},{1,17},{2,18},{3,19},{4,20},{5,21},{6,22},{7,23},{8,24},{9,... | collective-permute-start | bytes 786440 | tf_op jit(solution)/shard_map/ppermute | solution.py:237
  78.8 9.1 %collective-permute-start.16 = (bf16[64,2048]{1,0:T(8,128)(2,1)S(1)}, bf16[64,2048]{1,0:T(8,128)(2,1)S(1)}, u32[]{:S(2)}, u32[]{:S(2)}) collective-permute-start(bf16[64,2048]{1,0:T(8,128)(2,1)S(1)} %hidden.2.refs_0_), channel_id=1, source_target_pairs={{0,8},{1,17},{2,10},{3,19},{4,12},{5,21},{6,14},{7,23},{8,0},{9,25... | collective-permute-start | bytes 786440 | tf_op jit(solution)/shard_map/ppermute | solution.py:237
  80.8 12.7 %collective-permute-start.19 = (bf16[64,2048]{1,0:T(8,128)(2,1)S(1)}, bf16[64,2048]{1,0:T(8,128)(2,1)S(1)}, u32[]{:S(2)}, u32[]{:S(2)}) collective-permute-start(bf16[64,2048]{1,0:T(8,128)(2,1)S(1)} %hidden.3.refs_0_), channel_id=1, source_target_pairs={{0,8},{1,17},{2,10},{3,19},{4,12},{5,21},{6,14},{7,23},{8,0},{9,25... | collective-permute-start | bytes 786440 | tf_op jit(solution)/shard_map/ppermute | solution.py:237
  81.2 14.3 %collective-permute-start.17 = (bf16[64,2048]{1,0:T(8,128)(2,1)S(1)}, bf16[64,2048]{1,0:T(8,128)(2,1)S(1)}, u32[]{:S(2)}, u32[]{:S(2)}) collective-permute-start(bf16[64,2048]{1,0:T(8,128)(2,1)S(1)} %hidden.2.refs_0_), channel_id=1, source_target_pairs={{0,16},{1,9},{2,18},{3,11},{4,20},{5,13},{6,22},{7,15},{8,24},{9,1... | collective-permute-start | bytes 786440 | tf_op jit(solution)/shard_map/ppermute | solution.py:237
  87.9 7.6 %collective-permute-start.18 = (bf16[64,2048]{1,0:T(8,128)(2,1)S(1)}, bf16[64,2048]{1,0:T(8,128)(2,1)S(1)}, u32[]{:S(2)}, u32[]{:S(2)}) collective-permute-start(bf16[64,2048]{1,0:T(8,128)(2,1)S(1)} %collective-permute-done.16.refs_1_), channel_id=1, source_target_pairs={{0,16},{1,9},{2,18},{3,11},{4,20},{5,13},{6,22},{7,15},{8,24},{9,1... | collective-permute-start | bytes 786440 | tf_op jit(solution)/shard_map/ppermute | solution.py:237
  89.7 12.1 %collective-permute-start.20 = (bf16[64,2048]{1,0:T(8,128)(2,1)S(1)}, bf16[64,2048]{1,0:T(8,128)(2,1)S(1)}, u32[]{:S(2)}, u32[]{:S(2)}) collective-permute-start(bf16[64,2048]{1,0:T(8,128)(2,1)S(1)} %hidden.3.refs_0_), channel_id=1, source_target_pairs={{0,16},{1,9},{2,18},{3,11},{4,20},{5,13},{6,22},{7,15},{8,24},{9,1... | collective-permute-start | bytes 786440 | tf_op jit(solution)/shard_map/ppermute | solution.py:237
  93.5 8.3 %collective-permute-start.21 = (bf16[64,2048]{1,0:T(8,128)(2,1)S(1)}, bf16[64,2048]{1,0:T(8,128)(2,1)S(1)}, u32[]{:S(2)}, u32[]{:S(2)}) collective-permute-start(bf16[64,2048]{1,0:T(8,128)(2,1)S(1)} %collective-permute-done.19.refs_0_.refs_1_), channel_id=1, source_target_pairs={{0,16},{1,9},{2,18},{3,11},{4,20},{5,13},{6,22},{7,15},{8,24},{9,1... | collective-permute-start | bytes 786440 | tf_op jit(solution)/shard_map/ppermute | solution.py:237
  101.8 2.0 %collective-permute-start.22 = (bf16[4,32,2048]{2,1,0:T(8,128)(2,1)S(1)}, bf16[4,32,2048]{2,1,0:T(8,128)(2,1)S(1)}, u32[]{:S(2)}, u32[]{:S(2)}) collective-permute-start(bf16[4,32,2048]{2,1,0:T(8,128)(2,1)S(1)} %hold.2), channel_id=1, source_target_pairs={{0,1},{1,0},{2,3},{3,2},{4,5},{5,4},{6,7},{7,6},{8,9},{9,8},{10,11... | collective-permute-start | bytes 1572872 | tf_op jit(solution)/shard_map/ppermute | solution.py:237
  103.8 9.5 %collective-permute-start.24 = (bf16[32,2048]{1,0:T(8,128)(2,1)S(1)}, bf16[32,2048]{1,0:T(8,128)(2,1)S(1)}, u32[]{:S(2)}, u32[]{:S(2)}) collective-permute-start(bf16[32,2048]{1,0:T(8,128)(2,1)S(1)} %get-tuple-element.39), channel_id=1, source_target_pairs={{0,4},{1,5},{2,6},{3,7},{4,0},{5,1},{6,2},{7,3},{8,12},{9,13},{10,... | collective-permute-start | bytes 393224 | tf_op jit(solution)/shard_map/ppermute | solution.py:237
  113.4 3.8 %collective-permute-start.26 = (bf16[4,32,2048]{2,1,0:T(8,128)(2,1)S(1)}, bf16[4,32,2048]{2,1,0:T(8,128)(2,1)S(1)}, u32[]{:S(2)}, u32[]{:S(2)}) collective-permute-start(bf16[4,32,2048]{2,1,0:T(8,128)(2,1)S(1)} %hold.3), channel_id=1, source_target_pairs={{0,1},{1,0},{2,3},{3,2},{4,5},{5,4},{6,7},{7,6},{8,9},{9,8},{10,11... | collective-permute-start | bytes 1572872 | tf_op jit(solution)/shard_map/ppermute | solution.py:237
  113.5 7.3 %collective-permute-start.23 = (bf16[32,2048]{1,0:T(8,128)(2,1)S(1)}, bf16[32,2048]{1,0:T(8,128)(2,1)S(1)}, u32[]{:S(2)}, u32[]{:S(2)}) collective-permute-start(bf16[32,2048]{1,0:T(8,128)(2,1)S(1)} %get-tuple-element.37), channel_id=1, source_target_pairs={{0,2},{1,3},{2,0},{3,1},{4,6},{5,7},{6,4},{7,5},{8,10},{9,11},{10,... | collective-permute-start | bytes 393224 | tf_op jit(solution)/shard_map/ppermute | solution.py:237
  114.7 9.6 %collective-permute-start.25 = (bf16[32,2048]{1,0:T(8,128)(2,1)S(1)}, bf16[32,2048]{1,0:T(8,128)(2,1)S(1)}, u32[]{:S(2)}, u32[]{:S(2)}) collective-permute-start(bf16[32,2048]{1,0:T(8,128)(2,1)S(1)} %get-tuple-element.38), channel_id=1, source_target_pairs={{0,6},{1,7},{2,4},{3,5},{4,2},{5,3},{6,0},{7,1},{8,14},{9,15},{10,... | collective-permute-start | bytes 393224 | tf_op jit(solution)/shard_map/ppermute | solution.py:237
  117.3 8.4 %collective-permute-start.27 = (bf16[32,2048]{1,0:T(8,128)(2,1)S(1)}, bf16[32,2048]{1,0:T(8,128)(2,1)S(1)}, u32[]{:S(2)}, u32[]{:S(2)}) collective-permute-start(bf16[32,2048]{1,0:T(8,128)(2,1)S(1)} %get-tuple-element.40), channel_id=1, source_target_pairs={{0,2},{1,3},{2,0},{3,1},{4,6},{5,7},{6,4},{7,5},{8,10},{9,11},{10,... | collective-permute-start | bytes 393224 | tf_op jit(solution)/shard_map/ppermute | solution.py:237
  118.4 11.6 %collective-permute-start.29 = (bf16[32,2048]{1,0:T(8,128)(2,1)S(1)}, bf16[32,2048]{1,0:T(8,128)(2,1)S(1)}, u32[]{:S(2)}, u32[]{:S(2)}) collective-permute-start(bf16[32,2048]{1,0:T(8,128)(2,1)S(1)} %get-tuple-element.41), channel_id=1, source_target_pairs={{0,6},{1,7},{2,4},{3,5},{4,2},{5,3},{6,0},{7,1},{8,14},{9,15},{10,... | collective-permute-start | bytes 393224 | tf_op jit(solution)/shard_map/ppermute | solution.py:237
  119.3 16.3 %collective-permute-start.28 = (bf16[32,2048]{1,0:T(8,128)(2,1)S(1)}, bf16[32,2048]{1,0:T(8,128)(2,1)S(1)}, u32[]{:S(2)}, u32[]{:S(2)}) collective-permute-start(bf16[32,2048]{1,0:T(8,128)(2,1)S(1)} %get-tuple-element.42), channel_id=1, source_target_pairs={{0,4},{1,5},{2,6},{3,7},{4,0},{5,1},{6,2},{7,3},{8,12},{9,13},{10,... | collective-permute-start | bytes 393224 | tf_op jit(solution)/shard_map/ppermute | solution.py:237

commit v15 on v13

--- a/solution.py
+++ b/solution.py
@@ -61,7 +61,7 @@
     rows, half = own[0].shape
     depth, whole = weights[0].shape
     width = whole // STRIPS
-    tile = min(width, TILE // 2)
+    tile = min(width, TILE)
     steps = width // tile
     part = pl.BlockSpec((rows, half), lambda i, *_: (0, 0))
     out = pl.BlockSpec((n // 2, rows, tile), lambda i, *_: (0, 0, i))

time: 136 us -> 136 us (level)
  no operation moved by 1% of the time
where the time goes in v15:
time: 136 us; the launch traced here: 135 us
  waiting for transfers between devices  53.2 us (39%)
  starting transfers between devices  50.1 us (37%)
  Pallas kernels  29 us (21%)
  other arithmetic  2.48 us (2%)
    ppermute x30, waiting for transfers between devices, send(): return lax.ppermute(value, AXES, perm)  53.2 us
    ppermute x30, starting transfers between devices, send(): return lax.ppermute(value, AXES, perm)  50.1 us
    pallas_call x2, Pallas kernels, project(): pl.pallas_call(functools.partial(project_kernel, n), grid_spec=pltpu.Pref...  15.7 us
    pallas_call x2, Pallas kernels, down(): pl.pallas_call(functools.partial(down_kernel, n), grid_spec=pltpu.Prefetc...  12.5 us
  transfers between devices with their start and end apart: 30, of which 16 were waited for; matrix products, arithmetic and copies ran while one was open for 2% of the time, Pallas kernels for 15%

profile of v15, /device:TPU:0, one launch (start us, length us, event | category | flops | bytes accessed | tf_op | source)
XLA Modules:
  0.0 135.5 jit_solution(13031695849617368285)
XLA Ops:
  0.0 3.0 %collective-permute-start.1 = (bf16[128,1024]{1,0:T(8,128)(2,1)}, bf16[128,1024]{1,0:T(8,128)(2,1)S(1)}, u32[]{:S(2)}, u32[]{:S(2)}) collective-permute-start(bf16[128,1024]{1,0:T(8,128)(2,1)} %param.7), channel_id=1, source_target_pairs={{0,2},{1,3},{2,10},{3,11},{4,18},{5,19},{6,26},{7,27},{8,0},{9,1},... | collective-permute-start | bytes 786440 | tf_op jit(solution)/shard_map/ppermute | solution.py:237
  3.0 1.6 %collective-permute-start = (bf16[128,1024]{1,0:T(8,128)(2,1)}, bf16[128,1024]{1,0:T(8,128)(2,1)S(1)}, u32[]{:S(2)}, u32[]{:S(2)}) collective-permute-start(bf16[128,1024]{1,0:T(8,128)(2,1)} %param.7), channel_id=1, source_target_pairs={{0,0},{1,1},{2,8},{3,9},{4,16},{5,17},{6,24},{7,25},{8,2},{9,3},{1... | collective-permute-start | bytes 786440 | tf_op jit(solution)/shard_map/ppermute | solution.py:237
  4.6 7.0 %collective-permute-start.3 = (bf16[128,1024]{1,0:T(8,128)(2,1)}, bf16[128,1024]{1,0:T(8,128)(2,1)S(1)}, u32[]{:S(2)}, u32[]{:S(2)}) collective-permute-start(bf16[128,1024]{1,0:T(8,128)(2,1)} %param.7), channel_id=1, source_target_pairs={{0,6},{1,7},{2,14},{3,15},{4,22},{5,23},{6,30},{7,31},{8,4},{9,5},... | collective-permute-start | bytes 786440 | tf_op jit(solution)/shard_map/ppermute | solution.py:237
  11.6 0.7 convert_element_type.101
  12.3 0.7 convert_element_type.102
  13.2 0.5 collective-permute-start.4
  13.7 6.7 %collective-permute-done.3.refs_3_ = bf16[128,1024]{1,0:T(8,128)(2,1)S(1)} collective-permute-done((bf16[128,1024]{1,0:T(8,128)(2,1)}, bf16[128,1024]{1,0:T(8,128)(2,1)S(1)}, u32[]{:S(2)}, u32[]{:S(2)}) %collective-permute-start.3) | collective-permute-done | bytes 262176 | tf_op jit(solution)/shard_map/ppermute | solution.py:237
  20.4 3.9 %collective-permute-done.2.refs_2_ = bf16[128,1024]{1,0:T(8,128)(2,1)S(1)} collective-permute-done((bf16[128,1024]{1,0:T(8,128)(2,1)}, bf16[128,1024]{1,0:T(8,128)(2,1)S(1)}, u32[]{:S(2)}, u32[]{:S(2)}) %collective-permute-start.2) | collective-permute-done | bytes 262176 | tf_op jit(solution)/shard_map/ppermute | solution.py:237
  24.6 1.2 collective-permute-done.6.refs_6_
  25.8 7.8 %project.2 = (f32[2,128,1024]{2,1,0:T(8,128)S(1)}, f32[2,128,1024]{2,1,0:T(8,128)S(1)}, bf16[2,128,1024]{2,1,0:T(8,128)(2,1)S(1)}, bf16[2,128,1024]{2,1,0:T(8,128)(2,1)S(1)}) custom-call(s32[9]{0:T(128)S(1)} %stack.33.place_ref, bf16[128,1024]{1,0:T(8,128)(2,1)S(1)} %collective-permute-done.refs_0_, bf16[128,1024]{1,0:T(8,128)(2,1)S(1)} %collective-permute-done.1.refs_1_, ...), custom_call_target="tpu_custom_call" | custom-call | flops 4294967296 | bytes 8388608 | tf_op jit(solution)/shard_map/project/pallas_call | solution.py:68
  33.7 2.3 %collective-permute-start.9 = (bf16[2,128,1024]{2,1,0:T(8,128)(2,1)S(1)}, bf16[2,128,1024]{2,1,0:T(8,128)(2,1)S(1)}, u32[]{:S(2)}, u32[]{:S(2)}) collective-permute-start(bf16[2,128,1024]{2,1,0:T(8,128)(2,1)S(1)} %get-tuple-element.24), channel_id=1, source_target_pairs={{0,8},{1,9},{2,10},{3,11},{4,12},{5,13},{6,14},{7,15},{8,0},{9,1},... | collective-permute-start | bytes 1572872 | tf_op jit(solution)/shard_map/ppermute | solution.py:237
  36.0 7.8 %collective-permute-start.8 = (bf16[2,128,1024]{2,1,0:T(8,128)(2,1)S(1)}, bf16[2,128,1024]{2,1,0:T(8,128)(2,1)S(1)}, u32[]{:S(2)}, u32[]{:S(2)}) collective-permute-start(bf16[2,128,1024]{2,1,0:T(8,128)(2,1)S(1)} %get-tuple-element.22.refs_12_), channel_id=1, source_target_pairs={{0,16},{1,17},{2,18},{3,19},{4,20},{5,21},{6,22},{7,23},{8,24},{9,... | collective-permute-start | bytes 1572872 | tf_op jit(solution)/shard_map/ppermute | solution.py:237
  43.8 7.8 %project.3 = (f32[2,128,1024]{2,1,0:T(8,128)S(1)}, f32[2,128,1024]{2,1,0:T(8,128)S(1)}, bf16[2,128,1024]{2,1,0:T(8,128)(2,1)S(1)}, bf16[2,128,1024]{2,1,0:T(8,128)(2,1)S(1)}) custom-call(s32[9]{0:T(128)S(1)} %stack.33.place_ref, bf16[128,1024]{1,0:T(8,128)(2,1)S(1)} %collective-permute-done.refs_0_, bf16[128,1024]{1,0:T(8,128)(2,1)S(1)} %collective-permute-done.1.refs_1_, ...), custom_call_target="tpu_custom_call" | custom-call | flops 4294967296 | bytes 8388608 | tf_op jit(solution)/shard_map/project/pallas_call | solution.py:68
  51.6 2.0 %collective-permute-start.13 = (bf16[2,128,1024]{2,1,0:T(8,128)(2,1)S(1)}, bf16[2,128,1024]{2,1,0:T(8,128)(2,1)S(1)}, u32[]{:S(2)}, u32[]{:S(2)}) collective-permute-start(bf16[2,128,1024]{2,1,0:T(8,128)(2,1)S(1)} %get-tuple-element.30), channel_id=1, source_target_pairs={{0,8},{1,9},{2,10},{3,11},{4,12},{5,13},{6,14},{7,15},{8,0},{9,1},... | collective-permute-start | bytes 1572872 | tf_op jit(solution)/shard_map/ppermute | solution.py:237
  53.6 2.7 %collective-permute-done.8.refs_1_ = bf16[2,128,1024]{2,1,0:T(8,128)(2,1)S(1)} collective-permute-done((bf16[2,128,1024]{2,1,0:T(8,128)(2,1)S(1)}, bf16[2,128,1024]{2,1,0:T(8,128)(2,1)S(1)}, u32[]{:S(2)}, u32[]{:S(2)}) %collective-permute-start.8) | collective-permute-done | bytes 524320 | tf_op jit(solution)/shard_map/ppermute | solution.py:237
  56.5 2.2 %collective-permute-start.11 = (bf16[1,128,1024]{2,1,0:T(8,128)(2,1)S(1)}, bf16[1,128,1024]{2,1,0:T(8,128)(2,1)S(1)}, u32[]{:S(2)}, u32[]{:S(2)}) collective-permute-start(bf16[1,128,1024]{2,1,0:T(8,128)(2,1)S(1)} %get-tuple-element.27), channel_id=1, source_target_pairs={{0,16},{1,17},{2,18},{3,19},{4,20},{5,21},{6,22},{7,23},{8,24},{9,... | collective-permute-start | bytes 786440 | tf_op jit(solution)/shard_map/ppermute | solution.py:237
  58.7 2.0 %collective-permute-start.10 = (bf16[1,128,1024]{2,1,0:T(8,128)(2,1)S(1)}, bf16[1,128,1024]{2,1,0:T(8,128)(2,1)S(1)}, u32[]{:S(2)}, u32[]{:S(2)}) collective-permute-start(bf16[1,128,1024]{2,1,0:T(8,128)(2,1)S(1)} %get-tuple-element.26.refs_4_), channel_id=1, source_target_pairs={{0,8},{1,9},{2,10},{3,11},{4,12},{5,13},{6,14},{7,15},{8,0},{9,1},... | collective-permute-start | bytes 786440 | tf_op jit(solution)/shard_map/ppermute | solution.py:237
  60.7 5.8 %collective-permute-done.13.refs_3_ = bf16[2,128,1024]{2,1,0:T(8,128)(2,1)S(1)} collective-permute-done((bf16[2,128,1024]{2,1,0:T(8,128)(2,1)S(1)}, bf16[2,128,1024]{2,1,0:T(8,128)(2,1)S(1)}, u32[]{:S(2)}, u32[]{:S(2)}) %collective-permute-start.13) | collective-permute-done | bytes 524320 | tf_op jit(solution)/shard_map/ppermute | solution.py:237
  66.5 2.0 %collective-permute-done.12.refs_1_ = bf16[2,128,1024]{2,1,0:T(8,128)(2,1)S(1)} collective-permute-done((bf16[2,128,1024]{2,1,0:T(8,128)(2,1)S(1)}, bf16[2,128,1024]{2,1,0:T(8,128)(2,1)S(1)}, u32[]{:S(2)}, u32[]{:S(2)}) %collective-permute-start.12) | collective-permute-done | bytes 524320 | tf_op jit(solution)/shard_map/ppermute | solution.py:237
  68.6 1.3 collective-permute-start.14
  69.9 2.1 %collective-permute-start.15 = (bf16[1,128,1024]{2,1,0:T(8,128)(2,1)S(1)}, bf16[1,128,1024]{2,1,0:T(8,128)(2,1)S(1)}, u32[]{:S(2)}, u32[]{:S(2)}) collective-permute-start(bf16[1,128,1024]{2,1,0:T(8,128)(2,1)S(1)} %get-tuple-element.32), channel_id=1, source_target_pairs={{0,16},{1,17},{2,18},{3,19},{4,20},{5,21},{6,22},{7,23},{8,24},{9,... | collective-permute-start | bytes 786440 | tf_op jit(solution)/shard_map/ppermute | solution.py:237
  71.9 2.2 %collective-permute-done.11 = bf16[1,128,1024]{2,1,0:T(8,128)(2,1)S(1)} collective-permute-done((bf16[1,128,1024]{2,1,0:T(8,128)(2,1)S(1)}, bf16[1,128,1024]{2,1,0:T(8,128)(2,1)S(1)}, u32[]{:S(2)}, u32[]{:S(2)}) %collective-permute-start.11) | collective-permute-done | bytes 262176 | tf_op jit(solution)/shard_map/ppermute | solution.py:237
  74.1 2.5 %collective-permute-done.14 = bf16[1,128,1024]{2,1,0:T(8,128)(2,1)S(1)} collective-permute-done((bf16[1,128,1024]{2,1,0:T(8,128)(2,1)S(1)}, bf16[1,128,1024]{2,1,0:T(8,128)(2,1)S(1)}, u32[]{:S(2)}, u32[]{:S(2)}) %collective-permute-start.14) | collective-permute-done | bytes 262176 | tf_op jit(solution)/shard_map/ppermute | solution.py:237
  76.6 1.9 %collective-permute-done.15 = bf16[1,128,1024]{2,1,0:T(8,128)(2,1)S(1)} collective-permute-done((bf16[1,128,1024]{2,1,0:T(8,128)(2,1)S(1)}, bf16[1,128,1024]{2,1,0:T(8,128)(2,1)S(1)}, u32[]{:S(2)}, u32[]{:S(2)}) %collective-permute-start.15) | collective-permute-done | bytes 262176 | tf_op jit(solution)/shard_map/ppermute | solution.py:237
  78.5 0.3 hidden.2.refs_0_
  78.7 1.7 %collective-permute-start.16 = (bf16[64,2048]{1,0:T(8,128)(2,1)S(1)}, bf16[64,2048]{1,0:T(8,128)(2,1)S(1)}, u32[]{:S(2)}, u32[]{:S(2)}) collective-permute-start(bf16[64,2048]{1,0:T(8,128)(2,1)S(1)} %hidden.2.refs_0_), channel_id=1, source_target_pairs={{0,8},{1,17},{2,10},{3,19},{4,12},{5,21},{6,14},{7,23},{8,0},{9,25... | collective-permute-start | bytes 786440 | tf_op jit(solution)/shard_map/ppermute | solution.py:237
  80.5 0.3 hidden.3.refs_0_
  80.8 0.4 collective-permute-start.19
  81.2 1.7 %collective-permute-start.17 = (bf16[64,2048]{1,0:T(8,128)(2,1)S(1)}, bf16[64,2048]{1,0:T(8,128)(2,1)S(1)}, u32[]{:S(2)}, u32[]{:S(2)}) collective-permute-start(bf16[64,2048]{1,0:T(8,128)(2,1)S(1)} %hidden.2.refs_0_), channel_id=1, source_target_pairs={{0,16},{1,9},{2,18},{3,11},{4,20},{5,13},{6,22},{7,15},{8,24},{9,1... | collective-permute-start | bytes 786440 | tf_op jit(solution)/shard_map/ppermute | solution.py:237
  82.9 4.9 %collective-permute-done.16.refs_1_ = bf16[64,2048]{1,0:T(8,128)(2,1)S(1)} collective-permute-done((bf16[64,2048]{1,0:T(8,128)(2,1)S(1)}, bf16[64,2048]{1,0:T(8,128)(2,1)S(1)}, u32[]{:S(2)}, u32[]{:S(2)}) %collective-permute-start.16) | collective-permute-done | bytes 262176 | tf_op jit(solution)/shard_map/ppermute | solution.py:237
  87.8 1.8 %collective-permute-start.18 = (bf16[64,2048]{1,0:T(8,128)(2,1)S(1)}, bf16[64,2048]{1,0:T(8,128)(2,1)S(1)}, u32[]{:S(2)}, u32[]{:S(2)}) collective-permute-start(bf16[64,2048]{1,0:T(8,128)(2,1)S(1)} %collective-permute-done.16.refs_1_), channel_id=1, source_target_pairs={{0,16},{1,9},{2,18},{3,11},{4,20},{5,13},{6,22},{7,15},{8,24},{9,1... | collective-permute-start | bytes 786440 | tf_op jit(solution)/shard_map/ppermute | solution.py:237
  89.7 0.2 collective-permute-start.20
  89.9 3.6 %collective-permute-done.19.refs_0_.refs_1_ = bf16[64,2048]{1,0:T(8,128)(2,1)S(1)} collective-permute-done((bf16[64,2048]{1,0:T(8,128)(2,1)S(1)}, bf16[64,2048]{1,0:T(8,128)(2,1)S(1)}, u32[]{:S(2)}, u32[]{:S(2)}) %collective-permute-start.19) | collective-permute-done | bytes 262176 | tf_op jit(solution)/shard_map/ppermute | solution.py:237
  93.5 1.8 %collective-permute-start.21 = (bf16[64,2048]{1,0:T(8,128)(2,1)S(1)}, bf16[64,2048]{1,0:T(8,128)(2,1)S(1)}, u32[]{:S(2)}, u32[]{:S(2)}) collective-permute-start(bf16[64,2048]{1,0:T(8,128)(2,1)S(1)} %collective-permute-done.19.refs_0_.refs_1_), channel_id=1, source_target_pairs={{0,16},{1,9},{2,18},{3,11},{4,20},{5,13},{6,22},{7,15},{8,24},{9,1... | collective-permute-start | bytes 786440 | tf_op jit(solution)/shard_map/ppermute | solution.py:237
  95.4 6.2 %down.2 = (f32[4,32,2048]{2,1,0:T(8,128)S(1)}, bf16[4,32,2048]{2,1,0:T(8,128)(2,1)S(1)}) custom-call(s32[9]{0:T(128)S(1)} %stack.33.place_ref, bf16[64,2048]{1,0:T(8,128)(2,1)S(1)} %hidden.2.refs_0_, bf16[64,2048]{1,0:T(8,128)(2,1)S(1)} %collective-permute-done.16.refs_1_, bf16[64,2048]{1,0:T(8,128)(2,1)S(1)} %collective-permute-done.17.refs_2_, ...), custom_call_target="tpu_custom_call" | custom-call | flops 2147483648 | bytes 8388608 | tf_op jit(solution)/shard_map/down/pallas_call | solution.py:173
  101.8 1.9 %collective-permute-done.22 = bf16[4,32,2048]{2,1,0:T(8,128)(2,1)S(1)} collective-permute-done((bf16[4,32,2048]{2,1,0:T(8,128)(2,1)S(1)}, bf16[4,32,2048]{2,1,0:T(8,128)(2,1)S(1)}, u32[]{:S(2)}, u32[]{:S(2)}) %collective-permute-start.22) | collective-permute-done | bytes 524320 | tf_op jit(solution)/shard_map/ppermute | solution.py:237
  103.8 2.9 %collective-permute-start.24 = (bf16[32,2048]{1,0:T(8,128)(2,1)S(1)}, bf16[32,2048]{1,0:T(8,128)(2,1)S(1)}, u32[]{:S(2)}, u32[]{:S(2)}) collective-permute-start(bf16[32,2048]{1,0:T(8,128)(2,1)S(1)} %get-tuple-element.38), channel_id=1, source_target_pairs={{0,4},{1,5},{2,6},{3,7},{4,0},{5,1},{6,2},{7,3},{8,12},{9,13},{10,... | collective-permute-start | bytes 393224 | tf_op jit(solution)/shard_map/ppermute | solution.py:237
  106.8 1.5 %collective-permute-start.23 = (bf16[32,2048]{1,0:T(8,128)(2,1)S(1)}, bf16[32,2048]{1,0:T(8,128)(2,1)S(1)}, u32[]{:S(2)}, u32[]{:S(2)}) collective-permute-start(bf16[32,2048]{1,0:T(8,128)(2,1)S(1)} %get-tuple-element.39), channel_id=1, source_target_pairs={{0,2},{1,3},{2,0},{3,1},{4,6},{5,7},{6,4},{7,5},{8,10},{9,11},{10,... | collective-permute-start | bytes 393224 | tf_op jit(solution)/shard_map/ppermute | solution.py:237
  108.3 6.2 %down.3 = (f32[4,32,2048]{2,1,0:T(8,128)S(1)}, bf16[4,32,2048]{2,1,0:T(8,128)(2,1)S(1)}) custom-call(s32[9]{0:T(128)S(1)} %stack.33.place_ref, bf16[64,2048]{1,0:T(8,128)(2,1)S(1)} %hidden.3.refs_0_, bf16[64,2048]{1,0:T(8,128)(2,1)S(1)} %collective-permute-done.19.refs_0_.refs_1_, bf16[64,2048]{1,0:T(8,128)(2,1)S(1)} %collective-permute-done.20.refs_1_.refs_2_, ...), custom_call_target="tpu_custom_call" | custom-call | flops 2147483648 | bytes 8388608 | tf_op jit(solution)/shard_map/down/pallas_call | solution.py:173
  114.7 2.4 %collective-permute-start.25 = (bf16[32,2048]{1,0:T(8,128)(2,1)S(1)}, bf16[32,2048]{1,0:T(8,128)(2,1)S(1)}, u32[]{:S(2)}, u32[]{:S(2)}) collective-permute-start(bf16[32,2048]{1,0:T(8,128)(2,1)S(1)} %get-tuple-element.37), channel_id=1, source_target_pairs={{0,6},{1,7},{2,4},{3,5},{4,2},{5,3},{6,0},{7,1},{8,14},{9,15},{10,... | collective-permute-start | bytes 393224 | tf_op jit(solution)/shard_map/ppermute | solution.py:237
  117.2 0.1 collective-permute-start.27
  117.3 1.8 %collective-permute-start.29 = (bf16[32,2048]{1,0:T(8,128)(2,1)S(1)}, bf16[32,2048]{1,0:T(8,128)(2,1)S(1)}, u32[]{:S(2)}, u32[]{:S(2)}) collective-permute-start(bf16[32,2048]{1,0:T(8,128)(2,1)S(1)} %get-tuple-element.41), channel_id=1, source_target_pairs={{0,6},{1,7},{2,4},{3,5},{4,2},{5,3},{6,0},{7,1},{8,14},{9,15},{10,... | collective-permute-start | bytes 393224 | tf_op jit(solution)/shard_map/ppermute | solution.py:237
  119.2 1.6 %collective-permute-start.28 = (bf16[32,2048]{1,0:T(8,128)(2,1)S(1)}, bf16[32,2048]{1,0:T(8,128)(2,1)S(1)}, u32[]{:S(2)}, u32[]{:S(2)}) collective-permute-start(bf16[32,2048]{1,0:T(8,128)(2,1)S(1)} %get-tuple-element.42), channel_id=1, source_target_pairs={{0,4},{1,5},{2,6},{3,7},{4,0},{5,1},{6,2},{7,3},{8,12},{9,13},{10,... | collective-permute-start | bytes 393224 | tf_op jit(solution)/shard_map/ppermute | solution.py:237
  120.8 2.1 %collective-permute-done.25 = bf16[32,2048]{1,0:T(8,128)(2,1)S(1)} collective-permute-done((bf16[32,2048]{1,0:T(8,128)(2,1)S(1)}, bf16[32,2048]{1,0:T(8,128)(2,1)S(1)}, u32[]{:S(2)}, u32[]{:S(2)}) %collective-permute-start.25) | collective-permute-done | bytes 131104 | tf_op jit(solution)/shard_map/ppermute | solution.py:237
  123.0 2.8 %collective-permute-done.27 = bf16[32,2048]{1,0:T(8,128)(2,1)S(1)} collective-permute-done((bf16[32,2048]{1,0:T(8,128)(2,1)S(1)}, bf16[32,2048]{1,0:T(8,128)(2,1)S(1)}, u32[]{:S(2)}, u32[]{:S(2)}) %collective-permute-start.27) | collective-permute-done | bytes 131104 | tf_op jit(solution)/shard_map/ppermute | solution.py:237
  125.8 2.8 %collective-permute-done.29 = bf16[32,2048]{1,0:T(8,128)(2,1)S(1)} collective-permute-done((bf16[32,2048]{1,0:T(8,128)(2,1)S(1)}, bf16[32,2048]{1,0:T(8,128)(2,1)S(1)}, u32[]{:S(2)}, u32[]{:S(2)}) %collective-permute-start.29) | collective-permute-done | bytes 131104 | tf_op jit(solution)/shard_map/ppermute | solution.py:237
  128.6 6.1 %collective-permute-done.28 = bf16[32,2048]{1,0:T(8,128)(2,1)S(1)} collective-permute-done((bf16[32,2048]{1,0:T(8,128)(2,1)S(1)}, bf16[32,2048]{1,0:T(8,128)(2,1)S(1)}, u32[]{:S(2)}, u32[]{:S(2)}) %collective-permute-start.28) | collective-permute-done | bytes 131104 | tf_op jit(solution)/shard_map/ppermute | solution.py:237
  134.8 0.7 pad_maximum_fusion
  (38 shorter events, 1.4 us)
Async XLA Ops:
  0.0 13.1 %collective-permute-start.1 = (bf16[128,1024]{1,0:T(8,128)(2,1)}, bf16[128,1024]{1,0:T(8,128)(2,1)S(1)}, u32[]{:S(2)}, u32[]{:S(2)}) collective-permute-start(bf16[128,1024]{1,0:T(8,128)(2,1)} %param.7), channel_id=1, source_target_pairs={{0,2},{1,3},{2,10},{3,11},{4,18},{5,19},{6,26},{7,27},{8,0},{9,1},... | collective-permute-start | bytes 786440 | tf_op jit(solution)/shard_map/ppermute | solution.py:237
  3.0 10.2 %collective-permute-start = (bf16[128,1024]{1,0:T(8,128)(2,1)}, bf16[128,1024]{1,0:T(8,128)(2,1)S(1)}, u32[]{:S(2)}, u32[]{:S(2)}) collective-permute-start(bf16[128,1024]{1,0:T(8,128)(2,1)} %param.7), channel_id=1, source_target_pairs={{0,0},{1,1},{2,8},{3,9},{4,16},{5,17},{6,24},{7,25},{8,2},{9,3},{1... | collective-permute-start | bytes 786440 | tf_op jit(solution)/shard_map/ppermute | solution.py:237
  4.6 15.8 %collective-permute-start.3 = (bf16[128,1024]{1,0:T(8,128)(2,1)}, bf16[128,1024]{1,0:T(8,128)(2,1)S(1)}, u32[]{:S(2)}, u32[]{:S(2)}) collective-permute-start(bf16[128,1024]{1,0:T(8,128)(2,1)} %param.7), channel_id=1, source_target_pairs={{0,6},{1,7},{2,14},{3,15},{4,22},{5,23},{6,30},{7,31},{8,4},{9,5},... | collective-permute-start | bytes 786440 | tf_op jit(solution)/shard_map/ppermute | solution.py:237
  11.6 12.7 %collective-permute-start.2 = (bf16[128,1024]{1,0:T(8,128)(2,1)}, bf16[128,1024]{1,0:T(8,128)(2,1)S(1)}, u32[]{:S(2)}, u32[]{:S(2)}) collective-permute-start(bf16[128,1024]{1,0:T(8,128)(2,1)} %param.7), channel_id=1, source_target_pairs={{0,4},{1,5},{2,12},{3,13},{4,20},{5,21},{6,28},{7,29},{8,6},{9,7},... | collective-permute-start | bytes 786440 | tf_op jit(solution)/shard_map/ppermute | solution.py:237
  13.1 11.5 %collective-permute-start.5 = (bf16[128,1024]{1,0:T(8,128)(2,1)S(1)}, bf16[128,1024]{1,0:T(8,128)(2,1)S(1)}, u32[]{:S(2)}, u32[]{:S(2)}) collective-permute-start(bf16[128,1024]{1,0:T(8,128)(2,1)S(1)} %collective-permute-done.1.refs_1_), channel_id=1, source_target_pairs={{0,1},{1,0},{2,3},{3,2},{4,5},{5,4},{6,7},{7,6},{8,9},{9,8},{10,11... | collective-permute-start | bytes 786440 | tf_op jit(solution)/shard_map/ppermute | solution.py:237
  13.2 11.4 %collective-permute-start.4 = (bf16[128,1024]{1,0:T(8,128)(2,1)S(1)}, bf16[128,1024]{1,0:T(8,128)(2,1)S(1)}, u32[]{:S(2)}, u32[]{:S(2)}) collective-permute-start(bf16[128,1024]{1,0:T(8,128)(2,1)S(1)} %collective-permute-done.refs_0_), channel_id=1, source_target_pairs={{0,1},{1,0},{2,3},{3,2},{4,5},{5,4},{6,7},{7,6},{8,9},{9,8},{10,11... | collective-permute-start | bytes 786440 | tf_op jit(solution)/shard_map/ppermute | solution.py:237
  20.4 4.2 %collective-permute-start.7 = (bf16[128,1024]{1,0:T(8,128)(2,1)S(1)}, bf16[128,1024]{1,0:T(8,128)(2,1)S(1)}, u32[]{:S(2)}, u32[]{:S(2)}) collective-permute-start(bf16[128,1024]{1,0:T(8,128)(2,1)S(1)} %collective-permute-done.3.refs_3_), channel_id=1, source_target_pairs={{0,1},{1,0},{2,3},{3,2},{4,5},{5,4},{6,7},{7,6},{8,9},{9,8},{10,11... | collective-permute-start | bytes 786440 | tf_op jit(solution)/shard_map/ppermute | solution.py:237
  24.3 1.5 %collective-permute-start.6 = (bf16[128,1024]{1,0:T(8,128)(2,1)S(1)}, bf16[128,1024]{1,0:T(8,128)(2,1)S(1)}, u32[]{:S(2)}, u32[]{:S(2)}) collective-permute-start(bf16[128,1024]{1,0:T(8,128)(2,1)S(1)} %collective-permute-done.2.refs_2_), channel_id=1, source_target_pairs={{0,1},{1,0},{2,3},{3,2},{4,5},{5,4},{6,7},{7,6},{8,9},{9,8},{10,11... | collective-permute-start | bytes 786440 | tf_op jit(solution)/shard_map/ppermute | solution.py:237
  33.7 20.0 %collective-permute-start.9 = (bf16[2,128,1024]{2,1,0:T(8,128)(2,1)S(1)}, bf16[2,128,1024]{2,1,0:T(8,128)(2,1)S(1)}, u32[]{:S(2)}, u32[]{:S(2)}) collective-permute-start(bf16[2,128,1024]{2,1,0:T(8,128)(2,1)S(1)} %get-tuple-element.24), channel_id=1, source_target_pairs={{0,8},{1,9},{2,10},{3,11},{4,12},{5,13},{6,14},{7,15},{8,0},{9,1},... | collective-permute-start | bytes 1572872 | tf_op jit(solution)/shard_map/ppermute | solution.py:237
  36.0 20.4 %collective-permute-start.8 = (bf16[2,128,1024]{2,1,0:T(8,128)(2,1)S(1)}, bf16[2,128,1024]{2,1,0:T(8,128)(2,1)S(1)}, u32[]{:S(2)}, u32[]{:S(2)}) collective-permute-start(bf16[2,128,1024]{2,1,0:T(8,128)(2,1)S(1)} %get-tuple-element.22.refs_12_), channel_id=1, source_target_pairs={{0,16},{1,17},{2,18},{3,19},{4,20},{5,21},{6,22},{7,23},{8,24},{9,... | collective-permute-start | bytes 1572872 | tf_op jit(solution)/shard_map/ppermute | solution.py:237
  51.6 14.9 %collective-permute-start.13 = (bf16[2,128,1024]{2,1,0:T(8,128)(2,1)S(1)}, bf16[2,128,1024]{2,1,0:T(8,128)(2,1)S(1)}, u32[]{:S(2)}, u32[]{:S(2)}) collective-permute-start(bf16[2,128,1024]{2,1,0:T(8,128)(2,1)S(1)} %get-tuple-element.30), channel_id=1, source_target_pairs={{0,8},{1,9},{2,10},{3,11},{4,12},{5,13},{6,14},{7,15},{8,0},{9,1},... | collective-permute-start | bytes 1572872 | tf_op jit(solution)/shard_map/ppermute | solution.py:237
  53.6 14.9 %collective-permute-start.12 = (bf16[2,128,1024]{2,1,0:T(8,128)(2,1)S(1)}, bf16[2,128,1024]{2,1,0:T(8,128)(2,1)S(1)}, u32[]{:S(2)}, u32[]{:S(2)}) collective-permute-start(bf16[2,128,1024]{2,1,0:T(8,128)(2,1)S(1)} %get-tuple-element.25.refs_4_), channel_id=1, source_target_pairs={{0,16},{1,17},{2,18},{3,19},{4,20},{5,21},{6,22},{7,23},{8,24},{9,... | collective-permute-start | bytes 1572872 | tf_op jit(solution)/shard_map/ppermute | solution.py:237
  56.5 17.6 %collective-permute-start.11 = (bf16[1,128,1024]{2,1,0:T(8,128)(2,1)S(1)}, bf16[1,128,1024]{2,1,0:T(8,128)(2,1)S(1)}, u32[]{:S(2)}, u32[]{:S(2)}) collective-permute-start(bf16[1,128,1024]{2,1,0:T(8,128)(2,1)S(1)} %get-tuple-element.27), channel_id=1, source_target_pairs={{0,16},{1,17},{2,18},{3,19},{4,20},{5,21},{6,22},{7,23},{8,24},{9,... | collective-permute-start | bytes 786440 | tf_op jit(solution)/shard_map/ppermute | solution.py:237
  58.7 15.4 %collective-permute-start.10 = (bf16[1,128,1024]{2,1,0:T(8,128)(2,1)S(1)}, bf16[1,128,1024]{2,1,0:T(8,128)(2,1)S(1)}, u32[]{:S(2)}, u32[]{:S(2)}) collective-permute-start(bf16[1,128,1024]{2,1,0:T(8,128)(2,1)S(1)} %get-tuple-element.26.refs_4_), channel_id=1, source_target_pairs={{0,8},{1,9},{2,10},{3,11},{4,12},{5,13},{6,14},{7,15},{8,0},{9,1},... | collective-permute-start | bytes 786440 | tf_op jit(solution)/shard_map/ppermute | solution.py:237
  68.6 26.7 %copy-start = (s32[16,16]{1,0:T(8,128)S(1)}, s32[16,16]{1,0:T(8,128)}, u32[]{:S(2)}) copy-start(s32[16,16]{1,0:T(8,128)} %param.13) | copy-start | bytes 3076
  68.6 8.0 %collective-permute-start.14 = (bf16[1,128,1024]{2,1,0:T(8,128)(2,1)S(1)}, bf16[1,128,1024]{2,1,0:T(8,128)(2,1)S(1)}, u32[]{:S(2)}, u32[]{:S(2)}) collective-permute-start(bf16[1,128,1024]{2,1,0:T(8,128)(2,1)S(1)} %get-tuple-element.31), channel_id=1, source_target_pairs={{0,8},{1,9},{2,10},{3,11},{4,12},{5,13},{6,14},{7,15},{8,0},{9,1},... | collective-permute-start | bytes 786440 | tf_op jit(solution)/shard_map/ppermute | solution.py:237
  69.9 8.6 %collective-permute-start.15 = (bf16[1,128,1024]{2,1,0:T(8,128)(2,1)S(1)}, bf16[1,128,1024]{2,1,0:T(8,128)(2,1)S(1)}, u32[]{:S(2)}, u32[]{:S(2)}) collective-permute-start(bf16[1,128,1024]{2,1,0:T(8,128)(2,1)S(1)} %get-tuple-element.32), channel_id=1, source_target_pairs={{0,16},{1,17},{2,18},{3,19},{4,20},{5,21},{6,22},{7,23},{8,24},{9,... | collective-permute-start | bytes 786440 | tf_op jit(solution)/shard_map/ppermute | solution.py:237
  78.7 9.1 %collective-permute-start.16 = (bf16[64,2048]{1,0:T(8,128)(2,1)S(1)}, bf16[64,2048]{1,0:T(8,128)(2,1)S(1)}, u32[]{:S(2)}, u32[]{:S(2)}) collective-permute-start(bf16[64,2048]{1,0:T(8,128)(2,1)S(1)} %hidden.2.refs_0_), channel_id=1, source_target_pairs={{0,8},{1,17},{2,10},{3,19},{4,12},{5,21},{6,14},{7,23},{8,0},{9,25... | collective-permute-start | bytes 786440 | tf_op jit(solution)/shard_map/ppermute | solution.py:237
  80.8 12.7 %collective-permute-start.19 = (bf16[64,2048]{1,0:T(8,128)(2,1)S(1)}, bf16[64,2048]{1,0:T(8,128)(2,1)S(1)}, u32[]{:S(2)}, u32[]{:S(2)}) collective-permute-start(bf16[64,2048]{1,0:T(8,128)(2,1)S(1)} %hidden.3.refs_0_), channel_id=1, source_target_pairs={{0,8},{1,17},{2,10},{3,19},{4,12},{5,21},{6,14},{7,23},{8,0},{9,25... | collective-permute-start | bytes 786440 | tf_op jit(solution)/shard_map/ppermute | solution.py:237
  81.2 14.3 %collective-permute-start.17 = (bf16[64,2048]{1,0:T(8,128)(2,1)S(1)}, bf16[64,2048]{1,0:T(8,128)(2,1)S(1)}, u32[]{:S(2)}, u32[]{:S(2)}) collective-permute-start(bf16[64,2048]{1,0:T(8,128)(2,1)S(1)} %hidden.2.refs_0_), channel_id=1, source_target_pairs={{0,16},{1,9},{2,18},{3,11},{4,20},{5,13},{6,22},{7,15},{8,24},{9,1... | collective-permute-start | bytes 786440 | tf_op jit(solution)/shard_map/ppermute | solution.py:237
  87.8 7.6 %collective-permute-start.18 = (bf16[64,2048]{1,0:T(8,128)(2,1)S(1)}, bf16[64,2048]{1,0:T(8,128)(2,1)S(1)}, u32[]{:S(2)}, u32[]{:S(2)}) collective-permute-start(bf16[64,2048]{1,0:T(8,128)(2,1)S(1)} %collective-permute-done.16.refs_1_), channel_id=1, source_target_pairs={{0,16},{1,9},{2,18},{3,11},{4,20},{5,13},{6,22},{7,15},{8,24},{9,1... | collective-permute-start | bytes 786440 | tf_op jit(solution)/shard_map/ppermute | solution.py:237
  89.7 12.0 %collective-permute-start.20 = (bf16[64,2048]{1,0:T(8,128)(2,1)S(1)}, bf16[64,2048]{1,0:T(8,128)(2,1)S(1)}, u32[]{:S(2)}, u32[]{:S(2)}) collective-permute-start(bf16[64,2048]{1,0:T(8,128)(2,1)S(1)} %hidden.3.refs_0_), channel_id=1, source_target_pairs={{0,16},{1,9},{2,18},{3,11},{4,20},{5,13},{6,22},{7,15},{8,24},{9,1... | collective-permute-start | bytes 786440 | tf_op jit(solution)/shard_map/ppermute | solution.py:237
  93.5 8.3 %collective-permute-start.21 = (bf16[64,2048]{1,0:T(8,128)(2,1)S(1)}, bf16[64,2048]{1,0:T(8,128)(2,1)S(1)}, u32[]{:S(2)}, u32[]{:S(2)}) collective-permute-start(bf16[64,2048]{1,0:T(8,128)(2,1)S(1)} %collective-permute-done.19.refs_0_.refs_1_), channel_id=1, source_target_pairs={{0,16},{1,9},{2,18},{3,11},{4,20},{5,13},{6,22},{7,15},{8,24},{9,1... | collective-permute-start | bytes 786440 | tf_op jit(solution)/shard_map/ppermute | solution.py:237
  101.8 2.0 %collective-permute-start.22 = (bf16[4,32,2048]{2,1,0:T(8,128)(2,1)S(1)}, bf16[4,32,2048]{2,1,0:T(8,128)(2,1)S(1)}, u32[]{:S(2)}, u32[]{:S(2)}) collective-permute-start(bf16[4,32,2048]{2,1,0:T(8,128)(2,1)S(1)} %hold.2), channel_id=1, source_target_pairs={{0,1},{1,0},{2,3},{3,2},{4,5},{5,4},{6,7},{7,6},{8,9},{9,8},{10,11... | collective-permute-start | bytes 1572872 | tf_op jit(solution)/shard_map/ppermute | solution.py:237
  103.8 10.7 %collective-permute-start.24 = (bf16[32,2048]{1,0:T(8,128)(2,1)S(1)}, bf16[32,2048]{1,0:T(8,128)(2,1)S(1)}, u32[]{:S(2)}, u32[]{:S(2)}) collective-permute-start(bf16[32,2048]{1,0:T(8,128)(2,1)S(1)} %get-tuple-element.38), channel_id=1, source_target_pairs={{0,4},{1,5},{2,6},{3,7},{4,0},{5,1},{6,2},{7,3},{8,12},{9,13},{10,... | collective-permute-start | bytes 393224 | tf_op jit(solution)/shard_map/ppermute | solution.py:237
  106.8 7.8 %collective-permute-start.23 = (bf16[32,2048]{1,0:T(8,128)(2,1)S(1)}, bf16[32,2048]{1,0:T(8,128)(2,1)S(1)}, u32[]{:S(2)}, u32[]{:S(2)}) collective-permute-start(bf16[32,2048]{1,0:T(8,128)(2,1)S(1)} %get-tuple-element.39), channel_id=1, source_target_pairs={{0,2},{1,3},{2,0},{3,1},{4,6},{5,7},{6,4},{7,5},{8,10},{9,11},{10,... | collective-permute-start | bytes 393224 | tf_op jit(solution)/shard_map/ppermute | solution.py:237
  114.6 2.5 %collective-permute-start.26 = (bf16[4,32,2048]{2,1,0:T(8,128)(2,1)S(1)}, bf16[4,32,2048]{2,1,0:T(8,128)(2,1)S(1)}, u32[]{:S(2)}, u32[]{:S(2)}) collective-permute-start(bf16[4,32,2048]{2,1,0:T(8,128)(2,1)S(1)} %hold.3), channel_id=1, source_target_pairs={{0,1},{1,0},{2,3},{3,2},{4,5},{5,4},{6,7},{7,6},{8,9},{9,8},{10,11... | collective-permute-start | bytes 1572872 | tf_op jit(solution)/shard_map/ppermute | solution.py:237
  114.7 8.2 %collective-permute-start.25 = (bf16[32,2048]{1,0:T(8,128)(2,1)S(1)}, bf16[32,2048]{1,0:T(8,128)(2,1)S(1)}, u32[]{:S(2)}, u32[]{:S(2)}) collective-permute-start(bf16[32,2048]{1,0:T(8,128)(2,1)S(1)} %get-tuple-element.37), channel_id=1, source_target_pairs={{0,6},{1,7},{2,4},{3,5},{4,2},{5,3},{6,0},{7,1},{8,14},{9,15},{10,... | collective-permute-start | bytes 393224 | tf_op jit(solution)/shard_map/ppermute | solution.py:237
  117.2 8.6 %collective-permute-start.27 = (bf16[32,2048]{1,0:T(8,128)(2,1)S(1)}, bf16[32,2048]{1,0:T(8,128)(2,1)S(1)}, u32[]{:S(2)}, u32[]{:S(2)}) collective-permute-start(bf16[32,2048]{1,0:T(8,128)(2,1)S(1)} %get-tuple-element.40), channel_id=1, source_target_pairs={{0,2},{1,3},{2,0},{3,1},{4,6},{5,7},{6,4},{7,5},{8,10},{9,11},{10,... | collective-permute-start | bytes 393224 | tf_op jit(solution)/shard_map/ppermute | solution.py:237
  117.3 11.3 %collective-permute-start.29 = (bf16[32,2048]{1,0:T(8,128)(2,1)S(1)}, bf16[32,2048]{1,0:T(8,128)(2,1)S(1)}, u32[]{:S(2)}, u32[]{:S(2)}) collective-permute-start(bf16[32,2048]{1,0:T(8,128)(2,1)S(1)} %get-tuple-element.41), channel_id=1, source_target_pairs={{0,6},{1,7},{2,4},{3,5},{4,2},{5,3},{6,0},{7,1},{8,14},{9,15},{10,... | collective-permute-start | bytes 393224 | tf_op jit(solution)/shard_map/ppermute | solution.py:237
  119.2 15.5 %collective-permute-start.28 = (bf16[32,2048]{1,0:T(8,128)(2,1)S(1)}, bf16[32,2048]{1,0:T(8,128)(2,1)S(1)}, u32[]{:S(2)}, u32[]{:S(2)}) collective-permute-start(bf16[32,2048]{1,0:T(8,128)(2,1)S(1)} %get-tuple-element.42), channel_id=1, source_target_pairs={{0,4},{1,5},{2,6},{3,7},{4,0},{5,1},{6,2},{7,3},{8,12},{9,13},{10,... | collective-permute-start | bytes 393224 | tf_op jit(solution)/shard_map/ppermute | solution.py:237
